TPU v7x, 32 devices: a whole 2x2x4 slice. The times are simulated.
32 devices in a mesh: group: 2 (over x), dp: 8 (over z, y), basis: 2 (over core).
Axes of the slice: x: 2, y: 2, z: 4, core: 2. Of those that a mesh axis runs over, the one named last changes fastest.
Arguments:
- activations: bfloat16 [16, 256, 8192], P(('group', 'dp'), None, 'basis'), parts along dimension 0, may hold values from -6 to 6
- out_grads: bfloat16 [16, 256, 28672], P(('group', 'dp'), None, 'basis'), parts along dimension 0, may hold values from -6 to 6
- input_basis: bfloat16 [8192, 384], P('basis', 'dp'), may hold values from -0.0625 to 0.0625
- output_basis: bfloat16 [28672, 384], P('basis', 'dp'), may hold values from -0.03125 to 0.03125
Outputs:
- eigenvalues: float32 [768, 384], P(('group', 'dp', 'basis')), parts along dimension 0
There are 2 independent parts, one for each index of `group`. A program takes and returns all parts, laid end to end along the dimension named above; an argument that names none is the same for every part. Nothing has to cross between parts.
All inputs are finite; a program needn't handle non-finite values.
Results may differ from a plain program's by a relative error of at most 0.0028.
Values may be sent and summed in bfloat16 or wider, within the bound.
No kernel may reach another device: no remote copies, remote signals or barrier semaphores. Data moves between devices by JAX's collectives and lax.ppermute only.
A program may use at most 128 MiB of HBM per device.

v0:
```python
import jax
import jax.numpy as jnp
from jax import lax
from jax.sharding import PartitionSpec as P

TOK = 256
K = 384


def place_cols(left, piece):
    product = jnp.dot(left, piece, preferred_element_type=jnp.float32)
    return product


def per_device(activations, out_grads, input_basis, output_basis):
    acts = activations[0]
    grads = out_grads[0]
    tokens = acts.shape[0]
    part_in = place_cols(acts, lax.all_gather(input_basis, "dp", axis=1, tiled=True))
    part_out = place_cols(grads, lax.all_gather(output_basis, "dp", axis=1, tiled=True))
    rot_in = lax.psum(part_in, "basis").astype(jnp.bfloat16)
    data_count = lax.axis_size("dp")
    panel_count = lax.axis_size("basis")
    block = K // (data_count * panel_count)
    ordered = part_out.reshape(tokens, data_count, panel_count, block)
    ordered = jnp.transpose(ordered, (0, 2, 1, 3)).reshape(tokens, K)
    rot_out = lax.psum_scatter(ordered, "basis", scatter_dimension=1, tiled=True).astype(
        jnp.bfloat16
    )
    coeff = lax.dot_general(
        rot_out, rot_in, (((0,), (0,)), ((), ())), preferred_element_type=jnp.float32
    )
    coeff = coeff / jnp.sqrt(jnp.float32(TOK))
    summed = lax.psum_scatter(coeff * coeff, "dp", scatter_dimension=0, tiled=True)
    return summed / jnp.float32(data_count)


def solution(mesh):
    in_specs = (
        P(("group", "dp"), None, "basis"),
        P(("group", "dp"), None, "basis"),
        P("basis", "dp"),
        P("basis", "dp"),
    )
    out_specs = P(("group", "dp", "basis"), None)
    return jax.shard_map(
        per_device, mesh=mesh, in_specs=in_specs, out_specs=out_specs, check_vma=False
    )
```

profile of v0, /device:TPU:0, one launch (start us, length us, event | category | flops | bytes accessed | tf_op | source)
XLA Modules:
  0.0 310.4 jit_solution(17242727995451193259)
XLA Ops:
  6.5 0.0 copy-start
  6.5 0.0 all-gather.3.cloned.1.call-start
  6.5 0.7 all-gather.3.cloned.1.call-update
  7.3 0.0 all-gather.5.cloned.1.call-start
  7.3 0.7 all-gather.5.cloned.1.call-update
  8.0 0.0 reduce-scatter.5.cloned.1.call-start
  8.1 161.5 %all-gather.3.cloned.1.call-done = bf16[14336,384]{0,1:T(8,128)(2,1)} async-done(((bf16[14336,48]{0,1:T(8,128)(2,1)}), bf16[14336,384]{0,1:T(8,128)(2,1)}) %all-gather.3.cloned.1.call-update) | async-done | bytes 11010064 | tf_op jit(solution)/shard_map/all_gather | solution.py:20
  169.5 9.8 %fusion.4 = f32[256,2,8,24]{0,3,1,2:T(8,128)S(1)} fusion(bf16[8,2,24,14336]{3,2,1,0:T(8,128)(2,1)} %bitcast.23, bf16[1,256,14336]{2,1,0:T(8,128)(2,1)} %param.5), kind=kOutput, calls=%fused_computation.4 | convolution fusion | flops 2818572288 | bytes 18743296 | tf_op jit(solution)/shard_map/dot_general | solution.py:11
  179.4 0.8 copy.6
  180.2 0.0 reduce-scatter.5.cloned.1.call-update
  180.2 0.0 reduce-scatter.7.cloned.1.call-start
  180.2 50.1 %all-gather.5.cloned.1.call-done = bf16[4096,384]{0,1:T(8,128)(2,1)} async-done(((bf16[4096,48]{0,1:T(8,128)(2,1)}), bf16[4096,384]{0,1:T(8,128)(2,1)}) %all-gather.5.cloned.1.call-update) | async-done | bytes 3145744 | tf_op jit(solution)/shard_map/all_gather | solution.py:19
  230.4 0.0 copy-done
  230.4 3.1 %fusion.2 = f32[256,384]{1,0:T(8,128)S(1)} fusion(bf16[4096,384]{0,1:T(8,128)(2,1)} %all-gather.5.cloned.1.call-done, bf16[1,256,4096]{2,1,0:T(8,128)(2,1)S(1)} %copy-done), kind=kOutput, calls=%fused_computation.2 | convolution fusion | flops 805306368 | bytes 5636096 | tf_op jit(solution)/shard_map/dot_general | solution.py:11
  233.5 4.7 %all-reduce.2 = bf16[256,384]{1,0:T(8,128)(2,1)S(1)} all-reduce(f32[256,384]{1,0:T(8,128)S(1)} %fusion.2), channel_id=1, replica_groups=mesh['group'=2,'dp'=8,'basis'=2] {'basis'}, use_global_device_ids=true, to_apply=%region_1.0 | all-reduce | flops 98304 | bytes 589824 | tf_op jit(solution)/shard_map/psum | solution.py:21
  238.3 0.9 reduce-scatter.5.cloned.1.call-done
  239.1 1.8 fusion.7
  241.0 0.0 reduce-scatter.7.cloned.1.call-update
  241.0 61.5 %reduce-scatter.7.cloned.1.call-done = f32[24,384]{1,0:T(8,128)} async-done(((f32[192,384]{1,0:T(8,128)}), f32[24,384]{1,0:T(8,128)}) %reduce-scatter.7.cloned.1.call-update) | async-done | bytes 36880
  302.5 1.4 broadcast_multiply_fusion
Async XLA Ops:
  6.5 223.8 %copy-start = (bf16[1,256,4096]{2,1,0:T(8,128)(2,1)S(1)}, bf16[1,256,4096]{2,1,0:T(8,128)(2,1)}, u32[]{:S(2)}) copy-start(bf16[1,256,4096]{2,1,0:T(8,128)(2,1)} %param.4) | copy-start | bytes 6291460
  6.5 163.0 %all-gather.3.cloned.1.call-start = ((), (), s32[]{:S(2)}) async-start(), calls=%async_computation.2 | async-start | bytes 12386304 | tf_op jit(solution)/shard_map/all_gather | solution.py:20
  7.3 223.1 %all-gather.5.cloned.1.call-start = ((), (), s32[]{:S(2)}) async-start(), calls=%async_computation.4 | async-start | bytes 3538944 | tf_op jit(solution)/shard_map/all_gather | solution.py:19
  8.0 231.1 %reduce-scatter.5.cloned.1.call-start = ((), (), s32[]{:S(2)}) async-start(), calls=%async_computation.3 | async-start | bytes 589824 | tf_op jit(solution)/shard_map/reduce_scatter | solution.py:27
  180.2 122.3 %reduce-scatter.7.cloned.1.call-start = ((), (), s32[]{:S(2)}) async-start(), calls=%async_computation.5 | async-start | bytes 331776
Sparse Core Ops, SparseCore 0:
  9.5 159.9 all-gather.2
  171.7 58.6 all-gather.4
  232.6 6.4 reduce-scatter.4
  242.6 59.7 reduce-scatter.6
where the time goes:
time: 311 us; the launch traced here: 310 us
  waiting for transfers between devices  275 us (88%)
  matrix products  14.8 us (5%)
  between operations  13.1 us (4%)
  blocking collectives  4.74 us (2%)
    all_gather x1, waiting for transfers between devices, per_device(): lax.all_gather(output_basis, 'dp', axis=1, tiled=True)  161 us
    unnamed x5, waiting for transfers between devices  62.9 us
    all_gather x1, waiting for transfers between devices, per_device(): lax.all_gather(input_basis, 'dp', axis=1, tiled=True)  50.1 us
    dot_general x2, matrix products, place_cols(): product = jnp.dot(left, piece, preferred_element_type=jnp.float32)  13 us
  transfers between devices with their start and end apart: 4, of which 4 were waited for; matrix products, arithmetic and copies ran while one was open for 4% of the time, Pallas kernels for 0%

commit v1 on v0

--- a/solution.py
+++ b/solution.py
@@ -1,10 +1,15 @@
+import functools
+
 import jax
 import jax.numpy as jnp
 from jax import lax
+from jax.experimental import pallas as pl
+from jax.experimental.pallas import tpu as pltpu
 from jax.sharding import PartitionSpec as P
 
 TOK = 256
 K = 384
+LANES = 128
 
 
 def place_cols(left, piece):
@@ -12,7 +17,7 @@
     return product
 
 
-def per_device(activations, out_grads, input_basis, output_basis):
+def per_device_any(activations, out_grads, input_basis, output_basis):
     acts = activations[0]
     grads = out_grads[0]
     tokens = acts.shape[0]
@@ -35,6 +40,175 @@
     return summed / jnp.float32(data_count)
 
 
+def nt_dot(left, right):
+    return lax.dot_general(
+        left, right, (((1,), (1,)), ((), ())), preferred_element_type=jnp.float32
+    )
+
+
+def rotate_kernel(plan, where_ref, acts_ref, grads_ref, *refs):
+    in_half, out_half, chunks = plan
+    out_ref = refs[-1]
+    own, other, tail = refs[0 : 2 * len(chunks)], refs[2 * len(chunks) : -2], refs[-2]
+    x, core = where_ref[0], where_ref[1]
+    rows = own[0].shape[0]
+    rot_in = jnp.zeros((2 * rows, acts_ref.shape[0]), jnp.float32)
+    rot_out = rot_in
+    for side, pieces in ((x, own), (1 - x, other)):
+        in_at, out_at = 0, 0
+        for c, (in_w, out_w) in enumerate(chunks):
+            both = jnp.concatenate([pieces[2 * c][...], pieces[2 * c + 1][...]], axis=0)
+            if in_w:
+                cols = pl.ds(pl.multiple_of(side * in_half + in_at, LANES), in_w)
+                rot_in += nt_dot(both[:, :in_w], acts_ref[:, cols])
+                in_at += in_w
+            if out_w:
+                cols = pl.ds(pl.multiple_of(side * out_half + out_at, LANES), out_w)
+                rot_out += nt_dot(both[:, in_w:], grads_ref[:, cols])
+                out_at += out_w
+    rot_out += nt_dot(tail[...], grads_ref[:, 2 * out_half :])
+    half = rows // 2
+    out_ref[0, : 2 * rows] = rot_in
+    out_ref[1, : 2 * rows] = rot_in
+    for shard in range(2):
+        first = rot_out[shard * rows : shard * rows + half]
+        second = rot_out[shard * rows + half : (shard + 1) * rows]
+        at = pl.ds(2 * rows + shard * half, half)
+        out_ref[0, at] = jnp.where(core == 0, first, second)
+        out_ref[1, at] = jnp.where(core == 0, second, first)
+
+
+def finish_kernel(rows, where_ref, *refs):
+    count = 4
+    keep, come = refs[:count], refs[count : 2 * count]
+    outs = refs[2 * count : -2]
+    in_ref, out_ref = refs[-2:]
+    half = rows // 2
+    for slot in range(count):
+        total = keep[slot][...] + come[slot][...]
+        for shard in range(2):
+            owner = where_ref[2 * slot + shard]
+            at = pl.ds(pl.multiple_of(owner * rows, 16), rows)
+            in_ref[at, :] = total[shard * rows : (shard + 1) * rows].astype(jnp.bfloat16)
+            place = where_ref[2 * count + 2 * slot + shard]
+            at = pl.ds(pl.multiple_of(place * half, 8), half)
+            begin = 2 * rows + shard * half
+            out_ref[at, :] = total[begin : begin + half]
+    coeff = nt_dot(out_ref[...].astype(jnp.bfloat16), in_ref[...])
+    coeff = coeff * (1.0 / TOK**0.5)
+    square = coeff * coeff
+    for place, ref in enumerate(outs):
+        ref[...] = square[place * half : (place + 1) * half]
+
+
+def per_device_plane(activations, out_grads, input_basis, output_basis):
+    acts, grads = activations[0], out_grads[0]
+    in_t, out_t = input_basis.T, output_basis.T
+    rows = in_t.shape[0]
+    tokens = acts.shape[0]
+    x = lax.axis_index("group")
+    me = lax.axis_index("dp")
+    core = lax.axis_index("basis")
+    z, y = me // 2, me % 2
+    middle = (z == 1) | (z == 2)
+
+    in_half = in_t.shape[1] // 2
+    out_half = out_t.shape[1] * 3 // 8
+    width = (in_half + out_half) // 2
+    width = -(-width // 256) * 256
+    chunks = ((in_half, width - in_half), (0, out_half - width + in_half))
+
+    def along(pairs):
+        return [(2 * a + b, 2 * c + b) for a, c in pairs for b in range(2)]
+
+    def shift(value, pairs):
+        return lax.ppermute(value, "dp", along(pairs))
+
+    def swap_y(value):
+        return lax.ppermute(value, "dp", [(i, i ^ 1) for i in range(8)])
+
+    def swap_x(value):
+        return lax.ppermute(value, "group", [(0, 1), (1, 0)])
+
+    def share(side):
+        ins = lax.dynamic_slice_in_dim(in_t, side * in_half, in_half, 1)
+        outs = lax.dynamic_slice_in_dim(out_t, side * out_half, out_half, 1)
+        cut = chunks[0][1]
+        return [jnp.concatenate([ins, outs[:, :cut]], axis=1), outs[:, cut:]]
+
+    def line(value):
+        left = shift(value, [(1, 0), (2, 1), (3, 2)])
+        right = shift(value, [(0, 1), (1, 2), (2, 3)])
+        ends = shift(jnp.where(z == 1, left, right), [(1, 0), (2, 3)])
+        mids = shift(jnp.where(z == 2, left, right), [(2, 1), (1, 2)])
+        last = shift(mids, [(1, 0), (2, 3)])
+        return (
+            jnp.where(z == 3, right, left),
+            jnp.where(middle, right, ends),
+            jnp.where(middle, mids, last),
+        )
+
+    mine = share(x)
+    theirs = share(1 - x)
+    tail = out_t[:, 2 * out_half :]
+    other_y = [swap_y(c) for c in mine]
+    tails = jnp.concatenate([tail, swap_y(tail)], axis=0)
+    both = [swap_x(c) for c in other_y]
+
+    groups = [(mine, other_y, theirs, both)]
+    lines = [line(c) for c in mine]
+    for slot in range(3):
+        have = [chunk[slot] for chunk in lines]
+        by_y = [swap_y(c) for c in have]
+        by_x = [swap_x(c) for c in have]
+        far = [swap_x(by_y[0]), swap_y(by_x[1])]
+        groups.append((have, by_y, by_x, far))
+    tails = [tails, *line(tails)]
+
+    plan = (in_half, out_half, chunks)
+    place = jnp.stack([x, core]).astype(jnp.int32)
+    vmem = pl.BlockSpec(memory_space=pltpu.VMEM)
+    keeps, sends = [], []
+    for (have, by_y, by_x, far), end in zip(groups, tails):
+        flat = [v for pair in zip(have, by_y) for v in pair]
+        flat += [v for pair in zip(by_x, far) for v in pair]
+        got = pl.pallas_call(
+            functools.partial(rotate_kernel, plan),
+            out_shape=jax.ShapeDtypeStruct((2, 3 * rows, tokens), jnp.float32),
+            in_specs=[pl.BlockSpec(memory_space=pltpu.SMEM)] + [vmem] * (len(flat) + 3),
+            out_specs=vmem,
+            compiler_params=pltpu.CompilerParams(vmem_limit_bytes=40 * 2**20),
+            cost_estimate=pl.CostEstimate(
+                flops=4 * rows * tokens * (acts.shape[1] + grads.shape[1]),
+                bytes_accessed=2 * (tokens + 2 * rows) * (acts.shape[1] + grads.shape[1]),
+                transcendentals=0,
+            ),
+            name="rotate",
+        )(place, acts, grads, *flat, end)
+        keeps.append(got[0])
+        sends.append(got[1])
+    comes = [lax.ppermute(s, "basis", [(0, 1), (1, 0)]) for s in sends]
+
+    order = jnp.array([[0, 1, 2, 3], [1, 2, 0, 3], [2, 3, 1, 0], [3, 2, 1, 0]], jnp.int32)[z]
+    owners = jnp.stack([order * 2 + y, order * 2 + 1 - y], axis=1).reshape(-1)
+    table = jnp.concatenate([owners, owners ^ me]).astype(jnp.int32)
+    squares = pl.pallas_call(
+        functools.partial(finish_kernel, rows),
+        out_shape=[jax.ShapeDtypeStruct((rows // 2, K), jnp.float32)] * 8,
+        in_specs=[pl.BlockSpec(memory_space=pltpu.SMEM)] + [vmem] * 8,
+        out_specs=[vmem] * 8,
+        scratch_shapes=[
+            pltpu.VMEM((K, tokens), jnp.bfloat16),
+            pltpu.VMEM((K // 2, tokens), jnp.float32),
+        ],
+        name="finish",
+    )(table, *keeps, *comes)
+    total = squares[0]
+    for k in range(1, 8):
+        total = total + lax.ppermute(squares[k], "dp", [(i, i ^ k) for i in range(8)])
+    return total * (1.0 / 8)
+
+
 def solution(mesh):
     in_specs = (
         P(("group", "dp"), None, "basis"),
@@ -43,6 +217,11 @@
         P("basis", "dp"),
     )
     out_specs = P(("group", "dp", "basis"), None)
+    plane = (mesh.shape["group"], mesh.shape["dp"], mesh.shape["basis"]) == (2, 8, 2)
     return jax.shard_map(
-        per_device, mesh=mesh, in_specs=in_specs, out_specs=out_specs, check_vma=False
-    )
+        per_device_plane if plane else per_device_any,
+        mesh=mesh,
+        in_specs=in_specs,
+        out_specs=out_specs,
+        check_vma=False,
+    )

time: 311 us -> 197 us (0.63)
  waiting for transfers between devices: 275 us -> 89 us
  starting transfers between devices: 0.12 us -> 64.5 us
  Pallas kernels: 0 us -> 17.2 us
  local copies, waits for them, and re-layouts: 0.78 us -> 16.2 us
  matrix products: 14.8 us -> 0 us
  between operations: 13.1 us -> 0.37 us
  other arithmetic: 1.39 us -> 8.8 us
  blocking collectives: 4.74 us -> 0 us
    all_gather x2 -> x0, waiting for transfers between devices: 212 us -> none  [the longest x1 161 us: per_device(): lax.all_gather(output_basis, 'dp', axis=1, tiled=True)]
    ppermute x0 -> x49, waiting for transfers between devices: none -> 89 us  [the longest x15 46.9 us: shift(): return lax.ppermute(value, 'dp', along(pairs))]
    ppermute x0 -> x49, starting transfers between devices: none -> 64.5 us  [the longest x15 25.9 us: shift(): return lax.ppermute(value, 'dp', along(pairs))]
    unnamed x5 -> x0, waiting for transfers between devices: 62.9 us -> none
    pallas_call x0 -> x5, Pallas kernels: none -> 17.2 us  [the longest x4 14.9 us: per_device_plane(): pl.pallas_call(functools.partial(rotate_kernel, plan), out_shape=jax.Shap...]
    dot_general x3 -> x0, matrix products: 14.8 us -> none  [the longest x2 13 us: place_cols(): product = jnp.dot(left, piece, preferred_element_type=jnp.float32)]
    slice x0 -> x5, local copies, waits for them, and re-layouts: none -> 6.48 us  [the longest x4 4.76 us: share(): return [jnp.concatenate([ins, outs[:, :cut]], axis=1), outs[:, cut:]]]
    psum x1 -> x0, blocking collectives: 4.74 us -> none  [per_device(): rot_in = lax.psum(part_in, 'basis').astype(jnp.bfloat16)]
  transfers between devices with their start and end apart: 4 -> 49, of which waited for: 4 -> 19; matrix products, arithmetic and copies ran while one was open for 4% -> 8% of each run, Pallas kernels for 0% -> 8%
where the time goes in v1:
time: 197 us; the launch traced here: 196 us
  waiting for transfers between devices  89 us (45%)
  starting transfers between devices  64.5 us (33%)
  Pallas kernels  17.2 us (9%)
  local copies, waits for them, and re-layouts  16.2 us (8%)
  other arithmetic  8.8 us (4%)
    ppermute x15, waiting for transfers between devices, shift(): return lax.ppermute(value, 'dp', along(pairs))  46.9 us
    ppermute x15, starting transfers between devices, shift(): return lax.ppermute(value, 'dp', along(pairs))  25.9 us
    ppermute x11, waiting for transfers between devices, swap_x(): return lax.ppermute(value, 'group', [(0, 1), (1, 0)])  20 us
    ppermute x12, waiting for transfers between devices, swap_y(): return lax.ppermute(value, 'dp', [(i, i ^ 1) for i in range(8)])  19.5 us
    pallas_call x4, Pallas kernels, per_device_plane(): pl.pallas_call(functools.partial(rotate_kernel, plan), out_shape=jax.Shap...  14.9 us
    ppermute x12, starting transfers between devices, swap_y(): return lax.ppermute(value, 'dp', [(i, i ^ 1) for i in range(8)])  14.7 us
    ppermute x7, starting transfers between devices, per_device_plane(): lax.ppermute(squares[k], 'dp', [(i, i ^ k) for i in range(8)])  13.5 us
    ppermute x11, starting transfers between devices, swap_x(): return lax.ppermute(value, 'group', [(0, 1), (1, 0)])  10.3 us
  transfers between devices with their start and end apart: 49, of which 19 were waited for; matrix products, arithmetic and copies ran while one was open for 8% of the time, Pallas kernels for 8%

profile of v1, /device:TPU:0, one launch (start us, length us, event | category | flops | bytes accessed | tf_op | source)
XLA Modules:
  0.0 196.1 jit_solution(1799855857631097006)
XLA Ops:
  0.0 2.2 %dynamic-slice_bitcast_fusion = (bf16[48,5376]{1,0:T(8,128)(2,1)}, bf16[48,5376]{1,0:T(8,128)(2,1)S(1)}) fusion(bf16[14336,48]{0,1:T(8,128)(2,1)} %param.8, s32[]{:T(128)S(6)} %select_n.122, s32[]{:T(128)S(6)} %select_n.120), kind=kLoop, calls=%fused_computation.6 | loop fusion | bytes 2064392 | tf_op jit(solution)/shard_map/dynamic_slice | solution.py:135
  3.7 1.8 dynamic-slice_bitcast_fusion.2
  6.4 3.0 %collective-permute-start = (bf16[48,3840]{1,0:T(8,128)(2,1)S(1)}, bf16[48,3840]{1,0:T(8,128)(2,1)}, u32[]{:S(2)}, u32[]{:S(2)}) collective-permute-start(bf16[48,3840]{1,0:T(8,128)(2,1)S(1)} %pad_maximum_fusion.1.refs_0_), channel_id=1, source_target_pairs={{0,2},{2,0},{4,6},{6,4},{8,10},{10,8},{12,14},{14,12},{1,3},{3,1},... | collective-permute-start | bytes 1105928 | tf_op jit(solution)/shard_map/ppermute | solution.py:128
  12.8 1.7 slice.56
  14.5 2.0 %collective-permute-start.4 = (bf16[48,3584]{1,0:T(8,128)(2,1)}, bf16[48,3584]{1,0:T(8,128)(2,1)}, u32[]{:S(2)}, u32[]{:S(2)}) collective-permute-start(bf16[48,3584]{1,0:T(8,128)(2,1)} %slice.56), channel_id=1, source_target_pairs={{0,2},{2,0},{4,6},{6,4},{8,10},{10,8},{12,14},{14,12},{1,3},{3,1},... | collective-permute-start | bytes 1032200 | tf_op jit(solution)/shard_map/ppermute | solution.py:128
  16.5 1.6 slice.54
  18.1 1.7 slice.55.refs_6_
  22.0 10.9 %collective-permute-done.4 = bf16[48,3584]{1,0:T(8,128)(2,1)} collective-permute-done((bf16[48,3584]{1,0:T(8,128)(2,1)}, bf16[48,3584]{1,0:T(8,128)(2,1)}, u32[]{:S(2)}, u32[]{:S(2)}) %collective-permute-start.4) | collective-permute-done | bytes 344096 | tf_op jit(solution)/shard_map/ppermute | solution.py:128
  32.9 3.7 %collective-permute-start.8 = (bf16[48,3584]{1,0:T(8,128)(2,1)}, bf16[48,3584]{1,0:T(8,128)(2,1)S(1)}, u32[]{:S(2)}, u32[]{:S(2)}) collective-permute-start(bf16[48,3584]{1,0:T(8,128)(2,1)} %slice.53.refs_2_), channel_id=1, source_target_pairs={{0,4},{2,6},{4,8},{6,10},{8,12},{10,14},{1,5},{3,7},{5,9},{7,11},{... | collective-permute-start | bytes 1032200 | tf_op jit(solution)/shard_map/ppermute | solution.py:125
  37.7 3.5 %collective-permute-start.5 = (bf16[48,3840]{1,0:T(8,128)(2,1)S(1)}, bf16[48,3840]{1,0:T(8,128)(2,1)S(1)}, u32[]{:S(2)}, u32[]{:S(2)}) collective-permute-start(bf16[48,3840]{1,0:T(8,128)(2,1)S(1)} %pad_maximum_fusion.1.refs_0_), channel_id=1, source_target_pairs={{0,4},{2,6},{4,8},{6,10},{8,12},{10,14},{1,5},{3,7},{5,9},{7,11},{... | collective-permute-start | bytes 1105928 | tf_op jit(solution)/shard_map/ppermute | solution.py:125
  41.2 4.2 %collective-permute-done.8 = bf16[48,3584]{1,0:T(8,128)(2,1)S(1)} collective-permute-done((bf16[48,3584]{1,0:T(8,128)(2,1)}, bf16[48,3584]{1,0:T(8,128)(2,1)S(1)}, u32[]{:S(2)}, u32[]{:S(2)}) %collective-permute-start.8) | collective-permute-done | bytes 344096 | tf_op jit(solution)/shard_map/ppermute | solution.py:125
  47.8 5.0 %collective-permute-start.15 = (bf16[96,3584]{1,0:T(8,128)(2,1)S(1)}, bf16[96,3584]{1,0:T(8,128)(2,1)S(1)}, u32[]{:S(2)}, u32[]{:S(2)}) collective-permute-start(bf16[96,3584]{1,0:T(8,128)(2,1)S(1)} %pad_maximum_fusion.refs_8_), channel_id=1, source_target_pairs={{0,4},{2,6},{4,8},{6,10},{8,12},{10,14},{1,5},{3,7},{5,9},{7,11},{... | collective-permute-start | bytes 2064392 | tf_op jit(solution)/shard_map/ppermute | solution.py:125
  55.6 13.1 %collective-permute-done.19 = bf16[48,3584]{1,0:T(8,128)(2,1)S(1)} collective-permute-done((bf16[48,3584]{1,0:T(8,128)(2,1)S(1)}, bf16[48,3584]{1,0:T(8,128)(2,1)S(1)}, u32[]{:S(2)}, u32[]{:S(2)}) %collective-permute-start.19) | collective-permute-done | bytes 344096 | tf_op jit(solution)/shard_map/ppermute | solution.py:125
  70.8 1.6 collective-permute-start.3
  72.3 5.8 %collective-permute-done.17 = bf16[48,3840]{1,0:T(8,128)(2,1)S(1)} collective-permute-done((bf16[48,3840]{1,0:T(8,128)(2,1)S(1)}, bf16[48,3840]{1,0:T(8,128)(2,1)S(1)}, u32[]{:S(2)}, u32[]{:S(2)}) %collective-permute-start.17) | collective-permute-done | bytes 368672 | tf_op jit(solution)/shard_map/ppermute | solution.py:125
  78.1 1.5 collective-permute-start.2
  79.7 1.8 collective-permute-done.3.refs_7_
  81.5 1.5 collective-permute-start.10
  83.0 4.1 %collective-permute-done.2.refs_5_ = bf16[48,3840]{1,0:T(8,128)(2,1)S(1)} collective-permute-done((bf16[48,3840]{1,0:T(8,128)(2,1)}, bf16[48,3840]{1,0:T(8,128)(2,1)S(1)}, u32[]{:S(2)}, u32[]{:S(2)}) %collective-permute-start.2) | collective-permute-done | bytes 368672 | tf_op jit(solution)/shard_map/ppermute | solution.py:131
  87.1 1.5 collective-permute-start.13
  88.6 4.2 %rotate.4 = f32[2,144,256]{2,1,0:T(8,128)S(1)} custom-call(s32[2]{0:T(128)S(1)} %pad_add_fusion.2.where_ref, bf16[256,4096]{1,0:T(8,128)(2,1)S(1)} %bitcast.39, bf16[256,14336]{1,0:T(8,128)(2,1)S(1)} %bitcast.35, bf16[48,3840]{1,0:T(8,128)(2,1)S(1)} %pad_maximum_fusion.1.refs_0_, bf16[48,3840]{1,0:T(8,128)(2,1)} %collective-permute-done.refs_1_, ...), custom_call_target="tpu_custom_call" | custom-call | flops 905969664 | bytes 12976128 | tf_op jit(solution)/shard_map/rotate/pallas_call | solution.py:175
  93.5 1.5 collective-permute-start.7
  95.7 1.3 collective-permute-start.30
  98.3 6.7 %collective-permute-done.7.refs_1_ = bf16[48,3840]{1,0:T(8,128)(2,1)S(1)} collective-permute-done((bf16[48,3840]{1,0:T(8,128)(2,1)S(1)}, bf16[48,3840]{1,0:T(8,128)(2,1)S(1)}, u32[]{:S(2)}, u32[]{:S(2)}) %collective-permute-start.7) | collective-permute-done | bytes 368672 | tf_op jit(solution)/shard_map/ppermute | solution.py:128
  105.1 1.5 collective-permute-start.14
  107.1 11.3 %collective-permute-done.30 = bf16[48,3584]{1,0:T(8,128)(2,1)S(1)} collective-permute-done((bf16[48,3584]{1,0:T(8,128)(2,1)S(1)}, bf16[48,3584]{1,0:T(8,128)(2,1)S(1)}, u32[]{:S(2)}, u32[]{:S(2)}) %collective-permute-start.30) | collective-permute-done | bytes 344096 | tf_op jit(solution)/shard_map/ppermute | solution.py:125
  120.9 1.5 collective-permute-start.21
  122.4 1.3 collective-permute-start.25
  123.7 8.0 %collective-permute-done.27 = bf16[48,3840]{1,0:T(8,128)(2,1)S(1)} collective-permute-done((bf16[48,3840]{1,0:T(8,128)(2,1)S(1)}, bf16[48,3840]{1,0:T(8,128)(2,1)S(1)}, u32[]{:S(2)}, u32[]{:S(2)}) %collective-permute-start.27) | collective-permute-done | bytes 368672 | tf_op jit(solution)/shard_map/ppermute | solution.py:125
  132.5 3.6 %rotate.5 = f32[2,144,256]{2,1,0:T(8,128)S(1)} custom-call(s32[2]{0:T(128)S(1)} %pad_add_fusion.2.where_ref, bf16[256,4096]{1,0:T(8,128)(2,1)S(1)} %bitcast.40, bf16[256,14336]{1,0:T(8,128)(2,1)S(1)} %bitcast.36, bf16[48,3840]{1,0:T(8,128)(2,1)S(1)} %get-tuple-element.28.refs_0_, bf16[48,3840]{1,0:T(8,128)(2,1)S(1)} %collective-permute-done.7.refs_1_, ...), custom_call_target="tpu_custom_call" | custom-call | flops 905969664 | bytes 12976128 | tf_op jit(solution)/shard_map/rotate/pallas_call | solution.py:175
  137.5 1.9 collective-permute-start.28
  139.3 4.0 %collective-permute-done.25 = bf16[96,3584]{1,0:T(8,128)(2,1)S(1)} collective-permute-done((bf16[96,3584]{1,0:T(8,128)(2,1)S(1)}, bf16[96,3584]{1,0:T(8,128)(2,1)S(1)}, u32[]{:S(2)}, u32[]{:S(2)}) %collective-permute-start.25) | collective-permute-done | bytes 688160 | tf_op jit(solution)/shard_map/ppermute | solution.py:125
  143.4 1.5 collective-permute-start.37
  145.0 5.9 %collective-permute-done.22.refs_5_ = bf16[48,3840]{1,0:T(8,128)(2,1)S(1)} collective-permute-done((bf16[48,3840]{1,0:T(8,128)(2,1)S(1)}, bf16[48,3840]{1,0:T(8,128)(2,1)S(1)}, u32[]{:S(2)}, u32[]{:S(2)}) %collective-permute-start.22) | collective-permute-done | bytes 368672 | tf_op jit(solution)/shard_map/ppermute | solution.py:131
  150.9 1.3 collective-permute-start.31
  152.2 3.6 %rotate.6 = f32[2,144,256]{2,1,0:T(8,128)S(1)} custom-call(s32[2]{0:T(128)S(1)} %pad_add_fusion.2.where_ref, bf16[256,4096]{1,0:T(8,128)(2,1)S(1)} %bitcast.41, bf16[256,14336]{1,0:T(8,128)(2,1)S(1)} %bitcast.37, bf16[48,3840]{1,0:T(8,128)(2,1)S(1)} %broadcast_select_fusion.8.refs_0_, bf16[48,3840]{1,0:T(8,128)(2,1)S(1)} %collective-permute-done.18.refs_1_, ...), custom_call_target="tpu_custom_call" | custom-call | flops 905969664 | bytes 12976128 | tf_op jit(solution)/shard_map/rotate/pallas_call | solution.py:175
  157.2 2.0 collective-permute-start.33
  159.3 1.9 collective-permute-done.31.refs_3_
  161.2 4.3 %collective-permute-done.32.refs_4_ = bf16[48,3840]{1,0:T(8,128)(2,1)S(1)} collective-permute-done((bf16[48,3840]{1,0:T(8,128)(2,1)S(1)}, bf16[48,3840]{1,0:T(8,128)(2,1)S(1)}, u32[]{:S(2)}, u32[]{:S(2)}) %collective-permute-start.32) | collective-permute-done | bytes 368672 | tf_op jit(solution)/shard_map/ppermute | solution.py:131
  165.5 3.9 %collective-permute-done.33.refs_5_ = bf16[48,3840]{1,0:T(8,128)(2,1)S(1)} collective-permute-done((bf16[48,3840]{1,0:T(8,128)(2,1)S(1)}, bf16[48,3840]{1,0:T(8,128)(2,1)S(1)}, u32[]{:S(2)}, u32[]{:S(2)}) %collective-permute-start.33) | collective-permute-done | bytes 368672 | tf_op jit(solution)/shard_map/ppermute | solution.py:131
  169.4 3.6 %rotate.7 = f32[2,144,256]{2,1,0:T(8,128)S(1)} custom-call(s32[2]{0:T(128)S(1)} %pad_add_fusion.2.where_ref, bf16[256,4096]{1,0:T(8,128)(2,1)S(1)} %bitcast.42, bf16[256,14336]{1,0:T(8,128)(2,1)S(1)} %bitcast.38, bf16[48,3840]{1,0:T(8,128)(2,1)S(1)} %broadcast_select_fusion.7.refs_0_, bf16[48,3840]{1,0:T(8,128)(2,1)S(1)} %collective-permute-done.28.refs_1_, ...), custom_call_target="tpu_custom_call" | custom-call | flops 905969664 | bytes 12976128 | tf_op jit(solution)/shard_map/rotate/pallas_call | solution.py:175
  176.4 2.3 %finish.1 = (f32[24,384]{1,0:T(8,128)}, f32[24,384]{1,0:T(8,128)}, f32[24,384]{1,0:T(8,128)}, f32[24,384]{1,0:T(8,128)}, f32[24,384]{1,0:T(8,128)}, /*index=5*/f...) custom-call(s32[16]{0:T(128)} %pad_add_fusion.1.where_ref, f32[144,256]{1,0:T(8,128)} %get-tuple-element.41.refs_0_, ...), custom_call_target="tpu_custom_call" | custom-call | tf_op jit(solution)/shard_map/finish/pallas_call | solution.py:195
  178.6 5.6 %collective-permute-start.48 = (f32[24,384]{1,0:T(8,128)}, f32[24,384]{1,0:T(8,128)S(1)}, u32[]{:S(2)}, u32[]{:S(2)}) collective-permute-start(f32[24,384]{1,0:T(8,128)} %get-tuple-element.20), channel_id=1, source_target_pairs={{0,14},{2,12},{4,10},{6,8},{8,6},{10,4},{12,2},{14,0},{1,15},{3,13... | collective-permute-start | bytes 110600 | tf_op jit(solution)/shard_map/ppermute | solution.py:208
  184.9 3.4 %collective-permute-start.45 = (f32[24,384]{1,0:T(8,128)}, f32[24,384]{1,0:T(8,128)S(1)}, u32[]{:S(2)}, u32[]{:S(2)}) collective-permute-start(f32[24,384]{1,0:T(8,128)} %get-tuple-element.17), channel_id=1, source_target_pairs={{0,8},{2,10},{4,12},{6,14},{8,0},{10,2},{12,4},{14,6},{1,9},{3,11}... | collective-permute-start | bytes 110600 | tf_op jit(solution)/shard_map/ppermute | solution.py:208
  188.4 1.5 collective-permute-start.44
  190.5 1.6 collective-permute-start.42
  192.4 1.4 collective-permute-done.44
  194.7 1.4 add_multiply_fusion
  (107 shorter events, 31.6 us)
Async XLA Ops:
  6.4 64.4 %collective-permute-start = (bf16[48,3840]{1,0:T(8,128)(2,1)S(1)}, bf16[48,3840]{1,0:T(8,128)(2,1)}, u32[]{:S(2)}, u32[]{:S(2)}) collective-permute-start(bf16[48,3840]{1,0:T(8,128)(2,1)S(1)} %pad_maximum_fusion.1.refs_0_), channel_id=1, source_target_pairs={{0,2},{2,0},{4,6},{6,4},{8,10},{10,8},{12,14},{14,12},{1,3},{3,1},... | collective-permute-start | bytes 1105928 | tf_op jit(solution)/shard_map/ppermute | solution.py:128
  9.4 38.3 %collective-permute-start.6 = (bf16[48,3840]{1,0:T(8,128)(2,1)S(1)}, bf16[48,3840]{1,0:T(8,128)(2,1)}, u32[]{:S(2)}, u32[]{:S(2)}) collective-permute-start(bf16[48,3840]{1,0:T(8,128)(2,1)S(1)} %pad_maximum_fusion.1.refs_0_), channel_id=1, source_target_pairs={{4,0},{6,2},{8,4},{10,6},{12,8},{14,10},{5,1},{7,3},{9,5},{11,7},{... | collective-permute-start | bytes 1105928 | tf_op jit(solution)/shard_map/ppermute | solution.py:125
  11.5 58.6 %collective-permute-start.1 = (bf16[48,3584]{1,0:T(8,128)(2,1)}, bf16[48,3584]{1,0:T(8,128)(2,1)}, u32[]{:S(2)}, u32[]{:S(2)}) collective-permute-start(bf16[48,3584]{1,0:T(8,128)(2,1)} %slice.53.refs_2_), channel_id=1, source_target_pairs={{0,2},{2,0},{4,6},{6,4},{8,10},{10,8},{12,14},{14,12},{1,3},{3,1},... | collective-permute-start | bytes 1032200 | tf_op jit(solution)/shard_map/ppermute | solution.py:128
  11.5 26.2 %collective-permute-start.9 = (bf16[48,3584]{1,0:T(8,128)(2,1)}, bf16[48,3584]{1,0:T(8,128)(2,1)}, u32[]{:S(2)}, u32[]{:S(2)}) collective-permute-start(bf16[48,3584]{1,0:T(8,128)(2,1)} %slice.53.refs_2_), channel_id=1, source_target_pairs={{4,0},{6,2},{8,4},{10,6},{12,8},{14,10},{5,1},{7,3},{9,5},{11,7},{... | collective-permute-start | bytes 1032200 | tf_op jit(solution)/shard_map/ppermute | solution.py:125
  14.5 18.3 %collective-permute-start.4 = (bf16[48,3584]{1,0:T(8,128)(2,1)}, bf16[48,3584]{1,0:T(8,128)(2,1)}, u32[]{:S(2)}, u32[]{:S(2)}) collective-permute-start(bf16[48,3584]{1,0:T(8,128)(2,1)} %slice.56), channel_id=1, source_target_pairs={{0,2},{2,0},{4,6},{6,4},{8,10},{10,8},{12,14},{14,12},{1,3},{3,1},... | collective-permute-start | bytes 1032200 | tf_op jit(solution)/shard_map/ppermute | solution.py:128
  32.9 12.5 %collective-permute-start.8 = (bf16[48,3584]{1,0:T(8,128)(2,1)}, bf16[48,3584]{1,0:T(8,128)(2,1)S(1)}, u32[]{:S(2)}, u32[]{:S(2)}) collective-permute-start(bf16[48,3584]{1,0:T(8,128)(2,1)} %slice.53.refs_2_), channel_id=1, source_target_pairs={{0,4},{2,6},{4,8},{6,10},{8,12},{10,14},{1,5},{3,7},{5,9},{7,11},{... | collective-permute-start | bytes 1032200 | tf_op jit(solution)/shard_map/ppermute | solution.py:125
  37.7 15.4 %collective-permute-start.5 = (bf16[48,3840]{1,0:T(8,128)(2,1)S(1)}, bf16[48,3840]{1,0:T(8,128)(2,1)S(1)}, u32[]{:S(2)}, u32[]{:S(2)}) collective-permute-start(bf16[48,3840]{1,0:T(8,128)(2,1)S(1)} %pad_maximum_fusion.1.refs_0_), channel_id=1, source_target_pairs={{0,4},{2,6},{4,8},{6,10},{8,12},{10,14},{1,5},{3,7},{5,9},{7,11},{... | collective-permute-start | bytes 1105928 | tf_op jit(solution)/shard_map/ppermute | solution.py:125
  45.4 49.7 %collective-permute-start.16 = (bf16[96,3584]{1,0:T(8,128)(2,1)S(1)}, bf16[96,3584]{1,0:T(8,128)(2,1)S(1)}, u32[]{:S(2)}, u32[]{:S(2)}) collective-permute-start(bf16[96,3584]{1,0:T(8,128)(2,1)S(1)} %pad_maximum_fusion.refs_8_), channel_id=1, source_target_pairs={{4,0},{6,2},{8,4},{10,6},{12,8},{14,10},{5,1},{7,3},{9,5},{11,7},{... | collective-permute-start | bytes 2064392 | tf_op jit(solution)/shard_map/ppermute | solution.py:125
  47.8 48.0 %collective-permute-start.15 = (bf16[96,3584]{1,0:T(8,128)(2,1)S(1)}, bf16[96,3584]{1,0:T(8,128)(2,1)S(1)}, u32[]{:S(2)}, u32[]{:S(2)}) collective-permute-start(bf16[96,3584]{1,0:T(8,128)(2,1)S(1)} %pad_maximum_fusion.refs_8_), channel_id=1, source_target_pairs={{0,4},{2,6},{4,8},{6,10},{8,12},{10,14},{1,5},{3,7},{5,9},{7,11},{... | collective-permute-start | bytes 2064392 | tf_op jit(solution)/shard_map/ppermute | solution.py:125
  53.2 15.5 %collective-permute-start.19 = (bf16[48,3584]{1,0:T(8,128)(2,1)S(1)}, bf16[48,3584]{1,0:T(8,128)(2,1)S(1)}, u32[]{:S(2)}, u32[]{:S(2)}) collective-permute-start(bf16[48,3584]{1,0:T(8,128)(2,1)S(1)} %get-tuple-element.30), channel_id=1, source_target_pairs={{4,0},{6,2},{8,12},{10,14},{5,1},{7,3},{9,13},{11,15},{20,16},{22,... | collective-permute-start | bytes 1032200 | tf_op jit(solution)/shard_map/ppermute | solution.py:125
  68.7 9.4 %collective-permute-start.17 = (bf16[48,3840]{1,0:T(8,128)(2,1)S(1)}, bf16[48,3840]{1,0:T(8,128)(2,1)S(1)}, u32[]{:S(2)}, u32[]{:S(2)}) collective-permute-start(bf16[48,3840]{1,0:T(8,128)(2,1)S(1)} %get-tuple-element.27), channel_id=1, source_target_pairs={{4,0},{6,2},{8,12},{10,14},{5,1},{7,3},{9,13},{11,15},{20,16},{22,... | collective-permute-start | bytes 1105928 | tf_op jit(solution)/shard_map/ppermute | solution.py:125
  70.1 23.4 %collective-permute-start.29 = (bf16[48,3584]{1,0:T(8,128)(2,1)S(1)}, bf16[48,3584]{1,0:T(8,128)(2,1)S(1)}, u32[]{:S(2)}, u32[]{:S(2)}) collective-permute-start(bf16[48,3584]{1,0:T(8,128)(2,1)S(1)} %get-tuple-element.29), channel_id=1, source_target_pairs={{8,4},{10,6},{4,8},{6,10},{9,5},{11,7},{5,9},{7,11},{24,20},{26,22... | collective-permute-start | bytes 1032200 | tf_op jit(solution)/shard_map/ppermute | solution.py:125
  70.8 10.7 %collective-permute-start.3 = (bf16[48,3584]{1,0:T(8,128)(2,1)}, bf16[48,3584]{1,0:T(8,128)(2,1)S(1)}, u32[]{:S(2)}, u32[]{:S(2)}) collective-permute-start(bf16[48,3584]{1,0:T(8,128)(2,1)} %collective-permute-done.1.refs_3_), channel_id=1, source_target_pairs={{0,16},{16,0},{1,17},{17,1},{2,18},{18,2},{3,19},{19,3},{4,20},{20... | collective-permute-start | bytes 1032200 | tf_op jit(solution)/shard_map/ppermute | solution.py:131
  78.1 9.0 %collective-permute-start.2 = (bf16[48,3840]{1,0:T(8,128)(2,1)}, bf16[48,3840]{1,0:T(8,128)(2,1)S(1)}, u32[]{:S(2)}, u32[]{:S(2)}) collective-permute-start(bf16[48,3840]{1,0:T(8,128)(2,1)} %collective-permute-done.refs_1_), channel_id=1, source_target_pairs={{0,16},{16,0},{1,17},{17,1},{2,18},{18,2},{3,19},{19,3},{4,20},{20... | collective-permute-start | bytes 1105928 | tf_op jit(solution)/shard_map/ppermute | solution.py:131
  81.5 15.7 %collective-permute-start.10 = (bf16[48,3584]{1,0:T(8,128)(2,1)S(1)}, bf16[48,3584]{1,0:T(8,128)(2,1)S(1)}, u32[]{:S(2)}, u32[]{:S(2)}) collective-permute-start(bf16[48,3584]{1,0:T(8,128)(2,1)S(1)} %get-tuple-element.31.refs_2_), channel_id=1, source_target_pairs={{0,2},{2,0},{4,6},{6,4},{8,10},{10,8},{12,14},{14,12},{1,3},{3,1},... | collective-permute-start | bytes 1032200 | tf_op jit(solution)/shard_map/ppermute | solution.py:128
  87.1 10.7 %collective-permute-start.13 = (bf16[48,3584]{1,0:T(8,128)(2,1)S(1)}, bf16[48,3584]{1,0:T(8,128)(2,1)S(1)}, u32[]{:S(2)}, u32[]{:S(2)}) collective-permute-start(bf16[48,3584]{1,0:T(8,128)(2,1)S(1)} %get-tuple-element.31.refs_2_), channel_id=1, source_target_pairs={{0,16},{16,0},{1,17},{17,1},{2,18},{18,2},{3,19},{19,3},{4,20},{20... | collective-permute-start | bytes 1032200 | tf_op jit(solution)/shard_map/ppermute | solution.py:131
  93.5 11.5 %collective-permute-start.7 = (bf16[48,3840]{1,0:T(8,128)(2,1)S(1)}, bf16[48,3840]{1,0:T(8,128)(2,1)S(1)}, u32[]{:S(2)}, u32[]{:S(2)}) collective-permute-start(bf16[48,3840]{1,0:T(8,128)(2,1)S(1)} %get-tuple-element.28.refs_0_), channel_id=1, source_target_pairs={{0,2},{2,0},{4,6},{6,4},{8,10},{10,8},{12,14},{14,12},{1,3},{3,1},... | collective-permute-start | bytes 1105928 | tf_op jit(solution)/shard_map/ppermute | solution.py:128
  95.1 11.5 %collective-permute-start.26 = (bf16[48,3840]{1,0:T(8,128)(2,1)S(1)}, bf16[48,3840]{1,0:T(8,128)(2,1)S(1)}, u32[]{:S(2)}, u32[]{:S(2)}) collective-permute-start(bf16[48,3840]{1,0:T(8,128)(2,1)S(1)} %get-tuple-element.26), channel_id=1, source_target_pairs={{8,4},{10,6},{4,8},{6,10},{9,5},{11,7},{5,9},{7,11},{24,20},{26,22... | collective-permute-start | bytes 1105928 | tf_op jit(solution)/shard_map/ppermute | solution.py:125
  95.7 22.7 %collective-permute-start.30 = (bf16[48,3584]{1,0:T(8,128)(2,1)S(1)}, bf16[48,3584]{1,0:T(8,128)(2,1)S(1)}, u32[]{:S(2)}, u32[]{:S(2)}) collective-permute-start(bf16[48,3584]{1,0:T(8,128)(2,1)S(1)} %collective-permute-done.29), channel_id=1, source_target_pairs={{4,0},{6,2},{8,12},{10,14},{5,1},{7,3},{9,13},{11,15},{20,16},{22,... | collective-permute-start | bytes 1032200 | tf_op jit(solution)/shard_map/ppermute | solution.py:125
  97.2 22.6 %collective-permute-start.11 = (bf16[48,3840]{1,0:T(8,128)(2,1)S(1)}, bf16[48,3840]{1,0:T(8,128)(2,1)S(1)}, u32[]{:S(2)}, u32[]{:S(2)}) collective-permute-start(bf16[48,3840]{1,0:T(8,128)(2,1)S(1)} %get-tuple-element.28.refs_0_), channel_id=1, source_target_pairs={{0,16},{16,0},{1,17},{17,1},{2,18},{18,2},{3,19},{19,3},{4,20},{20... | collective-permute-start | bytes 1105928 | tf_op jit(solution)/shard_map/ppermute | solution.py:131
  97.8 23.1 %collective-permute-start.20 = (bf16[48,3584]{1,0:T(8,128)(2,1)S(1)}, bf16[48,3584]{1,0:T(8,128)(2,1)S(1)}, u32[]{:S(2)}, u32[]{:S(2)}) collective-permute-start(bf16[48,3584]{1,0:T(8,128)(2,1)S(1)} %broadcast_select_fusion.13.refs_2_), channel_id=1, source_target_pairs={{0,2},{2,0},{4,6},{6,4},{8,10},{10,8},{12,14},{14,12},{1,3},{3,1},... | collective-permute-start | bytes 1032200 | tf_op jit(solution)/shard_map/ppermute | solution.py:128
  105.1 15.3 %collective-permute-start.14 = (bf16[48,3584]{1,0:T(8,128)(2,1)S(1)}, bf16[48,3584]{1,0:T(8,128)(2,1)S(1)}, u32[]{:S(2)}, u32[]{:S(2)}) collective-permute-start(bf16[48,3584]{1,0:T(8,128)(2,1)S(1)} %collective-permute-done.13.refs_6_), channel_id=1, source_target_pairs={{0,2},{2,0},{4,6},{6,4},{8,10},{10,8},{12,14},{14,12},{1,3},{3,1},... | collective-permute-start | bytes 1032200 | tf_op jit(solution)/shard_map/ppermute | solution.py:128
  106.6 15.8 %collective-permute-start.12 = (bf16[48,3840]{1,0:T(8,128)(2,1)S(1)}, bf16[48,3840]{1,0:T(8,128)(2,1)S(1)}, u32[]{:S(2)}, u32[]{:S(2)}) collective-permute-start(bf16[48,3840]{1,0:T(8,128)(2,1)S(1)} %collective-permute-done.7.refs_1_), channel_id=1, source_target_pairs={{0,16},{16,0},{1,17},{17,1},{2,18},{18,2},{3,19},{19,3},{4,20},{20... | collective-permute-start | bytes 1105928 | tf_op jit(solution)/shard_map/ppermute | solution.py:131
  118.4 13.3 %collective-permute-start.27 = (bf16[48,3840]{1,0:T(8,128)(2,1)S(1)}, bf16[48,3840]{1,0:T(8,128)(2,1)S(1)}, u32[]{:S(2)}, u32[]{:S(2)}) collective-permute-start(bf16[48,3840]{1,0:T(8,128)(2,1)S(1)} %collective-permute-done.26), channel_id=1, source_target_pairs={{4,0},{6,2},{8,12},{10,14},{5,1},{7,3},{9,13},{11,15},{20,16},{22,... | collective-permute-start | bytes 1105928 | tf_op jit(solution)/shard_map/ppermute | solution.py:125
  119.8 16.9 %collective-permute-start.23 = (bf16[48,3584]{1,0:T(8,128)(2,1)S(1)}, bf16[48,3584]{1,0:T(8,128)(2,1)S(1)}, u32[]{:S(2)}, u32[]{:S(2)}) collective-permute-start(bf16[48,3584]{1,0:T(8,128)(2,1)S(1)} %broadcast_select_fusion.13.refs_2_), channel_id=1, source_target_pairs={{0,16},{16,0},{1,17},{17,1},{2,18},{18,2},{3,19},{19,3},{4,20},{20... | collective-permute-start | bytes 1032200 | tf_op jit(solution)/shard_map/ppermute | solution.py:131
  120.4 16.9 %collective-permute-start.18 = (bf16[48,3840]{1,0:T(8,128)(2,1)S(1)}, bf16[48,3840]{1,0:T(8,128)(2,1)S(1)}, u32[]{:S(2)}, u32[]{:S(2)}) collective-permute-start(bf16[48,3840]{1,0:T(8,128)(2,1)S(1)} %broadcast_select_fusion.8.refs_0_), channel_id=1, source_target_pairs={{0,2},{2,0},{4,6},{6,4},{8,10},{10,8},{12,14},{14,12},{1,3},{3,1},... | collective-permute-start | bytes 1105928 | tf_op jit(solution)/shard_map/ppermute | solution.py:128
  120.9 16.6 %collective-permute-start.21 = (bf16[48,3840]{1,0:T(8,128)(2,1)S(1)}, bf16[48,3840]{1,0:T(8,128)(2,1)S(1)}, u32[]{:S(2)}, u32[]{:S(2)}) collective-permute-start(bf16[48,3840]{1,0:T(8,128)(2,1)S(1)} %broadcast_select_fusion.8.refs_0_), channel_id=1, source_target_pairs={{0,16},{16,0},{1,17},{17,1},{2,18},{18,2},{3,19},{19,3},{4,20},{20... | collective-permute-start | bytes 1105928 | tf_op jit(solution)/shard_map/ppermute | solution.py:131
  122.4 21.0 %collective-permute-start.25 = (bf16[96,3584]{1,0:T(8,128)(2,1)S(1)}, bf16[96,3584]{1,0:T(8,128)(2,1)S(1)}, u32[]{:S(2)}, u32[]{:S(2)}) collective-permute-start(bf16[96,3584]{1,0:T(8,128)(2,1)S(1)} %get-tuple-element.22), channel_id=1, source_target_pairs={{4,0},{6,2},{8,12},{10,14},{5,1},{7,3},{9,13},{11,15},{20,16},{22,... | collective-permute-start | bytes 2064392 | tf_op jit(solution)/shard_map/ppermute | solution.py:125
  131.7 11.7 %collective-permute-start.36 = (bf16[96,3584]{1,0:T(8,128)(2,1)S(1)}, bf16[96,3584]{1,0:T(8,128)(2,1)S(1)}, u32[]{:S(2)}, u32[]{:S(2)}) collective-permute-start(bf16[96,3584]{1,0:T(8,128)(2,1)S(1)} %get-tuple-element.21), channel_id=1, source_target_pairs={{8,4},{10,6},{4,8},{6,10},{9,5},{11,7},{5,9},{7,11},{24,20},{26,22... | collective-permute-start | bytes 2064392 | tf_op jit(solution)/shard_map/ppermute | solution.py:125
  136.7 19.7 %collective-permute-start.34 = (bf16[48,3584]{1,0:T(8,128)(2,1)S(1)}, bf16[48,3584]{1,0:T(8,128)(2,1)S(1)}, u32[]{:S(2)}, u32[]{:S(2)}) collective-permute-start(bf16[48,3584]{1,0:T(8,128)(2,1)S(1)} %broadcast_select_fusion.12.refs_2_), channel_id=1, source_target_pairs={{0,16},{16,0},{1,17},{17,1},{2,18},{18,2},{3,19},{19,3},{4,20},{20... | collective-permute-start | bytes 1032200 | tf_op jit(solution)/shard_map/ppermute | solution.py:131
  137.3 7.6 %collective-permute-start.24 = (bf16[48,3584]{1,0:T(8,128)(2,1)S(1)}, bf16[48,3584]{1,0:T(8,128)(2,1)S(1)}, u32[]{:S(2)}, u32[]{:S(2)}) collective-permute-start(bf16[48,3584]{1,0:T(8,128)(2,1)S(1)} %collective-permute-done.23.refs_6_), channel_id=1, source_target_pairs={{0,2},{2,0},{4,6},{6,4},{8,10},{10,8},{12,14},{14,12},{1,3},{3,1},... | collective-permute-start | bytes 1032200 | tf_op jit(solution)/shard_map/ppermute | solution.py:128
  137.5 19.0 %collective-permute-start.28 = (bf16[48,3840]{1,0:T(8,128)(2,1)S(1)}, bf16[48,3840]{1,0:T(8,128)(2,1)S(1)}, u32[]{:S(2)}, u32[]{:S(2)}) collective-permute-start(bf16[48,3840]{1,0:T(8,128)(2,1)S(1)} %broadcast_select_fusion.7.refs_0_), channel_id=1, source_target_pairs={{0,2},{2,0},{4,6},{6,4},{8,10},{10,8},{12,14},{14,12},{1,3},{3,1},... | collective-permute-start | bytes 1105928 | tf_op jit(solution)/shard_map/ppermute | solution.py:128
  143.4 7.5 %collective-permute-start.22 = (bf16[48,3840]{1,0:T(8,128)(2,1)S(1)}, bf16[48,3840]{1,0:T(8,128)(2,1)S(1)}, u32[]{:S(2)}, u32[]{:S(2)}) collective-permute-start(bf16[48,3840]{1,0:T(8,128)(2,1)S(1)} %collective-permute-done.18.refs_1_), channel_id=1, source_target_pairs={{0,16},{16,0},{1,17},{17,1},{2,18},{18,2},{3,19},{19,3},{4,20},{20... | collective-permute-start | bytes 1105928 | tf_op jit(solution)/shard_map/ppermute | solution.py:131
  143.4 13.8 %collective-permute-start.37 = (bf16[96,3584]{1,0:T(8,128)(2,1)S(1)}, bf16[96,3584]{1,0:T(8,128)(2,1)S(1)}, u32[]{:S(2)}, u32[]{:S(2)}) collective-permute-start(bf16[96,3584]{1,0:T(8,128)(2,1)S(1)} %collective-permute-done.36), channel_id=1, source_target_pairs={{4,0},{6,2},{8,12},{10,14},{5,1},{7,3},{9,13},{11,15},{20,16},{22,... | collective-permute-start | bytes 2064392 | tf_op jit(solution)/shard_map/ppermute | solution.py:125
  144.9 29.4 %collective-permute-start.38 = (f32[144,256]{1,0:T(8,128)S(1)}, f32[144,256]{1,0:T(8,128)S(1)}, u32[]{:S(2)}, u32[]{:S(2)}) collective-permute-start(f32[144,256]{1,0:T(8,128)S(1)} %get-tuple-element.40), channel_id=1, source_target_pairs={{0,1},{1,0},{2,3},{3,2},{4,5},{5,4},{6,7},{7,6},{8,9},{9,8},{10,11... | collective-permute-start | bytes 442376 | tf_op jit(solution)/shard_map/ppermute | solution.py:190
  150.9 10.3 %collective-permute-start.31 = (bf16[48,3584]{1,0:T(8,128)(2,1)S(1)}, bf16[48,3584]{1,0:T(8,128)(2,1)S(1)}, u32[]{:S(2)}, u32[]{:S(2)}) collective-permute-start(bf16[48,3584]{1,0:T(8,128)(2,1)S(1)} %broadcast_select_fusion.12.refs_2_), channel_id=1, source_target_pairs={{0,2},{2,0},{4,6},{6,4},{8,10},{10,8},{12,14},{14,12},{1,3},{3,1},... | collective-permute-start | bytes 1032200 | tf_op jit(solution)/shard_map/ppermute | solution.py:128
  156.4 9.1 %collective-permute-start.32 = (bf16[48,3840]{1,0:T(8,128)(2,1)S(1)}, bf16[48,3840]{1,0:T(8,128)(2,1)S(1)}, u32[]{:S(2)}, u32[]{:S(2)}) collective-permute-start(bf16[48,3840]{1,0:T(8,128)(2,1)S(1)} %broadcast_select_fusion.7.refs_0_), channel_id=1, source_target_pairs={{0,16},{16,0},{1,17},{17,1},{2,18},{18,2},{3,19},{19,3},{4,20},{20... | collective-permute-start | bytes 1105928 | tf_op jit(solution)/shard_map/ppermute | solution.py:131
  156.4 9.1 %collective-permute-start.35 = (bf16[48,3584]{1,0:T(8,128)(2,1)S(1)}, bf16[48,3584]{1,0:T(8,128)(2,1)S(1)}, u32[]{:S(2)}, u32[]{:S(2)}) collective-permute-start(bf16[48,3584]{1,0:T(8,128)(2,1)S(1)} %collective-permute-done.34.refs_6_), channel_id=1, source_target_pairs={{0,2},{2,0},{4,6},{6,4},{8,10},{10,8},{12,14},{14,12},{1,3},{3,1},... | collective-permute-start | bytes 1032200 | tf_op jit(solution)/shard_map/ppermute | solution.py:128
  157.2 12.2 %collective-permute-start.33 = (bf16[48,3840]{1,0:T(8,128)(2,1)S(1)}, bf16[48,3840]{1,0:T(8,128)(2,1)S(1)}, u32[]{:S(2)}, u32[]{:S(2)}) collective-permute-start(bf16[48,3840]{1,0:T(8,128)(2,1)S(1)} %collective-permute-done.28.refs_1_), channel_id=1, source_target_pairs={{0,16},{16,0},{1,17},{17,1},{2,18},{18,2},{3,19},{19,3},{4,20},{20... | collective-permute-start | bytes 1105928 | tf_op jit(solution)/shard_map/ppermute | solution.py:131
  161.2 13.2 %collective-permute-start.39 = (f32[144,256]{1,0:T(8,128)S(1)}, f32[144,256]{1,0:T(8,128)S(1)}, u32[]{:S(2)}, u32[]{:S(2)}) collective-permute-start(f32[144,256]{1,0:T(8,128)S(1)} %get-tuple-element.38), channel_id=1, source_target_pairs={{0,1},{1,0},{2,3},{3,2},{4,5},{5,4},{6,7},{7,6},{8,9},{9,8},{10,11... | collective-permute-start | bytes 442376 | tf_op jit(solution)/shard_map/ppermute | solution.py:190
  165.5 8.9 %collective-permute-start.40 = (f32[144,256]{1,0:T(8,128)S(1)}, f32[144,256]{1,0:T(8,128)S(1)}, u32[]{:S(2)}, u32[]{:S(2)}) collective-permute-start(f32[144,256]{1,0:T(8,128)S(1)} %get-tuple-element.36), channel_id=1, source_target_pairs={{0,1},{1,0},{2,3},{3,2},{4,5},{5,4},{6,7},{7,6},{8,9},{9,8},{10,11... | collective-permute-start | bytes 442376 | tf_op jit(solution)/shard_map/ppermute | solution.py:190
  178.6 11.2 %collective-permute-start.48 = (f32[24,384]{1,0:T(8,128)}, f32[24,384]{1,0:T(8,128)S(1)}, u32[]{:S(2)}, u32[]{:S(2)}) collective-permute-start(f32[24,384]{1,0:T(8,128)} %get-tuple-element.20), channel_id=1, source_target_pairs={{0,14},{2,12},{4,10},{6,8},{8,6},{10,4},{12,2},{14,0},{1,15},{3,13... | collective-permute-start | bytes 110600 | tf_op jit(solution)/shard_map/ppermute | solution.py:208
  184.3 6.2 %collective-permute-start.47 = (f32[24,384]{1,0:T(8,128)}, f32[24,384]{1,0:T(8,128)S(1)}, u32[]{:S(2)}, u32[]{:S(2)}) collective-permute-start(f32[24,384]{1,0:T(8,128)} %get-tuple-element.19), channel_id=1, source_target_pairs={{0,12},{2,14},{4,8},{6,10},{8,4},{10,6},{12,0},{14,2},{1,13},{3,15... | collective-permute-start | bytes 110600 | tf_op jit(solution)/shard_map/ppermute | solution.py:208
  184.6 7.7 %collective-permute-start.46 = (f32[24,384]{1,0:T(8,128)}, f32[24,384]{1,0:T(8,128)S(1)}, u32[]{:S(2)}, u32[]{:S(2)}) collective-permute-start(f32[24,384]{1,0:T(8,128)} %get-tuple-element.18), channel_id=1, source_target_pairs={{0,10},{2,8},{4,14},{6,12},{8,2},{10,0},{12,6},{14,4},{1,11},{3,9}... | collective-permute-start | bytes 110600 | tf_op jit(solution)/shard_map/ppermute | solution.py:208
  184.9 7.4 %collective-permute-start.45 = (f32[24,384]{1,0:T(8,128)}, f32[24,384]{1,0:T(8,128)S(1)}, u32[]{:S(2)}, u32[]{:S(2)}) collective-permute-start(f32[24,384]{1,0:T(8,128)} %get-tuple-element.17), channel_id=1, source_target_pairs={{0,8},{2,10},{4,12},{6,14},{8,0},{10,2},{12,4},{14,6},{1,9},{3,11}... | collective-permute-start | bytes 110600 | tf_op jit(solution)/shard_map/ppermute | solution.py:208
  188.4 5.4 %collective-permute-start.44 = (f32[24,384]{1,0:T(8,128)}, f32[24,384]{1,0:T(8,128)S(1)}, u32[]{:S(2)}, u32[]{:S(2)}) collective-permute-start(f32[24,384]{1,0:T(8,128)} %get-tuple-element.16), channel_id=1, source_target_pairs={{0,6},{2,4},{4,2},{6,0},{8,14},{10,12},{12,10},{14,8},{1,7},{3,5},... | collective-permute-start | bytes 110600 | tf_op jit(solution)/shard_map/ppermute | solution.py:208
  189.8 4.2 %collective-permute-start.43 = (f32[24,384]{1,0:T(8,128)}, f32[24,384]{1,0:T(8,128)S(1)}, u32[]{:S(2)}, u32[]{:S(2)}) collective-permute-start(f32[24,384]{1,0:T(8,128)} %get-tuple-element.15), channel_id=1, source_target_pairs={{0,4},{2,6},{4,0},{6,2},{8,12},{10,14},{12,8},{14,10},{1,5},{3,7},... | collective-permute-start | bytes 110600 | tf_op jit(solution)/shard_map/ppermute | solution.py:208
  190.5 4.2 %collective-permute-start.42 = (f32[24,384]{1,0:T(8,128)}, f32[24,384]{1,0:T(8,128)S(1)}, u32[]{:S(2)}, u32[]{:S(2)}) collective-permute-start(f32[24,384]{1,0:T(8,128)} %get-tuple-element.14), channel_id=1, source_target_pairs={{0,2},{2,0},{4,6},{6,4},{8,10},{10,8},{12,14},{14,12},{1,3},{3,1},... | collective-permute-start | bytes 110600 | tf_op jit(solution)/shard_map/ppermute | solution.py:208
  (11 other events, 236.1 us)

commit v2 on v0

--- a/solution.py
+++ b/solution.py
@@ -1,10 +1,15 @@
+import functools
+
 import jax
 import jax.numpy as jnp
 from jax import lax
+from jax.experimental import pallas as pl
+from jax.experimental.pallas import tpu as pltpu
 from jax.sharding import PartitionSpec as P
 
 TOK = 256
 K = 384
+LANES = 128
 
 
 def place_cols(left, piece):
@@ -12,7 +17,7 @@
     return product
 
 
-def per_device(activations, out_grads, input_basis, output_basis):
+def per_device_any(activations, out_grads, input_basis, output_basis):
     acts = activations[0]
     grads = out_grads[0]
     tokens = acts.shape[0]
@@ -35,6 +40,240 @@
     return summed / jnp.float32(data_count)
 
 
+def nt_dot(left, right):
+    return lax.dot_general(
+        left, right, (((1,), (1,)), ((), ())), preferred_element_type=jnp.float32
+    )
+
+
+def cut_kernel(in_half, first, in_ref, out_ref, m0, m1, t0, t1):
+    x = lax.axis_index("group")
+    out_half = first + m1.shape[1]
+    for side, unit0, unit1 in ((x, m0, m1), (1 - x, t0, t1)):
+        in_at = pl.multiple_of(side * in_half, LANES)
+        out_at = pl.multiple_of(side * out_half, LANES)
+        next_at = pl.multiple_of(side * out_half + first, LANES)
+        unit0[:, :in_half] = in_ref[:, pl.ds(in_at, in_half)]
+        unit0[:, in_half:] = out_ref[:, pl.ds(out_at, first)]
+        unit1[...] = out_ref[:, pl.ds(next_at, unit1.shape[1])]
+
+
+def rotate_kernel(plan, in_half, first, acts_ref, grads_ref, *refs):
+    x = lax.axis_index("group")
+    core = lax.axis_index("basis")
+    terms, has_acc, last = plan
+    refs = list(refs)
+    out_half = grads_ref.shape[1] // 2
+    rot_in = rot_out = None
+    for mine, index, count in terms:
+        pieces, refs = refs[:count], refs[count:]
+        rows = jnp.concatenate([p[...] for p in pieces], axis=0)
+        side = x if mine else 1 - x
+        if index == 0:
+            cols = pl.ds(pl.multiple_of(side * in_half, LANES), in_half)
+            part = nt_dot(rows[:, :in_half], acts_ref[:, cols])
+            rot_in = part if rot_in is None else rot_in + part
+            cols = pl.ds(pl.multiple_of(side * out_half, LANES), first)
+            part = nt_dot(rows[:, in_half:], grads_ref[:, cols])
+        else:
+            cols = pl.ds(pl.multiple_of(side * out_half + first, LANES), out_half - first)
+            part = nt_dot(rows, grads_ref[:, cols])
+        rot_out = part if rot_out is None else rot_out + part
+    if has_acc:
+        if rot_in is not None:
+            rot_in += refs.pop(0)[...]
+        rot_out += refs.pop(0)[...]
+    if rot_in is not None:
+        refs.pop(0)[...] = rot_in
+    if not last:
+        refs.pop(0)[...] = rot_out
+        return
+    keep, send = refs
+    panel = pieces[0].shape[0] // 2
+    for shard in range(rot_out.shape[0] // (2 * panel)):
+        low = rot_out[2 * shard * panel : (2 * shard + 1) * panel]
+        high = rot_out[(2 * shard + 1) * panel : 2 * (shard + 1) * panel]
+        at = slice(shard * panel, (shard + 1) * panel)
+        keep[at] = jnp.where(core == 0, low, high)
+        send[at] = jnp.where(core == 0, high, low)
+
+
+def finish_kernel(rows, table_ref, *refs):
+    ins, keep, come = refs[0:4], refs[4:6], refs[6:8]
+    outs = refs[8:-2]
+    in_ref, out_ref = refs[-2:]
+    half = rows // 2
+    for shard in range(8):
+        part, local = (0, shard) if shard < 2 else (1, shard - 2)
+        owner = table_ref[shard]
+        block = ins[2 * part][pl.ds(local * rows, rows)] + ins[2 * part + 1][pl.ds(local * rows, rows)]
+        in_ref[pl.ds(pl.multiple_of(owner * rows, 16), rows), :] = block.astype(jnp.bfloat16)
+        place = table_ref[8 + shard]
+        at = pl.ds(local * half, half)
+        out_ref[pl.ds(pl.multiple_of(place * half, 8), half), :] = keep[part][at] + come[part][at]
+    coeff = nt_dot(out_ref[...].astype(jnp.bfloat16), in_ref[...])
+    coeff = coeff * (1.0 / TOK**0.5)
+    square = coeff * coeff
+    for place, ref in enumerate(outs):
+        ref[...] = square[place * half : (place + 1) * half]
+
+
+def per_device_plane(activations, out_grads, input_basis, output_basis):
+    acts, grads = activations[0], out_grads[0]
+    in_t, out_t = input_basis.T, output_basis.T
+    rows = in_t.shape[0]
+    tokens = acts.shape[0]
+    me = lax.axis_index("dp")
+    z, y = me // 2, me % 2
+    in_half = in_t.shape[1] // 2
+    width = (in_t.shape[1] + out_t.shape[1]) // 4
+    first = width - in_half
+
+    vmem = pl.BlockSpec(memory_space=pltpu.VMEM)
+
+    def shift(value, pairs):
+        return lax.ppermute(value, "dp", [(2 * a + b, 2 * c + b) for a, c in pairs for b in range(2)])
+
+    def swap_y(value):
+        return lax.ppermute(value, "dp", [(i, i ^ 1) for i in range(8)])
+
+    def swap_x(value):
+        return lax.ppermute(value, "group", [(0, 1), (1, 0)])
+
+    def swap_core(value):
+        return lax.ppermute(value, "basis", [(0, 1), (1, 0)])
+
+    def by_z(*choices):
+        out = choices[3]
+        for i in (2, 1, 0):
+            if choices[i] is not out:
+                out = jnp.where(z <= i, choices[i], out)
+        return out
+
+    unit = jax.ShapeDtypeStruct((rows, width), in_t.dtype)
+    m0, m1, t0, t1 = pl.pallas_call(
+        functools.partial(cut_kernel, in_half, first),
+        out_shape=[unit] * 4,
+        in_specs=[vmem] * 2,
+        out_specs=[vmem] * 4,
+        name="cut",
+    )(in_t, out_t)
+
+    down = [(1, 0), (2, 1), (3, 2)]
+    up = [(0, 1), (1, 2), (2, 3)]
+    L, R = {}, {}
+    held = [{}, {}, {}, {}]
+    own, one, two, three = held
+    own.update(m0=m0, m1=m1, t0=t0, t1=t1)
+
+    def settle(r):
+        names = [(h, k) for h in held for k in h]
+        sides = [(d, k) for d in (L, R) for k in d if k < r - 1]
+        values = [h[k] for h, k in names + sides]
+        for (h, k), v in zip(names + sides, lax.optimization_barrier(tuple(values))):
+            h[k] = v
+
+    def both_ways(r, at_end, count=3):
+        a, b = (m0, m0) if r == 1 else (m1, m1) if r == 2 else (L[r - 2], R[r - 2])
+        if at_end is not None:
+            a, b = jnp.where(z == 3, at_end, a), jnp.where(z == 0, at_end, b)
+        L[r], R[r] = shift(a, down[:count]), shift(b, up[3 - count :])
+
+    def ends(r):
+        L[r] = R[r] = shift(jnp.where(z == 1, L[r - 2], R[r - 2]), [(1, 0), (2, 3)])
+
+    plan_y = ["", "0om0", "0om1", "1om0", "1om1", "2om0", "2om1", "3om0", "2ot0", "3ot0", "1ot1"]
+    plan_x = ["", "", "", "0ot0", "0ot1", "1t1", "2t0", "1t0", "1ot0", "2t1", "2ot1"]
+    at_end = {3: "t0", 4: "t1", 5: "om1", 6: "ot1"}
+    other = {"m": "t", "t": "m"}
+    waiting = {}
+    for r in range(1, 11):
+        if r > 2:
+            for h, k, v in waiting.pop(r - 2):
+                h[k] = v
+            settle(r)
+        for i, (slot, name) in enumerate(((one, "m0"), (one, "m1"))):
+            if r == 3 + i:
+                slot[name] = by_z(L[1 + i], L[1 + i], R[1 + i], R[1 + i])
+        for i, name in enumerate(("m0", "m1")):
+            if r == 5 + i:
+                two[name] = by_z(L[3 + i], R[1 + i], L[1 + i], R[3 + i])
+        for i, name in enumerate(("m0", "m1", "t0", "t1")):
+            if r == 7 + i:
+                three[name] = by_z(L[5 + i], L[3 + i], R[3 + i], R[5 + i])
+        if r < 9:
+            both_ways(r, own[at_end[r]] if r in at_end else None, 3 if r < 7 else 2)
+        else:
+            ends(r)
+        waiting[r] = []
+        name = plan_y[r]
+        slot = held[int(name[0])]
+        waiting[r].append((slot, name[1:], swap_y(slot[name[2:]])))
+        if plan_x[r]:
+            name = plan_x[r]
+            slot = held[int(name[0])]
+            source = name[1:-2] + other[name[-2]] + name[-1]
+            waiting[r].append((slot, name[1:], swap_x(slot[source])))
+    for r in (9, 10):
+        for h, k, v in waiting.pop(r):
+            h[k] = v
+    three["om1"] = by_z(L[9], L[7], R[7], R[9])
+    three["ot1"] = by_z(L[10], L[8], R[8], R[10])
+
+    def rotate(slots, names, acc, last):
+        terms, pieces, out_shape = [], [], []
+        count = 2 * len(slots)
+        for name in names:
+            terms.append((name[0] == "m", int(name[1]), count))
+            pieces += [v for s in slots for v in (s[name], s["o" + name])]
+        full = jax.ShapeDtypeStruct((count * rows, tokens), jnp.float32)
+        panel = jax.ShapeDtypeStruct((count * rows // 2, tokens), jnp.float32)
+        if any(name[1] == "0" for name in names):
+            out_shape.append(full)
+        out_shape += [panel, panel] if last else [full]
+        return pl.pallas_call(
+            functools.partial(rotate_kernel, (terms, bool(acc), last), in_half, first),
+            out_shape=out_shape,
+            in_specs=[vmem] * (2 + len(pieces) + len(acc)),
+            out_specs=[vmem] * len(out_shape),
+            compiler_params=pltpu.CompilerParams(vmem_limit_bytes=40 * 2**20),
+            cost_estimate=pl.CostEstimate(
+                flops=2 * len(pieces) * rows * width * tokens,
+                bytes_accessed=2 * len(pieces) * rows * width,
+                transcendentals=0,
+            ),
+            name="rotate",
+        )(acts, grads, *pieces, *acc)
+
+    in_a, keep_a, send_a = rotate([own], ["m0", "m1", "t0", "t1"], [], True)
+    rest = [one, two, three]
+    acc = rotate(rest, ["m0"], [], False)
+    in_b, acc_out = rotate(rest, ["m1", "t0"], acc, False)
+    keep_b, send_b = rotate(rest, ["t1"], [acc_out], True)
+
+    order = jnp.array([[0, 1, 2, 3], [1, 2, 0, 3], [2, 1, 3, 0], [3, 2, 1, 0]], jnp.int32)[z]
+    owners = jnp.stack([order * 2 + y, order * 2 + 1 - y], axis=1).reshape(-1)
+    table = jnp.concatenate([owners, owners ^ me]).astype(jnp.int32)
+    squares = pl.pallas_call(
+        functools.partial(finish_kernel, rows),
+        out_shape=[jax.ShapeDtypeStruct((rows // 2, K), jnp.float32)] * 8,
+        in_specs=[pl.BlockSpec(memory_space=pltpu.SMEM)] + [vmem] * 8,
+        out_specs=[vmem] * 8,
+        scratch_shapes=[
+            pltpu.VMEM((K, tokens), jnp.bfloat16),
+            pltpu.VMEM((K // 2, tokens), jnp.float32),
+        ],
+        name="finish",
+    )(
+        table, in_a, swap_core(in_a), in_b, swap_core(in_b),
+        keep_a, keep_b, swap_core(send_a), swap_core(send_b),
+    )
+    total = squares[0]
+    for k in range(1, 8):
+        total = total + lax.ppermute(squares[k], "dp", [(i, i ^ k) for i in range(8)])
+    return total * (1.0 / 8)
+
+
 def solution(mesh):
     in_specs = (
         P(("group", "dp"), None, "basis"),
@@ -43,6 +282,11 @@
         P("basis", "dp"),
     )
     out_specs = P(("group", "dp", "basis"), None)
+    plane = (mesh.shape["group"], mesh.shape["dp"], mesh.shape["basis"]) == (2, 8, 2)
     return jax.shard_map(
-        per_device, mesh=mesh, in_specs=in_specs, out_specs=out_specs, check_vma=False
-    )
+        per_device_plane if plane else per_device_any,
+        mesh=mesh,
+        in_specs=in_specs,
+        out_specs=out_specs,
+        check_vma=False,
+    )

time: 311 us -> 154 us (0.50)
  waiting for transfers between devices: 275 us -> 59.2 us
  starting transfers between devices: 0.12 us -> 72.3 us
  matrix products: 14.8 us -> 0 us
  Pallas kernels: 0 us -> 14.8 us
  between operations: 13.1 us -> 0.67 us
  blocking collectives: 4.74 us -> 0 us
  other arithmetic: 1.39 us -> 4.61 us
    all_gather x2 -> x0, waiting for transfers between devices: 212 us -> none  [the longest x1 161 us: per_device(): lax.all_gather(output_basis, 'dp', axis=1, tiled=True)]
    ppermute x0 -> x47, starting transfers between devices: none -> 72.3 us  [the longest x18 41.4 us: shift(): lax.ppermute(value, 'dp', [(2 * a + b, 2 * c + b) for a, c in pairs for b...]
    unnamed x5 -> x0, waiting for transfers between devices: 62.9 us -> none
    ppermute x0 -> x47, waiting for transfers between devices: none -> 59.2 us  [the longest x18 33.6 us: shift(): lax.ppermute(value, 'dp', [(2 * a + b, 2 * c + b) for a, c in pairs for b...]
    dot_general x3 -> x0, matrix products: 14.8 us -> none  [the longest x2 13 us: place_cols(): product = jnp.dot(left, piece, preferred_element_type=jnp.float32)]
    pallas_call x0 -> x6, Pallas kernels: none -> 14.8 us  [the longest x4 9.7 us: rotate(): pl.pallas_call(functools.partial(rotate_kernel, (terms, bool(acc), last),...]
    psum x1 -> x0, blocking collectives: 4.74 us -> none  [per_device(): rot_in = lax.psum(part_in, 'basis').astype(jnp.bfloat16)]
  transfers between devices with their start and end apart: 4 -> 47, of which waited for: 4 -> 20; matrix products, arithmetic and copies ran while one was open for 4% -> 2% of each run, Pallas kernels for 0% -> 6%
where the time goes in v2:
time: 154 us; the launch traced here: 153 us
  starting transfers between devices  72.3 us (47%)
  waiting for transfers between devices  59.2 us (38%)
  Pallas kernels  14.8 us (10%)
  other arithmetic  4.61 us (3%)
  local copies, waits for them, and re-layouts  1.89 us (1%)
    ppermute x18, starting transfers between devices, shift(): lax.ppermute(value, 'dp', [(2 * a + b, 2 * c + b) for a, c in pairs for b...  41.4 us
    ppermute x18, waiting for transfers between devices, shift(): lax.ppermute(value, 'dp', [(2 * a + b, 2 * c + b) for a, c in pairs for b...  33.6 us
    ppermute x8, waiting for transfers between devices, swap_x(): return lax.ppermute(value, 'group', [(0, 1), (1, 0)])  16.1 us
    ppermute x8, starting transfers between devices, swap_x(): return lax.ppermute(value, 'group', [(0, 1), (1, 0)])  12.1 us
    ppermute x7, starting transfers between devices, per_device_plane(): lax.ppermute(squares[k], 'dp', [(i, i ^ k) for i in range(8)])  11.7 us
    pallas_call x4, Pallas kernels, rotate(): pl.pallas_call(functools.partial(rotate_kernel, (terms, bool(acc), last),...  9.7 us
    ppermute x10, waiting for transfers between devices, swap_y(): return lax.ppermute(value, 'dp', [(i, i ^ 1) for i in range(8)])  6.74 us
    ppermute x10, starting transfers between devices, swap_y(): return lax.ppermute(value, 'dp', [(i, i ^ 1) for i in range(8)])  6.46 us
  transfers between devices with their start and end apart: 47, of which 20 were waited for; matrix products, arithmetic and copies ran while one was open for 2% of the time, Pallas kernels for 6%

profile of v2, /device:TPU:0, one launch (start us, length us, event | category | flops | bytes accessed | tf_op | source)
XLA Modules:
  0.0 153.4 jit_solution(13832447382860854363)
XLA Ops:
  0.0 2.8 %cut.1 = (bf16[48,4608]{1,0:T(8,128)(2,1)}, bf16[48,4608]{1,0:T(8,128)(2,1)}, bf16[48,4608]{1,0:T(8,128)(2,1)}, bf16[48,4608]{1,0:T(8,128)(2,1)}) custom-call(bf16[48,4096]{1,0:T(8,128)(2,1)} %bitcast.21, bf16[48,14336]{1,0:T(8,128)(2,1)} %bitcast.20), custom_call_target="tpu_custom_call" | custom-call | tf_op jit(solution)/shard_map/cut/pallas_call | solution.py:154
  2.9 3.0 %collective-permute-start = (bf16[48,4608]{1,0:T(8,128)(2,1)}, bf16[48,4608]{1,0:T(8,128)(2,1)S(1)}, u32[]{:S(2)}, u32[]{:S(2)}) collective-permute-start(bf16[48,4608]{1,0:T(8,128)(2,1)} %get-tuple-element.317.refs_0_), channel_id=1, source_target_pairs={{0,2},{2,0},{4,6},{6,4},{8,10},{10,8},{12,14},{14,12},{1,3},{3,1},... | collective-permute-start | bytes 1327112 | tf_op jit(solution)/shard_map/ppermute | solution.py:138
  5.8 1.3 collective-permute-start.1
  7.1 4.6 %collective-permute-start.2 = (bf16[48,4608]{1,0:T(8,128)(2,1)}, bf16[48,4608]{1,0:T(8,128)(2,1)S(1)}, u32[]{:S(2)}, u32[]{:S(2)}) collective-permute-start(bf16[48,4608]{1,0:T(8,128)(2,1)} %get-tuple-element.317.refs_0_), channel_id=1, source_target_pairs={{0,4},{2,6},{4,8},{6,10},{8,12},{10,14},{1,5},{3,7},{5,9},{7,11},{... | collective-permute-start | bytes 1327112 | tf_op jit(solution)/shard_map/ppermute | solution.py:135
  11.9 1.3 collective-permute-start.4
  14.1 2.9 %collective-permute-done.refs_1_ = bf16[48,4608]{1,0:T(8,128)(2,1)S(1)} collective-permute-done((bf16[48,4608]{1,0:T(8,128)(2,1)}, bf16[48,4608]{1,0:T(8,128)(2,1)S(1)}, u32[]{:S(2)}, u32[]{:S(2)}) %collective-permute-start) | collective-permute-done | bytes 442400 | tf_op jit(solution)/shard_map/ppermute | solution.py:138
  17.0 4.0 %collective-permute-start.5 = (bf16[48,4608]{1,0:T(8,128)(2,1)}, bf16[48,4608]{1,0:T(8,128)(2,1)S(1)}, u32[]{:S(2)}, u32[]{:S(2)}) collective-permute-start(bf16[48,4608]{1,0:T(8,128)(2,1)} %get-tuple-element.319.refs_2_), channel_id=1, source_target_pairs={{0,4},{2,6},{4,8},{6,10},{8,12},{10,14},{1,5},{3,7},{5,9},{7,11},{... | collective-permute-start | bytes 1327112 | tf_op jit(solution)/shard_map/ppermute | solution.py:135
  21.1 1.2 collective-permute-done.2
  22.3 1.5 collective-permute-start.6
  26.5 2.5 %collective-permute-done.4 = bf16[48,4608]{1,0:T(8,128)(2,1)S(1)} collective-permute-done((bf16[48,4608]{1,0:T(8,128)(2,1)}, bf16[48,4608]{1,0:T(8,128)(2,1)S(1)}, u32[]{:S(2)}, u32[]{:S(2)}) %collective-permute-start.4) | collective-permute-done | bytes 442400 | tf_op jit(solution)/shard_map/ppermute | solution.py:135
  29.0 1.3 collective-permute-done.5
  30.3 1.3 collective-permute-start.8
  31.6 4.9 %collective-permute-start.9 = (bf16[48,4608]{1,0:T(8,128)(2,1)S(1)}, bf16[48,4608]{1,0:T(8,128)(2,1)S(1)}, u32[]{:S(2)}, u32[]{:S(2)}) collective-permute-start(bf16[48,4608]{1,0:T(8,128)(2,1)S(1)} %get-tuple-element.378), channel_id=1, source_target_pairs={{0,4},{2,6},{4,8},{6,10},{8,12},{10,14},{1,5},{3,7},{5,9},{7,11},{... | collective-permute-start | bytes 1327112 | tf_op jit(solution)/shard_map/ppermute | solution.py:135
  36.5 1.6 %collective-permute-start.10 = (bf16[48,4608]{1,0:T(8,128)(2,1)S(1)}, bf16[48,4608]{1,0:T(8,128)(2,1)S(1)}, u32[]{:S(2)}, u32[]{:S(2)}) collective-permute-start(bf16[48,4608]{1,0:T(8,128)(2,1)S(1)} %collective-permute-done.3.refs_3_), channel_id=1, source_target_pairs={{0,16},{16,0},{1,17},{17,1},{2,18},{18,2},{3,19},{19,3},{4,20},{20... | collective-permute-start | bytes 1327112 | tf_op jit(solution)/shard_map/ppermute | solution.py:141
  38.8 1.3 collective-permute-start.12
  40.1 5.6 %collective-permute-done.8 = bf16[48,4608]{1,0:T(8,128)(2,1)S(1)} collective-permute-done((bf16[48,4608]{1,0:T(8,128)(2,1)S(1)}, bf16[48,4608]{1,0:T(8,128)(2,1)S(1)}, u32[]{:S(2)}, u32[]{:S(2)}) %collective-permute-start.8) | collective-permute-done | bytes 442400 | tf_op jit(solution)/shard_map/ppermute | solution.py:135
  45.7 3.9 %collective-permute-start.13 = (bf16[48,4608]{1,0:T(8,128)(2,1)S(1)}, bf16[48,4608]{1,0:T(8,128)(2,1)S(1)}, u32[]{:S(2)}, u32[]{:S(2)}) collective-permute-start(bf16[48,4608]{1,0:T(8,128)(2,1)S(1)} %get-tuple-element.375), channel_id=1, source_target_pairs={{0,4},{2,6},{4,8},{6,10},{8,12},{10,14},{1,5},{3,7},{5,9},{7,11},{... | collective-permute-start | bytes 1327112 | tf_op jit(solution)/shard_map/ppermute | solution.py:135
  49.6 1.6 %collective-permute-start.14 = (bf16[48,4608]{1,0:T(8,128)(2,1)S(1)}, bf16[48,4608]{1,0:T(8,128)(2,1)S(1)}, u32[]{:S(2)}, u32[]{:S(2)}) collective-permute-start(bf16[48,4608]{1,0:T(8,128)(2,1)S(1)} %get-tuple-element.326.refs_0_), channel_id=1, source_target_pairs={{0,16},{16,0},{1,17},{17,1},{2,18},{18,2},{3,19},{19,3},{4,20},{20... | collective-permute-start | bytes 1327112 | tf_op jit(solution)/shard_map/ppermute | solution.py:141
  51.4 1.4 collective-permute-done.12
  52.8 2.5 %collective-permute-done.13 = bf16[48,4608]{1,0:T(8,128)(2,1)S(1)} collective-permute-done((bf16[48,4608]{1,0:T(8,128)(2,1)S(1)}, bf16[48,4608]{1,0:T(8,128)(2,1)S(1)}, u32[]{:S(2)}, u32[]{:S(2)}) %collective-permute-start.13) | collective-permute-done | bytes 442400 | tf_op jit(solution)/shard_map/ppermute | solution.py:135
  55.4 1.3 collective-permute-start.16
  56.7 5.0 %collective-permute-start.17 = (bf16[48,4608]{1,0:T(8,128)(2,1)S(1)}, bf16[48,4608]{1,0:T(8,128)(2,1)S(1)}, u32[]{:S(2)}, u32[]{:S(2)}) collective-permute-start(bf16[48,4608]{1,0:T(8,128)(2,1)S(1)} %get-tuple-element.372), channel_id=1, source_target_pairs={{0,4},{2,6},{4,8},{6,10},{8,12},{10,14},{1,5},{3,7},{5,9},{7,11},{... | collective-permute-start | bytes 1327112 | tf_op jit(solution)/shard_map/ppermute | solution.py:135
  61.9 1.6 %collective-permute-start.19 = (bf16[48,4608]{1,0:T(8,128)(2,1)S(1)}, bf16[48,4608]{1,0:T(8,128)(2,1)S(1)}, u32[]{:S(2)}, u32[]{:S(2)}) collective-permute-start(bf16[48,4608]{1,0:T(8,128)(2,1)S(1)} %get-tuple-element.340.refs_2_), channel_id=1, source_target_pairs={{0,16},{16,0},{1,17},{17,1},{2,18},{18,2},{3,19},{19,3},{4,20},{20... | collective-permute-start | bytes 1327112 | tf_op jit(solution)/shard_map/ppermute | solution.py:141
  63.5 1.3 collective-permute-start.20
  64.8 5.4 %collective-permute-done.16 = bf16[48,4608]{1,0:T(8,128)(2,1)S(1)} collective-permute-done((bf16[48,4608]{1,0:T(8,128)(2,1)S(1)}, bf16[48,4608]{1,0:T(8,128)(2,1)S(1)}, u32[]{:S(2)}, u32[]{:S(2)}) %collective-permute-start.16) | collective-permute-done | bytes 442400 | tf_op jit(solution)/shard_map/ppermute | solution.py:135
  70.2 4.7 %collective-permute-start.21 = (bf16[48,4608]{1,0:T(8,128)(2,1)S(1)}, bf16[48,4608]{1,0:T(8,128)(2,1)S(1)}, u32[]{:S(2)}, u32[]{:S(2)}) collective-permute-start(bf16[48,4608]{1,0:T(8,128)(2,1)S(1)} %get-tuple-element.369), channel_id=1, source_target_pairs={{0,4},{2,6},{4,8},{6,10},{8,12},{10,14},{1,5},{3,7},{5,9},{7,11},{... | collective-permute-start | bytes 1327112 | tf_op jit(solution)/shard_map/ppermute | solution.py:135
  74.9 1.3 collective-permute-start.24
  77.0 1.6 %collective-permute-start.22 = (bf16[48,4608]{1,0:T(8,128)(2,1)S(1)}, bf16[48,4608]{1,0:T(8,128)(2,1)S(1)}, u32[]{:S(2)}, u32[]{:S(2)}) collective-permute-start(bf16[48,4608]{1,0:T(8,128)(2,1)S(1)} %get-tuple-element.338.refs_0_), channel_id=1, source_target_pairs={{0,16},{16,0},{1,17},{17,1},{2,18},{18,2},{3,19},{19,3},{4,20},{20... | collective-permute-start | bytes 1327112 | tf_op jit(solution)/shard_map/ppermute | solution.py:141
  80.7 1.3 collective-permute-start.28
  82.1 7.2 %collective-permute-done.22.refs_6_ = bf16[48,4608]{1,0:T(8,128)(2,1)S(1)} collective-permute-done((bf16[48,4608]{1,0:T(8,128)(2,1)S(1)}, bf16[48,4608]{1,0:T(8,128)(2,1)S(1)}, u32[]{:S(2)}, u32[]{:S(2)}) %collective-permute-start.22) | collective-permute-done | bytes 442400 | tf_op jit(solution)/shard_map/ppermute | solution.py:141
  90.0 2.6 %collective-permute-done.23.refs_5_ = bf16[48,4608]{1,0:T(8,128)(2,1)S(1)} collective-permute-done((bf16[48,4608]{1,0:T(8,128)(2,1)S(1)}, bf16[48,4608]{1,0:T(8,128)(2,1)S(1)}, u32[]{:S(2)}, u32[]{:S(2)}) %collective-permute-start.23) | collective-permute-done | bytes 442400 | tf_op jit(solution)/shard_map/ppermute | solution.py:138
  92.6 2.2 %collective-permute-start.26 = (bf16[48,4608]{1,0:T(8,128)(2,1)S(1)}, bf16[48,4608]{1,0:T(8,128)(2,1)S(1)}, u32[]{:S(2)}, u32[]{:S(2)}) collective-permute-start(bf16[48,4608]{1,0:T(8,128)(2,1)S(1)} %collective-permute-done.7.refs_1_), channel_id=1, source_target_pairs={{0,16},{16,0},{1,17},{17,1},{2,18},{18,2},{3,19},{19,3},{4,20},{20... | collective-permute-start | bytes 1327112 | tf_op jit(solution)/shard_map/ppermute | solution.py:141
  95.0 2.1 %collective-permute-start.32 = (bf16[48,4608]{1,0:T(8,128)(2,1)S(1)}, bf16[48,4608]{1,0:T(8,128)(2,1)S(1)}, u32[]{:S(2)}, u32[]{:S(2)}) collective-permute-start(bf16[48,4608]{1,0:T(8,128)(2,1)S(1)} %get-tuple-element.337.refs_10_), channel_id=1, source_target_pairs={{0,2},{2,0},{4,6},{6,4},{8,10},{10,8},{12,14},{14,12},{1,3},{3,1},... | collective-permute-start | bytes 1327112 | tf_op jit(solution)/shard_map/ppermute | solution.py:138
  97.0 8.9 %collective-permute-done.26.refs_7_ = bf16[48,4608]{1,0:T(8,128)(2,1)S(1)} collective-permute-done((bf16[48,4608]{1,0:T(8,128)(2,1)S(1)}, bf16[48,4608]{1,0:T(8,128)(2,1)S(1)}, u32[]{:S(2)}, u32[]{:S(2)}) %collective-permute-start.26) | collective-permute-done | bytes 442400 | tf_op jit(solution)/shard_map/ppermute | solution.py:141
  105.9 2.0 %collective-permute-start.35 = (bf16[48,4608]{1,0:T(8,128)(2,1)S(1)}, bf16[48,4608]{1,0:T(8,128)(2,1)S(1)}, u32[]{:S(2)}, u32[]{:S(2)}) collective-permute-start(bf16[48,4608]{1,0:T(8,128)(2,1)S(1)} %get-tuple-element.328.refs_2_), channel_id=1, source_target_pairs={{0,16},{16,0},{1,17},{17,1},{2,18},{18,2},{3,19},{19,3},{4,20},{20... | collective-permute-start | bytes 1327112 | tf_op jit(solution)/shard_map/ppermute | solution.py:141
  107.9 1.3 collective-permute-start.31
  110.4 7.7 %collective-permute-done.31 = bf16[48,4608]{1,0:T(8,128)(2,1)S(1)} collective-permute-done((bf16[48,4608]{1,0:T(8,128)(2,1)S(1)}, bf16[48,4608]{1,0:T(8,128)(2,1)S(1)}, u32[]{:S(2)}, u32[]{:S(2)}) %collective-permute-start.31) | collective-permute-done | bytes 442400 | tf_op jit(solution)/shard_map/ppermute | solution.py:135
  118.1 1.3 collective-permute-start.37
  119.5 4.8 %rotate.6 = (f32[288,256]{1,0:T(8,128)S(1)}, f32[288,256]{1,0:T(8,128)S(1)}) custom-call(bf16[256,4096]{1,0:T(8,128)(2,1)S(1)} %bitcast.17, bf16[256,14336]{1,0:T(8,128)(2,1)} %bitcast.8, bf16[48,4608]{1,0:T(8,128)(2,1)S(1)} %get-tuple-element.326.refs_0_, bf16[48,4608]{1,0:T(8,128)(2,1)S(1)} %collective-permute-done.11.refs_1_, ...), custom_call_target="tpu_custom_call" | custom-call | flops 1358954496 | bytes 5308416 | tf_op jit(solution)/shard_map/rotate/pallas_call | solution.py:234
  124.4 3.9 %collective-permute-done.37 = bf16[48,4608]{1,0:T(8,128)(2,1)S(1)} collective-permute-done((bf16[48,4608]{1,0:T(8,128)(2,1)S(1)}, bf16[48,4608]{1,0:T(8,128)(2,1)S(1)}, u32[]{:S(2)}, u32[]{:S(2)}) %collective-permute-start.37) | collective-permute-done | bytes 442400 | tf_op jit(solution)/shard_map/ppermute | solution.py:135
  129.8 3.1 %rotate.4 = (f32[96,256]{1,0:T(8,128)S(1)}, f32[48,256]{1,0:T(8,128)S(1)}, f32[48,256]{1,0:T(8,128)S(1)}) custom-call(bf16[256,4096]{1,0:T(8,128)(2,1)S(1)} %bitcast.19, bf16[256,14336]{1,0:T(8,128)(2,1)S(1)} %bitcast.15, bf16[48,4608]{1,0:T(8,128)(2,1)S(1)} %copy-done.3, bf16[48,4608]{1,0:T(8,128)(2,1)S(1)} %collective-permute-done.refs_1_, ...), custom_call_target="tpu_custom_call" | custom-call | flops 905969664 | bytes 3538944 | tf_op jit(solution)/shard_map/rotate/pallas_call | solution.py:234
  135.8 2.2 %finish.1 = (f32[24,384]{1,0:T(8,128)}, f32[24,384]{1,0:T(8,128)}, f32[24,384]{1,0:T(8,128)}, f32[24,384]{1,0:T(8,128)}, f32[24,384]{1,0:T(8,128)}, /*index=5*/f...) custom-call(s32[16]{0:T(128)} %pad_add_fusion.1.table_ref, f32[96,256]{1,0:T(8,128)} %copy-done.7, ...), custom_call_target="tpu_custom_call" | custom-call | tf_op jit(solution)/shard_map/finish/pallas_call | solution.py:257
  138.1 3.9 %collective-permute-start.45 = (f32[24,384]{1,0:T(8,128)}, f32[24,384]{1,0:T(8,128)S(1)}, u32[]{:S(2)}, u32[]{:S(2)}) collective-permute-start(f32[24,384]{1,0:T(8,128)} %get-tuple-element.363), channel_id=1, source_target_pairs={{0,12},{2,14},{4,8},{6,10},{8,4},{10,6},{12,0},{14,2},{1,13},{3,15... | collective-permute-start | bytes 110600 | tf_op jit(solution)/shard_map/ppermute | solution.py:273
  142.9 2.8 %collective-permute-start.43 = (f32[24,384]{1,0:T(8,128)}, f32[24,384]{1,0:T(8,128)S(1)}, u32[]{:S(2)}, u32[]{:S(2)}) collective-permute-start(f32[24,384]{1,0:T(8,128)} %get-tuple-element.361), channel_id=1, source_target_pairs={{0,8},{2,10},{4,12},{6,14},{8,0},{10,2},{12,4},{14,6},{1,9},{3,11}... | collective-permute-start | bytes 110600 | tf_op jit(solution)/shard_map/ppermute | solution.py:273
  145.7 1.5 collective-permute-start.42
  147.9 1.9 %collective-permute-start.40 = (f32[24,384]{1,0:T(8,128)}, f32[24,384]{1,0:T(8,128)S(1)}, u32[]{:S(2)}, u32[]{:S(2)}) collective-permute-start(f32[24,384]{1,0:T(8,128)} %get-tuple-element.358), channel_id=1, source_target_pairs={{0,2},{2,0},{4,6},{6,4},{8,10},{10,8},{12,14},{14,12},{1,3},{3,1},... | collective-permute-start | bytes 110600 | tf_op jit(solution)/shard_map/ppermute | solution.py:273
  149.8 1.4 collective-permute-done.42
  152.0 1.4 add_multiply_fusion
  (109 shorter events, 16.5 us)
Async XLA Ops:
  2.9 14.2 %collective-permute-start = (bf16[48,4608]{1,0:T(8,128)(2,1)}, bf16[48,4608]{1,0:T(8,128)(2,1)S(1)}, u32[]{:S(2)}, u32[]{:S(2)}) collective-permute-start(bf16[48,4608]{1,0:T(8,128)(2,1)} %get-tuple-element.317.refs_0_), channel_id=1, source_target_pairs={{0,2},{2,0},{4,6},{6,4},{8,10},{10,8},{12,14},{14,12},{1,3},{3,1},... | collective-permute-start | bytes 1327112 | tf_op jit(solution)/shard_map/ppermute | solution.py:138
  5.8 15.3 %collective-permute-start.1 = (bf16[48,4608]{1,0:T(8,128)(2,1)}, bf16[48,4608]{1,0:T(8,128)(2,1)S(1)}, u32[]{:S(2)}, u32[]{:S(2)}) collective-permute-start(bf16[48,4608]{1,0:T(8,128)(2,1)} %get-tuple-element.317.refs_0_), channel_id=1, source_target_pairs={{4,0},{6,2},{8,4},{10,6},{12,8},{14,10},{5,1},{7,3},{9,5},{11,7},{... | collective-permute-start | bytes 1327112 | tf_op jit(solution)/shard_map/ppermute | solution.py:135
  7.1 15.2 %collective-permute-start.2 = (bf16[48,4608]{1,0:T(8,128)(2,1)}, bf16[48,4608]{1,0:T(8,128)(2,1)S(1)}, u32[]{:S(2)}, u32[]{:S(2)}) collective-permute-start(bf16[48,4608]{1,0:T(8,128)(2,1)} %get-tuple-element.317.refs_0_), channel_id=1, source_target_pairs={{0,4},{2,6},{4,8},{6,10},{8,12},{10,14},{1,5},{3,7},{5,9},{7,11},{... | collective-permute-start | bytes 1327112 | tf_op jit(solution)/shard_map/ppermute | solution.py:135
  11.7 14.8 %collective-permute-start.3 = (bf16[48,4608]{1,0:T(8,128)(2,1)}, bf16[48,4608]{1,0:T(8,128)(2,1)S(1)}, u32[]{:S(2)}, u32[]{:S(2)}) collective-permute-start(bf16[48,4608]{1,0:T(8,128)(2,1)} %get-tuple-element.319.refs_2_), channel_id=1, source_target_pairs={{0,2},{2,0},{4,6},{6,4},{8,10},{10,8},{12,14},{14,12},{1,3},{3,1},... | collective-permute-start | bytes 1327112 | tf_op jit(solution)/shard_map/ppermute | solution.py:138
  11.9 17.1 %collective-permute-start.4 = (bf16[48,4608]{1,0:T(8,128)(2,1)}, bf16[48,4608]{1,0:T(8,128)(2,1)S(1)}, u32[]{:S(2)}, u32[]{:S(2)}) collective-permute-start(bf16[48,4608]{1,0:T(8,128)(2,1)} %get-tuple-element.319.refs_2_), channel_id=1, source_target_pairs={{4,0},{6,2},{8,4},{10,6},{12,8},{14,10},{5,1},{7,3},{9,5},{11,7},{... | collective-permute-start | bytes 1327112 | tf_op jit(solution)/shard_map/ppermute | solution.py:135
  17.0 13.3 %collective-permute-start.5 = (bf16[48,4608]{1,0:T(8,128)(2,1)}, bf16[48,4608]{1,0:T(8,128)(2,1)S(1)}, u32[]{:S(2)}, u32[]{:S(2)}) collective-permute-start(bf16[48,4608]{1,0:T(8,128)(2,1)} %get-tuple-element.319.refs_2_), channel_id=1, source_target_pairs={{0,4},{2,6},{4,8},{6,10},{8,12},{10,14},{1,5},{3,7},{5,9},{7,11},{... | collective-permute-start | bytes 1327112 | tf_op jit(solution)/shard_map/ppermute | solution.py:135
  22.3 15.9 %collective-permute-start.6 = (bf16[48,4608]{1,0:T(8,128)(2,1)S(1)}, bf16[48,4608]{1,0:T(8,128)(2,1)S(1)}, u32[]{:S(2)}, u32[]{:S(2)}) collective-permute-start(bf16[48,4608]{1,0:T(8,128)(2,1)S(1)} %collective-permute-done.refs_1_), channel_id=1, source_target_pairs={{0,16},{16,0},{1,17},{17,1},{2,18},{18,2},{3,19},{19,3},{4,20},{20... | collective-permute-start | bytes 1327112 | tf_op jit(solution)/shard_map/ppermute | solution.py:141
  24.9 13.9 %collective-permute-start.7 = (bf16[48,4608]{1,0:T(8,128)(2,1)S(1)}, bf16[48,4608]{1,0:T(8,128)(2,1)S(1)}, u32[]{:S(2)}, u32[]{:S(2)}) collective-permute-start(bf16[48,4608]{1,0:T(8,128)(2,1)S(1)} %get-tuple-element.338.refs_0_), channel_id=1, source_target_pairs={{0,2},{2,0},{4,6},{6,4},{8,10},{10,8},{12,14},{14,12},{1,3},{3,1},... | collective-permute-start | bytes 1327112 | tf_op jit(solution)/shard_map/ppermute | solution.py:138
  30.3 15.3 %collective-permute-start.8 = (bf16[48,4608]{1,0:T(8,128)(2,1)S(1)}, bf16[48,4608]{1,0:T(8,128)(2,1)S(1)}, u32[]{:S(2)}, u32[]{:S(2)}) collective-permute-start(bf16[48,4608]{1,0:T(8,128)(2,1)S(1)} %get-tuple-element.380), channel_id=1, source_target_pairs={{4,0},{6,2},{8,4},{10,6},{12,8},{14,10},{5,1},{7,3},{9,5},{11,7},{... | collective-permute-start | bytes 1327112 | tf_op jit(solution)/shard_map/ppermute | solution.py:135
  31.6 18.0 %collective-permute-start.9 = (bf16[48,4608]{1,0:T(8,128)(2,1)S(1)}, bf16[48,4608]{1,0:T(8,128)(2,1)S(1)}, u32[]{:S(2)}, u32[]{:S(2)}) collective-permute-start(bf16[48,4608]{1,0:T(8,128)(2,1)S(1)} %get-tuple-element.378), channel_id=1, source_target_pairs={{0,4},{2,6},{4,8},{6,10},{8,12},{10,14},{1,5},{3,7},{5,9},{7,11},{... | collective-permute-start | bytes 1327112 | tf_op jit(solution)/shard_map/ppermute | solution.py:135
  36.5 14.8 %collective-permute-start.10 = (bf16[48,4608]{1,0:T(8,128)(2,1)S(1)}, bf16[48,4608]{1,0:T(8,128)(2,1)S(1)}, u32[]{:S(2)}, u32[]{:S(2)}) collective-permute-start(bf16[48,4608]{1,0:T(8,128)(2,1)S(1)} %collective-permute-done.3.refs_3_), channel_id=1, source_target_pairs={{0,16},{16,0},{1,17},{17,1},{2,18},{18,2},{3,19},{19,3},{4,20},{20... | collective-permute-start | bytes 1327112 | tf_op jit(solution)/shard_map/ppermute | solution.py:141
  38.2 13.2 %collective-permute-start.11 = (bf16[48,4608]{1,0:T(8,128)(2,1)S(1)}, bf16[48,4608]{1,0:T(8,128)(2,1)S(1)}, u32[]{:S(2)}, u32[]{:S(2)}) collective-permute-start(bf16[48,4608]{1,0:T(8,128)(2,1)S(1)} %get-tuple-element.326.refs_0_), channel_id=1, source_target_pairs={{0,2},{2,0},{4,6},{6,4},{8,10},{10,8},{12,14},{14,12},{1,3},{3,1},... | collective-permute-start | bytes 1327112 | tf_op jit(solution)/shard_map/ppermute | solution.py:138
  38.8 14.1 %collective-permute-start.12 = (bf16[48,4608]{1,0:T(8,128)(2,1)S(1)}, bf16[48,4608]{1,0:T(8,128)(2,1)S(1)}, u32[]{:S(2)}, u32[]{:S(2)}) collective-permute-start(bf16[48,4608]{1,0:T(8,128)(2,1)S(1)} %get-tuple-element.377), channel_id=1, source_target_pairs={{4,0},{6,2},{8,4},{10,6},{12,8},{14,10},{5,1},{7,3},{9,5},{11,7},{... | collective-permute-start | bytes 1327112 | tf_op jit(solution)/shard_map/ppermute | solution.py:135
  45.7 9.7 %collective-permute-start.13 = (bf16[48,4608]{1,0:T(8,128)(2,1)S(1)}, bf16[48,4608]{1,0:T(8,128)(2,1)S(1)}, u32[]{:S(2)}, u32[]{:S(2)}) collective-permute-start(bf16[48,4608]{1,0:T(8,128)(2,1)S(1)} %get-tuple-element.375), channel_id=1, source_target_pairs={{0,4},{2,6},{4,8},{6,10},{8,12},{10,14},{1,5},{3,7},{5,9},{7,11},{... | collective-permute-start | bytes 1327112 | tf_op jit(solution)/shard_map/ppermute | solution.py:135
  49.6 12.3 %collective-permute-start.14 = (bf16[48,4608]{1,0:T(8,128)(2,1)S(1)}, bf16[48,4608]{1,0:T(8,128)(2,1)S(1)}, u32[]{:S(2)}, u32[]{:S(2)}) collective-permute-start(bf16[48,4608]{1,0:T(8,128)(2,1)S(1)} %get-tuple-element.326.refs_0_), channel_id=1, source_target_pairs={{0,16},{16,0},{1,17},{17,1},{2,18},{18,2},{3,19},{19,3},{4,20},{20... | collective-permute-start | bytes 1327112 | tf_op jit(solution)/shard_map/ppermute | solution.py:141
  51.2 58.3 %slice-start = ((s8[7340032]{0:T(1024)(128)(4,1)}), s8[4194304]{0:T(1024)(128)(4,1)S(1)}, s32[]{:S(2)}) async-start(s8[7340032]{0:T(1024)(128)(4,1)} %bitcast.9), calls=%async_computation | async-start | bytes 8388608
  51.3 12.2 %collective-permute-start.15 = (bf16[48,4608]{1,0:T(8,128)(2,1)S(1)}, bf16[48,4608]{1,0:T(8,128)(2,1)S(1)}, u32[]{:S(2)}, u32[]{:S(2)}) collective-permute-start(bf16[48,4608]{1,0:T(8,128)(2,1)S(1)} %get-tuple-element.340.refs_2_), channel_id=1, source_target_pairs={{0,2},{2,0},{4,6},{6,4},{8,10},{10,8},{12,14},{14,12},{1,3},{3,1},... | collective-permute-start | bytes 1327112 | tf_op jit(solution)/shard_map/ppermute | solution.py:138
  55.4 14.8 %collective-permute-start.16 = (bf16[48,4608]{1,0:T(8,128)(2,1)S(1)}, bf16[48,4608]{1,0:T(8,128)(2,1)S(1)}, u32[]{:S(2)}, u32[]{:S(2)}) collective-permute-start(bf16[48,4608]{1,0:T(8,128)(2,1)S(1)} %get-tuple-element.374), channel_id=1, source_target_pairs={{4,0},{6,2},{8,4},{10,6},{12,8},{14,10},{5,1},{7,3},{9,5},{11,7},{... | collective-permute-start | bytes 1327112 | tf_op jit(solution)/shard_map/ppermute | solution.py:135
  56.7 18.2 %collective-permute-start.17 = (bf16[48,4608]{1,0:T(8,128)(2,1)S(1)}, bf16[48,4608]{1,0:T(8,128)(2,1)S(1)}, u32[]{:S(2)}, u32[]{:S(2)}) collective-permute-start(bf16[48,4608]{1,0:T(8,128)(2,1)S(1)} %get-tuple-element.372), channel_id=1, source_target_pairs={{0,4},{2,6},{4,8},{6,10},{8,12},{10,14},{1,5},{3,7},{5,9},{7,11},{... | collective-permute-start | bytes 1327112 | tf_op jit(solution)/shard_map/ppermute | solution.py:135
  61.8 14.5 %collective-permute-start.18 = (bf16[48,4608]{1,0:T(8,128)(2,1)S(1)}, bf16[48,4608]{1,0:T(8,128)(2,1)S(1)}, u32[]{:S(2)}, u32[]{:S(2)}) collective-permute-start(bf16[48,4608]{1,0:T(8,128)(2,1)S(1)} %get-tuple-element.328.refs_2_), channel_id=1, source_target_pairs={{0,2},{2,0},{4,6},{6,4},{8,10},{10,8},{12,14},{14,12},{1,3},{3,1},... | collective-permute-start | bytes 1327112 | tf_op jit(solution)/shard_map/ppermute | solution.py:138
  61.9 15.1 %collective-permute-start.19 = (bf16[48,4608]{1,0:T(8,128)(2,1)S(1)}, bf16[48,4608]{1,0:T(8,128)(2,1)S(1)}, u32[]{:S(2)}, u32[]{:S(2)}) collective-permute-start(bf16[48,4608]{1,0:T(8,128)(2,1)S(1)} %get-tuple-element.340.refs_2_), channel_id=1, source_target_pairs={{0,16},{16,0},{1,17},{17,1},{2,18},{18,2},{3,19},{19,3},{4,20},{20... | collective-permute-start | bytes 1327112 | tf_op jit(solution)/shard_map/ppermute | solution.py:141
  63.5 16.1 %collective-permute-start.20 = (bf16[48,4608]{1,0:T(8,128)(2,1)S(1)}, bf16[48,4608]{1,0:T(8,128)(2,1)S(1)}, u32[]{:S(2)}, u32[]{:S(2)}) collective-permute-start(bf16[48,4608]{1,0:T(8,128)(2,1)S(1)} %get-tuple-element.371), channel_id=1, source_target_pairs={{4,0},{6,2},{8,4},{10,6},{12,8},{14,10},{5,1},{7,3},{9,5},{11,7},{... | collective-permute-start | bytes 1327112 | tf_op jit(solution)/shard_map/ppermute | solution.py:135
  70.2 10.5 %collective-permute-start.21 = (bf16[48,4608]{1,0:T(8,128)(2,1)S(1)}, bf16[48,4608]{1,0:T(8,128)(2,1)S(1)}, u32[]{:S(2)}, u32[]{:S(2)}) collective-permute-start(bf16[48,4608]{1,0:T(8,128)(2,1)S(1)} %get-tuple-element.369), channel_id=1, source_target_pairs={{0,4},{2,6},{4,8},{6,10},{8,12},{10,14},{1,5},{3,7},{5,9},{7,11},{... | collective-permute-start | bytes 1327112 | tf_op jit(solution)/shard_map/ppermute | solution.py:135
  74.9 19.9 %collective-permute-start.24 = (bf16[48,4608]{1,0:T(8,128)(2,1)S(1)}, bf16[48,4608]{1,0:T(8,128)(2,1)S(1)}, u32[]{:S(2)}, u32[]{:S(2)}) collective-permute-start(bf16[48,4608]{1,0:T(8,128)(2,1)S(1)} %collective-permute-done.16), channel_id=1, source_target_pairs={{4,0},{6,2},{8,4},{10,6},{5,1},{7,3},{9,5},{11,7},{20,16},{22,18},... | collective-permute-start | bytes 1327112 | tf_op jit(solution)/shard_map/ppermute | solution.py:135
  76.3 18.5 %collective-permute-start.25 = (bf16[48,4608]{1,0:T(8,128)(2,1)S(1)}, bf16[48,4608]{1,0:T(8,128)(2,1)S(1)}, u32[]{:S(2)}, u32[]{:S(2)}) collective-permute-start(bf16[48,4608]{1,0:T(8,128)(2,1)S(1)} %collective-permute-done.17), channel_id=1, source_target_pairs={{4,8},{6,10},{8,12},{10,14},{5,9},{7,11},{9,13},{11,15},{20,24},{2... | collective-permute-start | bytes 1327112 | tf_op jit(solution)/shard_map/ppermute | solution.py:135
  77.0 12.3 %collective-permute-start.22 = (bf16[48,4608]{1,0:T(8,128)(2,1)S(1)}, bf16[48,4608]{1,0:T(8,128)(2,1)S(1)}, u32[]{:S(2)}, u32[]{:S(2)}) collective-permute-start(bf16[48,4608]{1,0:T(8,128)(2,1)S(1)} %get-tuple-element.338.refs_0_), channel_id=1, source_target_pairs={{0,16},{16,0},{1,17},{17,1},{2,18},{18,2},{3,19},{19,3},{4,20},{20... | collective-permute-start | bytes 1327112 | tf_op jit(solution)/shard_map/ppermute | solution.py:141
  79.6 13.0 %collective-permute-start.23 = (bf16[48,4608]{1,0:T(8,128)(2,1)S(1)}, bf16[48,4608]{1,0:T(8,128)(2,1)S(1)}, u32[]{:S(2)}, u32[]{:S(2)}) collective-permute-start(bf16[48,4608]{1,0:T(8,128)(2,1)S(1)} %select_select_fusion.7.refs_4_), channel_id=1, source_target_pairs={{0,2},{2,0},{4,6},{6,4},{8,10},{10,8},{12,14},{14,12},{1,3},{3,1},... | collective-permute-start | bytes 1327112 | tf_op jit(solution)/shard_map/ppermute | solution.py:138
  80.7 27.2 %collective-permute-start.28 = (bf16[48,4608]{1,0:T(8,128)(2,1)S(1)}, bf16[48,4608]{1,0:T(8,128)(2,1)S(1)}, u32[]{:S(2)}, u32[]{:S(2)}) collective-permute-start(bf16[48,4608]{1,0:T(8,128)(2,1)S(1)} %collective-permute-done.20), channel_id=1, source_target_pairs={{4,0},{6,2},{8,4},{10,6},{5,1},{7,3},{9,5},{11,7},{20,16},{22,18},... | collective-permute-start | bytes 1327112 | tf_op jit(solution)/shard_map/ppermute | solution.py:135
  89.3 18.6 %collective-permute-start.29 = (bf16[48,4608]{1,0:T(8,128)(2,1)S(1)}, bf16[48,4608]{1,0:T(8,128)(2,1)S(1)}, u32[]{:S(2)}, u32[]{:S(2)}) collective-permute-start(bf16[48,4608]{1,0:T(8,128)(2,1)S(1)} %collective-permute-done.21), channel_id=1, source_target_pairs={{4,8},{6,10},{8,12},{10,14},{5,9},{7,11},{9,13},{11,15},{20,24},{2... | collective-permute-start | bytes 1327112 | tf_op jit(solution)/shard_map/ppermute | solution.py:135
  92.6 13.3 %collective-permute-start.26 = (bf16[48,4608]{1,0:T(8,128)(2,1)S(1)}, bf16[48,4608]{1,0:T(8,128)(2,1)S(1)}, u32[]{:S(2)}, u32[]{:S(2)}) collective-permute-start(bf16[48,4608]{1,0:T(8,128)(2,1)S(1)} %collective-permute-done.7.refs_1_), channel_id=1, source_target_pairs={{0,16},{16,0},{1,17},{17,1},{2,18},{18,2},{3,19},{19,3},{4,20},{20... | collective-permute-start | bytes 1327112 | tf_op jit(solution)/shard_map/ppermute | solution.py:141
  94.8 13.1 %collective-permute-start.27 = (bf16[48,4608]{1,0:T(8,128)(2,1)S(1)}, bf16[48,4608]{1,0:T(8,128)(2,1)S(1)}, u32[]{:S(2)}, u32[]{:S(2)}) collective-permute-start(bf16[48,4608]{1,0:T(8,128)(2,1)S(1)} %collective-permute-done.19.refs_8_), channel_id=1, source_target_pairs={{0,2},{2,0},{4,6},{6,4},{8,10},{10,8},{12,14},{14,12},{1,3},{3,1},... | collective-permute-start | bytes 1327112 | tf_op jit(solution)/shard_map/ppermute | solution.py:138
  95.0 24.5 %collective-permute-start.32 = (bf16[48,4608]{1,0:T(8,128)(2,1)S(1)}, bf16[48,4608]{1,0:T(8,128)(2,1)S(1)}, u32[]{:S(2)}, u32[]{:S(2)}) collective-permute-start(bf16[48,4608]{1,0:T(8,128)(2,1)S(1)} %get-tuple-element.337.refs_10_), channel_id=1, source_target_pairs={{0,2},{2,0},{4,6},{6,4},{8,10},{10,8},{12,14},{14,12},{1,3},{3,1},... | collective-permute-start | bytes 1327112 | tf_op jit(solution)/shard_map/ppermute | solution.py:138
  105.9 22.5 %collective-permute-start.35 = (bf16[48,4608]{1,0:T(8,128)(2,1)S(1)}, bf16[48,4608]{1,0:T(8,128)(2,1)S(1)}, u32[]{:S(2)}, u32[]{:S(2)}) collective-permute-start(bf16[48,4608]{1,0:T(8,128)(2,1)S(1)} %get-tuple-element.328.refs_2_), channel_id=1, source_target_pairs={{0,16},{16,0},{1,17},{17,1},{2,18},{18,2},{3,19},{19,3},{4,20},{20... | collective-permute-start | bytes 1327112 | tf_op jit(solution)/shard_map/ppermute | solution.py:141
  107.9 10.2 %collective-permute-start.31 = (bf16[48,4608]{1,0:T(8,128)(2,1)S(1)}, bf16[48,4608]{1,0:T(8,128)(2,1)S(1)}, u32[]{:S(2)}, u32[]{:S(2)}) collective-permute-start(bf16[48,4608]{1,0:T(8,128)(2,1)S(1)} %get-tuple-element.367), channel_id=1, source_target_pairs={{4,0},{6,2},{8,12},{10,14},{5,1},{7,3},{9,13},{11,15},{20,16},{22,... | collective-permute-start | bytes 1327112 | tf_op jit(solution)/shard_map/ppermute | solution.py:135
  109.2 19.2 %collective-permute-start.34 = (bf16[48,4608]{1,0:T(8,128)(2,1)S(1)}, bf16[48,4608]{1,0:T(8,128)(2,1)S(1)}, u32[]{:S(2)}, u32[]{:S(2)}) collective-permute-start(bf16[48,4608]{1,0:T(8,128)(2,1)S(1)} %collective-permute-done.14.refs_0_), channel_id=1, source_target_pairs={{0,2},{2,0},{4,6},{6,4},{8,10},{10,8},{12,14},{14,12},{1,3},{3,1},... | collective-permute-start | bytes 1327112 | tf_op jit(solution)/shard_map/ppermute | solution.py:138
  109.3 19.1 %collective-permute-start.36 = (bf16[48,4608]{1,0:T(8,128)(2,1)S(1)}, bf16[48,4608]{1,0:T(8,128)(2,1)S(1)}, u32[]{:S(2)}, u32[]{:S(2)}) collective-permute-start(bf16[48,4608]{1,0:T(8,128)(2,1)S(1)} %collective-permute-done.18.refs_3_), channel_id=1, source_target_pairs={{0,16},{16,0},{1,17},{17,1},{2,18},{18,2},{3,19},{19,3},{4,20},{20... | collective-permute-start | bytes 1327112 | tf_op jit(solution)/shard_map/ppermute | solution.py:141
  118.1 10.2 %collective-permute-start.37 = (bf16[48,4608]{1,0:T(8,128)(2,1)S(1)}, bf16[48,4608]{1,0:T(8,128)(2,1)S(1)}, u32[]{:S(2)}, u32[]{:S(2)}) collective-permute-start(bf16[48,4608]{1,0:T(8,128)(2,1)S(1)} %broadcast_select_fusion), channel_id=1, source_target_pairs={{4,0},{6,2},{8,12},{10,14},{5,1},{7,3},{9,13},{11,15},{20,16},{22,... | collective-permute-start | bytes 1327112 | tf_op jit(solution)/shard_map/ppermute | solution.py:135
  124.4 10.6 %collective-permute-start.33 = (f32[288,256]{1,0:T(8,128)S(1)}, f32[288,256]{1,0:T(8,128)S(1)}, u32[]{:S(2)}, u32[]{:S(2)}) collective-permute-start(f32[288,256]{1,0:T(8,128)S(1)} %get-tuple-element.346.refs_2_), channel_id=1, source_target_pairs={{0,1},{1,0},{2,3},{3,2},{4,5},{5,4},{6,7},{7,6},{8,9},{9,8},{10,11... | collective-permute-start | bytes 884744 | tf_op jit(solution)/shard_map/ppermute | solution.py:144
  129.4 5.5 %collective-permute-start.39 = (f32[144,256]{1,0:T(8,128)S(1)}, f32[144,256]{1,0:T(8,128)S(1)}, u32[]{:S(2)}, u32[]{:S(2)}) collective-permute-start(f32[144,256]{1,0:T(8,128)S(1)} %get-tuple-element.356), channel_id=1, source_target_pairs={{0,1},{1,0},{2,3},{3,2},{4,5},{5,4},{6,7},{7,6},{8,9},{9,8},{10,11... | collective-permute-start | bytes 442376 | tf_op jit(solution)/shard_map/ppermute | solution.py:144
  133.5 1.5 collective-permute-start.30
  133.7 1.2 collective-permute-start.38
  138.1 9.2 %collective-permute-start.46 = (f32[24,384]{1,0:T(8,128)}, f32[24,384]{1,0:T(8,128)S(1)}, u32[]{:S(2)}, u32[]{:S(2)}) collective-permute-start(f32[24,384]{1,0:T(8,128)} %get-tuple-element.364), channel_id=1, source_target_pairs={{0,14},{2,12},{4,10},{6,8},{8,6},{10,4},{12,2},{14,0},{1,15},{3,13... | collective-permute-start | bytes 110600 | tf_op jit(solution)/shard_map/ppermute | solution.py:273
  138.1 9.8 %collective-permute-start.45 = (f32[24,384]{1,0:T(8,128)}, f32[24,384]{1,0:T(8,128)S(1)}, u32[]{:S(2)}, u32[]{:S(2)}) collective-permute-start(f32[24,384]{1,0:T(8,128)} %get-tuple-element.363), channel_id=1, source_target_pairs={{0,12},{2,14},{4,8},{6,10},{8,4},{10,6},{12,0},{14,2},{1,13},{3,15... | collective-permute-start | bytes 110600 | tf_op jit(solution)/shard_map/ppermute | solution.py:273
  142.0 7.8 %collective-permute-start.44 = (f32[24,384]{1,0:T(8,128)}, f32[24,384]{1,0:T(8,128)S(1)}, u32[]{:S(2)}, u32[]{:S(2)}) collective-permute-start(f32[24,384]{1,0:T(8,128)} %get-tuple-element.362), channel_id=1, source_target_pairs={{0,10},{2,8},{4,14},{6,12},{8,2},{10,0},{12,6},{14,4},{1,11},{3,9}... | collective-permute-start | bytes 110600 | tf_op jit(solution)/shard_map/ppermute | solution.py:273
  142.9 6.9 %collective-permute-start.43 = (f32[24,384]{1,0:T(8,128)}, f32[24,384]{1,0:T(8,128)S(1)}, u32[]{:S(2)}, u32[]{:S(2)}) collective-permute-start(f32[24,384]{1,0:T(8,128)} %get-tuple-element.361), channel_id=1, source_target_pairs={{0,8},{2,10},{4,12},{6,14},{8,0},{10,2},{12,4},{14,6},{1,9},{3,11}... | collective-permute-start | bytes 110600 | tf_op jit(solution)/shard_map/ppermute | solution.py:273
  145.7 5.5 %collective-permute-start.42 = (f32[24,384]{1,0:T(8,128)}, f32[24,384]{1,0:T(8,128)S(1)}, u32[]{:S(2)}, u32[]{:S(2)}) collective-permute-start(f32[24,384]{1,0:T(8,128)} %get-tuple-element.360), channel_id=1, source_target_pairs={{0,6},{2,4},{4,2},{6,0},{8,14},{10,12},{12,10},{14,8},{1,7},{3,5},... | collective-permute-start | bytes 110600 | tf_op jit(solution)/shard_map/ppermute | solution.py:273
  147.2 4.2 %collective-permute-start.41 = (f32[24,384]{1,0:T(8,128)}, f32[24,384]{1,0:T(8,128)S(1)}, u32[]{:S(2)}, u32[]{:S(2)}) collective-permute-start(f32[24,384]{1,0:T(8,128)} %get-tuple-element.359), channel_id=1, source_target_pairs={{0,4},{2,6},{4,0},{6,2},{8,12},{10,14},{12,8},{14,10},{1,5},{3,7},... | collective-permute-start | bytes 110600 | tf_op jit(solution)/shard_map/ppermute | solution.py:273
  147.9 4.2 %collective-permute-start.40 = (f32[24,384]{1,0:T(8,128)}, f32[24,384]{1,0:T(8,128)S(1)}, u32[]{:S(2)}, u32[]{:S(2)}) collective-permute-start(f32[24,384]{1,0:T(8,128)} %get-tuple-element.358), channel_id=1, source_target_pairs={{0,2},{2,0},{4,6},{6,4},{8,10},{10,8},{12,14},{14,12},{1,3},{3,1},... | collective-permute-start | bytes 110600 | tf_op jit(solution)/shard_map/ppermute | solution.py:273
  (18 other events, 159.8 us)

commit v3 on v2

v3 whole, which is shorter than its diff:
```python
import functools

import jax
import jax.numpy as jnp
from jax import lax
from jax.experimental import pallas as pl
from jax.experimental.pallas import tpu as pltpu
from jax.sharding import PartitionSpec as P

TOK = 256
K = 384
LANES = 128
AHEAD = 5


def place_cols(left, piece):
    product = jnp.dot(left, piece, preferred_element_type=jnp.float32)
    return product


def per_device_any(activations, out_grads, input_basis, output_basis):
    acts = activations[0]
    grads = out_grads[0]
    tokens = acts.shape[0]
    part_in = place_cols(acts, lax.all_gather(input_basis, "dp", axis=1, tiled=True))
    part_out = place_cols(grads, lax.all_gather(output_basis, "dp", axis=1, tiled=True))
    rot_in = lax.psum(part_in, "basis").astype(jnp.bfloat16)
    data_count = lax.axis_size("dp")
    panel_count = lax.axis_size("basis")
    block = K // (data_count * panel_count)
    ordered = part_out.reshape(tokens, data_count, panel_count, block)
    ordered = jnp.transpose(ordered, (0, 2, 1, 3)).reshape(tokens, K)
    rot_out = lax.psum_scatter(ordered, "basis", scatter_dimension=1, tiled=True).astype(
        jnp.bfloat16
    )
    coeff = lax.dot_general(
        rot_out, rot_in, (((0,), (0,)), ((), ())), preferred_element_type=jnp.float32
    )
    coeff = coeff / jnp.sqrt(jnp.float32(TOK))
    summed = lax.psum_scatter(coeff * coeff, "dp", scatter_dimension=0, tiled=True)
    return summed / jnp.float32(data_count)


def nt_dot(left, right):
    return lax.dot_general(
        left, right, (((1,), (1,)), ((), ())), preferred_element_type=jnp.float32
    )


def cut_kernel(in_half, first, in_ref, out_ref, m0, m1, t0, t1):
    x = lax.axis_index("group")
    out_half = first + m1.shape[1]
    for side, unit0, unit1 in ((x, m0, m1), (1 - x, t0, t1)):
        in_at = pl.multiple_of(side * in_half, LANES)
        out_at = pl.multiple_of(side * out_half, LANES)
        next_at = pl.multiple_of(side * out_half + first, LANES)
        unit0[:, :in_half] = in_ref[:, pl.ds(in_at, in_half)]
        unit0[:, in_half:] = out_ref[:, pl.ds(out_at, first)]
        unit1[...] = out_ref[:, pl.ds(next_at, unit1.shape[1])]


def rotate_kernel(plan, in_half, first, acts_ref, grads_ref, *refs):
    x = lax.axis_index("group")
    core = lax.axis_index("basis")
    terms, has_acc, last = plan
    refs = list(refs)
    stack = refs.pop()
    z = lax.axis_index("dp") // 2
    outer = (z == 0) | (z == 3)
    out_half = grads_ref.shape[1] // 2
    rot_in = rot_out = None
    for mine, index, pieces in terms:
        rows = refs[0].shape[0]
        for i, (at_outer, at_inner) in enumerate(pieces):
            at = slice(i * rows, (i + 1) * rows)
            if at_outer == at_inner:
                stack[at] = refs[at_outer][...]
                continue

            @pl.when(outer)
            def _():
                stack[at] = refs[at_outer][...]

            @pl.when(jnp.logical_not(outer))
            def _():
                stack[at] = refs[at_inner][...]

        side = x if mine else 1 - x
        if index == 0:
            cols = pl.ds(pl.multiple_of(side * in_half, LANES), in_half)
            part = nt_dot(stack[:, :in_half], acts_ref[:, cols])
            rot_in = part if rot_in is None else rot_in + part
            cols = pl.ds(pl.multiple_of(side * out_half, LANES), first)
            part = nt_dot(stack[:, in_half:], grads_ref[:, cols])
        else:
            cols = pl.ds(pl.multiple_of(side * out_half + first, LANES), out_half - first)
            part = nt_dot(stack[...], grads_ref[:, cols])
        rot_out = part if rot_out is None else rot_out + part
    panel = refs[0].shape[0] // 2
    refs = refs[1 + max(i for term in terms for pair in term[2] for i in pair) :]
    if has_acc:
        if rot_in is not None:
            rot_in += refs.pop(0)[...]
        rot_out += refs.pop(0)[...]
    if rot_in is not None:
        refs.pop(0)[...] = rot_in
    if not last:
        refs.pop(0)[...] = rot_out
        return
    keep, send = refs
    for shard in range(rot_out.shape[0] // (2 * panel)):
        low = rot_out[2 * shard * panel : (2 * shard + 1) * panel]
        high = rot_out[(2 * shard + 1) * panel : 2 * (shard + 1) * panel]
        at = slice(shard * panel, (shard + 1) * panel)
        keep[at] = jnp.where(core == 0, low, high)
        send[at] = jnp.where(core == 0, high, low)


def finish_kernel(rows, *refs):
    me = lax.axis_index("dp")
    z, y = me // 2, me % 2
    order = [z]
    for by_z in ((1, 2, 1, 2), (2, 0, 3, 1), (3, 3, 0, 0)):
        order.append(jnp.where(z == 0, by_z[0], jnp.where(z == 1, by_z[1], jnp.where(z == 2, by_z[2], by_z[3]))))
    ins, keep, come = refs[0:4], refs[4:6], refs[6:8]
    outs = refs[8:-2]
    in_ref, out_ref = refs[-2:]
    half = rows // 2
    for shard in range(8):
        part, local = (0, shard) if shard < 2 else (1, shard - 2)
        owner = order[shard // 2] * 2 + (y if shard % 2 == 0 else 1 - y)
        block = ins[2 * part][pl.ds(local * rows, rows)] + ins[2 * part + 1][pl.ds(local * rows, rows)]
        in_ref[pl.ds(pl.multiple_of(owner * rows, 16), rows), :] = block.astype(jnp.bfloat16)
        place = owner ^ me
        at = pl.ds(local * half, half)
        out_ref[pl.ds(pl.multiple_of(place * half, 8), half), :] = keep[part][at] + come[part][at]
    coeff = nt_dot(out_ref[...].astype(jnp.bfloat16), in_ref[...])
    coeff = coeff * (1.0 / TOK**0.5)
    square = coeff * coeff
    for place, ref in enumerate(outs):
        ref[...] = square[place * half : (place + 1) * half]


def per_device_plane(activations, out_grads, input_basis, output_basis):
    acts, grads = activations[0], out_grads[0]
    in_t, out_t = input_basis.T, output_basis.T
    rows = in_t.shape[0]
    tokens = acts.shape[0]
    me = lax.axis_index("dp")
    z, y = me // 2, me % 2
    in_half = in_t.shape[1] // 2
    width = (in_t.shape[1] + out_t.shape[1]) // 4
    first = width - in_half

    vmem = pl.BlockSpec(memory_space=pltpu.VMEM)

    def swap_core(value):
        return lax.ppermute(value, "basis", [(0, 1), (1, 0)])

    unit = jax.ShapeDtypeStruct((rows, width), in_t.dtype)
    m0, m1, t0, t1 = pl.pallas_call(
        functools.partial(cut_kernel, in_half, first),
        out_shape=[unit] * 4,
        in_specs=[vmem] * 2,
        out_specs=[vmem] * 4,
        name="cut",
    )(in_t, out_t)

    def rotate(slots, names, acc, last):
        terms, pieces, out_shape = [], [], []
        count = 2 * len(slots)

        def ref_of(value):
            for i, piece in enumerate(pieces):
                if piece is value:
                    return i
            pieces.append(value)
            return len(pieces) - 1

        for name in names:
            terms.append((name[0] == "m", int(name[1]), [
                (ref_of(at_outer[s + k]), ref_of(at_inner[s + k])) for s in slots for k in (name, "o" + name)
            ]))
        full = jax.ShapeDtypeStruct((count * rows, tokens), jnp.float32)
        panel = jax.ShapeDtypeStruct((count * rows // 2, tokens), jnp.float32)
        if any(name[1] == "0" for name in names):
            out_shape.append(full)
        out_shape += [panel, panel] if last else [full]
        return pl.pallas_call(
            functools.partial(rotate_kernel, (terms, bool(acc), last), in_half, first),
            out_shape=out_shape,
            in_specs=[vmem] * (2 + len(pieces) + len(acc)),
            out_specs=[vmem] * len(out_shape),
            scratch_shapes=[pltpu.VMEM((count * rows, width), in_t.dtype)],
            compiler_params=pltpu.CompilerParams(vmem_limit_bytes=20 * 2**20),
            cost_estimate=pl.CostEstimate(
                flops=2 * len(names) * count * rows * width * tokens,
                bytes_accessed=2 * len(pieces) * rows * width,
                transcendentals=0,
            ),
            name="rotate",
        )(acts, grads, *pieces, *acc)

    outer = (z == 0) | (z == 3)
    cells = range(8)
    link_a = [(i, i ^ 2) for i in cells]
    link_b = [(i, 2 * (3 - i // 2) + i % 2) for i in cells if 2 <= i < 6]
    link_y = [(i, i ^ 1) for i in cells]
    at_ends = [i for i in cells if i < 2 or i >= 6]

    def group_pairs(pairs):
        return [(8 * g + a, 8 * g + b) for g in range(2) for a, b in pairs]

    def across_x(where):
        return [(8 * g + i, 8 * (1 - g) + i) for g in range(2) for i in where]

    def send(value, pairs):
        return lax.ppermute(value, ("group", "dp"), pairs)

    def pick(for_outer, for_inner):
        if for_outer is for_inner:
            return for_outer
        return jnp.where(outer, for_outer, for_inner)

    at_outer = {"0m0": m0, "0m1": m1, "0t0": t0, "0t1": t1}
    at_inner = dict(at_outer)
    a_outer = ["1m0", "1m1", "2m0", "2m1", "3m0", "3m1", "3om0", "3t0", "3ot0", "3t1"]
    a_inner = ["2m0", "2m1", "2om0", "2t0", "2ot0", "2t1", "2om1", "2ot1"]
    b_inner = ["1m0", "1m1", "3m0", "3m1", "3om0", "3t0", "3ot0", "3t1", "3om1", "3ot1"]
    y_outer = ["0om0", "0om1", "1om0", "1om1", "2om0", "2om1", "1ot1", "3om1", "2ot0", "2ot1"]
    x_outer = [None, None, "0ot0", "0ot1", "1t1", "2t0", "1t0", "2t1", "1ot0", "3ot1"]
    y_inner = ["0om0", "0om1", None, None, "1om0", "1om1", None, None, None, "1ot1"]
    x_inner = [None, None, "0ot0", "0ot1", None, None, "1t0", "1t1", "1ot0", None]
    to_inner = ["0" + name[1:] for name in a_inner]

    def over_y(name):
        return name.replace("o", "")

    def over_x(name):
        return name.translate(str.maketrans("mt", "tm"))

    extra, sent = {}, []

    def settle():
        if len(sent) >= AHEAD:
            extra["sent"] = sent[-AHEAD]
        spots = [(u, k) for u in (at_outer, at_inner, extra) for k in u]
        unique = {id(u[k]): u[k] for u, k in spots}
        fresh = dict(zip(unique, lax.optimization_barrier(tuple(unique.values()))))
        for u, k in spots:
            u[k] = fresh[id(u[k])]

    def bring(value, pairs, *landings):
        got = send(value, pairs)
        sent.append(got)
        return [(units, name, got) for units, name in landings]

    landing = {}
    for r in range(1, 11):
        i = r - 1
        for units, name, value in landing.pop(r - 2, []):
            units[name] = value
        settle()
        outward = at_inner["0" + a_outer[i][1:]] if r < 3 else at_inner[b_inner[i - 2]]
        if r < 9:
            value, pairs = pick(at_outer[to_inner[i]], outward), group_pairs(link_a)
            spots = [(at_outer, a_outer[i]), (at_inner, a_inner[i])]
        else:
            value, pairs = outward, group_pairs([p for p in link_a if p[1] in at_ends])
            spots = [(at_outer, a_outer[i])]
        landing[r] = bring(value, pairs, *spots)
        settle()
        crossing = at_inner["0" + b_inner[i][1:]] if r < 3 else at_inner[a_inner[i - 2]]
        value = at_outer[over_y(y_outer[i])]
        spots = [(at_outer, y_outer[i])]
        if y_inner[i]:
            value, pairs = pick(value, at_inner[over_y(y_inner[i])]), group_pairs(link_y)
            spots.append((at_inner, y_inner[i]))
        else:
            y_pairs = [p for p in link_y if p[0] in at_ends]
            value, pairs = pick(value, crossing), group_pairs(y_pairs + link_b)
            spots.append((at_inner, b_inner[i]))
        landing[r] += bring(value, pairs, *spots)
        settle()
        if x_inner[i]:
            value = pick(at_outer[over_x(x_outer[i])], at_inner[over_x(x_inner[i])])
            spots, pairs = [(at_inner, x_inner[i])], across_x(cells)
        else:
            crossing = at_inner["0" + b_inner[i][1:]] if r < 3 else at_inner[a_inner[i - 2]]
            spots, pairs = [(at_inner, b_inner[i])], group_pairs(link_b)
            value = crossing
            if x_outer[i]:
                value = pick(at_outer[over_x(x_outer[i])], crossing)
                pairs = across_x(at_ends) + pairs
        if x_outer[i]:
            spots.append((at_outer, x_outer[i]))
        landing[r] += bring(value, pairs, *spots)
        if r == 7:
            extra["in_a"], extra["keep_a"], extra["send_a"] = rotate("0", ["m0", "m1", "t0", "t1"], [], True)
        if r == 9:
            extra["acc_in"], extra["acc_out"] = rotate("123", ["m0"], [], False)
    for r in (9, 10):
        for units, name, value in landing.pop(r):
            units[name] = value
    in_a, keep_a, send_a = extra["in_a"], extra["keep_a"], extra["send_a"]
    in_b, acc_out = rotate("123", ["t0"], [extra["acc_in"], extra["acc_out"]], False)
    (acc_out,) = rotate("123", ["m1"], [acc_out], False)
    keep_b, send_b = rotate("123", ["t1"], [acc_out], True)

    squares = pl.pallas_call(
        functools.partial(finish_kernel, rows),
        out_shape=[jax.ShapeDtypeStruct((rows // 2, K), jnp.float32)] * 8,
        in_specs=[vmem] * 8,
        out_specs=[vmem] * 8,
        scratch_shapes=[
            pltpu.VMEM((K, tokens), jnp.bfloat16),
            pltpu.VMEM((K // 2, tokens), jnp.float32),
        ],
        name="finish",
    )(
        in_a, swap_core(in_a), in_b, swap_core(in_b),
        keep_a, keep_b, swap_core(send_a), swap_core(send_b),
    )
    total = squares[0]
    for k in range(1, 8):
        total = total + lax.ppermute(squares[k], "dp", [(i, i ^ k) for i in range(8)])
    return total * (1.0 / 8)


def solution(mesh):
    in_specs = (
        P(("group", "dp"), None, "basis"),
        P(("group", "dp"), None, "basis"),
        P("basis", "dp"),
        P("basis", "dp"),
    )
    out_specs = P(("group", "dp", "basis"), None)
    plane = (mesh.shape["group"], mesh.shape["dp"], mesh.shape["basis"]) == (2, 8, 2)
    return jax.shard_map(
        per_device_plane if plane else per_device_any,
        mesh=mesh,
        in_specs=in_specs,
        out_specs=out_specs,
        check_vma=False,
    )
```

time: 154 us -> 141 us (0.916)
  starting transfers between devices: 72.3 us -> 58.9 us
  waiting for transfers between devices: 59.2 us -> 63.8 us
  Pallas kernels: 14.8 us -> 12.4 us
    ppermute x36 -> x30, starting transfers between devices: 60 us -> 47.1 us  [send(): return lax.ppermute(value, ('group', 'dp'), pairs)]
    ppermute x36 -> x30, waiting for transfers between devices: 56.5 us -> 59.3 us  [send(): return lax.ppermute(value, ('group', 'dp'), pairs)]
    pallas_call x4 -> x5, Pallas kernels: 9.7 us -> 7.35 us  [rotate(): pl.pallas_call(functools.partial(rotate_kernel, (terms, bool(acc), last),...]
  transfers between devices with their start and end apart: 47 -> 41, of which waited for: 20 -> 24; matrix products, arithmetic and copies ran while one was open for 2% -> 1% of each run, Pallas kernels for 6% -> 5%
where the time goes in v3:
time: 141 us; the launch traced here: 140 us
  waiting for transfers between devices  63.8 us (45%)
  starting transfers between devices  58.9 us (42%)
  Pallas kernels  12.4 us (9%)
  other arithmetic  3.19 us (2%)
  local copies, waits for them, and re-layouts  1.51 us (1%)
    ppermute x30, waiting for transfers between devices, send(): return lax.ppermute(value, ('group', 'dp'), pairs)  59.3 us
    ppermute x30, starting transfers between devices, send(): return lax.ppermute(value, ('group', 'dp'), pairs)  47.1 us
    ppermute x7, starting transfers between devices, per_device_plane(): lax.ppermute(squares[k], 'dp', [(i, i ^ k) for i in range(8)])  11.2 us
    pallas_call x5, Pallas kernels, rotate(): pl.pallas_call(functools.partial(rotate_kernel, (terms, bool(acc), last),...  7.35 us
    ppermute x7, waiting for transfers between devices, per_device_plane(): lax.ppermute(squares[k], 'dp', [(i, i ^ k) for i in range(8)])  3.29 us
    pallas_call x1, Pallas kernels, per_device_plane(): pl.pallas_call(functools.partial(cut_kernel, in_half, first), out_shape=[...  2.84 us
  transfers between devices with their start and end apart: 41, of which 24 were waited for; matrix products, arithmetic and copies ran while one was open for 1% of the time, Pallas kernels for 5%

profile of v3, /device:TPU:0, one launch (start us, length us, event | category | flops | bytes accessed | tf_op | source)
XLA Modules:
  0.0 140.2 jit_solution(18204723508234685090)
XLA Ops:
  0.0 2.8 %cut.1 = (bf16[48,4608]{1,0:T(8,128)(2,1)}, bf16[48,4608]{1,0:T(8,128)(2,1)}, bf16[48,4608]{1,0:T(8,128)(2,1)}, bf16[48,4608]{1,0:T(8,128)(2,1)}) custom-call(bf16[48,4096]{1,0:T(8,128)(2,1)} %bitcast.17, bf16[48,14336]{1,0:T(8,128)(2,1)} %bitcast.16), custom_call_target="tpu_custom_call" | custom-call | tf_op jit(solution)/shard_map/cut/pallas_call | solution.py:161
  2.8 3.0 %collective-permute-start = (bf16[48,4608]{1,0:T(8,128)(2,1)}, bf16[48,4608]{1,0:T(8,128)(2,1)S(1)}, u32[]{:S(2)}, u32[]{:S(2)}) collective-permute-start(bf16[48,4608]{1,0:T(8,128)(2,1)} %get-tuple-element.405), channel_id=1, source_target_pairs={{0,4},{2,6},{4,0},{6,2},{8,12},{10,14},{12,8},{14,10},{16,20},{18,... | collective-permute-start | bytes 1327112 | tf_op jit(solution)/shard_map/ppermute | solution.py:218
  5.9 1.5 %collective-permute-start.1 = (bf16[48,4608]{1,0:T(8,128)(2,1)}, bf16[48,4608]{1,0:T(8,128)(2,1)S(1)}, u32[]{:S(2)}, u32[]{:S(2)}) collective-permute-start(bf16[48,4608]{1,0:T(8,128)(2,1)} %get-tuple-element.405), channel_id=1, source_target_pairs={{0,2},{2,0},{4,6},{6,4},{8,10},{10,8},{12,14},{14,12},{16,18},{18,... | collective-permute-start | bytes 1327112 | tf_op jit(solution)/shard_map/ppermute | solution.py:218
  8.1 4.4 %collective-permute-start.3 = (bf16[48,4608]{1,0:T(8,128)(2,1)}, bf16[48,4608]{1,0:T(8,128)(2,1)S(1)}, u32[]{:S(2)}, u32[]{:S(2)}) collective-permute-start(bf16[48,4608]{1,0:T(8,128)(2,1)} %get-tuple-element.426), channel_id=1, source_target_pairs={{0,4},{2,6},{4,0},{6,2},{8,12},{10,14},{12,8},{14,10},{16,20},{18,... | collective-permute-start | bytes 1327112 | tf_op jit(solution)/shard_map/ppermute | solution.py:218
  13.0 4.1 %collective-permute-done.refs_0_ = bf16[48,4608]{1,0:T(8,128)(2,1)S(1)} collective-permute-done((bf16[48,4608]{1,0:T(8,128)(2,1)}, bf16[48,4608]{1,0:T(8,128)(2,1)S(1)}, u32[]{:S(2)}, u32[]{:S(2)}) %collective-permute-start) | collective-permute-done | bytes 442400 | tf_op jit(solution)/shard_map/ppermute | solution.py:218
  17.8 1.4 %collective-permute-done.1.refs_1_ = bf16[48,4608]{1,0:T(8,128)(2,1)S(1)} collective-permute-done((bf16[48,4608]{1,0:T(8,128)(2,1)}, bf16[48,4608]{1,0:T(8,128)(2,1)S(1)}, u32[]{:S(2)}, u32[]{:S(2)}) %collective-permute-start.1) | collective-permute-done | bytes 442400 | tf_op jit(solution)/shard_map/ppermute | solution.py:218
  19.2 1.6 %collective-permute-start.7 = (bf16[48,4608]{1,0:T(8,128)(2,1)S(1)}, bf16[48,4608]{1,0:T(8,128)(2,1)S(1)}, u32[]{:S(2)}, u32[]{:S(2)}) collective-permute-start(bf16[48,4608]{1,0:T(8,128)(2,1)S(1)} %collective-permute-done.refs_0_), channel_id=1, source_target_pairs={{0,2},{2,0},{12,14},{14,12},{4,8},{6,10},{8,4},{10,6},{16,18},{18,... | collective-permute-start | bytes 1327112 | tf_op jit(solution)/shard_map/ppermute | solution.py:218
  20.8 4.9 %collective-permute-done.3.refs_0_ = bf16[48,4608]{1,0:T(8,128)(2,1)S(1)} collective-permute-done((bf16[48,4608]{1,0:T(8,128)(2,1)}, bf16[48,4608]{1,0:T(8,128)(2,1)S(1)}, u32[]{:S(2)}, u32[]{:S(2)}) %collective-permute-start.3) | collective-permute-done | bytes 442400 | tf_op jit(solution)/shard_map/ppermute | solution.py:218
  25.7 1.7 %collective-permute-start.6 = (bf16[48,4608]{1,0:T(8,128)(2,1)S(1)}, bf16[48,4608]{1,0:T(8,128)(2,1)S(1)}, u32[]{:S(2)}, u32[]{:S(2)}) collective-permute-start(bf16[48,4608]{1,0:T(8,128)(2,1)S(1)} %broadcast_select_fusion.15), channel_id=1, source_target_pairs={{0,4},{2,6},{4,0},{6,2},{8,12},{10,14},{12,8},{14,10},{16,20},{18,... | collective-permute-start | bytes 1327112 | tf_op jit(solution)/shard_map/ppermute | solution.py:218
  27.5 1.5 %collective-permute-start.8 = (bf16[48,4608]{1,0:T(8,128)(2,1)S(1)}, bf16[48,4608]{1,0:T(8,128)(2,1)S(1)}, u32[]{:S(2)}, u32[]{:S(2)}) collective-permute-start(bf16[48,4608]{1,0:T(8,128)(2,1)S(1)} %collective-permute-done.1.refs_1_), channel_id=1, source_target_pairs={{0,16},{2,18},{4,20},{6,22},{8,24},{10,26},{12,28},{14,30},{16,0},... | collective-permute-start | bytes 1327112 | tf_op jit(solution)/shard_map/ppermute | solution.py:218
  29.0 1.1 broadcast_select_fusion.14
  30.0 1.6 %collective-permute-start.10 = (bf16[48,4608]{1,0:T(8,128)(2,1)S(1)}, bf16[48,4608]{1,0:T(8,128)(2,1)S(1)}, u32[]{:S(2)}, u32[]{:S(2)}) collective-permute-start(bf16[48,4608]{1,0:T(8,128)(2,1)S(1)} %collective-permute-done.3.refs_0_), channel_id=1, source_target_pairs={{0,2},{2,0},{12,14},{14,12},{4,8},{6,10},{8,4},{10,6},{16,18},{18,... | collective-permute-start | bytes 1327112 | tf_op jit(solution)/shard_map/ppermute | solution.py:218
  31.6 5.5 %collective-permute-done.6.refs_4_ = bf16[48,4608]{1,0:T(8,128)(2,1)S(1)} collective-permute-done((bf16[48,4608]{1,0:T(8,128)(2,1)S(1)}, bf16[48,4608]{1,0:T(8,128)(2,1)S(1)}, u32[]{:S(2)}, u32[]{:S(2)}) %collective-permute-start.6) | collective-permute-done | bytes 442400 | tf_op jit(solution)/shard_map/ppermute | solution.py:218
  37.1 1.3 collective-permute-start.11
  38.5 5.5 %collective-permute-start.9 = (bf16[48,4608]{1,0:T(8,128)(2,1)S(1)}, bf16[48,4608]{1,0:T(8,128)(2,1)S(1)}, u32[]{:S(2)}, u32[]{:S(2)}) collective-permute-start(bf16[48,4608]{1,0:T(8,128)(2,1)S(1)} %broadcast_select_fusion.14), channel_id=1, source_target_pairs={{0,4},{2,6},{4,0},{6,2},{8,12},{10,14},{12,8},{14,10},{16,20},{18,... | collective-permute-start | bytes 1327112 | tf_op jit(solution)/shard_map/ppermute | solution.py:218
  44.1 1.6 %collective-permute-start.13 = (bf16[48,4608]{1,0:T(8,128)(2,1)S(1)}, bf16[48,4608]{1,0:T(8,128)(2,1)S(1)}, u32[]{:S(2)}, u32[]{:S(2)}) collective-permute-start(bf16[48,4608]{1,0:T(8,128)(2,1)S(1)} %broadcast_select_fusion.12), channel_id=1, source_target_pairs={{0,2},{2,0},{4,6},{6,4},{8,10},{10,8},{12,14},{14,12},{16,18},{18,... | collective-permute-start | bytes 1327112 | tf_op jit(solution)/shard_map/ppermute | solution.py:218
  45.6 8.3 %collective-permute-done.9.refs_3_.refs_4_ = bf16[48,4608]{1,0:T(8,128)(2,1)S(1)} collective-permute-done((bf16[48,4608]{1,0:T(8,128)(2,1)S(1)}, bf16[48,4608]{1,0:T(8,128)(2,1)S(1)}, u32[]{:S(2)}, u32[]{:S(2)}) %collective-permute-start.9) | collective-permute-done | bytes 442400 | tf_op jit(solution)/shard_map/ppermute | solution.py:218
  54.1 6.0 %collective-permute-done.12.refs_5_ = bf16[48,4608]{1,0:T(8,128)(2,1)S(1)} collective-permute-done((bf16[48,4608]{1,0:T(8,128)(2,1)S(1)}, bf16[48,4608]{1,0:T(8,128)(2,1)S(1)}, u32[]{:S(2)}, u32[]{:S(2)}) %collective-permute-start.12) | collective-permute-done | bytes 442400 | tf_op jit(solution)/shard_map/ppermute | solution.py:218
  60.1 1.5 %collective-permute-start.14 = (bf16[48,4608]{1,0:T(8,128)(2,1)S(1)}, bf16[48,4608]{1,0:T(8,128)(2,1)S(1)}, u32[]{:S(2)}, u32[]{:S(2)}) collective-permute-start(bf16[48,4608]{1,0:T(8,128)(2,1)S(1)} %broadcast_select_fusion.11), channel_id=1, source_target_pairs={{0,16},{2,18},{12,28},{14,30},{16,0},{18,2},{28,12},{30,14},{4,8},... | collective-permute-start | bytes 1327112 | tf_op jit(solution)/shard_map/ppermute | solution.py:218
  61.6 3.7 %collective-permute-start.15 = (bf16[48,4608]{1,0:T(8,128)(2,1)S(1)}, bf16[48,4608]{1,0:T(8,128)(2,1)S(1)}, u32[]{:S(2)}, u32[]{:S(2)}) collective-permute-start(bf16[48,4608]{1,0:T(8,128)(2,1)S(1)} %broadcast_select_fusion.10), channel_id=1, source_target_pairs={{0,4},{2,6},{4,0},{6,2},{8,12},{10,14},{12,8},{14,10},{16,20},{18,... | collective-permute-start | bytes 1327112 | tf_op jit(solution)/shard_map/ppermute | solution.py:218
  65.5 1.4 %collective-permute-start.17 = (bf16[48,4608]{1,0:T(8,128)(2,1)S(1)}, bf16[48,4608]{1,0:T(8,128)(2,1)S(1)}, u32[]{:S(2)}, u32[]{:S(2)}) collective-permute-start(bf16[48,4608]{1,0:T(8,128)(2,1)S(1)} %broadcast_select_fusion.8), channel_id=1, source_target_pairs={{0,16},{2,18},{12,28},{14,30},{16,0},{18,2},{28,12},{30,14},{4,8},... | collective-permute-start | bytes 1327112 | tf_op jit(solution)/shard_map/ppermute | solution.py:218
  67.0 2.7 %collective-permute-done.14.refs_7_.refs_0_ = bf16[48,4608]{1,0:T(8,128)(2,1)S(1)} collective-permute-done((bf16[48,4608]{1,0:T(8,128)(2,1)S(1)}, bf16[48,4608]{1,0:T(8,128)(2,1)S(1)}, u32[]{:S(2)}, u32[]{:S(2)}) %collective-permute-start.14) | collective-permute-done | bytes 442400 | tf_op jit(solution)/shard_map/ppermute | solution.py:218
  69.8 4.1 %collective-permute-done.15.refs_6_.refs_4_ = bf16[48,4608]{1,0:T(8,128)(2,1)S(1)} collective-permute-done((bf16[48,4608]{1,0:T(8,128)(2,1)S(1)}, bf16[48,4608]{1,0:T(8,128)(2,1)S(1)}, u32[]{:S(2)}, u32[]{:S(2)}) %collective-permute-start.15) | collective-permute-done | bytes 442400 | tf_op jit(solution)/shard_map/ppermute | solution.py:218
  74.0 3.1 %rotate.5 = (f32[96,256]{1,0:T(8,128)S(1)}, f32[48,256]{1,0:T(8,128)S(1)}, f32[48,256]{1,0:T(8,128)S(1)}) custom-call(bf16[256,4096]{1,0:T(8,128)(2,1)S(1)} %bitcast.11, bf16[256,14336]{1,0:T(8,128)(2,1)S(1)} %bitcast.6, bf16[48,4608]{1,0:T(8,128)(2,1)S(1)} %copy-done.3, bf16[48,4608]{1,0:T(8,128)(2,1)S(1)} %collective-permute-done.1.refs_1_, ...), custom_call_target="tpu_custom_call" | custom-call | flops 905969664 | bytes 3538944 | tf_op jit(solution)/shard_map/rotate/pallas_call | solution.py:189
  77.8 3.7 %collective-permute-start.18 = (bf16[48,4608]{1,0:T(8,128)(2,1)S(1)}, bf16[48,4608]{1,0:T(8,128)(2,1)S(1)}, u32[]{:S(2)}, u32[]{:S(2)}) collective-permute-start(bf16[48,4608]{1,0:T(8,128)(2,1)S(1)} %broadcast_select_fusion.7), channel_id=1, source_target_pairs={{0,4},{2,6},{4,0},{6,2},{8,12},{10,14},{12,8},{14,10},{16,20},{18,... | collective-permute-start | bytes 1327112 | tf_op jit(solution)/shard_map/ppermute | solution.py:218
  81.7 1.9 %collective-permute-start.20 = (bf16[48,4608]{1,0:T(8,128)(2,1)S(1)}, bf16[48,4608]{1,0:T(8,128)(2,1)S(1)}, u32[]{:S(2)}, u32[]{:S(2)}) collective-permute-start(bf16[48,4608]{1,0:T(8,128)(2,1)S(1)} %broadcast_select_fusion.5), channel_id=1, source_target_pairs={{0,16},{2,18},{4,20},{6,22},{8,24},{10,26},{12,28},{14,30},{16,0},... | collective-permute-start | bytes 1327112 | tf_op jit(solution)/shard_map/ppermute | solution.py:218
  83.6 1.8 %collective-permute-start.21 = (bf16[48,4608]{1,0:T(8,128)(2,1)S(1)}, bf16[48,4608]{1,0:T(8,128)(2,1)S(1)}, u32[]{:S(2)}, u32[]{:S(2)}) collective-permute-start(bf16[48,4608]{1,0:T(8,128)(2,1)S(1)} %broadcast_select_fusion.4), channel_id=1, source_target_pairs={{0,4},{2,6},{4,0},{6,2},{8,12},{10,14},{12,8},{14,10},{16,20},{18,... | collective-permute-start | bytes 1327112 | tf_op jit(solution)/shard_map/ppermute | solution.py:218
  85.4 6.8 %collective-permute-done.18.refs_6_.refs_5_ = bf16[48,4608]{1,0:T(8,128)(2,1)S(1)} collective-permute-done((bf16[48,4608]{1,0:T(8,128)(2,1)S(1)}, bf16[48,4608]{1,0:T(8,128)(2,1)S(1)}, u32[]{:S(2)}, u32[]{:S(2)}) %collective-permute-start.18) | collective-permute-done | bytes 442400 | tf_op jit(solution)/shard_map/ppermute | solution.py:218
  92.3 2.3 %collective-permute-done.19.refs_8_.refs_2_ = bf16[48,4608]{1,0:T(8,128)(2,1)S(1)} collective-permute-done((bf16[48,4608]{1,0:T(8,128)(2,1)S(1)}, bf16[48,4608]{1,0:T(8,128)(2,1)S(1)}, u32[]{:S(2)}, u32[]{:S(2)}) %collective-permute-start.19) | collective-permute-done | bytes 442400 | tf_op jit(solution)/shard_map/ppermute | solution.py:218
  94.8 1.3 collective-permute-start.24
  96.2 2.7 %collective-permute-done.21.refs_6_.refs_5_ = bf16[48,4608]{1,0:T(8,128)(2,1)S(1)} collective-permute-done((bf16[48,4608]{1,0:T(8,128)(2,1)S(1)}, bf16[48,4608]{1,0:T(8,128)(2,1)S(1)}, u32[]{:S(2)}, u32[]{:S(2)}) %collective-permute-start.21) | collective-permute-done | bytes 442400 | tf_op jit(solution)/shard_map/ppermute | solution.py:218
  98.9 1.8 %collective-permute-start.23 = (bf16[48,4608]{1,0:T(8,128)(2,1)S(1)}, bf16[48,4608]{1,0:T(8,128)(2,1)S(1)}, u32[]{:S(2)}, u32[]{:S(2)}) collective-permute-start(bf16[48,4608]{1,0:T(8,128)(2,1)S(1)} %broadcast_select_fusion.3), channel_id=1, source_target_pairs={{0,16},{2,18},{4,20},{6,22},{8,24},{10,26},{12,28},{14,30},{16,0},... | collective-permute-start | bytes 1327112 | tf_op jit(solution)/shard_map/ppermute | solution.py:218
  102.1 1.3 collective-permute-done.22.refs_7_
  103.4 3.8 %collective-permute-done.23.refs_1_ = bf16[48,4608]{1,0:T(8,128)(2,1)S(1)} collective-permute-done((bf16[48,4608]{1,0:T(8,128)(2,1)S(1)}, bf16[48,4608]{1,0:T(8,128)(2,1)S(1)}, u32[]{:S(2)}, u32[]{:S(2)}) %collective-permute-start.23) | collective-permute-done | bytes 442400 | tf_op jit(solution)/shard_map/ppermute | solution.py:218
  107.2 1.3 collective-permute-start.30
  109.5 1.6 %collective-permute-start.31 = (bf16[48,4608]{1,0:T(8,128)(2,1)S(1)}, bf16[48,4608]{1,0:T(8,128)(2,1)S(1)}, u32[]{:S(2)}, u32[]{:S(2)}) collective-permute-start(bf16[48,4608]{1,0:T(8,128)(2,1)S(1)} %broadcast_select_fusion), channel_id=1, source_target_pairs={{0,16},{2,18},{12,28},{14,30},{16,0},{18,2},{28,12},{30,14},{4,8},... | collective-permute-start | bytes 1327112 | tf_op jit(solution)/shard_map/ppermute | solution.py:218
  113.1 1.1 rotate.8.refs_9_
  114.2 2.7 %collective-permute-done.29.refs_3_ = bf16[48,4608]{1,0:T(8,128)(2,1)S(1)} collective-permute-done((bf16[48,4608]{1,0:T(8,128)(2,1)S(1)}, bf16[48,4608]{1,0:T(8,128)(2,1)S(1)}, u32[]{:S(2)}, u32[]{:S(2)}) %collective-permute-start.29) | collective-permute-done | bytes 442400 | tf_op jit(solution)/shard_map/ppermute | solution.py:218
  120.1 1.2 collective-permute-done.32.refs_6_
  122.1 2.2 %finish.1 = (f32[24,384]{1,0:T(8,128)}, f32[24,384]{1,0:T(8,128)}, f32[24,384]{1,0:T(8,128)}, f32[24,384]{1,0:T(8,128)}, f32[24,384]{1,0:T(8,128)}, /*index=5*/f...) custom-call(f32[96,256]{1,0:T(8,128)} %copy-done.7, f32[96,256]{1,0:T(8,128)} %copy-done.11, f32[288,256]{1,0:T(8,128)} %copy-done.5, ...), custom_call_target="tpu_custom_call" | custom-call | tf_op jit(solution)/shard_map/finish/pallas_call | solution.py:310
  124.3 3.3 %collective-permute-start.40 = (f32[24,384]{1,0:T(8,128)}, f32[24,384]{1,0:T(8,128)S(1)}, u32[]{:S(2)}, u32[]{:S(2)}) collective-permute-start(f32[24,384]{1,0:T(8,128)} %get-tuple-element.796), channel_id=1, source_target_pairs={{0,14},{2,12},{4,10},{6,8},{8,6},{10,4},{12,2},{14,0},{1,15},{3,13... | collective-permute-start | bytes 110600 | tf_op jit(solution)/shard_map/ppermute | solution.py:326
  127.6 1.1 collective-permute-start.39
  128.8 3.1 %collective-permute-start.38 = (f32[24,384]{1,0:T(8,128)}, f32[24,384]{1,0:T(8,128)S(1)}, u32[]{:S(2)}, u32[]{:S(2)}) collective-permute-start(f32[24,384]{1,0:T(8,128)} %get-tuple-element.794), channel_id=1, source_target_pairs={{0,10},{2,8},{4,14},{6,12},{8,2},{10,0},{12,6},{14,4},{1,11},{3,9}... | collective-permute-start | bytes 110600 | tf_op jit(solution)/shard_map/ppermute | solution.py:326
  132.0 1.4 %collective-permute-start.36 = (f32[24,384]{1,0:T(8,128)}, f32[24,384]{1,0:T(8,128)S(1)}, u32[]{:S(2)}, u32[]{:S(2)}) collective-permute-start(f32[24,384]{1,0:T(8,128)} %get-tuple-element.792), channel_id=1, source_target_pairs={{0,6},{2,4},{4,2},{6,0},{8,14},{10,12},{12,10},{14,8},{1,7},{3,5},... | collective-permute-start | bytes 110600 | tf_op jit(solution)/shard_map/ppermute | solution.py:326
  133.5 1.2 collective-permute-start.35
  135.5 1.1 collective-permute-done.38
  137.7 1.1 collective-permute-done.34
  138.8 1.4 %add_multiply_fusion = f32[24,384]{1,0:T(8,128)} fusion(f32[24,384]{1,0:T(8,128)S(1)} %collective-permute-done.40, f32[24,384]{1,0:T(8,128)S(1)} %collective-permute-done.39, f32[24,384]{1,0:T(8,128)S(1)} %collective-permute-done.38, f32[24,384]{1,0:T(8,128)S(1)} %collective-permute-done.37, f32[24,384]{1,0:T(8,128)S(1)} %collective-permute-done.36, ...), kind=kLoop, calls=%fused_computation.16 | loop fusion | flops 73728 | bytes 331776 | tf_op jit(solution)/shard_map/mul | solution.py:327
  (89 shorter events, 14.4 us)
Async XLA Ops:
  2.8 14.2 %collective-permute-start = (bf16[48,4608]{1,0:T(8,128)(2,1)}, bf16[48,4608]{1,0:T(8,128)(2,1)S(1)}, u32[]{:S(2)}, u32[]{:S(2)}) collective-permute-start(bf16[48,4608]{1,0:T(8,128)(2,1)} %get-tuple-element.405), channel_id=1, source_target_pairs={{0,4},{2,6},{4,0},{6,2},{8,12},{10,14},{12,8},{14,10},{16,20},{18,... | collective-permute-start | bytes 1327112 | tf_op jit(solution)/shard_map/ppermute | solution.py:218
  5.9 13.3 %collective-permute-start.1 = (bf16[48,4608]{1,0:T(8,128)(2,1)}, bf16[48,4608]{1,0:T(8,128)(2,1)S(1)}, u32[]{:S(2)}, u32[]{:S(2)}) collective-permute-start(bf16[48,4608]{1,0:T(8,128)(2,1)} %get-tuple-element.405), channel_id=1, source_target_pairs={{0,2},{2,0},{4,6},{6,4},{8,10},{10,8},{12,14},{14,12},{16,18},{18,... | collective-permute-start | bytes 1327112 | tf_op jit(solution)/shard_map/ppermute | solution.py:218
  7.4 11.8 %collective-permute-start.2 = (bf16[48,4608]{1,0:T(8,128)(2,1)}, bf16[48,4608]{1,0:T(8,128)(2,1)S(1)}, u32[]{:S(2)}, u32[]{:S(2)}) collective-permute-start(bf16[48,4608]{1,0:T(8,128)(2,1)} %get-tuple-element.405), channel_id=1, source_target_pairs={{4,8},{6,10},{8,4},{10,6},{20,24},{22,26},{24,20},{26,22},{5,9},{7... | collective-permute-start | bytes 1327112 | tf_op jit(solution)/shard_map/ppermute | solution.py:218
  8.1 17.6 %collective-permute-start.3 = (bf16[48,4608]{1,0:T(8,128)(2,1)}, bf16[48,4608]{1,0:T(8,128)(2,1)S(1)}, u32[]{:S(2)}, u32[]{:S(2)}) collective-permute-start(bf16[48,4608]{1,0:T(8,128)(2,1)} %get-tuple-element.426), channel_id=1, source_target_pairs={{0,4},{2,6},{4,0},{6,2},{8,12},{10,14},{12,8},{14,10},{16,20},{18,... | collective-permute-start | bytes 1327112 | tf_op jit(solution)/shard_map/ppermute | solution.py:218
  12.5 16.5 %collective-permute-start.4 = (bf16[48,4608]{1,0:T(8,128)(2,1)}, bf16[48,4608]{1,0:T(8,128)(2,1)S(1)}, u32[]{:S(2)}, u32[]{:S(2)}) collective-permute-start(bf16[48,4608]{1,0:T(8,128)(2,1)} %get-tuple-element.426), channel_id=1, source_target_pairs={{0,2},{2,0},{4,6},{6,4},{8,10},{10,8},{12,14},{14,12},{16,18},{18,... | collective-permute-start | bytes 1327112 | tf_op jit(solution)/shard_map/ppermute | solution.py:218
  17.1 11.9 %collective-permute-start.5 = (bf16[48,4608]{1,0:T(8,128)(2,1)}, bf16[48,4608]{1,0:T(8,128)(2,1)S(1)}, u32[]{:S(2)}, u32[]{:S(2)}) collective-permute-start(bf16[48,4608]{1,0:T(8,128)(2,1)} %get-tuple-element.426), channel_id=1, source_target_pairs={{4,8},{6,10},{8,4},{10,6},{20,24},{22,26},{24,20},{26,22},{5,9},{7... | collective-permute-start | bytes 1327112 | tf_op jit(solution)/shard_map/ppermute | solution.py:218
  19.2 54.8 %slice-start = ((s8[7340032]{0:T(1024)(128)(4,1)}), s8[4194304]{0:T(1024)(128)(4,1)S(1)}, s32[]{:S(2)}) async-start(s8[7340032]{0:T(1024)(128)(4,1)} %bitcast.4), calls=%async_computation | async-start | bytes 8388608
  19.2 19.2 %collective-permute-start.7 = (bf16[48,4608]{1,0:T(8,128)(2,1)S(1)}, bf16[48,4608]{1,0:T(8,128)(2,1)S(1)}, u32[]{:S(2)}, u32[]{:S(2)}) collective-permute-start(bf16[48,4608]{1,0:T(8,128)(2,1)S(1)} %collective-permute-done.refs_0_), channel_id=1, source_target_pairs={{0,2},{2,0},{12,14},{14,12},{4,8},{6,10},{8,4},{10,6},{16,18},{18,... | collective-permute-start | bytes 1327112 | tf_op jit(solution)/shard_map/ppermute | solution.py:218
  25.7 11.4 %collective-permute-start.6 = (bf16[48,4608]{1,0:T(8,128)(2,1)S(1)}, bf16[48,4608]{1,0:T(8,128)(2,1)S(1)}, u32[]{:S(2)}, u32[]{:S(2)}) collective-permute-start(bf16[48,4608]{1,0:T(8,128)(2,1)S(1)} %broadcast_select_fusion.15), channel_id=1, source_target_pairs={{0,4},{2,6},{4,0},{6,2},{8,12},{10,14},{12,8},{14,10},{16,20},{18,... | collective-permute-start | bytes 1327112 | tf_op jit(solution)/shard_map/ppermute | solution.py:218
  27.5 11.0 %collective-permute-start.8 = (bf16[48,4608]{1,0:T(8,128)(2,1)S(1)}, bf16[48,4608]{1,0:T(8,128)(2,1)S(1)}, u32[]{:S(2)}, u32[]{:S(2)}) collective-permute-start(bf16[48,4608]{1,0:T(8,128)(2,1)S(1)} %collective-permute-done.1.refs_1_), channel_id=1, source_target_pairs={{0,16},{2,18},{4,20},{6,22},{8,24},{10,26},{12,28},{14,30},{16,0},... | collective-permute-start | bytes 1327112 | tf_op jit(solution)/shard_map/ppermute | solution.py:218
  30.0 24.0 %copy-start.2 = (bf16[48,4608]{1,0:T(8,128)(2,1)S(1)}, bf16[48,4608]{1,0:T(8,128)(2,1)}, u32[]{:S(2)}) copy-start(bf16[48,4608]{1,0:T(8,128)(2,1)} %get-tuple-element.592.refs_6_) | copy-start | bytes 1327108
  30.0 23.9 %collective-permute-start.10 = (bf16[48,4608]{1,0:T(8,128)(2,1)S(1)}, bf16[48,4608]{1,0:T(8,128)(2,1)S(1)}, u32[]{:S(2)}, u32[]{:S(2)}) collective-permute-start(bf16[48,4608]{1,0:T(8,128)(2,1)S(1)} %collective-permute-done.3.refs_0_), channel_id=1, source_target_pairs={{0,2},{2,0},{12,14},{14,12},{4,8},{6,10},{8,4},{10,6},{16,18},{18,... | collective-permute-start | bytes 1327112 | tf_op jit(solution)/shard_map/ppermute | solution.py:218
  37.1 16.9 %collective-permute-start.11 = (bf16[48,4608]{1,0:T(8,128)(2,1)S(1)}, bf16[48,4608]{1,0:T(8,128)(2,1)S(1)}, u32[]{:S(2)}, u32[]{:S(2)}) collective-permute-start(bf16[48,4608]{1,0:T(8,128)(2,1)S(1)} %collective-permute-done.4.refs_3_), channel_id=1, source_target_pairs={{0,16},{2,18},{4,20},{6,22},{8,24},{10,26},{12,28},{14,30},{16,0},... | collective-permute-start | bytes 1327112 | tf_op jit(solution)/shard_map/ppermute | solution.py:218
  38.5 15.4 %collective-permute-start.9 = (bf16[48,4608]{1,0:T(8,128)(2,1)S(1)}, bf16[48,4608]{1,0:T(8,128)(2,1)S(1)}, u32[]{:S(2)}, u32[]{:S(2)}) collective-permute-start(bf16[48,4608]{1,0:T(8,128)(2,1)S(1)} %broadcast_select_fusion.14), channel_id=1, source_target_pairs={{0,4},{2,6},{4,0},{6,2},{8,12},{10,14},{12,8},{14,10},{16,20},{18,... | collective-permute-start | bytes 1327112 | tf_op jit(solution)/shard_map/ppermute | solution.py:218
  43.9 16.1 %collective-permute-start.12 = (bf16[48,4608]{1,0:T(8,128)(2,1)S(1)}, bf16[48,4608]{1,0:T(8,128)(2,1)S(1)}, u32[]{:S(2)}, u32[]{:S(2)}) collective-permute-start(bf16[48,4608]{1,0:T(8,128)(2,1)S(1)} %broadcast_select_fusion.13), channel_id=1, source_target_pairs={{0,4},{2,6},{4,0},{6,2},{8,12},{10,14},{12,8},{14,10},{16,20},{18,... | collective-permute-start | bytes 1327112 | tf_op jit(solution)/shard_map/ppermute | solution.py:218
  44.1 22.9 %collective-permute-start.13 = (bf16[48,4608]{1,0:T(8,128)(2,1)S(1)}, bf16[48,4608]{1,0:T(8,128)(2,1)S(1)}, u32[]{:S(2)}, u32[]{:S(2)}) collective-permute-start(bf16[48,4608]{1,0:T(8,128)(2,1)S(1)} %broadcast_select_fusion.12), channel_id=1, source_target_pairs={{0,2},{2,0},{4,6},{6,4},{8,10},{10,8},{12,14},{14,12},{16,18},{18,... | collective-permute-start | bytes 1327112 | tf_op jit(solution)/shard_map/ppermute | solution.py:218
  53.9 20.0 %slice-start.1 = ((s8[7340032]{0:T(1024)(128)(4,1)}), s8[3145728]{0:T(1024)(128)(4,1)S(1)}, s32[]{:S(2)}) async-start(s8[7340032]{0:T(1024)(128)(4,1)} %bitcast.4), calls=%async_computation.1 | async-start | bytes 6291456
  60.1 9.6 %collective-permute-start.14 = (bf16[48,4608]{1,0:T(8,128)(2,1)S(1)}, bf16[48,4608]{1,0:T(8,128)(2,1)S(1)}, u32[]{:S(2)}, u32[]{:S(2)}) collective-permute-start(bf16[48,4608]{1,0:T(8,128)(2,1)S(1)} %broadcast_select_fusion.11), channel_id=1, source_target_pairs={{0,16},{2,18},{12,28},{14,30},{16,0},{18,2},{28,12},{30,14},{4,8},... | collective-permute-start | bytes 1327112 | tf_op jit(solution)/shard_map/ppermute | solution.py:218
  61.6 12.4 %collective-permute-start.15 = (bf16[48,4608]{1,0:T(8,128)(2,1)S(1)}, bf16[48,4608]{1,0:T(8,128)(2,1)S(1)}, u32[]{:S(2)}, u32[]{:S(2)}) collective-permute-start(bf16[48,4608]{1,0:T(8,128)(2,1)S(1)} %broadcast_select_fusion.10), channel_id=1, source_target_pairs={{0,4},{2,6},{4,0},{6,2},{8,12},{10,14},{12,8},{14,10},{16,20},{18,... | collective-permute-start | bytes 1327112 | tf_op jit(solution)/shard_map/ppermute | solution.py:218
  65.3 11.9 %collective-permute-start.16 = (bf16[48,4608]{1,0:T(8,128)(2,1)S(1)}, bf16[48,4608]{1,0:T(8,128)(2,1)S(1)}, u32[]{:S(2)}, u32[]{:S(2)}) collective-permute-start(bf16[48,4608]{1,0:T(8,128)(2,1)S(1)} %broadcast_select_fusion.9), channel_id=1, source_target_pairs={{0,2},{2,0},{4,6},{6,4},{8,10},{10,8},{12,14},{14,12},{16,18},{18,... | collective-permute-start | bytes 1327112 | tf_op jit(solution)/shard_map/ppermute | solution.py:218
  65.5 8.5 %copy-start = (bf16[1,256,4096]{2,1,0:T(8,128)(2,1)S(1)}, bf16[1,256,4096]{2,1,0:T(8,128)(2,1)}, u32[]{:S(2)}) copy-start(bf16[1,256,4096]{2,1,0:T(8,128)(2,1)} %param.4) | copy-start | bytes 6291460
  65.5 8.5 %copy-start.1 = (bf16[48,4608]{1,0:T(8,128)(2,1)S(1)}, bf16[48,4608]{1,0:T(8,128)(2,1)}, u32[]{:S(2)}) copy-start(bf16[48,4608]{1,0:T(8,128)(2,1)} %get-tuple-element.591.refs_4_) | copy-start | bytes 1327108
  65.5 12.3 %collective-permute-start.17 = (bf16[48,4608]{1,0:T(8,128)(2,1)S(1)}, bf16[48,4608]{1,0:T(8,128)(2,1)S(1)}, u32[]{:S(2)}, u32[]{:S(2)}) collective-permute-start(bf16[48,4608]{1,0:T(8,128)(2,1)S(1)} %broadcast_select_fusion.8), channel_id=1, source_target_pairs={{0,16},{2,18},{12,28},{14,30},{16,0},{18,2},{28,12},{30,14},{4,8},... | collective-permute-start | bytes 1327112 | tf_op jit(solution)/shard_map/ppermute | solution.py:218
  77.1 23.6 %copy-start.8 = (f32[48,256]{1,0:T(8,128)}, f32[48,256]{1,0:T(8,128)S(1)}, u32[]{:S(2)}) copy-start(f32[48,256]{1,0:T(8,128)S(1)} %get-tuple-element.775.refs_4_) | copy-start | bytes 147460
  77.2 42.4 %copy-start.7 = (f32[96,256]{1,0:T(8,128)}, f32[96,256]{1,0:T(8,128)S(1)}, u32[]{:S(2)}) copy-start(f32[96,256]{1,0:T(8,128)S(1)} %get-tuple-element.765.refs_0_) | copy-start | bytes 294916
  77.8 14.4 %collective-permute-start.18 = (bf16[48,4608]{1,0:T(8,128)(2,1)S(1)}, bf16[48,4608]{1,0:T(8,128)(2,1)S(1)}, u32[]{:S(2)}, u32[]{:S(2)}) collective-permute-start(bf16[48,4608]{1,0:T(8,128)(2,1)S(1)} %broadcast_select_fusion.7), channel_id=1, source_target_pairs={{0,4},{2,6},{4,0},{6,2},{8,12},{10,14},{12,8},{14,10},{16,20},{18,... | collective-permute-start | bytes 1327112 | tf_op jit(solution)/shard_map/ppermute | solution.py:218
  81.6 13.0 %collective-permute-start.19 = (bf16[48,4608]{1,0:T(8,128)(2,1)S(1)}, bf16[48,4608]{1,0:T(8,128)(2,1)S(1)}, u32[]{:S(2)}, u32[]{:S(2)}) collective-permute-start(bf16[48,4608]{1,0:T(8,128)(2,1)S(1)} %broadcast_select_fusion.6), channel_id=1, source_target_pairs={{0,2},{2,0},{12,14},{14,12},{4,8},{6,10},{8,4},{10,6},{16,18},{18,... | collective-permute-start | bytes 1327112 | tf_op jit(solution)/shard_map/ppermute | solution.py:218
  81.7 13.2 %collective-permute-start.20 = (bf16[48,4608]{1,0:T(8,128)(2,1)S(1)}, bf16[48,4608]{1,0:T(8,128)(2,1)S(1)}, u32[]{:S(2)}, u32[]{:S(2)}) collective-permute-start(bf16[48,4608]{1,0:T(8,128)(2,1)S(1)} %broadcast_select_fusion.5), channel_id=1, source_target_pairs={{0,16},{2,18},{4,20},{6,22},{8,24},{10,26},{12,28},{14,30},{16,0},... | collective-permute-start | bytes 1327112 | tf_op jit(solution)/shard_map/ppermute | solution.py:218
  83.6 15.3 %collective-permute-start.21 = (bf16[48,4608]{1,0:T(8,128)(2,1)S(1)}, bf16[48,4608]{1,0:T(8,128)(2,1)S(1)}, u32[]{:S(2)}, u32[]{:S(2)}) collective-permute-start(bf16[48,4608]{1,0:T(8,128)(2,1)S(1)} %broadcast_select_fusion.4), channel_id=1, source_target_pairs={{0,4},{2,6},{4,0},{6,2},{8,12},{10,14},{12,8},{14,10},{16,20},{18,... | collective-permute-start | bytes 1327112 | tf_op jit(solution)/shard_map/ppermute | solution.py:218
  85.4 18.0 %collective-permute-start.22 = (bf16[48,4608]{1,0:T(8,128)(2,1)S(1)}, bf16[48,4608]{1,0:T(8,128)(2,1)S(1)}, u32[]{:S(2)}, u32[]{:S(2)}) collective-permute-start(bf16[48,4608]{1,0:T(8,128)(2,1)S(1)} %collective-permute-done.15.refs_6_.refs_4_), channel_id=1, source_target_pairs={{0,2},{2,0},{12,14},{14,12},{4,8},{6,10},{8,4},{10,6},{16,18},{18,... | collective-permute-start | bytes 1327112 | tf_op jit(solution)/shard_map/ppermute | solution.py:218
  94.8 14.6 %collective-permute-start.24 = (bf16[48,4608]{1,0:T(8,128)(2,1)S(1)}, bf16[48,4608]{1,0:T(8,128)(2,1)S(1)}, u32[]{:S(2)}, u32[]{:S(2)}) collective-permute-start(bf16[48,4608]{1,0:T(8,128)(2,1)S(1)} %collective-permute-done.19.refs_8_.refs_2_), channel_id=1, source_target_pairs={{4,0},{6,2},{8,12},{10,14},{20,16},{22,18},{24,28},{26,30},{5,1},{... | collective-permute-start | bytes 1327112 | tf_op jit(solution)/shard_map/ppermute | solution.py:218
  98.9 8.3 %collective-permute-start.23 = (bf16[48,4608]{1,0:T(8,128)(2,1)S(1)}, bf16[48,4608]{1,0:T(8,128)(2,1)S(1)}, u32[]{:S(2)}, u32[]{:S(2)}) collective-permute-start(bf16[48,4608]{1,0:T(8,128)(2,1)S(1)} %broadcast_select_fusion.3), channel_id=1, source_target_pairs={{0,16},{2,18},{4,20},{6,22},{8,24},{10,26},{12,28},{14,30},{16,0},... | collective-permute-start | bytes 1327112 | tf_op jit(solution)/shard_map/ppermute | solution.py:218
  100.7 11.2 %collective-permute-start.26 = (bf16[48,4608]{1,0:T(8,128)(2,1)S(1)}, bf16[48,4608]{1,0:T(8,128)(2,1)S(1)}, u32[]{:S(2)}, u32[]{:S(2)}) collective-permute-start(bf16[48,4608]{1,0:T(8,128)(2,1)S(1)} %broadcast_select_fusion.2), channel_id=1, source_target_pairs={{0,16},{2,18},{4,20},{6,22},{8,24},{10,26},{12,28},{14,30},{16,0},... | collective-permute-start | bytes 1327112 | tf_op jit(solution)/shard_map/ppermute | solution.py:218
  101.0 10.9 %collective-permute-start.27 = (bf16[48,4608]{1,0:T(8,128)(2,1)S(1)}, bf16[48,4608]{1,0:T(8,128)(2,1)S(1)}, u32[]{:S(2)}, u32[]{:S(2)}) collective-permute-start(bf16[48,4608]{1,0:T(8,128)(2,1)S(1)} %broadcast_select_fusion.1), channel_id=1, source_target_pairs={{0,2},{2,0},{12,14},{14,12},{4,8},{6,10},{8,4},{10,6},{16,18},{18,... | collective-permute-start | bytes 1327112 | tf_op jit(solution)/shard_map/ppermute | solution.py:218
  107.2 10.2 %collective-permute-start.30 = (bf16[48,4608]{1,0:T(8,128)(2,1)S(1)}, bf16[48,4608]{1,0:T(8,128)(2,1)S(1)}, u32[]{:S(2)}, u32[]{:S(2)}) collective-permute-start(bf16[48,4608]{1,0:T(8,128)(2,1)S(1)} %collective-permute-done.22.refs_7_), channel_id=1, source_target_pairs={{4,0},{6,2},{8,12},{10,14},{20,16},{22,18},{24,28},{26,30},{5,1},{... | collective-permute-start | bytes 1327112 | tf_op jit(solution)/shard_map/ppermute | solution.py:218
  108.5 8.4 %collective-permute-start.29 = (bf16[48,4608]{1,0:T(8,128)(2,1)S(1)}, bf16[48,4608]{1,0:T(8,128)(2,1)S(1)}, u32[]{:S(2)}, u32[]{:S(2)}) collective-permute-start(bf16[48,4608]{1,0:T(8,128)(2,1)S(1)} %collective-permute-done.23.refs_1_), channel_id=1, source_target_pairs={{0,2},{2,0},{4,6},{6,4},{8,10},{10,8},{12,14},{14,12},{16,18},{18,... | collective-permute-start | bytes 1327112 | tf_op jit(solution)/shard_map/ppermute | solution.py:218
  109.5 8.4 %collective-permute-start.31 = (bf16[48,4608]{1,0:T(8,128)(2,1)S(1)}, bf16[48,4608]{1,0:T(8,128)(2,1)S(1)}, u32[]{:S(2)}, u32[]{:S(2)}) collective-permute-start(bf16[48,4608]{1,0:T(8,128)(2,1)S(1)} %broadcast_select_fusion), channel_id=1, source_target_pairs={{0,16},{2,18},{12,28},{14,30},{16,0},{18,2},{28,12},{30,14},{4,8},... | collective-permute-start | bytes 1327112 | tf_op jit(solution)/shard_map/ppermute | solution.py:218
  113.0 8.3 %collective-permute-start.28 = (f32[288,256]{1,0:T(8,128)S(1)}, f32[288,256]{1,0:T(8,128)S(1)}, u32[]{:S(2)}, u32[]{:S(2)}) collective-permute-start(f32[288,256]{1,0:T(8,128)S(1)} %get-tuple-element.774.refs_2_), channel_id=1, source_target_pairs={{0,1},{1,0},{2,3},{3,2},{4,5},{5,4},{6,7},{7,6},{8,9},{9,8},{10,11... | collective-permute-start | bytes 884744 | tf_op jit(solution)/shard_map/ppermute | solution.py:158
  119.5 1.8 %collective-permute-start.33 = (f32[144,256]{1,0:T(8,128)S(1)}, f32[144,256]{1,0:T(8,128)S(1)}, u32[]{:S(2)}, u32[]{:S(2)}) collective-permute-start(f32[144,256]{1,0:T(8,128)S(1)} %get-tuple-element.788), channel_id=1, source_target_pairs={{0,1},{1,0},{2,3},{3,2},{4,5},{5,4},{6,7},{7,6},{8,9},{9,8},{10,11... | collective-permute-start | bytes 442376 | tf_op jit(solution)/shard_map/ppermute | solution.py:158
  119.5 1.7 %collective-permute-start.25 = (f32[96,256]{1,0:T(8,128)S(1)}, f32[96,256]{1,0:T(8,128)S(1)}, u32[]{:S(2)}, u32[]{:S(2)}) collective-permute-start(f32[96,256]{1,0:T(8,128)S(1)} %get-tuple-element.765.refs_0_), channel_id=1, source_target_pairs={{0,1},{1,0},{2,3},{3,2},{4,5},{5,4},{6,7},{7,6},{8,9},{9,8},{10,11... | collective-permute-start | bytes 294920 | tf_op jit(solution)/shard_map/ppermute | solution.py:158
  120.1 1.2 collective-permute-start.32
  124.3 9.1 %collective-permute-start.40 = (f32[24,384]{1,0:T(8,128)}, f32[24,384]{1,0:T(8,128)S(1)}, u32[]{:S(2)}, u32[]{:S(2)}) collective-permute-start(f32[24,384]{1,0:T(8,128)} %get-tuple-element.796), channel_id=1, source_target_pairs={{0,14},{2,12},{4,10},{6,8},{8,6},{10,4},{12,2},{14,0},{1,15},{3,13... | collective-permute-start | bytes 110600 | tf_op jit(solution)/shard_map/ppermute | solution.py:326
  127.6 7.0 %collective-permute-start.39 = (f32[24,384]{1,0:T(8,128)}, f32[24,384]{1,0:T(8,128)S(1)}, u32[]{:S(2)}, u32[]{:S(2)}) collective-permute-start(f32[24,384]{1,0:T(8,128)} %get-tuple-element.795), channel_id=1, source_target_pairs={{0,12},{2,14},{4,8},{6,10},{8,4},{10,6},{12,0},{14,2},{1,13},{3,15... | collective-permute-start | bytes 110600 | tf_op jit(solution)/shard_map/ppermute | solution.py:326
  128.8 7.9 %collective-permute-start.38 = (f32[24,384]{1,0:T(8,128)}, f32[24,384]{1,0:T(8,128)S(1)}, u32[]{:S(2)}, u32[]{:S(2)}) collective-permute-start(f32[24,384]{1,0:T(8,128)} %get-tuple-element.794), channel_id=1, source_target_pairs={{0,10},{2,8},{4,14},{6,12},{8,2},{10,0},{12,6},{14,4},{1,11},{3,9}... | collective-permute-start | bytes 110600 | tf_op jit(solution)/shard_map/ppermute | solution.py:326
  131.8 5.2 %collective-permute-start.37 = (f32[24,384]{1,0:T(8,128)}, f32[24,384]{1,0:T(8,128)S(1)}, u32[]{:S(2)}, u32[]{:S(2)}) collective-permute-start(f32[24,384]{1,0:T(8,128)} %get-tuple-element.793), channel_id=1, source_target_pairs={{0,8},{2,10},{4,12},{6,14},{8,0},{10,2},{12,4},{14,6},{1,9},{3,11}... | collective-permute-start | bytes 110600 | tf_op jit(solution)/shard_map/ppermute | solution.py:326
  132.0 5.7 %collective-permute-start.36 = (f32[24,384]{1,0:T(8,128)}, f32[24,384]{1,0:T(8,128)S(1)}, u32[]{:S(2)}, u32[]{:S(2)}) collective-permute-start(f32[24,384]{1,0:T(8,128)} %get-tuple-element.792), channel_id=1, source_target_pairs={{0,6},{2,4},{4,2},{6,0},{8,14},{10,12},{12,10},{14,8},{1,7},{3,5},... | collective-permute-start | bytes 110600 | tf_op jit(solution)/shard_map/ppermute | solution.py:326
  133.5 4.2 %collective-permute-start.35 = (f32[24,384]{1,0:T(8,128)}, f32[24,384]{1,0:T(8,128)S(1)}, u32[]{:S(2)}, u32[]{:S(2)}) collective-permute-start(f32[24,384]{1,0:T(8,128)} %get-tuple-element.791), channel_id=1, source_target_pairs={{0,4},{2,6},{4,0},{6,2},{8,12},{10,14},{12,8},{14,10},{1,5},{3,7},... | collective-permute-start | bytes 110600 | tf_op jit(solution)/shard_map/ppermute | solution.py:326
  134.6 4.2 %collective-permute-start.34 = (f32[24,384]{1,0:T(8,128)}, f32[24,384]{1,0:T(8,128)S(1)}, u32[]{:S(2)}, u32[]{:S(2)}) collective-permute-start(f32[24,384]{1,0:T(8,128)} %get-tuple-element.790), channel_id=1, source_target_pairs={{0,2},{2,0},{4,6},{6,4},{8,10},{10,8},{12,14},{14,12},{1,3},{3,1},... | collective-permute-start | bytes 110600 | tf_op jit(solution)/shard_map/ppermute | solution.py:326
  (8 other events, 21.7 us)

commit v4 on v3

--- a/solution.py
+++ b/solution.py
@@ -11,6 +11,7 @@
 K = 384
 LANES = 128
 AHEAD = 5
+STEP = 1 * 10**8
 
 
 def place_cols(left, piece):
@@ -45,6 +46,19 @@
     return lax.dot_general(
         left, right, (((1,), (1,)), ((), ())), preferred_element_type=jnp.float32
     )
+
+
+def pick_kernel(outer_ref, inner_ref, out_ref):
+    z = lax.axis_index("dp") // 2
+    outer = (z == 0) | (z == 3)
+
+    @pl.when(outer)
+    def _():
+        out_ref[...] = outer_ref[...]
+
+    @pl.when(jnp.logical_not(outer))
+    def _():
+        out_ref[...] = inner_ref[...]
 
 
 def cut_kernel(in_half, first, in_ref, out_ref, m0, m1, t0, t1):
@@ -163,6 +177,7 @@
         out_shape=[unit] * 4,
         in_specs=[vmem] * 2,
         out_specs=[vmem] * 4,
+        compiler_params=pltpu.CompilerParams(vmem_limit_bytes=8 * 2**20),
         name="cut",
     )(in_t, out_t)
 
@@ -220,7 +235,15 @@
     def pick(for_outer, for_inner):
         if for_outer is for_inner:
             return for_outer
-        return jnp.where(outer, for_outer, for_inner)
+        return pl.pallas_call(
+            pick_kernel,
+            out_shape=unit,
+            in_specs=[vmem] * 2,
+            out_specs=vmem,
+            compiler_params=pltpu.CompilerParams(vmem_limit_bytes=4 * 2**20),
+            cost_estimate=pl.CostEstimate(flops=STEP, bytes_accessed=8192, transcendentals=0),
+            name="pick",
+        )(for_outer, for_inner)
 
     at_outer = {"0m0": m0, "0m1": m1, "0t0": t0, "0t1": t1}
     at_inner = dict(at_outer)
@@ -316,6 +339,7 @@
             pltpu.VMEM((K, tokens), jnp.bfloat16),
             pltpu.VMEM((K // 2, tokens), jnp.float32),
         ],
+        compiler_params=pltpu.CompilerParams(vmem_limit_bytes=8 * 2**20),
         name="finish",
     )(
         in_a, swap_core(in_a), in_b, swap_core(in_b),

time: 141 us -> 123 us (0.87)
  waiting for transfers between devices: 63.8 us -> 35.8 us
  starting transfers between devices: 58.9 us -> 75.3 us
  Pallas kernels: 12.4 us -> 8.24 us
  other arithmetic: 3.19 us -> 0.64 us
    ppermute x30, waiting for transfers between devices: 59.3 us -> 31.2 us  [send(): return lax.ppermute(value, ('group', 'dp'), pairs)]
    ppermute x30, starting transfers between devices: 47.1 us -> 63.3 us  [send(): return lax.ppermute(value, ('group', 'dp'), pairs)]
    pallas_call x1, Pallas kernels: 2.84 us -> 0.11 us  [per_device_plane(): pl.pallas_call(functools.partial(cut_kernel, in_half, first), out_shape=[...]
    pallas_call x1, Pallas kernels: 2.21 us -> 0.29 us  [per_device_plane(): pl.pallas_call(functools.partial(finish_kernel, rows), out_shape=[jax.Sha...]
    select_n x16 -> x0, other arithmetic: 1.78 us -> none  [pick(): return jnp.where(outer, for_outer, for_inner)]
  transfers between devices with their start and end apart: 41 -> 41, of which waited for: 24 -> 22; matrix products, arithmetic and copies ran while one was open for 1% -> 0% of each run, Pallas kernels for 5% -> 6%
where the time goes in v4:
time: 123 us
  starting transfers between devices  75.3 us (61%)
  waiting for transfers between devices  35.8 us (29%)
  Pallas kernels  8.24 us (7%)
  local copies, waits for them, and re-layouts  2.35 us (2%)
    ppermute x30, starting transfers between devices, send(): return lax.ppermute(value, ('group', 'dp'), pairs)  63.3 us
    ppermute x30, waiting for transfers between devices, send(): return lax.ppermute(value, ('group', 'dp'), pairs)  31.2 us
    ppermute x7, starting transfers between devices, per_device_plane(): lax.ppermute(squares[k], 'dp', [(i, i ^ k) for i in range(8)])  11.2 us
    pallas_call x5, Pallas kernels, rotate(): pl.pallas_call(functools.partial(rotate_kernel, (terms, bool(acc), last),...  7.32 us
    ppermute x7, waiting for transfers between devices, per_device_plane(): lax.ppermute(squares[k], 'dp', [(i, i ^ k) for i in range(8)])  3.38 us
  transfers between devices with their start and end apart: 41, of which 22 were waited for; matrix products, arithmetic and copies ran while one was open for 0% of the time, Pallas kernels for 6%

profile of v4, /device:TPU:0, one launch (start us, length us, event | category | flops | bytes accessed | tf_op | source)
XLA Modules:
  0.0 122.6 jit_solution(17010655975134718869)
XLA Ops:
  0.0 1.3 %copy-done.1 = bf16[14336,48]{0,1:T(8,128)(2,1)S(1)} copy-done((bf16[14336,48]{0,1:T(8,128)(2,1)S(1)}, bf16[14336,48]{0,1:T(8,128)(2,1)}, u32[]{:S(2)}) %copy-start.1) | copy-done | bytes 1376280
  1.3 1.0 copy-done.2
  2.5 3.1 %collective-permute-start = (bf16[48,4608]{1,0:T(8,128)(2,1)S(1)}, bf16[48,4608]{1,0:T(8,128)(2,1)S(1)}, u32[]{:S(2)}, u32[]{:S(2)}) collective-permute-start(bf16[48,4608]{1,0:T(8,128)(2,1)S(1)} %get-tuple-element.405), channel_id=1, source_target_pairs={{0,4},{2,6},{4,0},{6,2},{8,12},{10,14},{12,8},{14,10},{16,20},{18,... | collective-permute-start | bytes 1327112 | tf_op jit(solution)/shard_map/ppermute | solution.py:233
  5.5 1.5 %collective-permute-start.1 = (bf16[48,4608]{1,0:T(8,128)(2,1)S(1)}, bf16[48,4608]{1,0:T(8,128)(2,1)S(1)}, u32[]{:S(2)}, u32[]{:S(2)}) collective-permute-start(bf16[48,4608]{1,0:T(8,128)(2,1)S(1)} %get-tuple-element.405), channel_id=1, source_target_pairs={{0,2},{2,0},{4,6},{6,4},{8,10},{10,8},{12,14},{14,12},{16,18},{18,... | collective-permute-start | bytes 1327112 | tf_op jit(solution)/shard_map/ppermute | solution.py:233
  7.7 4.4 %collective-permute-start.3 = (bf16[48,4608]{1,0:T(8,128)(2,1)S(1)}, bf16[48,4608]{1,0:T(8,128)(2,1)S(1)}, u32[]{:S(2)}, u32[]{:S(2)}) collective-permute-start(bf16[48,4608]{1,0:T(8,128)(2,1)S(1)} %get-tuple-element.426), channel_id=1, source_target_pairs={{0,4},{2,6},{4,0},{6,2},{8,12},{10,14},{12,8},{14,10},{16,20},{18,... | collective-permute-start | bytes 1327112 | tf_op jit(solution)/shard_map/ppermute | solution.py:233
  12.7 3.8 %collective-permute-done.outer_ref.refs_0_ = bf16[48,4608]{1,0:T(8,128)(2,1)S(1)} collective-permute-done((bf16[48,4608]{1,0:T(8,128)(2,1)S(1)}, bf16[48,4608]{1,0:T(8,128)(2,1)S(1)}, u32[]{:S(2)}, u32[]{:S(2)}) %collective-permute-start) | collective-permute-done | bytes 442400 | tf_op jit(solution)/shard_map/ppermute | solution.py:233
  17.2 1.4 %collective-permute-done.1.outer_ref.refs_1_ = bf16[48,4608]{1,0:T(8,128)(2,1)S(1)} collective-permute-done((bf16[48,4608]{1,0:T(8,128)(2,1)S(1)}, bf16[48,4608]{1,0:T(8,128)(2,1)S(1)}, u32[]{:S(2)}, u32[]{:S(2)}) %collective-permute-start.1) | collective-permute-done | bytes 442400 | tf_op jit(solution)/shard_map/ppermute | solution.py:233
  18.7 3.9 %collective-permute-start.6 = (bf16[48,4608]{1,0:T(8,128)(2,1)S(1)}, bf16[48,4608]{1,0:T(8,128)(2,1)S(1)}, u32[]{:S(2)}, u32[]{:S(2)}) collective-permute-start(bf16[48,4608]{1,0:T(8,128)(2,1)S(1)} %pick.16), channel_id=1, source_target_pairs={{0,4},{2,6},{4,0},{6,2},{8,12},{10,14},{12,8},{14,10},{16,20},{18,... | collective-permute-start | bytes 1327112 | tf_op jit(solution)/shard_map/ppermute | solution.py:233
  22.6 1.2 collective-permute-start.7
  23.8 2.3 %collective-permute-done.3.outer_ref.refs_0_ = bf16[48,4608]{1,0:T(8,128)(2,1)S(1)} collective-permute-done((bf16[48,4608]{1,0:T(8,128)(2,1)S(1)}, bf16[48,4608]{1,0:T(8,128)(2,1)S(1)}, u32[]{:S(2)}, u32[]{:S(2)}) %collective-permute-start.3) | collective-permute-done | bytes 442400 | tf_op jit(solution)/shard_map/ppermute | solution.py:233
  26.0 2.0 %collective-permute-start.8 = (bf16[48,4608]{1,0:T(8,128)(2,1)S(1)}, bf16[48,4608]{1,0:T(8,128)(2,1)S(1)}, u32[]{:S(2)}, u32[]{:S(2)}) collective-permute-start(bf16[48,4608]{1,0:T(8,128)(2,1)S(1)} %collective-permute-done.1.outer_ref.refs_1_), channel_id=1, source_target_pairs={{0,16},{2,18},{4,20},{6,22},{8,24},{10,26},{12,28},{14,30},{16,0},... | collective-permute-start | bytes 1327112 | tf_op jit(solution)/shard_map/ppermute | solution.py:233
  28.2 5.5 %collective-permute-start.9 = (bf16[48,4608]{1,0:T(8,128)(2,1)S(1)}, bf16[48,4608]{1,0:T(8,128)(2,1)S(1)}, u32[]{:S(2)}, u32[]{:S(2)}) collective-permute-start(bf16[48,4608]{1,0:T(8,128)(2,1)S(1)} %pick.17), channel_id=1, source_target_pairs={{0,4},{2,6},{4,0},{6,2},{8,12},{10,14},{12,8},{14,10},{16,20},{18,... | collective-permute-start | bytes 1327112 | tf_op jit(solution)/shard_map/ppermute | solution.py:233
  33.7 1.5 %collective-permute-start.10 = (bf16[48,4608]{1,0:T(8,128)(2,1)S(1)}, bf16[48,4608]{1,0:T(8,128)(2,1)S(1)}, u32[]{:S(2)}, u32[]{:S(2)}) collective-permute-start(bf16[48,4608]{1,0:T(8,128)(2,1)S(1)} %collective-permute-done.3.outer_ref.refs_0_), channel_id=1, source_target_pairs={{0,2},{2,0},{12,14},{14,12},{4,8},{6,10},{8,4},{10,6},{16,18},{18,... | collective-permute-start | bytes 1327112 | tf_op jit(solution)/shard_map/ppermute | solution.py:233
  35.5 2.0 %collective-permute-start.11 = (bf16[48,4608]{1,0:T(8,128)(2,1)S(1)}, bf16[48,4608]{1,0:T(8,128)(2,1)S(1)}, u32[]{:S(2)}, u32[]{:S(2)}) collective-permute-start(bf16[48,4608]{1,0:T(8,128)(2,1)S(1)} %collective-permute-done.4.refs_3_.outer_ref), channel_id=1, source_target_pairs={{0,16},{2,18},{4,20},{6,22},{8,24},{10,26},{12,28},{14,30},{16,0},... | collective-permute-start | bytes 1327112 | tf_op jit(solution)/shard_map/ppermute | solution.py:233
  37.6 5.5 %collective-permute-start.12 = (bf16[48,4608]{1,0:T(8,128)(2,1)S(1)}, bf16[48,4608]{1,0:T(8,128)(2,1)S(1)}, u32[]{:S(2)}, u32[]{:S(2)}) collective-permute-start(bf16[48,4608]{1,0:T(8,128)(2,1)S(1)} %pick.18), channel_id=1, source_target_pairs={{0,4},{2,6},{4,0},{6,2},{8,12},{10,14},{12,8},{14,10},{16,20},{18,... | collective-permute-start | bytes 1327112 | tf_op jit(solution)/shard_map/ppermute | solution.py:233
  43.2 1.6 %collective-permute-start.13 = (bf16[48,4608]{1,0:T(8,128)(2,1)S(1)}, bf16[48,4608]{1,0:T(8,128)(2,1)S(1)}, u32[]{:S(2)}, u32[]{:S(2)}) collective-permute-start(bf16[48,4608]{1,0:T(8,128)(2,1)S(1)} %pick.19), channel_id=1, source_target_pairs={{0,2},{2,0},{4,6},{6,4},{8,10},{10,8},{12,14},{14,12},{16,18},{18,... | collective-permute-start | bytes 1327112 | tf_op jit(solution)/shard_map/ppermute | solution.py:233
  45.0 2.0 %collective-permute-start.14 = (bf16[48,4608]{1,0:T(8,128)(2,1)S(1)}, bf16[48,4608]{1,0:T(8,128)(2,1)S(1)}, u32[]{:S(2)}, u32[]{:S(2)}) collective-permute-start(bf16[48,4608]{1,0:T(8,128)(2,1)S(1)} %pick.20), channel_id=1, source_target_pairs={{0,16},{2,18},{12,28},{14,30},{16,0},{18,2},{28,12},{30,14},{4,8},... | collective-permute-start | bytes 1327112 | tf_op jit(solution)/shard_map/ppermute | solution.py:233
  47.1 5.5 %collective-permute-start.15 = (bf16[48,4608]{1,0:T(8,128)(2,1)S(1)}, bf16[48,4608]{1,0:T(8,128)(2,1)S(1)}, u32[]{:S(2)}, u32[]{:S(2)}) collective-permute-start(bf16[48,4608]{1,0:T(8,128)(2,1)S(1)} %pick.21), channel_id=1, source_target_pairs={{0,4},{2,6},{4,0},{6,2},{8,12},{10,14},{12,8},{14,10},{16,20},{18,... | collective-permute-start | bytes 1327112 | tf_op jit(solution)/shard_map/ppermute | solution.py:233
  52.7 1.8 %collective-permute-done.12.inner_ref.refs_5_ = bf16[48,4608]{1,0:T(8,128)(2,1)S(1)} collective-permute-done((bf16[48,4608]{1,0:T(8,128)(2,1)S(1)}, bf16[48,4608]{1,0:T(8,128)(2,1)S(1)}, u32[]{:S(2)}, u32[]{:S(2)}) %collective-permute-start.12) | collective-permute-done | bytes 442400 | tf_op jit(solution)/shard_map/ppermute | solution.py:233
  54.5 2.1 %collective-permute-start.16 = (bf16[48,4608]{1,0:T(8,128)(2,1)S(1)}, bf16[48,4608]{1,0:T(8,128)(2,1)S(1)}, u32[]{:S(2)}, u32[]{:S(2)}) collective-permute-start(bf16[48,4608]{1,0:T(8,128)(2,1)S(1)} %pick.22), channel_id=1, source_target_pairs={{0,2},{2,0},{4,6},{6,4},{8,10},{10,8},{12,14},{14,12},{16,18},{18,... | collective-permute-start | bytes 1327112 | tf_op jit(solution)/shard_map/ppermute | solution.py:233
  56.6 1.6 %collective-permute-start.17 = (bf16[48,4608]{1,0:T(8,128)(2,1)S(1)}, bf16[48,4608]{1,0:T(8,128)(2,1)S(1)}, u32[]{:S(2)}, u32[]{:S(2)}) collective-permute-start(bf16[48,4608]{1,0:T(8,128)(2,1)S(1)} %pick.23), channel_id=1, source_target_pairs={{0,16},{2,18},{12,28},{14,30},{16,0},{18,2},{28,12},{30,14},{4,8},... | collective-permute-start | bytes 1327112 | tf_op jit(solution)/shard_map/ppermute | solution.py:233
  58.2 2.7 %collective-permute-start.18 = (bf16[48,4608]{1,0:T(8,128)(2,1)S(1)}, bf16[48,4608]{1,0:T(8,128)(2,1)S(1)}, u32[]{:S(2)}, u32[]{:S(2)}) collective-permute-start(bf16[48,4608]{1,0:T(8,128)(2,1)S(1)} %pick.24), channel_id=1, source_target_pairs={{0,4},{2,6},{4,0},{6,2},{8,12},{10,14},{12,8},{14,10},{16,20},{18,... | collective-permute-start | bytes 1327112 | tf_op jit(solution)/shard_map/ppermute | solution.py:233
  61.0 3.0 %collective-permute-done.15.refs_6_.refs_4_ = bf16[48,4608]{1,0:T(8,128)(2,1)S(1)} collective-permute-done((bf16[48,4608]{1,0:T(8,128)(2,1)S(1)}, bf16[48,4608]{1,0:T(8,128)(2,1)S(1)}, u32[]{:S(2)}, u32[]{:S(2)}) %collective-permute-start.15) | collective-permute-done | bytes 442400 | tf_op jit(solution)/shard_map/ppermute | solution.py:233
  63.9 2.0 %collective-permute-start.19 = (bf16[48,4608]{1,0:T(8,128)(2,1)S(1)}, bf16[48,4608]{1,0:T(8,128)(2,1)S(1)}, u32[]{:S(2)}, u32[]{:S(2)}) collective-permute-start(bf16[48,4608]{1,0:T(8,128)(2,1)S(1)} %pick.25), channel_id=1, source_target_pairs={{0,2},{2,0},{12,14},{14,12},{4,8},{6,10},{8,4},{10,6},{16,18},{18,... | collective-permute-start | bytes 1327112 | tf_op jit(solution)/shard_map/ppermute | solution.py:233
  66.0 1.6 %collective-permute-start.20 = (bf16[48,4608]{1,0:T(8,128)(2,1)S(1)}, bf16[48,4608]{1,0:T(8,128)(2,1)S(1)}, u32[]{:S(2)}, u32[]{:S(2)}) collective-permute-start(bf16[48,4608]{1,0:T(8,128)(2,1)S(1)} %pick.26), channel_id=1, source_target_pairs={{0,16},{2,18},{4,20},{6,22},{8,24},{10,26},{12,28},{14,30},{16,0},... | collective-permute-start | bytes 1327112 | tf_op jit(solution)/shard_map/ppermute | solution.py:233
  67.5 3.1 %rotate.5 = (f32[96,256]{1,0:T(8,128)S(1)}, f32[48,256]{1,0:T(8,128)S(1)}, f32[48,256]{1,0:T(8,128)S(1)}) custom-call(bf16[256,4096]{1,0:T(8,128)(2,1)S(1)} %bitcast.11, bf16[256,14336]{1,0:T(8,128)(2,1)S(1)} %bitcast.6, bf16[48,4608]{1,0:T(8,128)(2,1)S(1)} %get-tuple-element.405, bf16[48,4608]{1,0:T(8,128)(2,1)S(1)} %collective-permute-done.1.outer_ref.refs_1_, ...), custom_call_target="tpu_custom_call" | custom-call | flops 905969664 | bytes 3538944 | tf_op jit(solution)/shard_map/rotate/pallas_call | solution.py:204
  70.7 1.7 %collective-permute-start.21 = (bf16[48,4608]{1,0:T(8,128)(2,1)S(1)}, bf16[48,4608]{1,0:T(8,128)(2,1)S(1)}, u32[]{:S(2)}, u32[]{:S(2)}) collective-permute-start(bf16[48,4608]{1,0:T(8,128)(2,1)S(1)} %pick.27), channel_id=1, source_target_pairs={{0,4},{2,6},{4,0},{6,2},{8,12},{10,14},{12,8},{14,10},{16,20},{18,... | collective-permute-start | bytes 1327112 | tf_op jit(solution)/shard_map/ppermute | solution.py:233
  72.4 1.5 %collective-permute-start.22 = (bf16[48,4608]{1,0:T(8,128)(2,1)S(1)}, bf16[48,4608]{1,0:T(8,128)(2,1)S(1)}, u32[]{:S(2)}, u32[]{:S(2)}) collective-permute-start(bf16[48,4608]{1,0:T(8,128)(2,1)S(1)} %collective-permute-done.15.refs_6_.refs_4_), channel_id=1, source_target_pairs={{0,2},{2,0},{12,14},{14,12},{4,8},{6,10},{8,4},{10,6},{16,18},{18,... | collective-permute-start | bytes 1327112 | tf_op jit(solution)/shard_map/ppermute | solution.py:233
  74.0 1.5 %collective-permute-start.23 = (bf16[48,4608]{1,0:T(8,128)(2,1)S(1)}, bf16[48,4608]{1,0:T(8,128)(2,1)S(1)}, u32[]{:S(2)}, u32[]{:S(2)}) collective-permute-start(bf16[48,4608]{1,0:T(8,128)(2,1)S(1)} %pick.28), channel_id=1, source_target_pairs={{0,16},{2,18},{4,20},{6,22},{8,24},{10,26},{12,28},{14,30},{16,0},... | collective-permute-start | bytes 1327112 | tf_op jit(solution)/shard_map/ppermute | solution.py:233
  75.5 1.6 %collective-permute-done.19.refs_8_.refs_2_ = bf16[48,4608]{1,0:T(8,128)(2,1)S(1)} collective-permute-done((bf16[48,4608]{1,0:T(8,128)(2,1)S(1)}, bf16[48,4608]{1,0:T(8,128)(2,1)S(1)}, u32[]{:S(2)}, u32[]{:S(2)}) %collective-permute-start.19) | collective-permute-done | bytes 442400 | tf_op jit(solution)/shard_map/ppermute | solution.py:233
  77.1 1.3 %collective-permute-start.24 = (bf16[48,4608]{1,0:T(8,128)(2,1)S(1)}, bf16[48,4608]{1,0:T(8,128)(2,1)S(1)}, u32[]{:S(2)}, u32[]{:S(2)}) collective-permute-start(bf16[48,4608]{1,0:T(8,128)(2,1)S(1)} %collective-permute-done.19.refs_8_.refs_2_), channel_id=1, source_target_pairs={{4,0},{6,2},{8,12},{10,14},{20,16},{22,18},{24,28},{26,30},{5,1},{... | collective-permute-start | bytes 1327112 | tf_op jit(solution)/shard_map/ppermute | solution.py:233
  78.3 5.6 %collective-permute-done.21.refs_6_.inner_ref.refs_5_ = bf16[48,4608]{1,0:T(8,128)(2,1)S(1)} collective-permute-done((bf16[48,4608]{1,0:T(8,128)(2,1)S(1)}, bf16[48,4608]{1,0:T(8,128)(2,1)S(1)}, u32[]{:S(2)}, u32[]{:S(2)}) %collective-permute-start.21) | collective-permute-done | bytes 442400 | tf_op jit(solution)/shard_map/ppermute | solution.py:233
  84.0 1.0 collective-permute-start.26
  85.0 1.5 %collective-permute-start.27 = (bf16[48,4608]{1,0:T(8,128)(2,1)S(1)}, bf16[48,4608]{1,0:T(8,128)(2,1)S(1)}, u32[]{:S(2)}, u32[]{:S(2)}) collective-permute-start(bf16[48,4608]{1,0:T(8,128)(2,1)S(1)} %pick.30), channel_id=1, source_target_pairs={{0,2},{2,0},{12,14},{14,12},{4,8},{6,10},{8,4},{10,6},{16,18},{18,... | collective-permute-start | bytes 1327112 | tf_op jit(solution)/shard_map/ppermute | solution.py:233
  86.6 1.1 rotate.6
  87.6 1.3 %collective-permute-start.30 = (bf16[48,4608]{1,0:T(8,128)(2,1)S(1)}, bf16[48,4608]{1,0:T(8,128)(2,1)S(1)}, u32[]{:S(2)}, u32[]{:S(2)}) collective-permute-start(bf16[48,4608]{1,0:T(8,128)(2,1)S(1)} %collective-permute-done.22.outer_ref.refs_7_), channel_id=1, source_target_pairs={{4,0},{6,2},{8,12},{10,14},{20,16},{22,18},{24,28},{26,30},{5,1},{... | collective-permute-start | bytes 1327112 | tf_op jit(solution)/shard_map/ppermute | solution.py:233
  89.5 3.9 %collective-permute-done.24.refs_7_ = bf16[48,4608]{1,0:T(8,128)(2,1)S(1)} collective-permute-done((bf16[48,4608]{1,0:T(8,128)(2,1)S(1)}, bf16[48,4608]{1,0:T(8,128)(2,1)S(1)}, u32[]{:S(2)}, u32[]{:S(2)}) %collective-permute-start.24) | collective-permute-done | bytes 442400 | tf_op jit(solution)/shard_map/ppermute | solution.py:233
  93.4 1.4 %collective-permute-start.31 = (bf16[48,4608]{1,0:T(8,128)(2,1)S(1)}, bf16[48,4608]{1,0:T(8,128)(2,1)S(1)}, u32[]{:S(2)}, u32[]{:S(2)}) collective-permute-start(bf16[48,4608]{1,0:T(8,128)(2,1)S(1)} %pick.31), channel_id=1, source_target_pairs={{0,16},{2,18},{12,28},{14,30},{16,0},{18,2},{28,12},{30,14},{4,8},... | collective-permute-start | bytes 1327112 | tf_op jit(solution)/shard_map/ppermute | solution.py:233
  94.8 1.8 %collective-permute-done.26.refs_1_ = bf16[48,4608]{1,0:T(8,128)(2,1)S(1)} collective-permute-done((bf16[48,4608]{1,0:T(8,128)(2,1)S(1)}, bf16[48,4608]{1,0:T(8,128)(2,1)S(1)}, u32[]{:S(2)}, u32[]{:S(2)}) %collective-permute-start.26) | collective-permute-done | bytes 442400 | tf_op jit(solution)/shard_map/ppermute | solution.py:233
  96.6 1.5 %collective-permute-done.27.refs_4_.refs_8_ = bf16[48,4608]{1,0:T(8,128)(2,1)S(1)} collective-permute-done((bf16[48,4608]{1,0:T(8,128)(2,1)S(1)}, bf16[48,4608]{1,0:T(8,128)(2,1)S(1)}, u32[]{:S(2)}, u32[]{:S(2)}) %collective-permute-start.27) | collective-permute-done | bytes 442400 | tf_op jit(solution)/shard_map/ppermute | solution.py:233
  98.1 1.1 rotate.7
  99.3 1.1 rotate.8.refs_9_
  100.4 3.8 %collective-permute-done.29.refs_3_ = bf16[48,4608]{1,0:T(8,128)(2,1)S(1)} collective-permute-done((bf16[48,4608]{1,0:T(8,128)(2,1)S(1)}, bf16[48,4608]{1,0:T(8,128)(2,1)S(1)}, u32[]{:S(2)}, u32[]{:S(2)}) %collective-permute-start.29) | collective-permute-done | bytes 442400 | tf_op jit(solution)/shard_map/ppermute | solution.py:233
  104.2 1.0 rotate.9
  105.9 1.2 collective-permute-done.32.refs_6_
  107.4 4.5 %collective-permute-start.40 = (f32[24,384]{1,0:T(8,128)S(1)}, f32[24,384]{1,0:T(8,128)S(1)}, u32[]{:S(2)}, u32[]{:S(2)}) collective-permute-start(f32[24,384]{1,0:T(8,128)S(1)} %get-tuple-element.796), channel_id=1, source_target_pairs={{0,14},{2,12},{4,10},{6,8},{8,6},{10,4},{12,2},{14,0},{1,15},{3,13... | collective-permute-start | bytes 110600 | tf_op jit(solution)/shard_map/ppermute | solution.py:350
  112.1 2.2 %collective-permute-start.38 = (f32[24,384]{1,0:T(8,128)S(1)}, f32[24,384]{1,0:T(8,128)S(1)}, u32[]{:S(2)}, u32[]{:S(2)}) collective-permute-start(f32[24,384]{1,0:T(8,128)S(1)} %get-tuple-element.794), channel_id=1, source_target_pairs={{0,10},{2,8},{4,14},{6,12},{8,2},{10,0},{12,6},{14,4},{1,11},{3,9}... | collective-permute-start | bytes 110600 | tf_op jit(solution)/shard_map/ppermute | solution.py:350
  115.1 2.1 %collective-permute-start.36 = (f32[24,384]{1,0:T(8,128)S(1)}, f32[24,384]{1,0:T(8,128)S(1)}, u32[]{:S(2)}, u32[]{:S(2)}) collective-permute-start(f32[24,384]{1,0:T(8,128)S(1)} %get-tuple-element.792), channel_id=1, source_target_pairs={{0,6},{2,4},{4,2},{6,0},{8,14},{10,12},{12,10},{14,8},{1,7},{3,5},... | collective-permute-start | bytes 110600 | tf_op jit(solution)/shard_map/ppermute | solution.py:350
  (69 shorter events, 11.3 us)
Async XLA Ops:
  0.0 1.3 %copy-start.1 = (bf16[14336,48]{0,1:T(8,128)(2,1)S(1)}, bf16[14336,48]{0,1:T(8,128)(2,1)}, u32[]{:S(2)}) copy-start(bf16[14336,48]{0,1:T(8,128)(2,1)} %param.7) | copy-start | bytes 4128772
  1.3 1.0 copy-start.2
  2.5 14.1 %collective-permute-start = (bf16[48,4608]{1,0:T(8,128)(2,1)S(1)}, bf16[48,4608]{1,0:T(8,128)(2,1)S(1)}, u32[]{:S(2)}, u32[]{:S(2)}) collective-permute-start(bf16[48,4608]{1,0:T(8,128)(2,1)S(1)} %get-tuple-element.405), channel_id=1, source_target_pairs={{0,4},{2,6},{4,0},{6,2},{8,12},{10,14},{12,8},{14,10},{16,20},{18,... | collective-permute-start | bytes 1327112 | tf_op jit(solution)/shard_map/ppermute | solution.py:233
  5.5 13.1 %collective-permute-start.1 = (bf16[48,4608]{1,0:T(8,128)(2,1)S(1)}, bf16[48,4608]{1,0:T(8,128)(2,1)S(1)}, u32[]{:S(2)}, u32[]{:S(2)}) collective-permute-start(bf16[48,4608]{1,0:T(8,128)(2,1)S(1)} %get-tuple-element.405), channel_id=1, source_target_pairs={{0,2},{2,0},{4,6},{6,4},{8,10},{10,8},{12,14},{14,12},{16,18},{18,... | collective-permute-start | bytes 1327112 | tf_op jit(solution)/shard_map/ppermute | solution.py:233
  7.1 11.6 %collective-permute-start.2 = (bf16[48,4608]{1,0:T(8,128)(2,1)S(1)}, bf16[48,4608]{1,0:T(8,128)(2,1)S(1)}, u32[]{:S(2)}, u32[]{:S(2)}) collective-permute-start(bf16[48,4608]{1,0:T(8,128)(2,1)S(1)} %get-tuple-element.405), channel_id=1, source_target_pairs={{4,8},{6,10},{8,4},{10,6},{20,24},{22,26},{24,20},{26,22},{5,9},{7... | collective-permute-start | bytes 1327112 | tf_op jit(solution)/shard_map/ppermute | solution.py:233
  7.7 18.3 %collective-permute-start.3 = (bf16[48,4608]{1,0:T(8,128)(2,1)S(1)}, bf16[48,4608]{1,0:T(8,128)(2,1)S(1)}, u32[]{:S(2)}, u32[]{:S(2)}) collective-permute-start(bf16[48,4608]{1,0:T(8,128)(2,1)S(1)} %get-tuple-element.426), channel_id=1, source_target_pairs={{0,4},{2,6},{4,0},{6,2},{8,12},{10,14},{12,8},{14,10},{16,20},{18,... | collective-permute-start | bytes 1327112 | tf_op jit(solution)/shard_map/ppermute | solution.py:233
  12.2 15.9 %collective-permute-start.4 = (bf16[48,4608]{1,0:T(8,128)(2,1)S(1)}, bf16[48,4608]{1,0:T(8,128)(2,1)S(1)}, u32[]{:S(2)}, u32[]{:S(2)}) collective-permute-start(bf16[48,4608]{1,0:T(8,128)(2,1)S(1)} %get-tuple-element.426), channel_id=1, source_target_pairs={{0,2},{2,0},{4,6},{6,4},{8,10},{10,8},{12,14},{14,12},{16,18},{18,... | collective-permute-start | bytes 1327112 | tf_op jit(solution)/shard_map/ppermute | solution.py:233
  16.5 11.6 %collective-permute-start.5 = (bf16[48,4608]{1,0:T(8,128)(2,1)S(1)}, bf16[48,4608]{1,0:T(8,128)(2,1)S(1)}, u32[]{:S(2)}, u32[]{:S(2)}) collective-permute-start(bf16[48,4608]{1,0:T(8,128)(2,1)S(1)} %get-tuple-element.426), channel_id=1, source_target_pairs={{4,8},{6,10},{8,4},{10,6},{20,24},{22,26},{24,20},{26,22},{5,9},{7... | collective-permute-start | bytes 1327112 | tf_op jit(solution)/shard_map/ppermute | solution.py:233
  18.6 48.9 %slice-start = ((s8[7340032]{0:T(1024)(128)(4,1)}), s8[4194304]{0:T(1024)(128)(4,1)S(1)}, s32[]{:S(2)}) async-start(s8[7340032]{0:T(1024)(128)(4,1)} %bitcast.4), calls=%async_computation | async-start | bytes 8388608
  18.7 16.8 %collective-permute-start.6 = (bf16[48,4608]{1,0:T(8,128)(2,1)S(1)}, bf16[48,4608]{1,0:T(8,128)(2,1)S(1)}, u32[]{:S(2)}, u32[]{:S(2)}) collective-permute-start(bf16[48,4608]{1,0:T(8,128)(2,1)S(1)} %pick.16), channel_id=1, source_target_pairs={{0,4},{2,6},{4,0},{6,2},{8,12},{10,14},{12,8},{14,10},{16,20},{18,... | collective-permute-start | bytes 1327112 | tf_op jit(solution)/shard_map/ppermute | solution.py:233
  22.6 15.0 %collective-permute-start.7 = (bf16[48,4608]{1,0:T(8,128)(2,1)S(1)}, bf16[48,4608]{1,0:T(8,128)(2,1)S(1)}, u32[]{:S(2)}, u32[]{:S(2)}) collective-permute-start(bf16[48,4608]{1,0:T(8,128)(2,1)S(1)} %collective-permute-done.outer_ref.refs_0_), channel_id=1, source_target_pairs={{0,2},{2,0},{12,14},{14,12},{4,8},{6,10},{8,4},{10,6},{16,18},{18,... | collective-permute-start | bytes 1327112 | tf_op jit(solution)/shard_map/ppermute | solution.py:233
  26.0 11.6 %collective-permute-start.8 = (bf16[48,4608]{1,0:T(8,128)(2,1)S(1)}, bf16[48,4608]{1,0:T(8,128)(2,1)S(1)}, u32[]{:S(2)}, u32[]{:S(2)}) collective-permute-start(bf16[48,4608]{1,0:T(8,128)(2,1)S(1)} %collective-permute-done.1.outer_ref.refs_1_), channel_id=1, source_target_pairs={{0,16},{2,18},{4,20},{6,22},{8,24},{10,26},{12,28},{14,30},{16,0},... | collective-permute-start | bytes 1327112 | tf_op jit(solution)/shard_map/ppermute | solution.py:233
  28.2 16.8 %collective-permute-start.9 = (bf16[48,4608]{1,0:T(8,128)(2,1)S(1)}, bf16[48,4608]{1,0:T(8,128)(2,1)S(1)}, u32[]{:S(2)}, u32[]{:S(2)}) collective-permute-start(bf16[48,4608]{1,0:T(8,128)(2,1)S(1)} %pick.17), channel_id=1, source_target_pairs={{0,4},{2,6},{4,0},{6,2},{8,12},{10,14},{12,8},{14,10},{16,20},{18,... | collective-permute-start | bytes 1327112 | tf_op jit(solution)/shard_map/ppermute | solution.py:233
  33.7 13.4 %collective-permute-start.10 = (bf16[48,4608]{1,0:T(8,128)(2,1)S(1)}, bf16[48,4608]{1,0:T(8,128)(2,1)S(1)}, u32[]{:S(2)}, u32[]{:S(2)}) collective-permute-start(bf16[48,4608]{1,0:T(8,128)(2,1)S(1)} %collective-permute-done.3.outer_ref.refs_0_), channel_id=1, source_target_pairs={{0,2},{2,0},{12,14},{14,12},{4,8},{6,10},{8,4},{10,6},{16,18},{18,... | collective-permute-start | bytes 1327112 | tf_op jit(solution)/shard_map/ppermute | solution.py:233
  35.5 11.6 %collective-permute-start.11 = (bf16[48,4608]{1,0:T(8,128)(2,1)S(1)}, bf16[48,4608]{1,0:T(8,128)(2,1)S(1)}, u32[]{:S(2)}, u32[]{:S(2)}) collective-permute-start(bf16[48,4608]{1,0:T(8,128)(2,1)S(1)} %collective-permute-done.4.refs_3_.outer_ref), channel_id=1, source_target_pairs={{0,16},{2,18},{4,20},{6,22},{8,24},{10,26},{12,28},{14,30},{16,0},... | collective-permute-start | bytes 1327112 | tf_op jit(solution)/shard_map/ppermute | solution.py:233
  37.6 16.8 %collective-permute-start.12 = (bf16[48,4608]{1,0:T(8,128)(2,1)S(1)}, bf16[48,4608]{1,0:T(8,128)(2,1)S(1)}, u32[]{:S(2)}, u32[]{:S(2)}) collective-permute-start(bf16[48,4608]{1,0:T(8,128)(2,1)S(1)} %pick.18), channel_id=1, source_target_pairs={{0,4},{2,6},{4,0},{6,2},{8,12},{10,14},{12,8},{14,10},{16,20},{18,... | collective-permute-start | bytes 1327112 | tf_op jit(solution)/shard_map/ppermute | solution.py:233
  43.2 15.0 %collective-permute-start.13 = (bf16[48,4608]{1,0:T(8,128)(2,1)S(1)}, bf16[48,4608]{1,0:T(8,128)(2,1)S(1)}, u32[]{:S(2)}, u32[]{:S(2)}) collective-permute-start(bf16[48,4608]{1,0:T(8,128)(2,1)S(1)} %pick.19), channel_id=1, source_target_pairs={{0,2},{2,0},{4,6},{6,4},{8,10},{10,8},{12,14},{14,12},{16,18},{18,... | collective-permute-start | bytes 1327112 | tf_op jit(solution)/shard_map/ppermute | solution.py:233
  45.0 22.5 %slice-start.1 = ((s8[7340032]{0:T(1024)(128)(4,1)}), s8[3145728]{0:T(1024)(128)(4,1)S(1)}, s32[]{:S(2)}) async-start(s8[7340032]{0:T(1024)(128)(4,1)} %bitcast.4), calls=%async_computation.1 | async-start | bytes 6291456
  45.0 13.1 %collective-permute-start.14 = (bf16[48,4608]{1,0:T(8,128)(2,1)S(1)}, bf16[48,4608]{1,0:T(8,128)(2,1)S(1)}, u32[]{:S(2)}, u32[]{:S(2)}) collective-permute-start(bf16[48,4608]{1,0:T(8,128)(2,1)S(1)} %pick.20), channel_id=1, source_target_pairs={{0,16},{2,18},{12,28},{14,30},{16,0},{18,2},{28,12},{30,14},{4,8},... | collective-permute-start | bytes 1327112 | tf_op jit(solution)/shard_map/ppermute | solution.py:233
  47.1 16.8 %collective-permute-start.15 = (bf16[48,4608]{1,0:T(8,128)(2,1)S(1)}, bf16[48,4608]{1,0:T(8,128)(2,1)S(1)}, u32[]{:S(2)}, u32[]{:S(2)}) collective-permute-start(bf16[48,4608]{1,0:T(8,128)(2,1)S(1)} %pick.21), channel_id=1, source_target_pairs={{0,4},{2,6},{4,0},{6,2},{8,12},{10,14},{12,8},{14,10},{16,20},{18,... | collective-permute-start | bytes 1327112 | tf_op jit(solution)/shard_map/ppermute | solution.py:233
  54.5 16.2 %collective-permute-start.16 = (bf16[48,4608]{1,0:T(8,128)(2,1)S(1)}, bf16[48,4608]{1,0:T(8,128)(2,1)S(1)}, u32[]{:S(2)}, u32[]{:S(2)}) collective-permute-start(bf16[48,4608]{1,0:T(8,128)(2,1)S(1)} %pick.22), channel_id=1, source_target_pairs={{0,2},{2,0},{4,6},{6,4},{8,10},{10,8},{12,14},{14,12},{16,18},{18,... | collective-permute-start | bytes 1327112 | tf_op jit(solution)/shard_map/ppermute | solution.py:233
  56.6 10.9 %copy-start = (bf16[1,256,4096]{2,1,0:T(8,128)(2,1)S(1)}, bf16[1,256,4096]{2,1,0:T(8,128)(2,1)}, u32[]{:S(2)}) copy-start(bf16[1,256,4096]{2,1,0:T(8,128)(2,1)} %param.4) | copy-start | bytes 6291460
  56.6 14.0 %collective-permute-start.17 = (bf16[48,4608]{1,0:T(8,128)(2,1)S(1)}, bf16[48,4608]{1,0:T(8,128)(2,1)S(1)}, u32[]{:S(2)}, u32[]{:S(2)}) collective-permute-start(bf16[48,4608]{1,0:T(8,128)(2,1)S(1)} %pick.23), channel_id=1, source_target_pairs={{0,16},{2,18},{12,28},{14,30},{16,0},{18,2},{28,12},{30,14},{4,8},... | collective-permute-start | bytes 1327112 | tf_op jit(solution)/shard_map/ppermute | solution.py:233
  58.2 15.7 %collective-permute-start.18 = (bf16[48,4608]{1,0:T(8,128)(2,1)S(1)}, bf16[48,4608]{1,0:T(8,128)(2,1)S(1)}, u32[]{:S(2)}, u32[]{:S(2)}) collective-permute-start(bf16[48,4608]{1,0:T(8,128)(2,1)S(1)} %pick.24), channel_id=1, source_target_pairs={{0,4},{2,6},{4,0},{6,2},{8,12},{10,14},{12,8},{14,10},{16,20},{18,... | collective-permute-start | bytes 1327112 | tf_op jit(solution)/shard_map/ppermute | solution.py:233
  63.9 13.1 %collective-permute-start.19 = (bf16[48,4608]{1,0:T(8,128)(2,1)S(1)}, bf16[48,4608]{1,0:T(8,128)(2,1)S(1)}, u32[]{:S(2)}, u32[]{:S(2)}) collective-permute-start(bf16[48,4608]{1,0:T(8,128)(2,1)S(1)} %pick.25), channel_id=1, source_target_pairs={{0,2},{2,0},{12,14},{14,12},{4,8},{6,10},{8,4},{10,6},{16,18},{18,... | collective-permute-start | bytes 1327112 | tf_op jit(solution)/shard_map/ppermute | solution.py:233
  66.0 11.1 %collective-permute-start.20 = (bf16[48,4608]{1,0:T(8,128)(2,1)S(1)}, bf16[48,4608]{1,0:T(8,128)(2,1)S(1)}, u32[]{:S(2)}, u32[]{:S(2)}) collective-permute-start(bf16[48,4608]{1,0:T(8,128)(2,1)S(1)} %pick.26), channel_id=1, source_target_pairs={{0,16},{2,18},{4,20},{6,22},{8,24},{10,26},{12,28},{14,30},{16,0},... | collective-permute-start | bytes 1327112 | tf_op jit(solution)/shard_map/ppermute | solution.py:233
  70.7 13.2 %collective-permute-start.21 = (bf16[48,4608]{1,0:T(8,128)(2,1)S(1)}, bf16[48,4608]{1,0:T(8,128)(2,1)S(1)}, u32[]{:S(2)}, u32[]{:S(2)}) collective-permute-start(bf16[48,4608]{1,0:T(8,128)(2,1)S(1)} %pick.27), channel_id=1, source_target_pairs={{0,4},{2,6},{4,0},{6,2},{8,12},{10,14},{12,8},{14,10},{16,20},{18,... | collective-permute-start | bytes 1327112 | tf_op jit(solution)/shard_map/ppermute | solution.py:233
  72.4 15.2 %collective-permute-start.22 = (bf16[48,4608]{1,0:T(8,128)(2,1)S(1)}, bf16[48,4608]{1,0:T(8,128)(2,1)S(1)}, u32[]{:S(2)}, u32[]{:S(2)}) collective-permute-start(bf16[48,4608]{1,0:T(8,128)(2,1)S(1)} %collective-permute-done.15.refs_6_.refs_4_), channel_id=1, source_target_pairs={{0,2},{2,0},{12,14},{14,12},{4,8},{6,10},{8,4},{10,6},{16,18},{18,... | collective-permute-start | bytes 1327112 | tf_op jit(solution)/shard_map/ppermute | solution.py:233
  74.0 13.6 %collective-permute-start.23 = (bf16[48,4608]{1,0:T(8,128)(2,1)S(1)}, bf16[48,4608]{1,0:T(8,128)(2,1)S(1)}, u32[]{:S(2)}, u32[]{:S(2)}) collective-permute-start(bf16[48,4608]{1,0:T(8,128)(2,1)S(1)} %pick.28), channel_id=1, source_target_pairs={{0,16},{2,18},{4,20},{6,22},{8,24},{10,26},{12,28},{14,30},{16,0},... | collective-permute-start | bytes 1327112 | tf_op jit(solution)/shard_map/ppermute | solution.py:233
  77.1 16.3 %collective-permute-start.24 = (bf16[48,4608]{1,0:T(8,128)(2,1)S(1)}, bf16[48,4608]{1,0:T(8,128)(2,1)S(1)}, u32[]{:S(2)}, u32[]{:S(2)}) collective-permute-start(bf16[48,4608]{1,0:T(8,128)(2,1)S(1)} %collective-permute-done.19.refs_8_.refs_2_), channel_id=1, source_target_pairs={{4,0},{6,2},{8,12},{10,14},{20,16},{22,18},{24,28},{26,30},{5,1},{... | collective-permute-start | bytes 1327112 | tf_op jit(solution)/shard_map/ppermute | solution.py:233
  84.0 12.6 %collective-permute-start.26 = (bf16[48,4608]{1,0:T(8,128)(2,1)S(1)}, bf16[48,4608]{1,0:T(8,128)(2,1)S(1)}, u32[]{:S(2)}, u32[]{:S(2)}) collective-permute-start(bf16[48,4608]{1,0:T(8,128)(2,1)S(1)} %pick.29), channel_id=1, source_target_pairs={{0,16},{2,18},{4,20},{6,22},{8,24},{10,26},{12,28},{14,30},{16,0},... | collective-permute-start | bytes 1327112 | tf_op jit(solution)/shard_map/ppermute | solution.py:233
  85.0 13.1 %collective-permute-start.27 = (bf16[48,4608]{1,0:T(8,128)(2,1)S(1)}, bf16[48,4608]{1,0:T(8,128)(2,1)S(1)}, u32[]{:S(2)}, u32[]{:S(2)}) collective-permute-start(bf16[48,4608]{1,0:T(8,128)(2,1)S(1)} %pick.30), channel_id=1, source_target_pairs={{0,2},{2,0},{12,14},{14,12},{4,8},{6,10},{8,4},{10,6},{16,18},{18,... | collective-permute-start | bytes 1327112 | tf_op jit(solution)/shard_map/ppermute | solution.py:233
  87.6 16.5 %collective-permute-start.30 = (bf16[48,4608]{1,0:T(8,128)(2,1)S(1)}, bf16[48,4608]{1,0:T(8,128)(2,1)S(1)}, u32[]{:S(2)}, u32[]{:S(2)}) collective-permute-start(bf16[48,4608]{1,0:T(8,128)(2,1)S(1)} %collective-permute-done.22.outer_ref.refs_7_), channel_id=1, source_target_pairs={{4,0},{6,2},{8,12},{10,14},{20,16},{22,18},{24,28},{26,30},{5,1},{... | collective-permute-start | bytes 1327112 | tf_op jit(solution)/shard_map/ppermute | solution.py:233
  88.9 15.2 %collective-permute-start.29 = (bf16[48,4608]{1,0:T(8,128)(2,1)S(1)}, bf16[48,4608]{1,0:T(8,128)(2,1)S(1)}, u32[]{:S(2)}, u32[]{:S(2)}) collective-permute-start(bf16[48,4608]{1,0:T(8,128)(2,1)S(1)} %collective-permute-done.23.refs_1_), channel_id=1, source_target_pairs={{0,2},{2,0},{4,6},{6,4},{8,10},{10,8},{12,14},{14,12},{16,18},{18,... | collective-permute-start | bytes 1327112 | tf_op jit(solution)/shard_map/ppermute | solution.py:233
  93.4 10.8 %collective-permute-start.31 = (bf16[48,4608]{1,0:T(8,128)(2,1)S(1)}, bf16[48,4608]{1,0:T(8,128)(2,1)S(1)}, u32[]{:S(2)}, u32[]{:S(2)}) collective-permute-start(bf16[48,4608]{1,0:T(8,128)(2,1)S(1)} %pick.31), channel_id=1, source_target_pairs={{0,16},{2,18},{12,28},{14,30},{16,0},{18,2},{28,12},{30,14},{4,8},... | collective-permute-start | bytes 1327112 | tf_op jit(solution)/shard_map/ppermute | solution.py:233
  99.2 7.9 %collective-permute-start.28 = (f32[288,256]{1,0:T(8,128)S(1)}, f32[288,256]{1,0:T(8,128)S(1)}, u32[]{:S(2)}, u32[]{:S(2)}) collective-permute-start(f32[288,256]{1,0:T(8,128)S(1)} %get-tuple-element.774.refs_2_), channel_id=1, source_target_pairs={{0,1},{1,0},{2,3},{3,2},{4,5},{5,4},{6,7},{7,6},{8,9},{9,8},{10,11... | collective-permute-start | bytes 884744 | tf_op jit(solution)/shard_map/ppermute | solution.py:172
  105.2 1.8 %collective-permute-start.33 = (f32[144,256]{1,0:T(8,128)S(1)}, f32[144,256]{1,0:T(8,128)S(1)}, u32[]{:S(2)}, u32[]{:S(2)}) collective-permute-start(f32[144,256]{1,0:T(8,128)S(1)} %get-tuple-element.788), channel_id=1, source_target_pairs={{0,1},{1,0},{2,3},{3,2},{4,5},{5,4},{6,7},{7,6},{8,9},{9,8},{10,11... | collective-permute-start | bytes 442376 | tf_op jit(solution)/shard_map/ppermute | solution.py:172
  105.3 1.7 %collective-permute-start.25 = (f32[96,256]{1,0:T(8,128)S(1)}, f32[96,256]{1,0:T(8,128)S(1)}, u32[]{:S(2)}, u32[]{:S(2)}) collective-permute-start(f32[96,256]{1,0:T(8,128)S(1)} %get-tuple-element.765.refs_0_), channel_id=1, source_target_pairs={{0,1},{1,0},{2,3},{3,2},{4,5},{5,4},{6,7},{7,6},{8,9},{9,8},{10,11... | collective-permute-start | bytes 294920 | tf_op jit(solution)/shard_map/ppermute | solution.py:172
  105.8 1.2 %collective-permute-start.32 = (f32[48,256]{1,0:T(8,128)S(1)}, f32[48,256]{1,0:T(8,128)S(1)}, u32[]{:S(2)}, u32[]{:S(2)}) collective-permute-start(f32[48,256]{1,0:T(8,128)S(1)} %get-tuple-element.787), channel_id=1, source_target_pairs={{0,1},{1,0},{2,3},{3,2},{4,5},{5,4},{6,7},{7,6},{8,9},{9,8},{10,11... | collective-permute-start | bytes 147464 | tf_op jit(solution)/shard_map/ppermute | solution.py:172
  107.4 9.8 %collective-permute-start.40 = (f32[24,384]{1,0:T(8,128)S(1)}, f32[24,384]{1,0:T(8,128)S(1)}, u32[]{:S(2)}, u32[]{:S(2)}) collective-permute-start(f32[24,384]{1,0:T(8,128)S(1)} %get-tuple-element.796), channel_id=1, source_target_pairs={{0,14},{2,12},{4,10},{6,8},{8,6},{10,4},{12,2},{14,0},{1,15},{3,13... | collective-permute-start | bytes 110600 | tf_op jit(solution)/shard_map/ppermute | solution.py:350
  111.9 6.1 %collective-permute-start.39 = (f32[24,384]{1,0:T(8,128)S(1)}, f32[24,384]{1,0:T(8,128)S(1)}, u32[]{:S(2)}, u32[]{:S(2)}) collective-permute-start(f32[24,384]{1,0:T(8,128)S(1)} %get-tuple-element.795), channel_id=1, source_target_pairs={{0,12},{2,14},{4,8},{6,10},{8,4},{10,6},{12,0},{14,2},{1,13},{3,15... | collective-permute-start | bytes 110600 | tf_op jit(solution)/shard_map/ppermute | solution.py:350
  112.1 6.8 %collective-permute-start.38 = (f32[24,384]{1,0:T(8,128)S(1)}, f32[24,384]{1,0:T(8,128)S(1)}, u32[]{:S(2)}, u32[]{:S(2)}) collective-permute-start(f32[24,384]{1,0:T(8,128)S(1)} %get-tuple-element.794), channel_id=1, source_target_pairs={{0,10},{2,8},{4,14},{6,12},{8,2},{10,0},{12,6},{14,4},{1,11},{3,9}... | collective-permute-start | bytes 110600 | tf_op jit(solution)/shard_map/ppermute | solution.py:350
  114.3 5.1 %collective-permute-start.37 = (f32[24,384]{1,0:T(8,128)S(1)}, f32[24,384]{1,0:T(8,128)S(1)}, u32[]{:S(2)}, u32[]{:S(2)}) collective-permute-start(f32[24,384]{1,0:T(8,128)S(1)} %get-tuple-element.793), channel_id=1, source_target_pairs={{0,8},{2,10},{4,12},{6,14},{8,0},{10,2},{12,4},{14,6},{1,9},{3,11}... | collective-permute-start | bytes 110600 | tf_op jit(solution)/shard_map/ppermute | solution.py:350
  115.1 5.2 %collective-permute-start.36 = (f32[24,384]{1,0:T(8,128)S(1)}, f32[24,384]{1,0:T(8,128)S(1)}, u32[]{:S(2)}, u32[]{:S(2)}) collective-permute-start(f32[24,384]{1,0:T(8,128)S(1)} %get-tuple-element.792), channel_id=1, source_target_pairs={{0,6},{2,4},{4,2},{6,0},{8,14},{10,12},{12,10},{14,8},{1,7},{3,5},... | collective-permute-start | bytes 110600 | tf_op jit(solution)/shard_map/ppermute | solution.py:350
  117.2 4.0 %collective-permute-start.35 = (f32[24,384]{1,0:T(8,128)S(1)}, f32[24,384]{1,0:T(8,128)S(1)}, u32[]{:S(2)}, u32[]{:S(2)}) collective-permute-start(f32[24,384]{1,0:T(8,128)S(1)} %get-tuple-element.791), channel_id=1, source_target_pairs={{0,4},{2,6},{4,0},{6,2},{8,12},{10,14},{12,8},{14,10},{1,5},{3,7},... | collective-permute-start | bytes 110600 | tf_op jit(solution)/shard_map/ppermute | solution.py:350
  118.0 4.0 %collective-permute-start.34 = (f32[24,384]{1,0:T(8,128)S(1)}, f32[24,384]{1,0:T(8,128)S(1)}, u32[]{:S(2)}, u32[]{:S(2)}) collective-permute-start(f32[24,384]{1,0:T(8,128)S(1)} %get-tuple-element.790), channel_id=1, source_target_pairs={{0,2},{2,0},{4,6},{6,4},{8,10},{10,8},{12,14},{14,12},{1,3},{3,1},... | collective-permute-start | bytes 110600 | tf_op jit(solution)/shard_map/ppermute | solution.py:350

commit v5 on v4

--- a/solution.py
+++ b/solution.py
@@ -10,7 +10,8 @@
 TOK = 256
 K = 384
 LANES = 128
-AHEAD = 5
+AHEAD = 30
+ORDER = "APQ"
 STEP = 1 * 10**8
 
 
@@ -61,22 +62,30 @@
         out_ref[...] = inner_ref[...]
 
 
-def cut_kernel(in_half, first, in_ref, out_ref, m0, m1, t0, t1):
+def cut_kernel(in_half, first, in_ref, out_ref, m0, m1, t0, t1, sems):
     x = lax.axis_index("group")
     out_half = first + m1.shape[1]
+    copies = []
     for side, unit0, unit1 in ((x, m0, m1), (1 - x, t0, t1)):
         in_at = pl.multiple_of(side * in_half, LANES)
         out_at = pl.multiple_of(side * out_half, LANES)
         next_at = pl.multiple_of(side * out_half + first, LANES)
-        unit0[:, :in_half] = in_ref[:, pl.ds(in_at, in_half)]
-        unit0[:, in_half:] = out_ref[:, pl.ds(out_at, first)]
-        unit1[...] = out_ref[:, pl.ds(next_at, unit1.shape[1])]
+        copies += [
+            (in_ref.at[:, pl.ds(in_at, in_half)], unit0.at[:, :in_half]),
+            (out_ref.at[:, pl.ds(out_at, first)], unit0.at[:, in_half:]),
+            (out_ref.at[:, pl.ds(next_at, unit1.shape[1])], unit1),
+        ]
+    started = [pltpu.make_async_copy(a, b, sems.at[i]) for i, (a, b) in enumerate(copies)]
+    for copy in started:
+        copy.start()
+    for copy in started:
+        copy.wait()
 
 
 def rotate_kernel(plan, in_half, first, acts_ref, grads_ref, *refs):
     x = lax.axis_index("group")
     core = lax.axis_index("basis")
-    terms, has_acc, last = plan
+    terms, acc_from, last = plan
     refs = list(refs)
     stack = refs.pop()
     z = lax.axis_index("dp") // 2
@@ -112,10 +121,11 @@
         rot_out = part if rot_out is None else rot_out + part
     panel = refs[0].shape[0] // 2
     refs = refs[1 + max(i for term in terms for pair in term[2] for i in pair) :]
-    if has_acc:
+    if acc_from is not None:
+        at = slice(acc_from, acc_from + rot_out.shape[0])
         if rot_in is not None:
-            rot_in += refs.pop(0)[...]
-        rot_out += refs.pop(0)[...]
+            rot_in += refs.pop(0)[at]
+        rot_out += refs.pop(0)[at]
     if rot_in is not None:
         refs.pop(0)[...] = rot_in
     if not last:
@@ -130,29 +140,27 @@
         send[at] = jnp.where(core == 0, high, low)
 
 
-def finish_kernel(rows, *refs):
+def store_squares(keep, come, rot_in, outs):
+    rot_out = (keep[...] + come[...]).astype(jnp.bfloat16)
+    coeff = nt_dot(rot_out, rot_in) * (1.0 / TOK**0.5)
+    square = coeff * coeff
+    panel = outs[0].shape[0]
+    for block, ref in enumerate(outs):
+        ref[...] = square[block * panel : (block + 1) * panel]
+
+
+def rotated_kernel(rows, in_a, in_a2, in_b, in_b2, keep, come, in_ref, *outs):
     me = lax.axis_index("dp")
-    z, y = me // 2, me % 2
-    order = [z]
-    for by_z in ((1, 2, 1, 2), (2, 0, 3, 1), (3, 3, 0, 0)):
-        order.append(jnp.where(z == 0, by_z[0], jnp.where(z == 1, by_z[1], jnp.where(z == 2, by_z[2], by_z[3]))))
-    ins, keep, come = refs[0:4], refs[4:6], refs[6:8]
-    outs = refs[8:-2]
-    in_ref, out_ref = refs[-2:]
-    half = rows // 2
-    for shard in range(8):
-        part, local = (0, shard) if shard < 2 else (1, shard - 2)
-        owner = order[shard // 2] * 2 + (y if shard % 2 == 0 else 1 - y)
-        block = ins[2 * part][pl.ds(local * rows, rows)] + ins[2 * part + 1][pl.ds(local * rows, rows)]
-        in_ref[pl.ds(pl.multiple_of(owner * rows, 16), rows), :] = block.astype(jnp.bfloat16)
-        place = owner ^ me
-        at = pl.ds(local * half, half)
-        out_ref[pl.ds(pl.multiple_of(place * half, 8), half), :] = keep[part][at] + come[part][at]
-    coeff = nt_dot(out_ref[...].astype(jnp.bfloat16), in_ref[...])
-    coeff = coeff * (1.0 / TOK**0.5)
-    square = coeff * coeff
-    for place, ref in enumerate(outs):
-        ref[...] = square[place * half : (place + 1) * half]
+    for block in range(8):
+        at = pl.ds((block if block < 2 else block - 2) * rows, rows)
+        total = in_a[at] + in_a2[at] if block < 2 else in_b[at] + in_b2[at]
+        begin = pl.multiple_of((me ^ block) * rows, 16)
+        in_ref[pl.ds(begin, rows), :] = total.astype(jnp.bfloat16)
+    store_squares(keep, come, in_ref[...], outs)
+
+
+def squares_kernel(in_ref, keep, come, *outs):
+    store_squares(keep, come, in_ref[...], outs)
 
 
 def per_device_plane(activations, out_grads, input_basis, output_basis):
@@ -175,13 +183,14 @@
     m0, m1, t0, t1 = pl.pallas_call(
         functools.partial(cut_kernel, in_half, first),
         out_shape=[unit] * 4,
-        in_specs=[vmem] * 2,
+        in_specs=[pl.BlockSpec(memory_space=pltpu.HBM)] * 2,
         out_specs=[vmem] * 4,
+        scratch_shapes=[pltpu.SemaphoreType.DMA((6,))],
         compiler_params=pltpu.CompilerParams(vmem_limit_bytes=8 * 2**20),
         name="cut",
     )(in_t, out_t)
 
-    def rotate(slots, names, acc, last):
+    def rotate(slots, names, acc, acc_from, last):
         terms, pieces, out_shape = [], [], []
         count = 2 * len(slots)
 
@@ -202,7 +211,7 @@
             out_shape.append(full)
         out_shape += [panel, panel] if last else [full]
         return pl.pallas_call(
-            functools.partial(rotate_kernel, (terms, bool(acc), last), in_half, first),
+            functools.partial(rotate_kernel, (terms, acc_from, last), in_half, first),
             out_shape=out_shape,
             in_specs=[vmem] * (2 + len(pieces) + len(acc)),
             out_specs=[vmem] * len(out_shape),
@@ -247,14 +256,16 @@
 
     at_outer = {"0m0": m0, "0m1": m1, "0t0": t0, "0t1": t1}
     at_inner = dict(at_outer)
-    a_outer = ["1m0", "1m1", "2m0", "2m1", "3m0", "3m1", "3om0", "3t0", "3ot0", "3t1"]
-    a_inner = ["2m0", "2m1", "2om0", "2t0", "2ot0", "2t1", "2om1", "2ot1"]
-    b_inner = ["1m0", "1m1", "3m0", "3m1", "3om0", "3t0", "3ot0", "3t1", "3om1", "3ot1"]
-    y_outer = ["0om0", "0om1", "1om0", "1om1", "2om0", "2om1", "1ot1", "3om1", "2ot0", "2ot1"]
-    x_outer = [None, None, "0ot0", "0ot1", "1t1", "2t0", "1t0", "2t1", "1ot0", "3ot1"]
-    y_inner = ["0om0", "0om1", None, None, "1om0", "1om1", None, None, None, "1ot1"]
-    x_inner = [None, None, "0ot0", "0ot1", None, None, "1t0", "1t1", "1ot0", None]
-    to_inner = ["0" + name[1:] for name in a_inner]
+    a_outer = ["1m0", "1m1", "2m0", "2m1", "3m0", "3t0", "3m1", "3om0", "3ot1", "1ot1"]
+    outward = ["0m0", "0m1", "3m0", "3m1", "2m0", "2t0", "2m1", "2om0", "2ot1", "0ot1"]
+    a_inner = ["1m0", "1t0", "1m1", "1om0", "1ot1", "1ot0", "1t1", "3om1", "3t1", "1om1"]
+    inward = ["0m0", "0t0", "0m1", "0om0", "0ot1", "0ot0", "0t1", "2om1", "2t1", "0om1"]
+    b_inner = ["3m0", "3m1", "2m0", "2t0", "2m1", "2om0", "2ot1", "2ot0", "3ot1", None]
+    crossing = ["0m0", "0m1", "1m0", "1t0", "1m1", "1om0", "1ot1", "1ot0", "0ot1", None]
+    y_outer = ["0om1", "0om0", "1om0", "0ot0", "2om0", "2om1", "2ot0", "3ot0", "3om1", "1om1"]
+    x_outer = [None, None, "0ot1", "1t0", "2t0", "2t1", "1ot0", "2ot1", "3t1", "1t1"]
+    y_inner = ["0om1", "0om0", None, "0ot0", "3om0", None, None, "2om1", None, None]
+    x_inner = [None, None, "0ot1", None, None, "3t0", "3ot0", None, "2t1", None]
 
     def over_y(name):
         return name.replace("o", "")
@@ -283,71 +294,74 @@
         i = r - 1
         for units, name, value in landing.pop(r - 2, []):
             units[name] = value
-        settle()
-        outward = at_inner["0" + a_outer[i][1:]] if r < 3 else at_inner[b_inner[i - 2]]
-        if r < 9:
-            value, pairs = pick(at_outer[to_inner[i]], outward), group_pairs(link_a)
-            spots = [(at_outer, a_outer[i]), (at_inner, a_inner[i])]
-        else:
-            value, pairs = outward, group_pairs([p for p in link_a if p[1] in at_ends])
-            spots = [(at_outer, a_outer[i])]
-        landing[r] = bring(value, pairs, *spots)
-        settle()
-        crossing = at_inner["0" + b_inner[i][1:]] if r < 3 else at_inner[a_inner[i - 2]]
-        value = at_outer[over_y(y_outer[i])]
-        spots = [(at_outer, y_outer[i])]
-        if y_inner[i]:
-            value, pairs = pick(value, at_inner[over_y(y_inner[i])]), group_pairs(link_y)
-            spots.append((at_inner, y_inner[i]))
-        else:
-            y_pairs = [p for p in link_y if p[0] in at_ends]
-            value, pairs = pick(value, crossing), group_pairs(y_pairs + link_b)
-            spots.append((at_inner, b_inner[i]))
-        landing[r] += bring(value, pairs, *spots)
-        settle()
-        if x_inner[i]:
-            value = pick(at_outer[over_x(x_outer[i])], at_inner[over_x(x_inner[i])])
-            spots, pairs = [(at_inner, x_inner[i])], across_x(cells)
-        else:
-            crossing = at_inner["0" + b_inner[i][1:]] if r < 3 else at_inner[a_inner[i - 2]]
-            spots, pairs = [(at_inner, b_inner[i])], group_pairs(link_b)
-            value = crossing
-            if x_outer[i]:
-                value = pick(at_outer[over_x(x_outer[i])], crossing)
-                pairs = across_x(at_ends) + pairs
-        if x_outer[i]:
-            spots.append((at_outer, x_outer[i]))
-        landing[r] += bring(value, pairs, *spots)
         if r == 7:
-            extra["in_a"], extra["keep_a"], extra["send_a"] = rotate("0", ["m0", "m1", "t0", "t1"], [], True)
-        if r == 9:
-            extra["acc_in"], extra["acc_out"] = rotate("123", ["m0"], [], False)
-    for r in (9, 10):
-        for units, name, value in landing.pop(r):
-            units[name] = value
+            extra["in_a"], extra["keep_a"], extra["send_a"] = rotate("0", ["m0", "m1", "t0", "t1"], [], None, True)
+        landing[r] = []
+        if r == 10:
+            acc_in, acc_out = rotate("123", ["m0"], [], None, False)
+            extra["in_b"], extra["acc"] = rotate("123", ["t0"], [acc_in, acc_out], 0, False)
+        for link in ORDER if r > 2 else "APQ":
+            settle()
+            if link == "A":
+                value = pick(at_outer[inward[i]], at_inner[outward[i]])
+                landing[r] += bring(value, group_pairs(link_a), (at_outer, a_outer[i]), (at_inner, a_inner[i]))
+                continue
+            over, from_outer, from_inner, around = (
+                (over_y, y_outer[i], y_inner[i], lambda where: group_pairs([p for p in link_y if p[0] in where]))
+                if link == "P"
+                else (over_x, x_outer[i], x_inner[i], across_x)
+            )
+            spots, pairs, choices = [], [], []
+            if from_outer:
+                spots.append((at_outer, from_outer))
+                choices.append(at_outer[over(from_outer)])
+                pairs += around(at_ends)
+            if from_inner:
+                spots.append((at_inner, from_inner))
+                choices.append(at_inner[over(from_inner)])
+                pairs += around([c for c in cells if c not in at_ends])
+            elif b_inner[i]:
+                spots.append((at_inner, b_inner[i]))
+                choices.append(at_inner[crossing[i]])
+                pairs += group_pairs(link_b)
+            landing[r] += bring(pick(choices[0], choices[-1]), pairs, *spots)
+
+    block = jax.ShapeDtypeStruct((rows // 2, K), jnp.float32)
+
+    def squares(kernel, name, out_shape, *values):
+        return pl.pallas_call(
+            kernel,
+            out_shape=out_shape,
+            in_specs=[vmem] * len(values),
+            out_specs=[vmem] * len(out_shape),
+            compiler_params=pltpu.CompilerParams(vmem_limit_bytes=6 * 2**20),
+            name=name,
+        )(*values)
+
+    def to_owner(k, value):
+        return lax.ppermute(value, "dp", [(i, i ^ k) for i in range(8)])
+
     in_a, keep_a, send_a = extra["in_a"], extra["keep_a"], extra["send_a"]
-    in_b, acc_out = rotate("123", ["t0"], [extra["acc_in"], extra["acc_out"]], False)
-    (acc_out,) = rotate("123", ["m1"], [acc_out], False)
-    keep_b, send_b = rotate("123", ["t1"], [acc_out], True)
-
-    squares = pl.pallas_call(
-        functools.partial(finish_kernel, rows),
-        out_shape=[jax.ShapeDtypeStruct((rows // 2, K), jnp.float32)] * 8,
-        in_specs=[vmem] * 8,
-        out_specs=[vmem] * 8,
-        scratch_shapes=[
-            pltpu.VMEM((K, tokens), jnp.bfloat16),
-            pltpu.VMEM((K // 2, tokens), jnp.float32),
-        ],
-        compiler_params=pltpu.CompilerParams(vmem_limit_bytes=8 * 2**20),
-        name="finish",
-    )(
-        in_a, swap_core(in_a), in_b, swap_core(in_b),
-        keep_a, keep_b, swap_core(send_a), swap_core(send_b),
-    )
-    total = squares[0]
-    for k in range(1, 8):
-        total = total + lax.ppermute(squares[k], "dp", [(i, i ^ k) for i in range(8)])
+    in_b, acc = extra["in_b"], extra["acc"]
+    rot_in, *near = squares(
+        functools.partial(rotated_kernel, rows), "rotated",
+        [jax.ShapeDtypeStruct((K, tokens), jnp.bfloat16)] + [block] * 2,
+        in_a, swap_core(in_a), in_b, swap_core(in_b), keep_a, swap_core(send_a),
+    )
+    early = near[0] + to_owner(1, near[1])
+    for units, name, value in landing.pop(9):
+        units[name] = value
+    keep_b, send_b = rotate("23", ["m1", "t1"], [acc], 2 * rows, True)
+    far = squares(squares_kernel, "squares", [block] * 4, rot_in, keep_b, swap_core(send_b))
+    for k in range(4):
+        early = early + to_owner(4 + k, far[k])
+
+    for units, name, value in landing.pop(10):
+        units[name] = value
+    keep_c, send_c = rotate("1", ["m1", "t1"], [acc], 0, True)
+    early, come_c = lax.optimization_barrier((early, swap_core(send_c)))
+    late = squares(squares_kernel, "squares", [block] * 2, rot_in, keep_c, come_c)
+    total = early + to_owner(2, late[0]) + to_owner(3, late[1])
     return total * (1.0 / 8)
 
 

time: 123 us -> 120 us (0.976)
  waiting for transfers between devices: 35.8 us -> 23 us
  starting transfers between devices: 75.3 us -> 82.6 us
  Pallas kernels: 8.24 us -> 10.8 us
    ppermute x30, waiting for transfers between devices: 31.2 us -> 18.9 us  [send(): return lax.ppermute(value, ('group', 'dp'), pairs)]
    ppermute x30, starting transfers between devices: 63.3 us -> 69 us  [send(): return lax.ppermute(value, ('group', 'dp'), pairs)]
    pallas_call x6 -> x8, Pallas kernels: 7.6 us -> 9.84 us  [the longest x5 9.21 us: rotate(): pl.pallas_call(functools.partial(rotate_kernel, (terms, acc_from, last),...]
    ppermute x7, starting transfers between devices: 11.2 us -> 12.8 us  [to_owner(): return lax.ppermute(value, 'dp', [(i, i ^ k) for i in range(8)])]
  transfers between devices with their start and end apart: 41 -> 42, of which waited for: 22 -> 20; matrix products, arithmetic and copies ran while one was open for 0% -> 0% of each run, Pallas kernels for 6% -> 9%
where the time goes in v5:
time: 120 us
  starting transfers between devices  82.6 us (69%)
  waiting for transfers between devices  23 us (19%)
  Pallas kernels  10.8 us (9%)
  local copies, waits for them, and re-layouts  2.34 us (2%)
    ppermute x30, starting transfers between devices, send(): return lax.ppermute(value, ('group', 'dp'), pairs)  69 us
    ppermute x30, waiting for transfers between devices, send(): return lax.ppermute(value, ('group', 'dp'), pairs)  18.9 us
    ppermute x7, starting transfers between devices, to_owner(): return lax.ppermute(value, 'dp', [(i, i ^ k) for i in range(8)])  12.8 us
    pallas_call x5, Pallas kernels, rotate(): pl.pallas_call(functools.partial(rotate_kernel, (terms, acc_from, last),...  9.21 us
    ppermute x7, waiting for transfers between devices, to_owner(): return lax.ppermute(value, 'dp', [(i, i ^ k) for i in range(8)])  3.23 us
  transfers between devices with their start and end apart: 42, of which 20 were waited for; matrix products, arithmetic and copies ran while one was open for 0% of the time, Pallas kernels for 9%

profile of v5, /device:TPU:0, one launch (start us, length us, event | category | flops | bytes accessed | tf_op | source)
XLA Modules:
  0.0 119.7 jit_solution(1267757648173300403)
XLA Ops:
  0.0 1.3 %copy-done.2 = bf16[14336,48]{0,1:T(8,128)(2,1)S(1)} copy-done((bf16[14336,48]{0,1:T(8,128)(2,1)S(1)}, bf16[14336,48]{0,1:T(8,128)(2,1)}, u32[]{:S(2)}) %copy-start.2) | copy-done | bytes 1376280
  1.3 1.0 copy-done.3
  2.7 3.1 %collective-permute-start = (bf16[48,4608]{1,0:T(8,128)(2,1)S(1)}, bf16[48,4608]{1,0:T(8,128)(2,1)S(1)}, u32[]{:S(2)}, u32[]{:S(2)}) collective-permute-start(bf16[48,4608]{1,0:T(8,128)(2,1)S(1)} %get-tuple-element.372), channel_id=1, source_target_pairs={{0,4},{2,6},{4,0},{6,2},{8,12},{10,14},{12,8},{14,10},{16,20},{18,... | collective-permute-start | bytes 1327112 | tf_op jit(solution)/shard_map/ppermute | solution.py:242
  5.8 1.5 %collective-permute-start.1 = (bf16[48,4608]{1,0:T(8,128)(2,1)S(1)}, bf16[48,4608]{1,0:T(8,128)(2,1)S(1)}, u32[]{:S(2)}, u32[]{:S(2)}) collective-permute-start(bf16[48,4608]{1,0:T(8,128)(2,1)S(1)} %get-tuple-element.373), channel_id=1, source_target_pairs={{0,2},{2,0},{12,14},{14,12},{16,18},{18,16},{28,30},{30,28},{4,6},... | collective-permute-start | bytes 1327112 | tf_op jit(solution)/shard_map/ppermute | solution.py:242
  8.1 4.4 %collective-permute-start.3 = (bf16[48,4608]{1,0:T(8,128)(2,1)S(1)}, bf16[48,4608]{1,0:T(8,128)(2,1)S(1)}, u32[]{:S(2)}, u32[]{:S(2)}) collective-permute-start(bf16[48,4608]{1,0:T(8,128)(2,1)S(1)} %pick.17), channel_id=1, source_target_pairs={{0,4},{2,6},{4,0},{6,2},{8,12},{10,14},{12,8},{14,10},{16,20},{18,... | collective-permute-start | bytes 1327112 | tf_op jit(solution)/shard_map/ppermute | solution.py:242
  13.0 3.8 %collective-permute-done.outer_ref.refs_0_ = bf16[48,4608]{1,0:T(8,128)(2,1)S(1)} collective-permute-done((bf16[48,4608]{1,0:T(8,128)(2,1)S(1)}, bf16[48,4608]{1,0:T(8,128)(2,1)S(1)}, u32[]{:S(2)}, u32[]{:S(2)}) %collective-permute-start) | collective-permute-done | bytes 442400 | tf_op jit(solution)/shard_map/ppermute | solution.py:242
  17.5 1.4 %collective-permute-done.1.refs_3_.outer_ref = bf16[48,4608]{1,0:T(8,128)(2,1)S(1)} collective-permute-done((bf16[48,4608]{1,0:T(8,128)(2,1)S(1)}, bf16[48,4608]{1,0:T(8,128)(2,1)S(1)}, u32[]{:S(2)}, u32[]{:S(2)}) %collective-permute-start.1) | collective-permute-done | bytes 442400 | tf_op jit(solution)/shard_map/ppermute | solution.py:242
  18.9 3.9 %collective-permute-start.6 = (bf16[48,4608]{1,0:T(8,128)(2,1)S(1)}, bf16[48,4608]{1,0:T(8,128)(2,1)S(1)}, u32[]{:S(2)}, u32[]{:S(2)}) collective-permute-start(bf16[48,4608]{1,0:T(8,128)(2,1)S(1)} %pick.18), channel_id=1, source_target_pairs={{0,4},{2,6},{4,0},{6,2},{8,12},{10,14},{12,8},{14,10},{16,20},{18,... | collective-permute-start | bytes 1327112 | tf_op jit(solution)/shard_map/ppermute | solution.py:242
  22.8 1.2 collective-permute-start.7
  24.0 2.3 %collective-permute-done.3.inner_ref.refs_1_.refs_0_ = bf16[48,4608]{1,0:T(8,128)(2,1)S(1)} collective-permute-done((bf16[48,4608]{1,0:T(8,128)(2,1)S(1)}, bf16[48,4608]{1,0:T(8,128)(2,1)S(1)}, u32[]{:S(2)}, u32[]{:S(2)}) %collective-permute-start.3) | collective-permute-done | bytes 442400 | tf_op jit(solution)/shard_map/ppermute | solution.py:242
  26.3 2.0 %collective-permute-start.8 = (bf16[48,4608]{1,0:T(8,128)(2,1)S(1)}, bf16[48,4608]{1,0:T(8,128)(2,1)S(1)}, u32[]{:S(2)}, u32[]{:S(2)}) collective-permute-start(bf16[48,4608]{1,0:T(8,128)(2,1)S(1)} %collective-permute-done.1.refs_3_.outer_ref), channel_id=1, source_target_pairs={{0,16},{2,18},{12,28},{14,30},{16,0},{18,2},{28,12},{30,14},{4,20}... | collective-permute-start | bytes 1327112 | tf_op jit(solution)/shard_map/ppermute | solution.py:242
  28.4 5.5 %collective-permute-start.9 = (bf16[48,4608]{1,0:T(8,128)(2,1)S(1)}, bf16[48,4608]{1,0:T(8,128)(2,1)S(1)}, u32[]{:S(2)}, u32[]{:S(2)}) collective-permute-start(bf16[48,4608]{1,0:T(8,128)(2,1)S(1)} %pick.19), channel_id=1, source_target_pairs={{0,4},{2,6},{4,0},{6,2},{8,12},{10,14},{12,8},{14,10},{16,20},{18,... | collective-permute-start | bytes 1327112 | tf_op jit(solution)/shard_map/ppermute | solution.py:242
  33.9 1.5 %collective-permute-start.10 = (bf16[48,4608]{1,0:T(8,128)(2,1)S(1)}, bf16[48,4608]{1,0:T(8,128)(2,1)S(1)}, u32[]{:S(2)}, u32[]{:S(2)}) collective-permute-start(bf16[48,4608]{1,0:T(8,128)(2,1)S(1)} %get-tuple-element.381.outer_ref), channel_id=1, source_target_pairs={{0,2},{2,0},{12,14},{14,12},{16,18},{18,16},{28,30},{30,28},{4,6},... | collective-permute-start | bytes 1327112 | tf_op jit(solution)/shard_map/ppermute | solution.py:242
  35.7 2.0 %collective-permute-start.11 = (bf16[48,4608]{1,0:T(8,128)(2,1)S(1)}, bf16[48,4608]{1,0:T(8,128)(2,1)S(1)}, u32[]{:S(2)}, u32[]{:S(2)}) collective-permute-start(bf16[48,4608]{1,0:T(8,128)(2,1)S(1)} %pick.20), channel_id=1, source_target_pairs={{0,16},{2,18},{12,28},{14,30},{16,0},{18,2},{28,12},{30,14},{4,8},... | collective-permute-start | bytes 1327112 | tf_op jit(solution)/shard_map/ppermute | solution.py:242
  37.9 5.5 %collective-permute-start.12 = (bf16[48,4608]{1,0:T(8,128)(2,1)S(1)}, bf16[48,4608]{1,0:T(8,128)(2,1)S(1)}, u32[]{:S(2)}, u32[]{:S(2)}) collective-permute-start(bf16[48,4608]{1,0:T(8,128)(2,1)S(1)} %pick.21), channel_id=1, source_target_pairs={{0,4},{2,6},{4,0},{6,2},{8,12},{10,14},{12,8},{14,10},{16,20},{18,... | collective-permute-start | bytes 1327112 | tf_op jit(solution)/shard_map/ppermute | solution.py:242
  43.6 1.6 %collective-permute-done.9.outer_ref.refs_2_.refs_0_ = bf16[48,4608]{1,0:T(8,128)(2,1)S(1)} collective-permute-done((bf16[48,4608]{1,0:T(8,128)(2,1)S(1)}, bf16[48,4608]{1,0:T(8,128)(2,1)S(1)}, u32[]{:S(2)}, u32[]{:S(2)}) %collective-permute-start.9) | collective-permute-done | bytes 442400 | tf_op jit(solution)/shard_map/ppermute | solution.py:242
  45.2 2.0 %collective-permute-start.14 = (bf16[48,4608]{1,0:T(8,128)(2,1)S(1)}, bf16[48,4608]{1,0:T(8,128)(2,1)S(1)}, u32[]{:S(2)}, u32[]{:S(2)}) collective-permute-start(bf16[48,4608]{1,0:T(8,128)(2,1)S(1)} %collective-permute-done.6.outer_ref.refs_3_.refs_1_), channel_id=1, source_target_pairs={{0,16},{2,18},{12,28},{14,30},{16,0},{18,2},{28,12},{30,14},{4,8},... | collective-permute-start | bytes 1327112 | tf_op jit(solution)/shard_map/ppermute | solution.py:242
  47.4 5.5 %collective-permute-start.15 = (bf16[48,4608]{1,0:T(8,128)(2,1)S(1)}, bf16[48,4608]{1,0:T(8,128)(2,1)S(1)}, u32[]{:S(2)}, u32[]{:S(2)}) collective-permute-start(bf16[48,4608]{1,0:T(8,128)(2,1)S(1)} %pick.23), channel_id=1, source_target_pairs={{0,4},{2,6},{4,0},{6,2},{8,12},{10,14},{12,8},{14,10},{16,20},{18,... | collective-permute-start | bytes 1327112 | tf_op jit(solution)/shard_map/ppermute | solution.py:242
  53.0 1.7 %collective-permute-done.12.inner_ref.refs_6_ = bf16[48,4608]{1,0:T(8,128)(2,1)S(1)} collective-permute-done((bf16[48,4608]{1,0:T(8,128)(2,1)S(1)}, bf16[48,4608]{1,0:T(8,128)(2,1)S(1)}, u32[]{:S(2)}, u32[]{:S(2)}) %collective-permute-start.12) | collective-permute-done | bytes 442400 | tf_op jit(solution)/shard_map/ppermute | solution.py:242
  54.7 2.0 %collective-permute-start.17 = (bf16[48,4608]{1,0:T(8,128)(2,1)S(1)}, bf16[48,4608]{1,0:T(8,128)(2,1)S(1)}, u32[]{:S(2)}, u32[]{:S(2)}) collective-permute-start(bf16[48,4608]{1,0:T(8,128)(2,1)S(1)} %pick.24), channel_id=1, source_target_pairs={{0,16},{2,18},{12,28},{14,30},{16,0},{18,2},{28,12},{30,14},{4,20}... | collective-permute-start | bytes 1327112 | tf_op jit(solution)/shard_map/ppermute | solution.py:242
  56.7 3.1 %rotate.5 = (f32[96,256]{1,0:T(8,128)S(1)}, f32[48,256]{1,0:T(8,128)S(1)}, f32[48,256]{1,0:T(8,128)S(1)}) custom-call(bf16[256,4096]{1,0:T(8,128)(2,1)S(1)} %bitcast.9, bf16[256,14336]{1,0:T(8,128)(2,1)S(1)} %bitcast.4, bf16[48,4608]{1,0:T(8,128)(2,1)S(1)} %get-tuple-element.372, bf16[48,4608]{1,0:T(8,128)(2,1)S(1)} %collective-permute-done.4.outer_ref.refs_1_, ...), custom_call_target="tpu_custom_call" | custom-call | flops 905969664 | bytes 3538944 | tf_op jit(solution)/shard_map/rotate/pallas_call | solution.py:213
  59.8 2.5 %collective-permute-start.18 = (bf16[48,4608]{1,0:T(8,128)(2,1)S(1)}, bf16[48,4608]{1,0:T(8,128)(2,1)S(1)}, u32[]{:S(2)}, u32[]{:S(2)}) collective-permute-start(bf16[48,4608]{1,0:T(8,128)(2,1)S(1)} %pick.25), channel_id=1, source_target_pairs={{0,4},{2,6},{4,0},{6,2},{8,12},{10,14},{12,8},{14,10},{16,20},{18,... | collective-permute-start | bytes 1327112 | tf_op jit(solution)/shard_map/ppermute | solution.py:242
  62.4 0.7 collective-permute-start.19
  63.1 1.0 collective-permute-done.15.outer_ref.inner_ref.refs_3_
  64.2 2.0 %collective-permute-start.20 = (bf16[48,4608]{1,0:T(8,128)(2,1)S(1)}, bf16[48,4608]{1,0:T(8,128)(2,1)S(1)}, u32[]{:S(2)}, u32[]{:S(2)}) collective-permute-start(bf16[48,4608]{1,0:T(8,128)(2,1)S(1)} %pick.27), channel_id=1, source_target_pairs={{0,16},{2,18},{12,28},{14,30},{16,0},{18,2},{28,12},{30,14},{4,20}... | collective-permute-start | bytes 1327112 | tf_op jit(solution)/shard_map/ppermute | solution.py:242
  66.3 5.5 %collective-permute-start.21 = (bf16[48,4608]{1,0:T(8,128)(2,1)S(1)}, bf16[48,4608]{1,0:T(8,128)(2,1)S(1)}, u32[]{:S(2)}, u32[]{:S(2)}) collective-permute-start(bf16[48,4608]{1,0:T(8,128)(2,1)S(1)} %collective-permute-done.16.outer_ref.refs_5_.refs_2_), channel_id=1, source_target_pairs={{0,4},{2,6},{4,0},{6,2},{8,12},{10,14},{12,8},{14,10},{16,20},{18,... | collective-permute-start | bytes 1327112 | tf_op jit(solution)/shard_map/ppermute | solution.py:242
  72.0 1.6 %collective-permute-done.18.outer_ref.refs_4_.refs_5_ = bf16[48,4608]{1,0:T(8,128)(2,1)S(1)} collective-permute-done((bf16[48,4608]{1,0:T(8,128)(2,1)S(1)}, bf16[48,4608]{1,0:T(8,128)(2,1)S(1)}, u32[]{:S(2)}, u32[]{:S(2)}) %collective-permute-start.18) | collective-permute-done | bytes 442400 | tf_op jit(solution)/shard_map/ppermute | solution.py:242
  73.7 2.0 %collective-permute-start.23 = (bf16[48,4608]{1,0:T(8,128)(2,1)S(1)}, bf16[48,4608]{1,0:T(8,128)(2,1)S(1)}, u32[]{:S(2)}, u32[]{:S(2)}) collective-permute-start(bf16[48,4608]{1,0:T(8,128)(2,1)S(1)} %pick.29), channel_id=1, source_target_pairs={{0,16},{2,18},{12,28},{14,30},{16,0},{18,2},{28,12},{30,14},{4,8},... | collective-permute-start | bytes 1327112 | tf_op jit(solution)/shard_map/ppermute | solution.py:242
  75.8 1.6 %collective-permute-start.28 = (bf16[48,4608]{1,0:T(8,128)(2,1)S(1)}, bf16[48,4608]{1,0:T(8,128)(2,1)S(1)}, u32[]{:S(2)}, u32[]{:S(2)}) collective-permute-start(bf16[48,4608]{1,0:T(8,128)(2,1)S(1)} %pick.30), channel_id=1, source_target_pairs={{0,2},{2,0},{12,14},{14,12},{16,18},{18,16},{28,30},{30,28},{4,8},... | collective-permute-start | bytes 1327112 | tf_op jit(solution)/shard_map/ppermute | solution.py:242
  77.4 1.6 %collective-permute-start.29 = (bf16[48,4608]{1,0:T(8,128)(2,1)S(1)}, bf16[48,4608]{1,0:T(8,128)(2,1)S(1)}, u32[]{:S(2)}, u32[]{:S(2)}) collective-permute-start(bf16[48,4608]{1,0:T(8,128)(2,1)S(1)} %pick.31), channel_id=1, source_target_pairs={{0,16},{2,18},{12,28},{14,30},{16,0},{18,2},{28,12},{30,14},{4,20}... | collective-permute-start | bytes 1327112 | tf_op jit(solution)/shard_map/ppermute | solution.py:242
  79.0 3.3 %collective-permute-done.21.refs_8_.refs_7_ = bf16[48,4608]{1,0:T(8,128)(2,1)S(1)} collective-permute-done((bf16[48,4608]{1,0:T(8,128)(2,1)S(1)}, bf16[48,4608]{1,0:T(8,128)(2,1)S(1)}, u32[]{:S(2)}, u32[]{:S(2)}) %collective-permute-start.21) | collective-permute-done | bytes 442400 | tf_op jit(solution)/shard_map/ppermute | solution.py:242
  82.3 2.3 %collective-permute-start.30 = (bf16[48,4608]{1,0:T(8,128)(2,1)S(1)}, bf16[48,4608]{1,0:T(8,128)(2,1)S(1)}, u32[]{:S(2)}, u32[]{:S(2)}) collective-permute-start(bf16[48,4608]{1,0:T(8,128)(2,1)S(1)} %pick.32), channel_id=1, source_target_pairs={{0,4},{2,6},{4,0},{6,2},{8,12},{10,14},{12,8},{14,10},{16,20},{18,... | collective-permute-start | bytes 1327112 | tf_op jit(solution)/shard_map/ppermute | solution.py:242
  84.6 1.1 rotate.6
  85.7 1.1 collective-permute-done.23.refs_6_.refs_10_
  86.8 1.1 rotate.7
  87.9 3.9 %collective-permute-start.36 = (bf16[48,4608]{1,0:T(8,128)(2,1)S(1)}, bf16[48,4608]{1,0:T(8,128)(2,1)S(1)}, u32[]{:S(2)}, u32[]{:S(2)}) collective-permute-start(bf16[48,4608]{1,0:T(8,128)(2,1)S(1)} %collective-permute-done.3.inner_ref.refs_1_.refs_0_), channel_id=1, source_target_pairs={{0,2},{2,0},{12,14},{14,12},{16,18},{18,16},{28,30},{30,28},{1,3},... | collective-permute-start | bytes 1327112 | tf_op jit(solution)/shard_map/ppermute | solution.py:242
  91.9 1.2 collective-permute-start.37
  93.3 3.4 %collective-permute-start.38 = (bf16[48,4608]{1,0:T(8,128)(2,1)S(1)}, bf16[48,4608]{1,0:T(8,128)(2,1)S(1)}, u32[]{:S(2)}, u32[]{:S(2)}) collective-permute-start(bf16[48,4608]{1,0:T(8,128)(2,1)S(1)} %collective-permute-done.3.inner_ref.refs_1_.refs_0_), channel_id=1, source_target_pairs={{0,16},{2,18},{12,28},{14,30},{16,0},{18,2},{28,12},{30,14},{1,17}... | collective-permute-start | bytes 1327112 | tf_op jit(solution)/shard_map/ppermute | solution.py:242
  97.2 2.1 %rotate.8 = (f32[96,256]{1,0:T(8,128)S(1)}, f32[96,256]{1,0:T(8,128)S(1)}) custom-call(bf16[256,4096]{1,0:T(8,128)(2,1)S(1)} %bitcast.12, bf16[256,14336]{1,0:T(8,128)(2,1)S(1)} %bitcast.7, bf16[48,4608]{1,0:T(8,128)(2,1)S(1)} %collective-permute-done.9.outer_ref.refs_2_.refs_0_, ...), custom_call_target="tpu_custom_call" | custom-call | flops 905969664 | bytes 5750784 | tf_op jit(solution)/shard_map/rotate/pallas_call | solution.py:213
  99.8 1.6 %collective-permute-start.27 = (f32[24,384]{1,0:T(8,128)S(1)}, f32[24,384]{1,0:T(8,128)S(1)}, u32[]{:S(2)}, u32[]{:S(2)}) collective-permute-start(f32[24,384]{1,0:T(8,128)S(1)} %get-tuple-element.546), channel_id=1, source_target_pairs={{0,2},{2,0},{4,6},{6,4},{8,10},{10,8},{12,14},{14,12},{1,3},{3,1},... | collective-permute-start | bytes 110600 | tf_op jit(solution)/shard_map/ppermute | solution.py:342
  101.6 2.9 %collective-permute-start.35 = (f32[24,384]{1,0:T(8,128)S(1)}, f32[24,384]{1,0:T(8,128)S(1)}, u32[]{:S(2)}, u32[]{:S(2)}) collective-permute-start(f32[24,384]{1,0:T(8,128)S(1)} %get-tuple-element.568), channel_id=1, source_target_pairs={{0,14},{2,12},{4,10},{6,8},{8,6},{10,4},{12,2},{14,0},{1,15},{3,13... | collective-permute-start | bytes 110600 | tf_op jit(solution)/shard_map/ppermute | solution.py:342
  104.5 2.4 %collective-permute-start.34 = (f32[24,384]{1,0:T(8,128)S(1)}, f32[24,384]{1,0:T(8,128)S(1)}, u32[]{:S(2)}, u32[]{:S(2)}) collective-permute-start(f32[24,384]{1,0:T(8,128)S(1)} %get-tuple-element.567), channel_id=1, source_target_pairs={{0,12},{2,14},{4,8},{6,10},{8,4},{10,6},{12,0},{14,2},{1,13},{3,15... | collective-permute-start | bytes 110600 | tf_op jit(solution)/shard_map/ppermute | solution.py:342
  107.0 3.8 %collective-permute-start.32 = (f32[24,384]{1,0:T(8,128)S(1)}, f32[24,384]{1,0:T(8,128)S(1)}, u32[]{:S(2)}, u32[]{:S(2)}) collective-permute-start(f32[24,384]{1,0:T(8,128)S(1)} %get-tuple-element.565), channel_id=1, source_target_pairs={{0,8},{2,10},{4,12},{6,14},{8,0},{10,2},{12,4},{14,6},{1,9},{3,11}... | collective-permute-start | bytes 110600 | tf_op jit(solution)/shard_map/ppermute | solution.py:342
  110.7 1.9 %rotate.9 = (f32[48,256]{1,0:T(8,128)S(1)}, f32[48,256]{1,0:T(8,128)S(1)}) custom-call(bf16[256,4096]{1,0:T(8,128)(2,1)S(1)} %bitcast.13, bf16[256,14336]{1,0:T(8,128)(2,1)S(1)} %bitcast.8, bf16[48,4608]{1,0:T(8,128)(2,1)S(1)} %collective-permute-done.3.inner_ref.refs_1_.refs_0_, bf16[48,4608]{1,0:T(8,128)(2,1)S(1)} %collective-permute-done.6.outer_ref.refs_3_.refs_1_, ...), custom_call_target="tpu_custom_call" | custom-call | flops 452984832 | bytes 3096576 | tf_op jit(solution)/shard_map/rotate/pallas_call | solution.py:213
  113.1 0.8 collective-permute-done.39.come
  114.1 0.8 collective-permute-start.41
  114.9 1.2 %collective-permute-start.40 = (f32[24,384]{1,0:T(8,128)S(1)}, f32[24,384]{1,0:T(8,128)S(1)}, u32[]{:S(2)}, u32[]{:S(2)}) collective-permute-start(f32[24,384]{1,0:T(8,128)S(1)} %get-tuple-element.579), channel_id=1, source_target_pairs={{0,4},{2,6},{4,0},{6,2},{8,12},{10,14},{12,8},{14,10},{1,5},{3,7},... | collective-permute-start | bytes 110600 | tf_op jit(solution)/shard_map/ppermute | solution.py:342
  116.2 2.9 %collective-permute-done.41 = f32[24,384]{1,0:T(8,128)S(1)} collective-permute-done((f32[24,384]{1,0:T(8,128)S(1)}, f32[24,384]{1,0:T(8,128)S(1)}, u32[]{:S(2)}, u32[]{:S(2)}) %collective-permute-start.41) | collective-permute-done | bytes 36896 | tf_op jit(solution)/shard_map/ppermute | solution.py:342
  (72 shorter events, 7.0 us)
Async XLA Ops:
  0.0 1.3 %copy-start.2 = (bf16[14336,48]{0,1:T(8,128)(2,1)S(1)}, bf16[14336,48]{0,1:T(8,128)(2,1)}, u32[]{:S(2)}) copy-start(bf16[14336,48]{0,1:T(8,128)(2,1)} %param.7) | copy-start | bytes 4128772
  1.3 1.0 copy-start.3
  2.7 14.1 %collective-permute-start = (bf16[48,4608]{1,0:T(8,128)(2,1)S(1)}, bf16[48,4608]{1,0:T(8,128)(2,1)S(1)}, u32[]{:S(2)}, u32[]{:S(2)}) collective-permute-start(bf16[48,4608]{1,0:T(8,128)(2,1)S(1)} %get-tuple-element.372), channel_id=1, source_target_pairs={{0,4},{2,6},{4,0},{6,2},{8,12},{10,14},{12,8},{14,10},{16,20},{18,... | collective-permute-start | bytes 1327112 | tf_op jit(solution)/shard_map/ppermute | solution.py:242
  5.8 13.1 %collective-permute-start.1 = (bf16[48,4608]{1,0:T(8,128)(2,1)S(1)}, bf16[48,4608]{1,0:T(8,128)(2,1)S(1)}, u32[]{:S(2)}, u32[]{:S(2)}) collective-permute-start(bf16[48,4608]{1,0:T(8,128)(2,1)S(1)} %get-tuple-element.373), channel_id=1, source_target_pairs={{0,2},{2,0},{12,14},{14,12},{16,18},{18,16},{28,30},{30,28},{4,6},... | collective-permute-start | bytes 1327112 | tf_op jit(solution)/shard_map/ppermute | solution.py:242
  7.3 11.6 %collective-permute-start.2 = (bf16[48,4608]{1,0:T(8,128)(2,1)S(1)}, bf16[48,4608]{1,0:T(8,128)(2,1)S(1)}, u32[]{:S(2)}, u32[]{:S(2)}) collective-permute-start(bf16[48,4608]{1,0:T(8,128)(2,1)S(1)} %get-tuple-element.372), channel_id=1, source_target_pairs={{4,8},{6,10},{8,4},{10,6},{20,24},{22,26},{24,20},{26,22},{5,9},{7... | collective-permute-start | bytes 1327112 | tf_op jit(solution)/shard_map/ppermute | solution.py:242
  8.0 48.7 %copy-start.1 = (bf16[1,256,4096]{2,1,0:T(8,128)(2,1)S(1)}, bf16[1,256,4096]{2,1,0:T(8,128)(2,1)}, u32[]{:S(2)}) copy-start(bf16[1,256,4096]{2,1,0:T(8,128)(2,1)} %param.4) | copy-start | bytes 6291460
  8.1 18.2 %collective-permute-start.3 = (bf16[48,4608]{1,0:T(8,128)(2,1)S(1)}, bf16[48,4608]{1,0:T(8,128)(2,1)S(1)}, u32[]{:S(2)}, u32[]{:S(2)}) collective-permute-start(bf16[48,4608]{1,0:T(8,128)(2,1)S(1)} %pick.17), channel_id=1, source_target_pairs={{0,4},{2,6},{4,0},{6,2},{8,12},{10,14},{12,8},{14,10},{16,20},{18,... | collective-permute-start | bytes 1327112 | tf_op jit(solution)/shard_map/ppermute | solution.py:242
  12.5 15.9 %collective-permute-start.4 = (bf16[48,4608]{1,0:T(8,128)(2,1)S(1)}, bf16[48,4608]{1,0:T(8,128)(2,1)S(1)}, u32[]{:S(2)}, u32[]{:S(2)}) collective-permute-start(bf16[48,4608]{1,0:T(8,128)(2,1)S(1)} %get-tuple-element.372), channel_id=1, source_target_pairs={{0,2},{2,0},{12,14},{14,12},{16,18},{18,16},{28,30},{30,28},{4,6},... | collective-permute-start | bytes 1327112 | tf_op jit(solution)/shard_map/ppermute | solution.py:242
  16.8 11.6 %collective-permute-start.5 = (bf16[48,4608]{1,0:T(8,128)(2,1)S(1)}, bf16[48,4608]{1,0:T(8,128)(2,1)S(1)}, u32[]{:S(2)}, u32[]{:S(2)}) collective-permute-start(bf16[48,4608]{1,0:T(8,128)(2,1)S(1)} %get-tuple-element.373), channel_id=1, source_target_pairs={{4,8},{6,10},{8,4},{10,6},{20,24},{22,26},{24,20},{26,22},{5,9},{7... | collective-permute-start | bytes 1327112 | tf_op jit(solution)/shard_map/ppermute | solution.py:242
  18.9 16.8 %collective-permute-start.6 = (bf16[48,4608]{1,0:T(8,128)(2,1)S(1)}, bf16[48,4608]{1,0:T(8,128)(2,1)S(1)}, u32[]{:S(2)}, u32[]{:S(2)}) collective-permute-start(bf16[48,4608]{1,0:T(8,128)(2,1)S(1)} %pick.18), channel_id=1, source_target_pairs={{0,4},{2,6},{4,0},{6,2},{8,12},{10,14},{12,8},{14,10},{16,20},{18,... | collective-permute-start | bytes 1327112 | tf_op jit(solution)/shard_map/ppermute | solution.py:242
  22.8 15.0 %collective-permute-start.7 = (bf16[48,4608]{1,0:T(8,128)(2,1)S(1)}, bf16[48,4608]{1,0:T(8,128)(2,1)S(1)}, u32[]{:S(2)}, u32[]{:S(2)}) collective-permute-start(bf16[48,4608]{1,0:T(8,128)(2,1)S(1)} %collective-permute-done.outer_ref.refs_0_), channel_id=1, source_target_pairs={{0,2},{2,0},{12,14},{14,12},{16,18},{18,16},{28,30},{30,28},{4,8},... | collective-permute-start | bytes 1327112 | tf_op jit(solution)/shard_map/ppermute | solution.py:242
  26.3 11.6 %collective-permute-start.8 = (bf16[48,4608]{1,0:T(8,128)(2,1)S(1)}, bf16[48,4608]{1,0:T(8,128)(2,1)S(1)}, u32[]{:S(2)}, u32[]{:S(2)}) collective-permute-start(bf16[48,4608]{1,0:T(8,128)(2,1)S(1)} %collective-permute-done.1.refs_3_.outer_ref), channel_id=1, source_target_pairs={{0,16},{2,18},{12,28},{14,30},{16,0},{18,2},{28,12},{30,14},{4,20}... | collective-permute-start | bytes 1327112 | tf_op jit(solution)/shard_map/ppermute | solution.py:242
  28.4 28.3 %copy-start = (bf16[1,256,14336]{2,1,0:T(8,128)(2,1)S(1)}, bf16[1,256,14336]{2,1,0:T(8,128)(2,1)}, u32[]{:S(2)}) copy-start(bf16[1,256,14336]{2,1,0:T(8,128)(2,1)} %param.5) | copy-start | bytes 22020100
  28.4 16.8 %collective-permute-start.9 = (bf16[48,4608]{1,0:T(8,128)(2,1)S(1)}, bf16[48,4608]{1,0:T(8,128)(2,1)S(1)}, u32[]{:S(2)}, u32[]{:S(2)}) collective-permute-start(bf16[48,4608]{1,0:T(8,128)(2,1)S(1)} %pick.19), channel_id=1, source_target_pairs={{0,4},{2,6},{4,0},{6,2},{8,12},{10,14},{12,8},{14,10},{16,20},{18,... | collective-permute-start | bytes 1327112 | tf_op jit(solution)/shard_map/ppermute | solution.py:242
  33.9 13.4 %collective-permute-start.10 = (bf16[48,4608]{1,0:T(8,128)(2,1)S(1)}, bf16[48,4608]{1,0:T(8,128)(2,1)S(1)}, u32[]{:S(2)}, u32[]{:S(2)}) collective-permute-start(bf16[48,4608]{1,0:T(8,128)(2,1)S(1)} %get-tuple-element.381.outer_ref), channel_id=1, source_target_pairs={{0,2},{2,0},{12,14},{14,12},{16,18},{18,16},{28,30},{30,28},{4,6},... | collective-permute-start | bytes 1327112 | tf_op jit(solution)/shard_map/ppermute | solution.py:242
  35.7 11.6 %collective-permute-start.11 = (bf16[48,4608]{1,0:T(8,128)(2,1)S(1)}, bf16[48,4608]{1,0:T(8,128)(2,1)S(1)}, u32[]{:S(2)}, u32[]{:S(2)}) collective-permute-start(bf16[48,4608]{1,0:T(8,128)(2,1)S(1)} %pick.20), channel_id=1, source_target_pairs={{0,16},{2,18},{12,28},{14,30},{16,0},{18,2},{28,12},{30,14},{4,8},... | collective-permute-start | bytes 1327112 | tf_op jit(solution)/shard_map/ppermute | solution.py:242
  37.9 16.8 %collective-permute-start.12 = (bf16[48,4608]{1,0:T(8,128)(2,1)S(1)}, bf16[48,4608]{1,0:T(8,128)(2,1)S(1)}, u32[]{:S(2)}, u32[]{:S(2)}) collective-permute-start(bf16[48,4608]{1,0:T(8,128)(2,1)S(1)} %pick.21), channel_id=1, source_target_pairs={{0,4},{2,6},{4,0},{6,2},{8,12},{10,14},{12,8},{14,10},{16,20},{18,... | collective-permute-start | bytes 1327112 | tf_op jit(solution)/shard_map/ppermute | solution.py:242
  43.5 16.3 %collective-permute-start.13 = (bf16[48,4608]{1,0:T(8,128)(2,1)S(1)}, bf16[48,4608]{1,0:T(8,128)(2,1)S(1)}, u32[]{:S(2)}, u32[]{:S(2)}) collective-permute-start(bf16[48,4608]{1,0:T(8,128)(2,1)S(1)} %pick.22), channel_id=1, source_target_pairs={{0,2},{2,0},{12,14},{14,12},{16,18},{18,16},{28,30},{30,28},{4,6},... | collective-permute-start | bytes 1327112 | tf_op jit(solution)/shard_map/ppermute | solution.py:242
  45.2 14.6 %collective-permute-start.14 = (bf16[48,4608]{1,0:T(8,128)(2,1)S(1)}, bf16[48,4608]{1,0:T(8,128)(2,1)S(1)}, u32[]{:S(2)}, u32[]{:S(2)}) collective-permute-start(bf16[48,4608]{1,0:T(8,128)(2,1)S(1)} %collective-permute-done.6.outer_ref.refs_3_.refs_1_), channel_id=1, source_target_pairs={{0,16},{2,18},{12,28},{14,30},{16,0},{18,2},{28,12},{30,14},{4,8},... | collective-permute-start | bytes 1327112 | tf_op jit(solution)/shard_map/ppermute | solution.py:242
  47.4 16.8 %collective-permute-start.15 = (bf16[48,4608]{1,0:T(8,128)(2,1)S(1)}, bf16[48,4608]{1,0:T(8,128)(2,1)S(1)}, u32[]{:S(2)}, u32[]{:S(2)}) collective-permute-start(bf16[48,4608]{1,0:T(8,128)(2,1)S(1)} %pick.23), channel_id=1, source_target_pairs={{0,4},{2,6},{4,0},{6,2},{8,12},{10,14},{12,8},{14,10},{16,20},{18,... | collective-permute-start | bytes 1327112 | tf_op jit(solution)/shard_map/ppermute | solution.py:242
  52.9 13.4 %collective-permute-start.16 = (bf16[48,4608]{1,0:T(8,128)(2,1)S(1)}, bf16[48,4608]{1,0:T(8,128)(2,1)S(1)}, u32[]{:S(2)}, u32[]{:S(2)}) collective-permute-start(bf16[48,4608]{1,0:T(8,128)(2,1)S(1)} %collective-permute-done.9.outer_ref.refs_2_.refs_0_), channel_id=1, source_target_pairs={{0,2},{2,0},{12,14},{14,12},{16,18},{18,16},{28,30},{30,28},{4,8},... | collective-permute-start | bytes 1327112 | tf_op jit(solution)/shard_map/ppermute | solution.py:242
  54.7 11.6 %collective-permute-start.17 = (bf16[48,4608]{1,0:T(8,128)(2,1)S(1)}, bf16[48,4608]{1,0:T(8,128)(2,1)S(1)}, u32[]{:S(2)}, u32[]{:S(2)}) collective-permute-start(bf16[48,4608]{1,0:T(8,128)(2,1)S(1)} %pick.24), channel_id=1, source_target_pairs={{0,16},{2,18},{12,28},{14,30},{16,0},{18,2},{28,12},{30,14},{4,20}... | collective-permute-start | bytes 1327112 | tf_op jit(solution)/shard_map/ppermute | solution.py:242
  59.8 13.8 %collective-permute-start.18 = (bf16[48,4608]{1,0:T(8,128)(2,1)S(1)}, bf16[48,4608]{1,0:T(8,128)(2,1)S(1)}, u32[]{:S(2)}, u32[]{:S(2)}) collective-permute-start(bf16[48,4608]{1,0:T(8,128)(2,1)S(1)} %pick.25), channel_id=1, source_target_pairs={{0,4},{2,6},{4,0},{6,2},{8,12},{10,14},{12,8},{14,10},{16,20},{18,... | collective-permute-start | bytes 1327112 | tf_op jit(solution)/shard_map/ppermute | solution.py:242
  62.4 13.3 %collective-permute-start.19 = (bf16[48,4608]{1,0:T(8,128)(2,1)S(1)}, bf16[48,4608]{1,0:T(8,128)(2,1)S(1)}, u32[]{:S(2)}, u32[]{:S(2)}) collective-permute-start(bf16[48,4608]{1,0:T(8,128)(2,1)S(1)} %pick.26), channel_id=1, source_target_pairs={{0,2},{2,0},{12,14},{14,12},{16,18},{18,16},{28,30},{30,28},{4,8},... | collective-permute-start | bytes 1327112 | tf_op jit(solution)/shard_map/ppermute | solution.py:242
  64.2 11.6 %collective-permute-start.20 = (bf16[48,4608]{1,0:T(8,128)(2,1)S(1)}, bf16[48,4608]{1,0:T(8,128)(2,1)S(1)}, u32[]{:S(2)}, u32[]{:S(2)}) collective-permute-start(bf16[48,4608]{1,0:T(8,128)(2,1)S(1)} %pick.27), channel_id=1, source_target_pairs={{0,16},{2,18},{12,28},{14,30},{16,0},{18,2},{28,12},{30,14},{4,20}... | collective-permute-start | bytes 1327112 | tf_op jit(solution)/shard_map/ppermute | solution.py:242
  66.3 16.0 %collective-permute-start.21 = (bf16[48,4608]{1,0:T(8,128)(2,1)S(1)}, bf16[48,4608]{1,0:T(8,128)(2,1)S(1)}, u32[]{:S(2)}, u32[]{:S(2)}) collective-permute-start(bf16[48,4608]{1,0:T(8,128)(2,1)S(1)} %collective-permute-done.16.outer_ref.refs_5_.refs_2_), channel_id=1, source_target_pairs={{0,4},{2,6},{4,0},{6,2},{8,12},{10,14},{12,8},{14,10},{16,20},{18,... | collective-permute-start | bytes 1327112 | tf_op jit(solution)/shard_map/ppermute | solution.py:242
  71.8 13.9 %collective-permute-start.22 = (bf16[48,4608]{1,0:T(8,128)(2,1)S(1)}, bf16[48,4608]{1,0:T(8,128)(2,1)S(1)}, u32[]{:S(2)}, u32[]{:S(2)}) collective-permute-start(bf16[48,4608]{1,0:T(8,128)(2,1)S(1)} %pick.28), channel_id=1, source_target_pairs={{0,2},{2,0},{12,14},{14,12},{16,18},{18,16},{28,30},{30,28},{4,6},... | collective-permute-start | bytes 1327112 | tf_op jit(solution)/shard_map/ppermute | solution.py:242
  73.7 13.1 %collective-permute-start.23 = (bf16[48,4608]{1,0:T(8,128)(2,1)S(1)}, bf16[48,4608]{1,0:T(8,128)(2,1)S(1)}, u32[]{:S(2)}, u32[]{:S(2)}) collective-permute-start(bf16[48,4608]{1,0:T(8,128)(2,1)S(1)} %pick.29), channel_id=1, source_target_pairs={{0,16},{2,18},{12,28},{14,30},{16,0},{18,2},{28,12},{30,14},{4,8},... | collective-permute-start | bytes 1327112 | tf_op jit(solution)/shard_map/ppermute | solution.py:242
  75.8 17.5 %collective-permute-start.28 = (bf16[48,4608]{1,0:T(8,128)(2,1)S(1)}, bf16[48,4608]{1,0:T(8,128)(2,1)S(1)}, u32[]{:S(2)}, u32[]{:S(2)}) collective-permute-start(bf16[48,4608]{1,0:T(8,128)(2,1)S(1)} %pick.30), channel_id=1, source_target_pairs={{0,2},{2,0},{12,14},{14,12},{16,18},{18,16},{28,30},{30,28},{4,8},... | collective-permute-start | bytes 1327112 | tf_op jit(solution)/shard_map/ppermute | solution.py:242
  77.4 19.2 %collective-permute-start.29 = (bf16[48,4608]{1,0:T(8,128)(2,1)S(1)}, bf16[48,4608]{1,0:T(8,128)(2,1)S(1)}, u32[]{:S(2)}, u32[]{:S(2)}) collective-permute-start(bf16[48,4608]{1,0:T(8,128)(2,1)S(1)} %pick.31), channel_id=1, source_target_pairs={{0,16},{2,18},{12,28},{14,30},{16,0},{18,2},{28,12},{30,14},{4,20}... | collective-permute-start | bytes 1327112 | tf_op jit(solution)/shard_map/ppermute | solution.py:242
  82.3 14.4 %collective-permute-start.30 = (bf16[48,4608]{1,0:T(8,128)(2,1)S(1)}, bf16[48,4608]{1,0:T(8,128)(2,1)S(1)}, u32[]{:S(2)}, u32[]{:S(2)}) collective-permute-start(bf16[48,4608]{1,0:T(8,128)(2,1)S(1)} %pick.32), channel_id=1, source_target_pairs={{0,4},{2,6},{4,0},{6,2},{8,12},{10,14},{12,8},{14,10},{16,20},{18,... | collective-permute-start | bytes 1327112 | tf_op jit(solution)/shard_map/ppermute | solution.py:242
  87.8 4.1 %collective-permute-start.26 = (f32[48,256]{1,0:T(8,128)S(1)}, f32[48,256]{1,0:T(8,128)S(1)}, u32[]{:S(2)}, u32[]{:S(2)}) collective-permute-start(f32[48,256]{1,0:T(8,128)S(1)} %get-tuple-element.544), channel_id=1, source_target_pairs={{0,1},{1,0},{2,3},{3,2},{4,5},{5,4},{6,7},{7,6},{8,9},{9,8},{10,11... | collective-permute-start | bytes 147464 | tf_op jit(solution)/shard_map/ppermute | solution.py:180
  87.9 16.5 %collective-permute-start.36 = (bf16[48,4608]{1,0:T(8,128)(2,1)S(1)}, bf16[48,4608]{1,0:T(8,128)(2,1)S(1)}, u32[]{:S(2)}, u32[]{:S(2)}) collective-permute-start(bf16[48,4608]{1,0:T(8,128)(2,1)S(1)} %collective-permute-done.3.inner_ref.refs_1_.refs_0_), channel_id=1, source_target_pairs={{0,2},{2,0},{12,14},{14,12},{16,18},{18,16},{28,30},{30,28},{1,3},... | collective-permute-start | bytes 1327112 | tf_op jit(solution)/shard_map/ppermute | solution.py:242
  91.9 14.9 %collective-permute-start.37 = (bf16[48,4608]{1,0:T(8,128)(2,1)S(1)}, bf16[48,4608]{1,0:T(8,128)(2,1)S(1)}, u32[]{:S(2)}, u32[]{:S(2)}) collective-permute-start(bf16[48,4608]{1,0:T(8,128)(2,1)S(1)} %pick.33), channel_id=1, source_target_pairs={{0,4},{2,6},{4,0},{6,2},{8,12},{10,14},{12,8},{14,10},{16,20},{18,... | collective-permute-start | bytes 1327112 | tf_op jit(solution)/shard_map/ppermute | solution.py:242
  93.3 13.7 %collective-permute-start.38 = (bf16[48,4608]{1,0:T(8,128)(2,1)S(1)}, bf16[48,4608]{1,0:T(8,128)(2,1)S(1)}, u32[]{:S(2)}, u32[]{:S(2)}) collective-permute-start(bf16[48,4608]{1,0:T(8,128)(2,1)S(1)} %collective-permute-done.3.inner_ref.refs_1_.refs_0_), channel_id=1, source_target_pairs={{0,16},{2,18},{12,28},{14,30},{16,0},{18,2},{28,12},{30,14},{1,17}... | collective-permute-start | bytes 1327112 | tf_op jit(solution)/shard_map/ppermute | solution.py:242
  96.7 2.9 %collective-permute-start.25 = (f32[288,256]{1,0:T(8,128)S(1)}, f32[288,256]{1,0:T(8,128)S(1)}, u32[]{:S(2)}, u32[]{:S(2)}) collective-permute-start(f32[288,256]{1,0:T(8,128)S(1)} %get-tuple-element.542.in_b), channel_id=1, source_target_pairs={{0,1},{1,0},{2,3},{3,2},{4,5},{5,4},{6,7},{7,6},{8,9},{9,8},{10,11... | collective-permute-start | bytes 884744 | tf_op jit(solution)/shard_map/ppermute | solution.py:180
  96.8 2.6 %collective-permute-start.24 = (f32[96,256]{1,0:T(8,128)S(1)}, f32[96,256]{1,0:T(8,128)S(1)}, u32[]{:S(2)}, u32[]{:S(2)}) collective-permute-start(f32[96,256]{1,0:T(8,128)S(1)} %get-tuple-element.541.in_a), channel_id=1, source_target_pairs={{0,1},{1,0},{2,3},{3,2},{4,5},{5,4},{6,7},{7,6},{8,9},{9,8},{10,11... | collective-permute-start | bytes 294920 | tf_op jit(solution)/shard_map/ppermute | solution.py:180
  99.4 2.0 %collective-permute-start.31 = (f32[96,256]{1,0:T(8,128)S(1)}, f32[96,256]{1,0:T(8,128)S(1)}, u32[]{:S(2)}, u32[]{:S(2)}) collective-permute-start(f32[96,256]{1,0:T(8,128)S(1)} %get-tuple-element.564), channel_id=1, source_target_pairs={{0,1},{1,0},{2,3},{3,2},{4,5},{5,4},{6,7},{7,6},{8,9},{9,8},{10,11... | collective-permute-start | bytes 294920 | tf_op jit(solution)/shard_map/ppermute | solution.py:180
  99.8 12.8 %collective-permute-start.27 = (f32[24,384]{1,0:T(8,128)S(1)}, f32[24,384]{1,0:T(8,128)S(1)}, u32[]{:S(2)}, u32[]{:S(2)}) collective-permute-start(f32[24,384]{1,0:T(8,128)S(1)} %get-tuple-element.546), channel_id=1, source_target_pairs={{0,2},{2,0},{4,6},{6,4},{8,10},{10,8},{12,14},{14,12},{1,3},{3,1},... | collective-permute-start | bytes 110600 | tf_op jit(solution)/shard_map/ppermute | solution.py:342
  101.6 11.1 %collective-permute-start.35 = (f32[24,384]{1,0:T(8,128)S(1)}, f32[24,384]{1,0:T(8,128)S(1)}, u32[]{:S(2)}, u32[]{:S(2)}) collective-permute-start(f32[24,384]{1,0:T(8,128)S(1)} %get-tuple-element.568), channel_id=1, source_target_pairs={{0,14},{2,12},{4,10},{6,8},{8,6},{10,4},{12,2},{14,0},{1,15},{3,13... | collective-permute-start | bytes 110600 | tf_op jit(solution)/shard_map/ppermute | solution.py:342
  104.5 8.3 %collective-permute-start.34 = (f32[24,384]{1,0:T(8,128)S(1)}, f32[24,384]{1,0:T(8,128)S(1)}, u32[]{:S(2)}, u32[]{:S(2)}) collective-permute-start(f32[24,384]{1,0:T(8,128)S(1)} %get-tuple-element.567), channel_id=1, source_target_pairs={{0,12},{2,14},{4,8},{6,10},{8,4},{10,6},{12,0},{14,2},{1,13},{3,15... | collective-permute-start | bytes 110600 | tf_op jit(solution)/shard_map/ppermute | solution.py:342
  106.8 5.9 %collective-permute-start.33 = (f32[24,384]{1,0:T(8,128)S(1)}, f32[24,384]{1,0:T(8,128)S(1)}, u32[]{:S(2)}, u32[]{:S(2)}) collective-permute-start(f32[24,384]{1,0:T(8,128)S(1)} %get-tuple-element.566), channel_id=1, source_target_pairs={{0,10},{2,8},{4,14},{6,12},{8,2},{10,0},{12,6},{14,4},{1,11},{3,9}... | collective-permute-start | bytes 110600 | tf_op jit(solution)/shard_map/ppermute | solution.py:342
  107.0 6.1 %collective-permute-start.32 = (f32[24,384]{1,0:T(8,128)S(1)}, f32[24,384]{1,0:T(8,128)S(1)}, u32[]{:S(2)}, u32[]{:S(2)}) collective-permute-start(f32[24,384]{1,0:T(8,128)S(1)} %get-tuple-element.565), channel_id=1, source_target_pairs={{0,8},{2,10},{4,12},{6,14},{8,0},{10,2},{12,4},{14,6},{1,9},{3,11}... | collective-permute-start | bytes 110600 | tf_op jit(solution)/shard_map/ppermute | solution.py:342
  112.6 1.3 %collective-permute-start.39 = (f32[48,256]{1,0:T(8,128)S(1)}, f32[48,256]{1,0:T(8,128)S(1)}, u32[]{:S(2)}, u32[]{:S(2)}) collective-permute-start(f32[48,256]{1,0:T(8,128)S(1)} %get-tuple-element.575), channel_id=1, source_target_pairs={{0,1},{1,0},{2,3},{3,2},{4,5},{5,4},{6,7},{7,6},{8,9},{9,8},{10,11... | collective-permute-start | bytes 147464 | tf_op jit(solution)/shard_map/ppermute | solution.py:180
  114.1 4.9 %collective-permute-start.41 = (f32[24,384]{1,0:T(8,128)S(1)}, f32[24,384]{1,0:T(8,128)S(1)}, u32[]{:S(2)}, u32[]{:S(2)}) collective-permute-start(f32[24,384]{1,0:T(8,128)S(1)} %get-tuple-element.580), channel_id=1, source_target_pairs={{0,6},{2,4},{4,2},{6,0},{8,14},{10,12},{12,10},{14,8},{1,7},{3,5},... | collective-permute-start | bytes 110600 | tf_op jit(solution)/shard_map/ppermute | solution.py:342
  114.9 4.1 %collective-permute-start.40 = (f32[24,384]{1,0:T(8,128)S(1)}, f32[24,384]{1,0:T(8,128)S(1)}, u32[]{:S(2)}, u32[]{:S(2)}) collective-permute-start(f32[24,384]{1,0:T(8,128)S(1)} %get-tuple-element.579), channel_id=1, source_target_pairs={{0,4},{2,6},{4,0},{6,2},{8,12},{10,14},{12,8},{14,10},{1,5},{3,7},... | collective-permute-start | bytes 110600 | tf_op jit(solution)/shard_map/ppermute | solution.py:342

commit v6 on v5

--- a/solution.py
+++ b/solution.py
@@ -12,7 +12,7 @@
 LANES = 128
 AHEAD = 30
 ORDER = "APQ"
-STEP = 1 * 10**8
+STEP = 5 * 10**8
 
 
 def place_cols(left, piece):
@@ -62,24 +62,31 @@
         out_ref[...] = inner_ref[...]
 
 
-def cut_kernel(in_half, first, in_ref, out_ref, m0, m1, t0, t1, sems):
+def first_cut_kernel(in_ref, out_ref, m0, sems):
+    x = lax.axis_index("group")
+    in_half = in_ref.shape[1] // 2
+    first = m0.shape[1] - in_half
+    in_at = pl.multiple_of(x * in_half, LANES)
+    out_at = pl.multiple_of(x * (out_ref.shape[1] // 2), LANES)
+    ins = pltpu.make_async_copy(in_ref.at[:, pl.ds(in_at, in_half)], m0.at[:, :in_half], sems.at[0])
+    outs = pltpu.make_async_copy(out_ref.at[:, pl.ds(out_at, first)], m0.at[:, in_half:], sems.at[1])
+    ins.start()
+    outs.start()
+    ins.wait()
+    outs.wait()
+
+
+def cut_kernel(in_half, first, in_ref, out_ref, m1, t0, t1):
     x = lax.axis_index("group")
     out_half = first + m1.shape[1]
-    copies = []
-    for side, unit0, unit1 in ((x, m0, m1), (1 - x, t0, t1)):
+    for side, unit0, unit1 in ((x, None, m1), (1 - x, t0, t1)):
         in_at = pl.multiple_of(side * in_half, LANES)
         out_at = pl.multiple_of(side * out_half, LANES)
         next_at = pl.multiple_of(side * out_half + first, LANES)
-        copies += [
-            (in_ref.at[:, pl.ds(in_at, in_half)], unit0.at[:, :in_half]),
-            (out_ref.at[:, pl.ds(out_at, first)], unit0.at[:, in_half:]),
-            (out_ref.at[:, pl.ds(next_at, unit1.shape[1])], unit1),
-        ]
-    started = [pltpu.make_async_copy(a, b, sems.at[i]) for i, (a, b) in enumerate(copies)]
-    for copy in started:
-        copy.start()
-    for copy in started:
-        copy.wait()
+        if unit0 is not None:
+            unit0[:, :in_half] = in_ref[:, pl.ds(in_at, in_half)]
+            unit0[:, in_half:] = out_ref[:, pl.ds(out_at, first)]
+        unit1[...] = out_ref[:, pl.ds(next_at, unit1.shape[1])]
 
 
 def rotate_kernel(plan, in_half, first, acts_ref, grads_ref, *refs):
@@ -146,7 +153,7 @@
     square = coeff * coeff
     panel = outs[0].shape[0]
     for block, ref in enumerate(outs):
-        ref[...] = square[block * panel : (block + 1) * panel]
+        ref[...] = square[block * panel : (block + 1) * panel].astype(ref.dtype)
 
 
 def rotated_kernel(rows, in_a, in_a2, in_b, in_b2, keep, come, in_ref, *outs):
@@ -180,12 +187,20 @@
         return lax.ppermute(value, "basis", [(0, 1), (1, 0)])
 
     unit = jax.ShapeDtypeStruct((rows, width), in_t.dtype)
-    m0, m1, t0, t1 = pl.pallas_call(
+    m0 = pl.pallas_call(
+        first_cut_kernel,
+        out_shape=unit,
+        in_specs=[pl.BlockSpec(memory_space=pltpu.HBM)] * 2,
+        out_specs=vmem,
+        scratch_shapes=[pltpu.SemaphoreType.DMA((2,))],
+        compiler_params=pltpu.CompilerParams(vmem_limit_bytes=62 * 2**20),
+        name="first_cut",
+    )(in_t, out_t)
+    m1, t0, t1 = pl.pallas_call(
         functools.partial(cut_kernel, in_half, first),
-        out_shape=[unit] * 4,
-        in_specs=[pl.BlockSpec(memory_space=pltpu.HBM)] * 2,
-        out_specs=[vmem] * 4,
-        scratch_shapes=[pltpu.SemaphoreType.DMA((6,))],
+        out_shape=[unit] * 3,
+        in_specs=[vmem] * 2,
+        out_specs=[vmem] * 3,
         compiler_params=pltpu.CompilerParams(vmem_limit_bytes=8 * 2**20),
         name="cut",
     )(in_t, out_t)
@@ -326,7 +341,7 @@
                 pairs += group_pairs(link_b)
             landing[r] += bring(pick(choices[0], choices[-1]), pairs, *spots)
 
-    block = jax.ShapeDtypeStruct((rows // 2, K), jnp.float32)
+    block = jax.ShapeDtypeStruct((rows // 2, K), jnp.bfloat16)
 
     def squares(kernel, name, out_shape, *values):
         return pl.pallas_call(
@@ -339,7 +354,7 @@
         )(*values)
 
     def to_owner(k, value):
-        return lax.ppermute(value, "dp", [(i, i ^ k) for i in range(8)])
+        return lax.ppermute(value, "dp", [(i, i ^ k) for i in range(8)]).astype(jnp.float32)
 
     in_a, keep_a, send_a = extra["in_a"], extra["keep_a"], extra["send_a"]
     in_b, acc = extra["in_b"], extra["acc"]
@@ -348,7 +363,7 @@
         [jax.ShapeDtypeStruct((K, tokens), jnp.bfloat16)] + [block] * 2,
         in_a, swap_core(in_a), in_b, swap_core(in_b), keep_a, swap_core(send_a),
     )
-    early = near[0] + to_owner(1, near[1])
+    early = near[0].astype(jnp.float32) + to_owner(1, near[1])
     for units, name, value in landing.pop(9):
         units[name] = value
     keep_b, send_b = rotate("23", ["m1", "t1"], [acc], 2 * rows, True)

time: 120 us -> 119 us (level)
  local copies, waits for them, and re-layouts: 2.34 us -> 0.03 us
  Pallas kernels: 10.8 us -> 12.5 us
    unnamed x8 -> x12, local copies, waits for them, and re-layouts: 2.34 us -> 0.03 us
    pallas_call x0 -> x1, Pallas kernels: none -> 1.95 us  [per_device_plane(): pl.pallas_call(first_cut_kernel, out_shape=unit, in_specs=[pl.BlockSpec(m...]
  transfers between devices with their start and end apart: 42 -> 42, of which waited for: 20 -> 12; matrix products, arithmetic and copies ran while one was open for 0% -> 0% of each run, Pallas kernels for 9% -> 9%
where the time goes in v6:
time: 119 us
  starting transfers between devices  83.2 us (70%)
  waiting for transfers between devices  22.1 us (19%)
  Pallas kernels  12.5 us (11%)
    ppermute x30, starting transfers between devices, send(): return lax.ppermute(value, ('group', 'dp'), pairs)  69.6 us
    ppermute x30, waiting for transfers between devices, send(): return lax.ppermute(value, ('group', 'dp'), pairs)  18.2 us
    ppermute x7, starting transfers between devices, to_owner(): lax.ppermute(value, 'dp', [(i, i ^ k) for i in range(8)])  12.7 us
    pallas_call x5, Pallas kernels, rotate(): pl.pallas_call(functools.partial(rotate_kernel, (terms, acc_from, last),...  9.2 us
    ppermute x7, waiting for transfers between devices, to_owner(): lax.ppermute(value, 'dp', [(i, i ^ k) for i in range(8)])  2.7 us
  transfers between devices with their start and end apart: 42, of which 12 were waited for; matrix products, arithmetic and copies ran while one was open for 0% of the time, Pallas kernels for 9%

profile of v6, /device:TPU:0, one launch (start us, length us, event | category | flops | bytes accessed | tf_op | source)
XLA Modules:
  0.0 118.9 jit_solution(1415564164957604848)
XLA Ops:
  0.0 1.9 %first_cut.1.refs_0_ = bf16[48,4608]{1,0:T(8,128)(2,1)} custom-call(bf16[48,4096]{1,0:T(8,128)(2,1)} %bitcast.18, bf16[48,14336]{1,0:T(8,128)(2,1)} %bitcast.16), custom_call_target="tpu_custom_call" | custom-call | tf_op jit(solution)/shard_map/first_cut/pallas_call | solution.py:190
  2.1 3.1 %collective-permute-start = (bf16[48,4608]{1,0:T(8,128)(2,1)}, bf16[48,4608]{1,0:T(8,128)(2,1)S(1)}, u32[]{:S(2)}, u32[]{:S(2)}) collective-permute-start(bf16[48,4608]{1,0:T(8,128)(2,1)} %first_cut.1.refs_0_), channel_id=1, source_target_pairs={{0,4},{2,6},{4,0},{6,2},{8,12},{10,14},{12,8},{14,10},{16,20},{18,... | collective-permute-start | bytes 1327112 | tf_op jit(solution)/shard_map/ppermute | solution.py:257
  5.2 1.5 %collective-permute-start.1 = (bf16[48,4608]{1,0:T(8,128)(2,1)S(1)}, bf16[48,4608]{1,0:T(8,128)(2,1)S(1)}, u32[]{:S(2)}, u32[]{:S(2)}) collective-permute-start(bf16[48,4608]{1,0:T(8,128)(2,1)S(1)} %get-tuple-element.421.inner_ref.outer_ref.refs_2_), channel_id=1, source_target_pairs={{0,2},{2,0},{12,14},{14,12},{16,18},{18,16},{28,30},{30,28},{4,6},... | collective-permute-start | bytes 1327112 | tf_op jit(solution)/shard_map/ppermute | solution.py:257
  6.7 0.7 collective-permute-start.2
  7.5 4.4 %collective-permute-start.3 = (bf16[48,4608]{1,0:T(8,128)(2,1)S(1)}, bf16[48,4608]{1,0:T(8,128)(2,1)S(1)}, u32[]{:S(2)}, u32[]{:S(2)}) collective-permute-start(bf16[48,4608]{1,0:T(8,128)(2,1)S(1)} %pick.17), channel_id=1, source_target_pairs={{0,4},{2,6},{4,0},{6,2},{8,12},{10,14},{12,8},{14,10},{16,20},{18,... | collective-permute-start | bytes 1327112 | tf_op jit(solution)/shard_map/ppermute | solution.py:257
  12.4 4.0 %collective-permute-done.outer_ref.refs_0_ = bf16[48,4608]{1,0:T(8,128)(2,1)S(1)} collective-permute-done((bf16[48,4608]{1,0:T(8,128)(2,1)}, bf16[48,4608]{1,0:T(8,128)(2,1)S(1)}, u32[]{:S(2)}, u32[]{:S(2)}) %collective-permute-start) | collective-permute-done | bytes 442400 | tf_op jit(solution)/shard_map/ppermute | solution.py:257
  16.4 0.7 collective-permute-start.5
  17.1 1.2 %collective-permute-done.1.refs_3_.outer_ref = bf16[48,4608]{1,0:T(8,128)(2,1)S(1)} collective-permute-done((bf16[48,4608]{1,0:T(8,128)(2,1)S(1)}, bf16[48,4608]{1,0:T(8,128)(2,1)S(1)}, u32[]{:S(2)}, u32[]{:S(2)}) %collective-permute-start.1) | collective-permute-done | bytes 442400 | tf_op jit(solution)/shard_map/ppermute | solution.py:257
  18.3 4.1 %collective-permute-start.6 = (bf16[48,4608]{1,0:T(8,128)(2,1)S(1)}, bf16[48,4608]{1,0:T(8,128)(2,1)S(1)}, u32[]{:S(2)}, u32[]{:S(2)}) collective-permute-start(bf16[48,4608]{1,0:T(8,128)(2,1)S(1)} %pick.18), channel_id=1, source_target_pairs={{0,4},{2,6},{4,0},{6,2},{8,12},{10,14},{12,8},{14,10},{16,20},{18,... | collective-permute-start | bytes 1327112 | tf_op jit(solution)/shard_map/ppermute | solution.py:257
  22.4 1.2 collective-permute-start.7
  23.6 2.3 %collective-permute-done.3.inner_ref.refs_1_.refs_0_ = bf16[48,4608]{1,0:T(8,128)(2,1)S(1)} collective-permute-done((bf16[48,4608]{1,0:T(8,128)(2,1)S(1)}, bf16[48,4608]{1,0:T(8,128)(2,1)S(1)}, u32[]{:S(2)}, u32[]{:S(2)}) %collective-permute-start.3) | collective-permute-done | bytes 442400 | tf_op jit(solution)/shard_map/ppermute | solution.py:257
  25.9 2.0 %collective-permute-start.8 = (bf16[48,4608]{1,0:T(8,128)(2,1)S(1)}, bf16[48,4608]{1,0:T(8,128)(2,1)S(1)}, u32[]{:S(2)}, u32[]{:S(2)}) collective-permute-start(bf16[48,4608]{1,0:T(8,128)(2,1)S(1)} %collective-permute-done.1.refs_3_.outer_ref), channel_id=1, source_target_pairs={{0,16},{2,18},{12,28},{14,30},{16,0},{18,2},{28,12},{30,14},{4,20}... | collective-permute-start | bytes 1327112 | tf_op jit(solution)/shard_map/ppermute | solution.py:257
  27.9 5.7 %collective-permute-start.9 = (bf16[48,4608]{1,0:T(8,128)(2,1)S(1)}, bf16[48,4608]{1,0:T(8,128)(2,1)S(1)}, u32[]{:S(2)}, u32[]{:S(2)}) collective-permute-start(bf16[48,4608]{1,0:T(8,128)(2,1)S(1)} %pick.19), channel_id=1, source_target_pairs={{0,4},{2,6},{4,0},{6,2},{8,12},{10,14},{12,8},{14,10},{16,20},{18,... | collective-permute-start | bytes 1327112 | tf_op jit(solution)/shard_map/ppermute | solution.py:257
  33.6 1.5 %collective-permute-start.10 = (bf16[48,4608]{1,0:T(8,128)(2,1)S(1)}, bf16[48,4608]{1,0:T(8,128)(2,1)S(1)}, u32[]{:S(2)}, u32[]{:S(2)}) collective-permute-start(bf16[48,4608]{1,0:T(8,128)(2,1)S(1)} %get-tuple-element.422.outer_ref.refs_4_), channel_id=1, source_target_pairs={{0,2},{2,0},{12,14},{14,12},{16,18},{18,16},{28,30},{30,28},{4,6},... | collective-permute-start | bytes 1327112 | tf_op jit(solution)/shard_map/ppermute | solution.py:257
  35.4 2.0 %collective-permute-start.11 = (bf16[48,4608]{1,0:T(8,128)(2,1)S(1)}, bf16[48,4608]{1,0:T(8,128)(2,1)S(1)}, u32[]{:S(2)}, u32[]{:S(2)}) collective-permute-start(bf16[48,4608]{1,0:T(8,128)(2,1)S(1)} %pick.20), channel_id=1, source_target_pairs={{0,16},{2,18},{12,28},{14,30},{16,0},{18,2},{28,12},{30,14},{4,8},... | collective-permute-start | bytes 1327112 | tf_op jit(solution)/shard_map/ppermute | solution.py:257
  37.4 5.7 %collective-permute-start.12 = (bf16[48,4608]{1,0:T(8,128)(2,1)S(1)}, bf16[48,4608]{1,0:T(8,128)(2,1)S(1)}, u32[]{:S(2)}, u32[]{:S(2)}) collective-permute-start(bf16[48,4608]{1,0:T(8,128)(2,1)S(1)} %pick.21), channel_id=1, source_target_pairs={{0,4},{2,6},{4,0},{6,2},{8,12},{10,14},{12,8},{14,10},{16,20},{18,... | collective-permute-start | bytes 1327112 | tf_op jit(solution)/shard_map/ppermute | solution.py:257
  43.3 1.6 %collective-permute-done.9.outer_ref.refs_2_.refs_0_ = bf16[48,4608]{1,0:T(8,128)(2,1)S(1)} collective-permute-done((bf16[48,4608]{1,0:T(8,128)(2,1)S(1)}, bf16[48,4608]{1,0:T(8,128)(2,1)S(1)}, u32[]{:S(2)}, u32[]{:S(2)}) %collective-permute-start.9) | collective-permute-done | bytes 442400 | tf_op jit(solution)/shard_map/ppermute | solution.py:257
  44.8 2.0 %collective-permute-start.14 = (bf16[48,4608]{1,0:T(8,128)(2,1)S(1)}, bf16[48,4608]{1,0:T(8,128)(2,1)S(1)}, u32[]{:S(2)}, u32[]{:S(2)}) collective-permute-start(bf16[48,4608]{1,0:T(8,128)(2,1)S(1)} %collective-permute-done.6.outer_ref.refs_3_.refs_1_), channel_id=1, source_target_pairs={{0,16},{2,18},{12,28},{14,30},{16,0},{18,2},{28,12},{30,14},{4,8},... | collective-permute-start | bytes 1327112 | tf_op jit(solution)/shard_map/ppermute | solution.py:257
  46.9 5.6 %collective-permute-start.15 = (bf16[48,4608]{1,0:T(8,128)(2,1)S(1)}, bf16[48,4608]{1,0:T(8,128)(2,1)S(1)}, u32[]{:S(2)}, u32[]{:S(2)}) collective-permute-start(bf16[48,4608]{1,0:T(8,128)(2,1)S(1)} %pick.23), channel_id=1, source_target_pairs={{0,4},{2,6},{4,0},{6,2},{8,12},{10,14},{12,8},{14,10},{16,20},{18,... | collective-permute-start | bytes 1327112 | tf_op jit(solution)/shard_map/ppermute | solution.py:257
  52.7 1.7 %collective-permute-done.12.inner_ref.refs_6_ = bf16[48,4608]{1,0:T(8,128)(2,1)S(1)} collective-permute-done((bf16[48,4608]{1,0:T(8,128)(2,1)S(1)}, bf16[48,4608]{1,0:T(8,128)(2,1)S(1)}, u32[]{:S(2)}, u32[]{:S(2)}) %collective-permute-start.12) | collective-permute-done | bytes 442400 | tf_op jit(solution)/shard_map/ppermute | solution.py:257
  54.3 2.0 %collective-permute-start.17 = (bf16[48,4608]{1,0:T(8,128)(2,1)S(1)}, bf16[48,4608]{1,0:T(8,128)(2,1)S(1)}, u32[]{:S(2)}, u32[]{:S(2)}) collective-permute-start(bf16[48,4608]{1,0:T(8,128)(2,1)S(1)} %pick.24), channel_id=1, source_target_pairs={{0,16},{2,18},{12,28},{14,30},{16,0},{18,2},{28,12},{30,14},{4,20}... | collective-permute-start | bytes 1327112 | tf_op jit(solution)/shard_map/ppermute | solution.py:257
  56.3 3.1 %rotate.5 = (f32[96,256]{1,0:T(8,128)S(1)}, f32[48,256]{1,0:T(8,128)S(1)}, f32[48,256]{1,0:T(8,128)S(1)}) custom-call(bf16[256,4096]{1,0:T(8,128)(2,1)S(1)} %bitcast.11, bf16[256,14336]{1,0:T(8,128)(2,1)S(1)} %bitcast.6, bf16[48,4608]{1,0:T(8,128)(2,1)S(1)} %copy-done.2, bf16[48,4608]{1,0:T(8,128)(2,1)S(1)} %collective-permute-done.4.outer_ref.refs_1_, ...), custom_call_target="tpu_custom_call" | custom-call | flops 905969664 | bytes 3538944 | tf_op jit(solution)/shard_map/rotate/pallas_call | solution.py:228
  59.5 2.5 %collective-permute-start.18 = (bf16[48,4608]{1,0:T(8,128)(2,1)S(1)}, bf16[48,4608]{1,0:T(8,128)(2,1)S(1)}, u32[]{:S(2)}, u32[]{:S(2)}) collective-permute-start(bf16[48,4608]{1,0:T(8,128)(2,1)S(1)} %pick.25), channel_id=1, source_target_pairs={{0,4},{2,6},{4,0},{6,2},{8,12},{10,14},{12,8},{14,10},{16,20},{18,... | collective-permute-start | bytes 1327112 | tf_op jit(solution)/shard_map/ppermute | solution.py:257
  62.0 0.7 collective-permute-start.19
  62.8 1.0 collective-permute-done.15.outer_ref.inner_ref.refs_3_
  63.8 2.0 %collective-permute-start.20 = (bf16[48,4608]{1,0:T(8,128)(2,1)S(1)}, bf16[48,4608]{1,0:T(8,128)(2,1)S(1)}, u32[]{:S(2)}, u32[]{:S(2)}) collective-permute-start(bf16[48,4608]{1,0:T(8,128)(2,1)S(1)} %pick.27), channel_id=1, source_target_pairs={{0,16},{2,18},{12,28},{14,30},{16,0},{18,2},{28,12},{30,14},{4,20}... | collective-permute-start | bytes 1327112 | tf_op jit(solution)/shard_map/ppermute | solution.py:257
  65.8 5.6 %collective-permute-start.21 = (bf16[48,4608]{1,0:T(8,128)(2,1)S(1)}, bf16[48,4608]{1,0:T(8,128)(2,1)S(1)}, u32[]{:S(2)}, u32[]{:S(2)}) collective-permute-start(bf16[48,4608]{1,0:T(8,128)(2,1)S(1)} %collective-permute-done.16.outer_ref.refs_5_.refs_2_), channel_id=1, source_target_pairs={{0,4},{2,6},{4,0},{6,2},{8,12},{10,14},{12,8},{14,10},{16,20},{18,... | collective-permute-start | bytes 1327112 | tf_op jit(solution)/shard_map/ppermute | solution.py:257
  71.6 1.6 %collective-permute-done.18.outer_ref.refs_4_.refs_5_ = bf16[48,4608]{1,0:T(8,128)(2,1)S(1)} collective-permute-done((bf16[48,4608]{1,0:T(8,128)(2,1)S(1)}, bf16[48,4608]{1,0:T(8,128)(2,1)S(1)}, u32[]{:S(2)}, u32[]{:S(2)}) %collective-permute-start.18) | collective-permute-done | bytes 442400 | tf_op jit(solution)/shard_map/ppermute | solution.py:257
  73.3 2.0 %collective-permute-start.23 = (bf16[48,4608]{1,0:T(8,128)(2,1)S(1)}, bf16[48,4608]{1,0:T(8,128)(2,1)S(1)}, u32[]{:S(2)}, u32[]{:S(2)}) collective-permute-start(bf16[48,4608]{1,0:T(8,128)(2,1)S(1)} %pick.29), channel_id=1, source_target_pairs={{0,16},{2,18},{12,28},{14,30},{16,0},{18,2},{28,12},{30,14},{4,8},... | collective-permute-start | bytes 1327112 | tf_op jit(solution)/shard_map/ppermute | solution.py:257
  75.3 1.6 %collective-permute-start.28 = (bf16[48,4608]{1,0:T(8,128)(2,1)S(1)}, bf16[48,4608]{1,0:T(8,128)(2,1)S(1)}, u32[]{:S(2)}, u32[]{:S(2)}) collective-permute-start(bf16[48,4608]{1,0:T(8,128)(2,1)S(1)} %pick.30), channel_id=1, source_target_pairs={{0,2},{2,0},{12,14},{14,12},{16,18},{18,16},{28,30},{30,28},{4,8},... | collective-permute-start | bytes 1327112 | tf_op jit(solution)/shard_map/ppermute | solution.py:257
  76.9 1.5 %collective-permute-start.29 = (bf16[48,4608]{1,0:T(8,128)(2,1)S(1)}, bf16[48,4608]{1,0:T(8,128)(2,1)S(1)}, u32[]{:S(2)}, u32[]{:S(2)}) collective-permute-start(bf16[48,4608]{1,0:T(8,128)(2,1)S(1)} %pick.31), channel_id=1, source_target_pairs={{0,16},{2,18},{12,28},{14,30},{16,0},{18,2},{28,12},{30,14},{4,20}... | collective-permute-start | bytes 1327112 | tf_op jit(solution)/shard_map/ppermute | solution.py:257
  78.4 3.5 %collective-permute-done.21.refs_8_.refs_7_ = bf16[48,4608]{1,0:T(8,128)(2,1)S(1)} collective-permute-done((bf16[48,4608]{1,0:T(8,128)(2,1)S(1)}, bf16[48,4608]{1,0:T(8,128)(2,1)S(1)}, u32[]{:S(2)}, u32[]{:S(2)}) %collective-permute-start.21) | collective-permute-done | bytes 442400 | tf_op jit(solution)/shard_map/ppermute | solution.py:257
  81.9 2.3 %collective-permute-start.30 = (bf16[48,4608]{1,0:T(8,128)(2,1)S(1)}, bf16[48,4608]{1,0:T(8,128)(2,1)S(1)}, u32[]{:S(2)}, u32[]{:S(2)}) collective-permute-start(bf16[48,4608]{1,0:T(8,128)(2,1)S(1)} %pick.32), channel_id=1, source_target_pairs={{0,4},{2,6},{4,0},{6,2},{8,12},{10,14},{12,8},{14,10},{16,20},{18,... | collective-permute-start | bytes 1327112 | tf_op jit(solution)/shard_map/ppermute | solution.py:257
  84.2 1.1 rotate.6
  85.3 1.1 collective-permute-done.23.refs_6_.refs_10_
  86.4 1.1 rotate.7
  87.5 3.9 %collective-permute-start.36 = (bf16[48,4608]{1,0:T(8,128)(2,1)S(1)}, bf16[48,4608]{1,0:T(8,128)(2,1)S(1)}, u32[]{:S(2)}, u32[]{:S(2)}) collective-permute-start(bf16[48,4608]{1,0:T(8,128)(2,1)S(1)} %collective-permute-done.3.inner_ref.refs_1_.refs_0_), channel_id=1, source_target_pairs={{0,2},{2,0},{12,14},{14,12},{16,18},{18,16},{28,30},{30,28},{1,3},... | collective-permute-start | bytes 1327112 | tf_op jit(solution)/shard_map/ppermute | solution.py:257
  91.5 1.2 collective-permute-start.37
  92.7 3.4 %collective-permute-start.38 = (bf16[48,4608]{1,0:T(8,128)(2,1)S(1)}, bf16[48,4608]{1,0:T(8,128)(2,1)S(1)}, u32[]{:S(2)}, u32[]{:S(2)}) collective-permute-start(bf16[48,4608]{1,0:T(8,128)(2,1)S(1)} %collective-permute-done.3.inner_ref.refs_1_.refs_0_), channel_id=1, source_target_pairs={{0,16},{2,18},{12,28},{14,30},{16,0},{18,2},{28,12},{30,14},{1,17}... | collective-permute-start | bytes 1327112 | tf_op jit(solution)/shard_map/ppermute | solution.py:257
  96.7 2.1 %rotate.8 = (f32[96,256]{1,0:T(8,128)S(1)}, f32[96,256]{1,0:T(8,128)S(1)}) custom-call(bf16[256,4096]{1,0:T(8,128)(2,1)S(1)} %bitcast.14, bf16[256,14336]{1,0:T(8,128)(2,1)S(1)} %bitcast.9, bf16[48,4608]{1,0:T(8,128)(2,1)S(1)} %collective-permute-done.9.outer_ref.refs_2_.refs_0_, ...), custom_call_target="tpu_custom_call" | custom-call | flops 905969664 | bytes 5750784 | tf_op jit(solution)/shard_map/rotate/pallas_call | solution.py:228
  99.2 1.6 %collective-permute-start.27 = (bf16[24,384]{1,0:T(8,128)(2,1)S(1)}, bf16[24,384]{1,0:T(8,128)(2,1)S(1)}, u32[]{:S(2)}, u32[]{:S(2)}) collective-permute-start(bf16[24,384]{1,0:T(8,128)(2,1)S(1)} %get-tuple-element.552), channel_id=1, source_target_pairs={{0,2},{2,0},{4,6},{6,4},{8,10},{10,8},{12,14},{14,12},{1,3},{3,1},... | collective-permute-start | bytes 55304 | tf_op jit(solution)/shard_map/ppermute | solution.py:357
  101.0 2.9 %collective-permute-start.35 = (bf16[24,384]{1,0:T(8,128)(2,1)S(1)}, bf16[24,384]{1,0:T(8,128)(2,1)S(1)}, u32[]{:S(2)}, u32[]{:S(2)}) collective-permute-start(bf16[24,384]{1,0:T(8,128)(2,1)S(1)} %get-tuple-element.574), channel_id=1, source_target_pairs={{0,14},{2,12},{4,10},{6,8},{8,6},{10,4},{12,2},{14,0},{1,15},{3,13... | collective-permute-start | bytes 55304 | tf_op jit(solution)/shard_map/ppermute | solution.py:357
  103.9 2.4 %collective-permute-start.34 = (bf16[24,384]{1,0:T(8,128)(2,1)S(1)}, bf16[24,384]{1,0:T(8,128)(2,1)S(1)}, u32[]{:S(2)}, u32[]{:S(2)}) collective-permute-start(bf16[24,384]{1,0:T(8,128)(2,1)S(1)} %get-tuple-element.573), channel_id=1, source_target_pairs={{0,12},{2,14},{4,8},{6,10},{8,4},{10,6},{12,0},{14,2},{1,13},{3,15... | collective-permute-start | bytes 55304 | tf_op jit(solution)/shard_map/ppermute | solution.py:357
  106.6 3.6 %collective-permute-start.32 = (bf16[24,384]{1,0:T(8,128)(2,1)S(1)}, bf16[24,384]{1,0:T(8,128)(2,1)S(1)}, u32[]{:S(2)}, u32[]{:S(2)}) collective-permute-start(bf16[24,384]{1,0:T(8,128)(2,1)S(1)} %get-tuple-element.571), channel_id=1, source_target_pairs={{0,8},{2,10},{4,12},{6,14},{8,0},{10,2},{12,4},{14,6},{1,9},{3,11}... | collective-permute-start | bytes 55304 | tf_op jit(solution)/shard_map/ppermute | solution.py:357
  110.1 1.9 %rotate.9 = (f32[48,256]{1,0:T(8,128)S(1)}, f32[48,256]{1,0:T(8,128)S(1)}) custom-call(bf16[256,4096]{1,0:T(8,128)(2,1)S(1)} %bitcast.15, bf16[256,14336]{1,0:T(8,128)(2,1)S(1)} %bitcast.10, bf16[48,4608]{1,0:T(8,128)(2,1)S(1)} %collective-permute-done.3.inner_ref.refs_1_.refs_0_, bf16[48,4608]{1,0:T(8,128)(2,1)S(1)} %collective-permute-done.6.outer_ref.refs_3_.refs_1_, ...), custom_call_target="tpu_custom_call" | custom-call | flops 452984832 | bytes 3096576 | tf_op jit(solution)/shard_map/rotate/pallas_call | solution.py:228
  112.2 1.1 collective-permute-done.39.come
  114.1 1.4 %collective-permute-start.40 = (bf16[24,384]{1,0:T(8,128)(2,1)S(1)}, bf16[24,384]{1,0:T(8,128)(2,1)S(1)}, u32[]{:S(2)}, u32[]{:S(2)}) collective-permute-start(bf16[24,384]{1,0:T(8,128)(2,1)S(1)} %get-tuple-element.585), channel_id=1, source_target_pairs={{0,4},{2,6},{4,0},{6,2},{8,12},{10,14},{12,8},{14,10},{1,5},{3,7},... | collective-permute-start | bytes 55304 | tf_op jit(solution)/shard_map/ppermute | solution.py:357
  115.6 2.7 %collective-permute-done.41 = bf16[24,384]{1,0:T(8,128)(2,1)S(1)} collective-permute-done((bf16[24,384]{1,0:T(8,128)(2,1)S(1)}, bf16[24,384]{1,0:T(8,128)(2,1)S(1)}, u32[]{:S(2)}, u32[]{:S(2)}) %collective-permute-start.41) | collective-permute-done | bytes 18464 | tf_op jit(solution)/shard_map/ppermute | solution.py:357
  (78 shorter events, 5.0 us)
Async XLA Ops:
  0.0 2.0 %copy-start.3 = (bf16[4096,48]{0,1:T(8,128)(2,1)S(1)}, bf16[4096,48]{0,1:T(8,128)(2,1)}, u32[]{:S(2)}) copy-start(bf16[4096,48]{0,1:T(8,128)(2,1)} %param.6) | copy-start | bytes 1179652
  0.0 2.0 %copy-start.1 = (bf16[14336,48]{0,1:T(8,128)(2,1)S(1)}, bf16[14336,48]{0,1:T(8,128)(2,1)}, u32[]{:S(2)}) copy-start(bf16[14336,48]{0,1:T(8,128)(2,1)} %param.7) | copy-start | bytes 4128772
  2.0 54.3 %slice-start = ((s8[7340032]{0:T(1024)(128)(4,1)}), s8[4194304]{0:T(1024)(128)(4,1)S(1)}, s32[]{:S(2)}) async-start(s8[7340032]{0:T(1024)(128)(4,1)} %bitcast.4), calls=%async_computation | async-start | bytes 8388608
  2.1 14.3 %collective-permute-start = (bf16[48,4608]{1,0:T(8,128)(2,1)}, bf16[48,4608]{1,0:T(8,128)(2,1)S(1)}, u32[]{:S(2)}, u32[]{:S(2)}) collective-permute-start(bf16[48,4608]{1,0:T(8,128)(2,1)} %first_cut.1.refs_0_), channel_id=1, source_target_pairs={{0,4},{2,6},{4,0},{6,2},{8,12},{10,14},{12,8},{14,10},{16,20},{18,... | collective-permute-start | bytes 1327112 | tf_op jit(solution)/shard_map/ppermute | solution.py:257
  5.2 13.1 %collective-permute-start.1 = (bf16[48,4608]{1,0:T(8,128)(2,1)S(1)}, bf16[48,4608]{1,0:T(8,128)(2,1)S(1)}, u32[]{:S(2)}, u32[]{:S(2)}) collective-permute-start(bf16[48,4608]{1,0:T(8,128)(2,1)S(1)} %get-tuple-element.421.inner_ref.outer_ref.refs_2_), channel_id=1, source_target_pairs={{0,2},{2,0},{12,14},{14,12},{16,18},{18,16},{28,30},{30,28},{4,6},... | collective-permute-start | bytes 1327112 | tf_op jit(solution)/shard_map/ppermute | solution.py:257
  6.7 11.6 %collective-permute-start.2 = (bf16[48,4608]{1,0:T(8,128)(2,1)}, bf16[48,4608]{1,0:T(8,128)(2,1)S(1)}, u32[]{:S(2)}, u32[]{:S(2)}) collective-permute-start(bf16[48,4608]{1,0:T(8,128)(2,1)} %first_cut.1.refs_0_), channel_id=1, source_target_pairs={{4,8},{6,10},{8,4},{10,6},{20,24},{22,26},{24,20},{26,22},{5,9},{7... | collective-permute-start | bytes 1327112 | tf_op jit(solution)/shard_map/ppermute | solution.py:257
  7.5 18.4 %collective-permute-start.3 = (bf16[48,4608]{1,0:T(8,128)(2,1)S(1)}, bf16[48,4608]{1,0:T(8,128)(2,1)S(1)}, u32[]{:S(2)}, u32[]{:S(2)}) collective-permute-start(bf16[48,4608]{1,0:T(8,128)(2,1)S(1)} %pick.17), channel_id=1, source_target_pairs={{0,4},{2,6},{4,0},{6,2},{8,12},{10,14},{12,8},{14,10},{16,20},{18,... | collective-permute-start | bytes 1327112 | tf_op jit(solution)/shard_map/ppermute | solution.py:257
  11.9 16.0 %collective-permute-start.4 = (bf16[48,4608]{1,0:T(8,128)(2,1)}, bf16[48,4608]{1,0:T(8,128)(2,1)S(1)}, u32[]{:S(2)}, u32[]{:S(2)}) collective-permute-start(bf16[48,4608]{1,0:T(8,128)(2,1)} %first_cut.1.refs_0_), channel_id=1, source_target_pairs={{0,2},{2,0},{12,14},{14,12},{16,18},{18,16},{28,30},{30,28},{4,6},... | collective-permute-start | bytes 1327112 | tf_op jit(solution)/shard_map/ppermute | solution.py:257
  16.4 11.5 %collective-permute-start.5 = (bf16[48,4608]{1,0:T(8,128)(2,1)S(1)}, bf16[48,4608]{1,0:T(8,128)(2,1)S(1)}, u32[]{:S(2)}, u32[]{:S(2)}) collective-permute-start(bf16[48,4608]{1,0:T(8,128)(2,1)S(1)} %get-tuple-element.421.inner_ref.outer_ref.refs_2_), channel_id=1, source_target_pairs={{4,8},{6,10},{8,4},{10,6},{20,24},{22,26},{24,20},{26,22},{5,9},{7... | collective-permute-start | bytes 1327112 | tf_op jit(solution)/shard_map/ppermute | solution.py:257
  18.3 17.0 %collective-permute-start.6 = (bf16[48,4608]{1,0:T(8,128)(2,1)S(1)}, bf16[48,4608]{1,0:T(8,128)(2,1)S(1)}, u32[]{:S(2)}, u32[]{:S(2)}) collective-permute-start(bf16[48,4608]{1,0:T(8,128)(2,1)S(1)} %pick.18), channel_id=1, source_target_pairs={{0,4},{2,6},{4,0},{6,2},{8,12},{10,14},{12,8},{14,10},{16,20},{18,... | collective-permute-start | bytes 1327112 | tf_op jit(solution)/shard_map/ppermute | solution.py:257
  22.4 14.9 %collective-permute-start.7 = (bf16[48,4608]{1,0:T(8,128)(2,1)S(1)}, bf16[48,4608]{1,0:T(8,128)(2,1)S(1)}, u32[]{:S(2)}, u32[]{:S(2)}) collective-permute-start(bf16[48,4608]{1,0:T(8,128)(2,1)S(1)} %collective-permute-done.outer_ref.refs_0_), channel_id=1, source_target_pairs={{0,2},{2,0},{12,14},{14,12},{16,18},{18,16},{28,30},{30,28},{4,8},... | collective-permute-start | bytes 1327112 | tf_op jit(solution)/shard_map/ppermute | solution.py:257
  25.9 11.5 %collective-permute-start.8 = (bf16[48,4608]{1,0:T(8,128)(2,1)S(1)}, bf16[48,4608]{1,0:T(8,128)(2,1)S(1)}, u32[]{:S(2)}, u32[]{:S(2)}) collective-permute-start(bf16[48,4608]{1,0:T(8,128)(2,1)S(1)} %collective-permute-done.1.refs_3_.outer_ref), channel_id=1, source_target_pairs={{0,16},{2,18},{12,28},{14,30},{16,0},{18,2},{28,12},{30,14},{4,20}... | collective-permute-start | bytes 1327112 | tf_op jit(solution)/shard_map/ppermute | solution.py:257
  27.9 28.4 %slice-start.1 = ((s8[7340032]{0:T(1024)(128)(4,1)}), s8[3145728]{0:T(1024)(128)(4,1)S(1)}, s32[]{:S(2)}) async-start(s8[7340032]{0:T(1024)(128)(4,1)} %bitcast.4), calls=%async_computation.1 | async-start | bytes 6291456
  27.9 16.9 %collective-permute-start.9 = (bf16[48,4608]{1,0:T(8,128)(2,1)S(1)}, bf16[48,4608]{1,0:T(8,128)(2,1)S(1)}, u32[]{:S(2)}, u32[]{:S(2)}) collective-permute-start(bf16[48,4608]{1,0:T(8,128)(2,1)S(1)} %pick.19), channel_id=1, source_target_pairs={{0,4},{2,6},{4,0},{6,2},{8,12},{10,14},{12,8},{14,10},{16,20},{18,... | collective-permute-start | bytes 1327112 | tf_op jit(solution)/shard_map/ppermute | solution.py:257
  33.6 13.3 %collective-permute-start.10 = (bf16[48,4608]{1,0:T(8,128)(2,1)S(1)}, bf16[48,4608]{1,0:T(8,128)(2,1)S(1)}, u32[]{:S(2)}, u32[]{:S(2)}) collective-permute-start(bf16[48,4608]{1,0:T(8,128)(2,1)S(1)} %get-tuple-element.422.outer_ref.refs_4_), channel_id=1, source_target_pairs={{0,2},{2,0},{12,14},{14,12},{16,18},{18,16},{28,30},{30,28},{4,6},... | collective-permute-start | bytes 1327112 | tf_op jit(solution)/shard_map/ppermute | solution.py:257
  35.4 11.5 %collective-permute-start.11 = (bf16[48,4608]{1,0:T(8,128)(2,1)S(1)}, bf16[48,4608]{1,0:T(8,128)(2,1)S(1)}, u32[]{:S(2)}, u32[]{:S(2)}) collective-permute-start(bf16[48,4608]{1,0:T(8,128)(2,1)S(1)} %pick.20), channel_id=1, source_target_pairs={{0,16},{2,18},{12,28},{14,30},{16,0},{18,2},{28,12},{30,14},{4,8},... | collective-permute-start | bytes 1327112 | tf_op jit(solution)/shard_map/ppermute | solution.py:257
  37.4 16.9 %collective-permute-start.12 = (bf16[48,4608]{1,0:T(8,128)(2,1)S(1)}, bf16[48,4608]{1,0:T(8,128)(2,1)S(1)}, u32[]{:S(2)}, u32[]{:S(2)}) collective-permute-start(bf16[48,4608]{1,0:T(8,128)(2,1)S(1)} %pick.21), channel_id=1, source_target_pairs={{0,4},{2,6},{4,0},{6,2},{8,12},{10,14},{12,8},{14,10},{16,20},{18,... | collective-permute-start | bytes 1327112 | tf_op jit(solution)/shard_map/ppermute | solution.py:257
  43.1 13.2 %copy-start = (bf16[1,256,4096]{2,1,0:T(8,128)(2,1)S(1)}, bf16[1,256,4096]{2,1,0:T(8,128)(2,1)}, u32[]{:S(2)}) copy-start(bf16[1,256,4096]{2,1,0:T(8,128)(2,1)} %param.4) | copy-start | bytes 6291460
  43.1 13.2 %copy-start.2 = (bf16[48,4608]{1,0:T(8,128)(2,1)S(1)}, bf16[48,4608]{1,0:T(8,128)(2,1)}, u32[]{:S(2)}) copy-start(bf16[48,4608]{1,0:T(8,128)(2,1)} %first_cut.1.refs_0_) | copy-start | bytes 1327108
  43.1 16.3 %collective-permute-start.13 = (bf16[48,4608]{1,0:T(8,128)(2,1)S(1)}, bf16[48,4608]{1,0:T(8,128)(2,1)S(1)}, u32[]{:S(2)}, u32[]{:S(2)}) collective-permute-start(bf16[48,4608]{1,0:T(8,128)(2,1)S(1)} %pick.22), channel_id=1, source_target_pairs={{0,2},{2,0},{12,14},{14,12},{16,18},{18,16},{28,30},{30,28},{4,6},... | collective-permute-start | bytes 1327112 | tf_op jit(solution)/shard_map/ppermute | solution.py:257
  44.8 14.6 %collective-permute-start.14 = (bf16[48,4608]{1,0:T(8,128)(2,1)S(1)}, bf16[48,4608]{1,0:T(8,128)(2,1)S(1)}, u32[]{:S(2)}, u32[]{:S(2)}) collective-permute-start(bf16[48,4608]{1,0:T(8,128)(2,1)S(1)} %collective-permute-done.6.outer_ref.refs_3_.refs_1_), channel_id=1, source_target_pairs={{0,16},{2,18},{12,28},{14,30},{16,0},{18,2},{28,12},{30,14},{4,8},... | collective-permute-start | bytes 1327112 | tf_op jit(solution)/shard_map/ppermute | solution.py:257
  46.9 16.9 %collective-permute-start.15 = (bf16[48,4608]{1,0:T(8,128)(2,1)S(1)}, bf16[48,4608]{1,0:T(8,128)(2,1)S(1)}, u32[]{:S(2)}, u32[]{:S(2)}) collective-permute-start(bf16[48,4608]{1,0:T(8,128)(2,1)S(1)} %pick.23), channel_id=1, source_target_pairs={{0,4},{2,6},{4,0},{6,2},{8,12},{10,14},{12,8},{14,10},{16,20},{18,... | collective-permute-start | bytes 1327112 | tf_op jit(solution)/shard_map/ppermute | solution.py:257
  52.5 13.3 %collective-permute-start.16 = (bf16[48,4608]{1,0:T(8,128)(2,1)S(1)}, bf16[48,4608]{1,0:T(8,128)(2,1)S(1)}, u32[]{:S(2)}, u32[]{:S(2)}) collective-permute-start(bf16[48,4608]{1,0:T(8,128)(2,1)S(1)} %collective-permute-done.9.outer_ref.refs_2_.refs_0_), channel_id=1, source_target_pairs={{0,2},{2,0},{12,14},{14,12},{16,18},{18,16},{28,30},{30,28},{4,8},... | collective-permute-start | bytes 1327112 | tf_op jit(solution)/shard_map/ppermute | solution.py:257
  54.3 11.5 %collective-permute-start.17 = (bf16[48,4608]{1,0:T(8,128)(2,1)S(1)}, bf16[48,4608]{1,0:T(8,128)(2,1)S(1)}, u32[]{:S(2)}, u32[]{:S(2)}) collective-permute-start(bf16[48,4608]{1,0:T(8,128)(2,1)S(1)} %pick.24), channel_id=1, source_target_pairs={{0,16},{2,18},{12,28},{14,30},{16,0},{18,2},{28,12},{30,14},{4,20}... | collective-permute-start | bytes 1327112 | tf_op jit(solution)/shard_map/ppermute | solution.py:257
  59.5 13.8 %collective-permute-start.18 = (bf16[48,4608]{1,0:T(8,128)(2,1)S(1)}, bf16[48,4608]{1,0:T(8,128)(2,1)S(1)}, u32[]{:S(2)}, u32[]{:S(2)}) collective-permute-start(bf16[48,4608]{1,0:T(8,128)(2,1)S(1)} %pick.25), channel_id=1, source_target_pairs={{0,4},{2,6},{4,0},{6,2},{8,12},{10,14},{12,8},{14,10},{16,20},{18,... | collective-permute-start | bytes 1327112 | tf_op jit(solution)/shard_map/ppermute | solution.py:257
  62.0 13.2 %collective-permute-start.19 = (bf16[48,4608]{1,0:T(8,128)(2,1)S(1)}, bf16[48,4608]{1,0:T(8,128)(2,1)S(1)}, u32[]{:S(2)}, u32[]{:S(2)}) collective-permute-start(bf16[48,4608]{1,0:T(8,128)(2,1)S(1)} %pick.26), channel_id=1, source_target_pairs={{0,2},{2,0},{12,14},{14,12},{16,18},{18,16},{28,30},{30,28},{4,8},... | collective-permute-start | bytes 1327112 | tf_op jit(solution)/shard_map/ppermute | solution.py:257
  63.8 11.5 %collective-permute-start.20 = (bf16[48,4608]{1,0:T(8,128)(2,1)S(1)}, bf16[48,4608]{1,0:T(8,128)(2,1)S(1)}, u32[]{:S(2)}, u32[]{:S(2)}) collective-permute-start(bf16[48,4608]{1,0:T(8,128)(2,1)S(1)} %pick.27), channel_id=1, source_target_pairs={{0,16},{2,18},{12,28},{14,30},{16,0},{18,2},{28,12},{30,14},{4,20}... | collective-permute-start | bytes 1327112 | tf_op jit(solution)/shard_map/ppermute | solution.py:257
  65.8 16.2 %collective-permute-start.21 = (bf16[48,4608]{1,0:T(8,128)(2,1)S(1)}, bf16[48,4608]{1,0:T(8,128)(2,1)S(1)}, u32[]{:S(2)}, u32[]{:S(2)}) collective-permute-start(bf16[48,4608]{1,0:T(8,128)(2,1)S(1)} %collective-permute-done.16.outer_ref.refs_5_.refs_2_), channel_id=1, source_target_pairs={{0,4},{2,6},{4,0},{6,2},{8,12},{10,14},{12,8},{14,10},{16,20},{18,... | collective-permute-start | bytes 1327112 | tf_op jit(solution)/shard_map/ppermute | solution.py:257
  71.4 13.9 %collective-permute-start.22 = (bf16[48,4608]{1,0:T(8,128)(2,1)S(1)}, bf16[48,4608]{1,0:T(8,128)(2,1)S(1)}, u32[]{:S(2)}, u32[]{:S(2)}) collective-permute-start(bf16[48,4608]{1,0:T(8,128)(2,1)S(1)} %pick.28), channel_id=1, source_target_pairs={{0,2},{2,0},{12,14},{14,12},{16,18},{18,16},{28,30},{30,28},{4,6},... | collective-permute-start | bytes 1327112 | tf_op jit(solution)/shard_map/ppermute | solution.py:257
  73.3 13.1 %collective-permute-start.23 = (bf16[48,4608]{1,0:T(8,128)(2,1)S(1)}, bf16[48,4608]{1,0:T(8,128)(2,1)S(1)}, u32[]{:S(2)}, u32[]{:S(2)}) collective-permute-start(bf16[48,4608]{1,0:T(8,128)(2,1)S(1)} %pick.29), channel_id=1, source_target_pairs={{0,16},{2,18},{12,28},{14,30},{16,0},{18,2},{28,12},{30,14},{4,8},... | collective-permute-start | bytes 1327112 | tf_op jit(solution)/shard_map/ppermute | solution.py:257
  75.3 17.4 %collective-permute-start.28 = (bf16[48,4608]{1,0:T(8,128)(2,1)S(1)}, bf16[48,4608]{1,0:T(8,128)(2,1)S(1)}, u32[]{:S(2)}, u32[]{:S(2)}) collective-permute-start(bf16[48,4608]{1,0:T(8,128)(2,1)S(1)} %pick.30), channel_id=1, source_target_pairs={{0,2},{2,0},{12,14},{14,12},{16,18},{18,16},{28,30},{30,28},{4,8},... | collective-permute-start | bytes 1327112 | tf_op jit(solution)/shard_map/ppermute | solution.py:257
  76.9 19.2 %collective-permute-start.29 = (bf16[48,4608]{1,0:T(8,128)(2,1)S(1)}, bf16[48,4608]{1,0:T(8,128)(2,1)S(1)}, u32[]{:S(2)}, u32[]{:S(2)}) collective-permute-start(bf16[48,4608]{1,0:T(8,128)(2,1)S(1)} %pick.31), channel_id=1, source_target_pairs={{0,16},{2,18},{12,28},{14,30},{16,0},{18,2},{28,12},{30,14},{4,20}... | collective-permute-start | bytes 1327112 | tf_op jit(solution)/shard_map/ppermute | solution.py:257
  81.9 14.2 %collective-permute-start.30 = (bf16[48,4608]{1,0:T(8,128)(2,1)S(1)}, bf16[48,4608]{1,0:T(8,128)(2,1)S(1)}, u32[]{:S(2)}, u32[]{:S(2)}) collective-permute-start(bf16[48,4608]{1,0:T(8,128)(2,1)S(1)} %pick.32), channel_id=1, source_target_pairs={{0,4},{2,6},{4,0},{6,2},{8,12},{10,14},{12,8},{14,10},{16,20},{18,... | collective-permute-start | bytes 1327112 | tf_op jit(solution)/shard_map/ppermute | solution.py:257
  87.4 4.1 %collective-permute-start.26 = (f32[48,256]{1,0:T(8,128)S(1)}, f32[48,256]{1,0:T(8,128)S(1)}, u32[]{:S(2)}, u32[]{:S(2)}) collective-permute-start(f32[48,256]{1,0:T(8,128)S(1)} %get-tuple-element.550), channel_id=1, source_target_pairs={{0,1},{1,0},{2,3},{3,2},{4,5},{5,4},{6,7},{7,6},{8,9},{9,8},{10,11... | collective-permute-start | bytes 147464 | tf_op jit(solution)/shard_map/ppermute | solution.py:187
  87.5 16.3 %collective-permute-start.36 = (bf16[48,4608]{1,0:T(8,128)(2,1)S(1)}, bf16[48,4608]{1,0:T(8,128)(2,1)S(1)}, u32[]{:S(2)}, u32[]{:S(2)}) collective-permute-start(bf16[48,4608]{1,0:T(8,128)(2,1)S(1)} %collective-permute-done.3.inner_ref.refs_1_.refs_0_), channel_id=1, source_target_pairs={{0,2},{2,0},{12,14},{14,12},{16,18},{18,16},{28,30},{30,28},{1,3},... | collective-permute-start | bytes 1327112 | tf_op jit(solution)/shard_map/ppermute | solution.py:257
  91.5 14.8 %collective-permute-start.37 = (bf16[48,4608]{1,0:T(8,128)(2,1)S(1)}, bf16[48,4608]{1,0:T(8,128)(2,1)S(1)}, u32[]{:S(2)}, u32[]{:S(2)}) collective-permute-start(bf16[48,4608]{1,0:T(8,128)(2,1)S(1)} %pick.33), channel_id=1, source_target_pairs={{0,4},{2,6},{4,0},{6,2},{8,12},{10,14},{12,8},{14,10},{16,20},{18,... | collective-permute-start | bytes 1327112 | tf_op jit(solution)/shard_map/ppermute | solution.py:257
  92.7 13.9 %collective-permute-start.38 = (bf16[48,4608]{1,0:T(8,128)(2,1)S(1)}, bf16[48,4608]{1,0:T(8,128)(2,1)S(1)}, u32[]{:S(2)}, u32[]{:S(2)}) collective-permute-start(bf16[48,4608]{1,0:T(8,128)(2,1)S(1)} %collective-permute-done.3.inner_ref.refs_1_.refs_0_), channel_id=1, source_target_pairs={{0,16},{2,18},{12,28},{14,30},{16,0},{18,2},{28,12},{30,14},{1,17}... | collective-permute-start | bytes 1327112 | tf_op jit(solution)/shard_map/ppermute | solution.py:257
  96.1 2.9 %collective-permute-start.25 = (f32[288,256]{1,0:T(8,128)S(1)}, f32[288,256]{1,0:T(8,128)S(1)}, u32[]{:S(2)}, u32[]{:S(2)}) collective-permute-start(f32[288,256]{1,0:T(8,128)S(1)} %get-tuple-element.548.in_b), channel_id=1, source_target_pairs={{0,1},{1,0},{2,3},{3,2},{4,5},{5,4},{6,7},{7,6},{8,9},{9,8},{10,11... | collective-permute-start | bytes 884744 | tf_op jit(solution)/shard_map/ppermute | solution.py:187
  96.2 2.6 %collective-permute-start.24 = (f32[96,256]{1,0:T(8,128)S(1)}, f32[96,256]{1,0:T(8,128)S(1)}, u32[]{:S(2)}, u32[]{:S(2)}) collective-permute-start(f32[96,256]{1,0:T(8,128)S(1)} %get-tuple-element.547.in_a), channel_id=1, source_target_pairs={{0,1},{1,0},{2,3},{3,2},{4,5},{5,4},{6,7},{7,6},{8,9},{9,8},{10,11... | collective-permute-start | bytes 294920 | tf_op jit(solution)/shard_map/ppermute | solution.py:187
  98.8 2.0 %collective-permute-start.31 = (f32[96,256]{1,0:T(8,128)S(1)}, f32[96,256]{1,0:T(8,128)S(1)}, u32[]{:S(2)}, u32[]{:S(2)}) collective-permute-start(f32[96,256]{1,0:T(8,128)S(1)} %get-tuple-element.570), channel_id=1, source_target_pairs={{0,1},{1,0},{2,3},{3,2},{4,5},{5,4},{6,7},{7,6},{8,9},{9,8},{10,11... | collective-permute-start | bytes 294920 | tf_op jit(solution)/shard_map/ppermute | solution.py:187
  99.2 12.8 %collective-permute-start.27 = (bf16[24,384]{1,0:T(8,128)(2,1)S(1)}, bf16[24,384]{1,0:T(8,128)(2,1)S(1)}, u32[]{:S(2)}, u32[]{:S(2)}) collective-permute-start(bf16[24,384]{1,0:T(8,128)(2,1)S(1)} %get-tuple-element.552), channel_id=1, source_target_pairs={{0,2},{2,0},{4,6},{6,4},{8,10},{10,8},{12,14},{14,12},{1,3},{3,1},... | collective-permute-start | bytes 55304 | tf_op jit(solution)/shard_map/ppermute | solution.py:357
  101.0 11.1 %collective-permute-start.35 = (bf16[24,384]{1,0:T(8,128)(2,1)S(1)}, bf16[24,384]{1,0:T(8,128)(2,1)S(1)}, u32[]{:S(2)}, u32[]{:S(2)}) collective-permute-start(bf16[24,384]{1,0:T(8,128)(2,1)S(1)} %get-tuple-element.574), channel_id=1, source_target_pairs={{0,14},{2,12},{4,10},{6,8},{8,6},{10,4},{12,2},{14,0},{1,15},{3,13... | collective-permute-start | bytes 55304 | tf_op jit(solution)/shard_map/ppermute | solution.py:357
  103.9 8.3 %collective-permute-start.34 = (bf16[24,384]{1,0:T(8,128)(2,1)S(1)}, bf16[24,384]{1,0:T(8,128)(2,1)S(1)}, u32[]{:S(2)}, u32[]{:S(2)}) collective-permute-start(bf16[24,384]{1,0:T(8,128)(2,1)S(1)} %get-tuple-element.573), channel_id=1, source_target_pairs={{0,12},{2,14},{4,8},{6,10},{8,4},{10,6},{12,0},{14,2},{1,13},{3,15... | collective-permute-start | bytes 55304 | tf_op jit(solution)/shard_map/ppermute | solution.py:357
  106.3 5.9 %collective-permute-start.33 = (bf16[24,384]{1,0:T(8,128)(2,1)S(1)}, bf16[24,384]{1,0:T(8,128)(2,1)S(1)}, u32[]{:S(2)}, u32[]{:S(2)}) collective-permute-start(bf16[24,384]{1,0:T(8,128)(2,1)S(1)} %get-tuple-element.572), channel_id=1, source_target_pairs={{0,10},{2,8},{4,14},{6,12},{8,2},{10,0},{12,6},{14,4},{1,11},{3,9}... | collective-permute-start | bytes 55304 | tf_op jit(solution)/shard_map/ppermute | solution.py:357
  106.6 5.6 %collective-permute-start.32 = (bf16[24,384]{1,0:T(8,128)(2,1)S(1)}, bf16[24,384]{1,0:T(8,128)(2,1)S(1)}, u32[]{:S(2)}, u32[]{:S(2)}) collective-permute-start(bf16[24,384]{1,0:T(8,128)(2,1)S(1)} %get-tuple-element.571), channel_id=1, source_target_pairs={{0,8},{2,10},{4,12},{6,14},{8,0},{10,2},{12,4},{14,6},{1,9},{3,11}... | collective-permute-start | bytes 55304 | tf_op jit(solution)/shard_map/ppermute | solution.py:357
  112.0 1.3 %collective-permute-start.39 = (f32[48,256]{1,0:T(8,128)S(1)}, f32[48,256]{1,0:T(8,128)S(1)}, u32[]{:S(2)}, u32[]{:S(2)}) collective-permute-start(f32[48,256]{1,0:T(8,128)S(1)} %get-tuple-element.581), channel_id=1, source_target_pairs={{0,1},{1,0},{2,3},{3,2},{4,5},{5,4},{6,7},{7,6},{8,9},{9,8},{10,11... | collective-permute-start | bytes 147464 | tf_op jit(solution)/shard_map/ppermute | solution.py:187
  113.5 4.7 %collective-permute-start.41 = (bf16[24,384]{1,0:T(8,128)(2,1)S(1)}, bf16[24,384]{1,0:T(8,128)(2,1)S(1)}, u32[]{:S(2)}, u32[]{:S(2)}) collective-permute-start(bf16[24,384]{1,0:T(8,128)(2,1)S(1)} %get-tuple-element.586), channel_id=1, source_target_pairs={{0,6},{2,4},{4,2},{6,0},{8,14},{10,12},{12,10},{14,8},{1,7},{3,5},... | collective-permute-start | bytes 55304 | tf_op jit(solution)/shard_map/ppermute | solution.py:357
  114.1 4.1 %collective-permute-start.40 = (bf16[24,384]{1,0:T(8,128)(2,1)S(1)}, bf16[24,384]{1,0:T(8,128)(2,1)S(1)}, u32[]{:S(2)}, u32[]{:S(2)}) collective-permute-start(bf16[24,384]{1,0:T(8,128)(2,1)S(1)} %get-tuple-element.585), channel_id=1, source_target_pairs={{0,4},{2,6},{4,0},{6,2},{8,12},{10,14},{12,8},{14,10},{1,5},{3,7},... | collective-permute-start | bytes 55304 | tf_op jit(solution)/shard_map/ppermute | solution.py:357

commit v7 on v6

--- a/solution.py
+++ b/solution.py
@@ -363,13 +363,14 @@
         [jax.ShapeDtypeStruct((K, tokens), jnp.bfloat16)] + [block] * 2,
         in_a, swap_core(in_a), in_b, swap_core(in_b), keep_a, swap_core(send_a),
     )
-    early = near[0].astype(jnp.float32) + to_owner(1, near[1])
     for units, name, value in landing.pop(9):
         units[name] = value
     keep_b, send_b = rotate("23", ["m1", "t1"], [acc], 2 * rows, True)
     far = squares(squares_kernel, "squares", [block] * 4, rot_in, keep_b, swap_core(send_b))
-    for k in range(4):
-        early = early + to_owner(4 + k, far[k])
+    waiting = {1: near[1], 4: far[0], 5: far[1], 6: far[2], 7: far[3]}
+    early = near[0].astype(jnp.float32)
+    for k in (6, 7):
+        early = early + to_owner(k, waiting[k])
 
     for units, name, value in landing.pop(10):
         units[name] = value
@@ -377,6 +378,8 @@
     early, come_c = lax.optimization_barrier((early, swap_core(send_c)))
     late = squares(squares_kernel, "squares", [block] * 2, rot_in, keep_c, come_c)
     total = early + to_owner(2, late[0]) + to_owner(3, late[1])
+    for k in (1, 4, 5):
+        total = total + to_owner(k, waiting[k])
     return total * (1.0 / 8)
 
 

time: 119 us -> 118 us (level)
  waiting for transfers between devices: 22.1 us -> 20.9 us
where the time goes in v7:
time: 118 us
  starting transfers between devices  83.3 us (71%)
  waiting for transfers between devices  20.9 us (18%)
  Pallas kernels  12.5 us (11%)
    ppermute x30, starting transfers between devices, send(): return lax.ppermute(value, ('group', 'dp'), pairs)  69.6 us
    ppermute x30, waiting for transfers between devices, send(): return lax.ppermute(value, ('group', 'dp'), pairs)  18.5 us
    ppermute x7, starting transfers between devices, to_owner(): lax.ppermute(value, 'dp', [(i, i ^ k) for i in range(8)])  12.8 us
    pallas_call x5, Pallas kernels, rotate(): pl.pallas_call(functools.partial(rotate_kernel, (terms, acc_from, last),...  9.2 us
    ppermute x7, waiting for transfers between devices, to_owner(): lax.ppermute(value, 'dp', [(i, i ^ k) for i in range(8)])  2.44 us
  transfers between devices with their start and end apart: 42, of which 12 were waited for; matrix products, arithmetic and copies ran while one was open for 0% of the time, Pallas kernels for 9%

profile of v7, /device:TPU:0, one launch (start us, length us, event | category | flops | bytes accessed | tf_op | source)
XLA Modules:
  0.0 117.8 jit_solution(5529169009011542937)
XLA Ops:
  0.0 1.9 %first_cut.1.refs_0_ = bf16[48,4608]{1,0:T(8,128)(2,1)} custom-call(bf16[48,4096]{1,0:T(8,128)(2,1)} %bitcast.18, bf16[48,14336]{1,0:T(8,128)(2,1)} %bitcast.16), custom_call_target="tpu_custom_call" | custom-call | tf_op jit(solution)/shard_map/first_cut/pallas_call | solution.py:190
  2.1 3.1 %collective-permute-start = (bf16[48,4608]{1,0:T(8,128)(2,1)}, bf16[48,4608]{1,0:T(8,128)(2,1)S(1)}, u32[]{:S(2)}, u32[]{:S(2)}) collective-permute-start(bf16[48,4608]{1,0:T(8,128)(2,1)} %first_cut.1.refs_0_), channel_id=1, source_target_pairs={{0,4},{2,6},{4,0},{6,2},{8,12},{10,14},{12,8},{14,10},{16,20},{18,... | collective-permute-start | bytes 1327112 | tf_op jit(solution)/shard_map/ppermute | solution.py:257
  5.2 1.5 %collective-permute-start.1 = (bf16[48,4608]{1,0:T(8,128)(2,1)S(1)}, bf16[48,4608]{1,0:T(8,128)(2,1)S(1)}, u32[]{:S(2)}, u32[]{:S(2)}) collective-permute-start(bf16[48,4608]{1,0:T(8,128)(2,1)S(1)} %get-tuple-element.421.inner_ref.outer_ref.refs_2_), channel_id=1, source_target_pairs={{0,2},{2,0},{12,14},{14,12},{16,18},{18,16},{28,30},{30,28},{4,6},... | collective-permute-start | bytes 1327112 | tf_op jit(solution)/shard_map/ppermute | solution.py:257
  6.7 0.7 collective-permute-start.2
  7.5 4.4 %collective-permute-start.3 = (bf16[48,4608]{1,0:T(8,128)(2,1)S(1)}, bf16[48,4608]{1,0:T(8,128)(2,1)S(1)}, u32[]{:S(2)}, u32[]{:S(2)}) collective-permute-start(bf16[48,4608]{1,0:T(8,128)(2,1)S(1)} %pick.17), channel_id=1, source_target_pairs={{0,4},{2,6},{4,0},{6,2},{8,12},{10,14},{12,8},{14,10},{16,20},{18,... | collective-permute-start | bytes 1327112 | tf_op jit(solution)/shard_map/ppermute | solution.py:257
  12.4 4.0 %collective-permute-done.outer_ref.refs_0_ = bf16[48,4608]{1,0:T(8,128)(2,1)S(1)} collective-permute-done((bf16[48,4608]{1,0:T(8,128)(2,1)}, bf16[48,4608]{1,0:T(8,128)(2,1)S(1)}, u32[]{:S(2)}, u32[]{:S(2)}) %collective-permute-start) | collective-permute-done | bytes 442400 | tf_op jit(solution)/shard_map/ppermute | solution.py:257
  16.4 0.7 collective-permute-start.5
  17.1 1.2 %collective-permute-done.1.refs_3_.outer_ref = bf16[48,4608]{1,0:T(8,128)(2,1)S(1)} collective-permute-done((bf16[48,4608]{1,0:T(8,128)(2,1)S(1)}, bf16[48,4608]{1,0:T(8,128)(2,1)S(1)}, u32[]{:S(2)}, u32[]{:S(2)}) %collective-permute-start.1) | collective-permute-done | bytes 442400 | tf_op jit(solution)/shard_map/ppermute | solution.py:257
  18.3 4.1 %collective-permute-start.6 = (bf16[48,4608]{1,0:T(8,128)(2,1)S(1)}, bf16[48,4608]{1,0:T(8,128)(2,1)S(1)}, u32[]{:S(2)}, u32[]{:S(2)}) collective-permute-start(bf16[48,4608]{1,0:T(8,128)(2,1)S(1)} %pick.18), channel_id=1, source_target_pairs={{0,4},{2,6},{4,0},{6,2},{8,12},{10,14},{12,8},{14,10},{16,20},{18,... | collective-permute-start | bytes 1327112 | tf_op jit(solution)/shard_map/ppermute | solution.py:257
  22.4 1.2 %collective-permute-start.7 = (bf16[48,4608]{1,0:T(8,128)(2,1)S(1)}, bf16[48,4608]{1,0:T(8,128)(2,1)S(1)}, u32[]{:S(2)}, u32[]{:S(2)}) collective-permute-start(bf16[48,4608]{1,0:T(8,128)(2,1)S(1)} %collective-permute-done.outer_ref.refs_0_), channel_id=1, source_target_pairs={{0,2},{2,0},{12,14},{14,12},{16,18},{18,16},{28,30},{30,28},{4,8},... | collective-permute-start | bytes 1327112 | tf_op jit(solution)/shard_map/ppermute | solution.py:257
  23.6 2.3 %collective-permute-done.3.inner_ref.refs_1_.refs_0_ = bf16[48,4608]{1,0:T(8,128)(2,1)S(1)} collective-permute-done((bf16[48,4608]{1,0:T(8,128)(2,1)S(1)}, bf16[48,4608]{1,0:T(8,128)(2,1)S(1)}, u32[]{:S(2)}, u32[]{:S(2)}) %collective-permute-start.3) | collective-permute-done | bytes 442400 | tf_op jit(solution)/shard_map/ppermute | solution.py:257
  25.9 2.0 %collective-permute-start.8 = (bf16[48,4608]{1,0:T(8,128)(2,1)S(1)}, bf16[48,4608]{1,0:T(8,128)(2,1)S(1)}, u32[]{:S(2)}, u32[]{:S(2)}) collective-permute-start(bf16[48,4608]{1,0:T(8,128)(2,1)S(1)} %collective-permute-done.1.refs_3_.outer_ref), channel_id=1, source_target_pairs={{0,16},{2,18},{12,28},{14,30},{16,0},{18,2},{28,12},{30,14},{4,20}... | collective-permute-start | bytes 1327112 | tf_op jit(solution)/shard_map/ppermute | solution.py:257
  27.9 5.7 %collective-permute-start.9 = (bf16[48,4608]{1,0:T(8,128)(2,1)S(1)}, bf16[48,4608]{1,0:T(8,128)(2,1)S(1)}, u32[]{:S(2)}, u32[]{:S(2)}) collective-permute-start(bf16[48,4608]{1,0:T(8,128)(2,1)S(1)} %pick.19), channel_id=1, source_target_pairs={{0,4},{2,6},{4,0},{6,2},{8,12},{10,14},{12,8},{14,10},{16,20},{18,... | collective-permute-start | bytes 1327112 | tf_op jit(solution)/shard_map/ppermute | solution.py:257
  33.6 1.5 %collective-permute-start.10 = (bf16[48,4608]{1,0:T(8,128)(2,1)S(1)}, bf16[48,4608]{1,0:T(8,128)(2,1)S(1)}, u32[]{:S(2)}, u32[]{:S(2)}) collective-permute-start(bf16[48,4608]{1,0:T(8,128)(2,1)S(1)} %get-tuple-element.422.outer_ref.refs_4_), channel_id=1, source_target_pairs={{0,2},{2,0},{12,14},{14,12},{16,18},{18,16},{28,30},{30,28},{4,6},... | collective-permute-start | bytes 1327112 | tf_op jit(solution)/shard_map/ppermute | solution.py:257
  35.4 2.0 %collective-permute-start.11 = (bf16[48,4608]{1,0:T(8,128)(2,1)S(1)}, bf16[48,4608]{1,0:T(8,128)(2,1)S(1)}, u32[]{:S(2)}, u32[]{:S(2)}) collective-permute-start(bf16[48,4608]{1,0:T(8,128)(2,1)S(1)} %pick.20), channel_id=1, source_target_pairs={{0,16},{2,18},{12,28},{14,30},{16,0},{18,2},{28,12},{30,14},{4,8},... | collective-permute-start | bytes 1327112 | tf_op jit(solution)/shard_map/ppermute | solution.py:257
  37.4 5.7 %collective-permute-start.12 = (bf16[48,4608]{1,0:T(8,128)(2,1)S(1)}, bf16[48,4608]{1,0:T(8,128)(2,1)S(1)}, u32[]{:S(2)}, u32[]{:S(2)}) collective-permute-start(bf16[48,4608]{1,0:T(8,128)(2,1)S(1)} %pick.21), channel_id=1, source_target_pairs={{0,4},{2,6},{4,0},{6,2},{8,12},{10,14},{12,8},{14,10},{16,20},{18,... | collective-permute-start | bytes 1327112 | tf_op jit(solution)/shard_map/ppermute | solution.py:257
  43.3 1.6 %collective-permute-done.9.outer_ref.refs_2_.refs_0_ = bf16[48,4608]{1,0:T(8,128)(2,1)S(1)} collective-permute-done((bf16[48,4608]{1,0:T(8,128)(2,1)S(1)}, bf16[48,4608]{1,0:T(8,128)(2,1)S(1)}, u32[]{:S(2)}, u32[]{:S(2)}) %collective-permute-start.9) | collective-permute-done | bytes 442400 | tf_op jit(solution)/shard_map/ppermute | solution.py:257
  44.8 2.0 %collective-permute-start.14 = (bf16[48,4608]{1,0:T(8,128)(2,1)S(1)}, bf16[48,4608]{1,0:T(8,128)(2,1)S(1)}, u32[]{:S(2)}, u32[]{:S(2)}) collective-permute-start(bf16[48,4608]{1,0:T(8,128)(2,1)S(1)} %collective-permute-done.6.outer_ref.refs_3_.refs_1_), channel_id=1, source_target_pairs={{0,16},{2,18},{12,28},{14,30},{16,0},{18,2},{28,12},{30,14},{4,8},... | collective-permute-start | bytes 1327112 | tf_op jit(solution)/shard_map/ppermute | solution.py:257
  46.9 5.6 %collective-permute-start.15 = (bf16[48,4608]{1,0:T(8,128)(2,1)S(1)}, bf16[48,4608]{1,0:T(8,128)(2,1)S(1)}, u32[]{:S(2)}, u32[]{:S(2)}) collective-permute-start(bf16[48,4608]{1,0:T(8,128)(2,1)S(1)} %pick.23), channel_id=1, source_target_pairs={{0,4},{2,6},{4,0},{6,2},{8,12},{10,14},{12,8},{14,10},{16,20},{18,... | collective-permute-start | bytes 1327112 | tf_op jit(solution)/shard_map/ppermute | solution.py:257
  52.7 1.7 %collective-permute-done.12.inner_ref.refs_6_ = bf16[48,4608]{1,0:T(8,128)(2,1)S(1)} collective-permute-done((bf16[48,4608]{1,0:T(8,128)(2,1)S(1)}, bf16[48,4608]{1,0:T(8,128)(2,1)S(1)}, u32[]{:S(2)}, u32[]{:S(2)}) %collective-permute-start.12) | collective-permute-done | bytes 442400 | tf_op jit(solution)/shard_map/ppermute | solution.py:257
  54.3 2.0 %collective-permute-start.17 = (bf16[48,4608]{1,0:T(8,128)(2,1)S(1)}, bf16[48,4608]{1,0:T(8,128)(2,1)S(1)}, u32[]{:S(2)}, u32[]{:S(2)}) collective-permute-start(bf16[48,4608]{1,0:T(8,128)(2,1)S(1)} %pick.24), channel_id=1, source_target_pairs={{0,16},{2,18},{12,28},{14,30},{16,0},{18,2},{28,12},{30,14},{4,20}... | collective-permute-start | bytes 1327112 | tf_op jit(solution)/shard_map/ppermute | solution.py:257
  56.3 3.1 %rotate.5 = (f32[96,256]{1,0:T(8,128)S(1)}, f32[48,256]{1,0:T(8,128)S(1)}, f32[48,256]{1,0:T(8,128)S(1)}) custom-call(bf16[256,4096]{1,0:T(8,128)(2,1)S(1)} %bitcast.11, bf16[256,14336]{1,0:T(8,128)(2,1)S(1)} %bitcast.6, bf16[48,4608]{1,0:T(8,128)(2,1)S(1)} %copy-done.2, bf16[48,4608]{1,0:T(8,128)(2,1)S(1)} %collective-permute-done.4.outer_ref.refs_1_, ...), custom_call_target="tpu_custom_call" | custom-call | flops 905969664 | bytes 3538944 | tf_op jit(solution)/shard_map/rotate/pallas_call | solution.py:228
  59.5 2.5 %collective-permute-start.18 = (bf16[48,4608]{1,0:T(8,128)(2,1)S(1)}, bf16[48,4608]{1,0:T(8,128)(2,1)S(1)}, u32[]{:S(2)}, u32[]{:S(2)}) collective-permute-start(bf16[48,4608]{1,0:T(8,128)(2,1)S(1)} %pick.25), channel_id=1, source_target_pairs={{0,4},{2,6},{4,0},{6,2},{8,12},{10,14},{12,8},{14,10},{16,20},{18,... | collective-permute-start | bytes 1327112 | tf_op jit(solution)/shard_map/ppermute | solution.py:257
  62.0 0.7 collective-permute-start.19
  62.8 1.0 collective-permute-done.15.outer_ref.inner_ref.refs_3_
  63.8 2.0 %collective-permute-start.20 = (bf16[48,4608]{1,0:T(8,128)(2,1)S(1)}, bf16[48,4608]{1,0:T(8,128)(2,1)S(1)}, u32[]{:S(2)}, u32[]{:S(2)}) collective-permute-start(bf16[48,4608]{1,0:T(8,128)(2,1)S(1)} %pick.27), channel_id=1, source_target_pairs={{0,16},{2,18},{12,28},{14,30},{16,0},{18,2},{28,12},{30,14},{4,20}... | collective-permute-start | bytes 1327112 | tf_op jit(solution)/shard_map/ppermute | solution.py:257
  65.8 5.6 %collective-permute-start.21 = (bf16[48,4608]{1,0:T(8,128)(2,1)S(1)}, bf16[48,4608]{1,0:T(8,128)(2,1)S(1)}, u32[]{:S(2)}, u32[]{:S(2)}) collective-permute-start(bf16[48,4608]{1,0:T(8,128)(2,1)S(1)} %collective-permute-done.16.outer_ref.refs_5_.refs_2_), channel_id=1, source_target_pairs={{0,4},{2,6},{4,0},{6,2},{8,12},{10,14},{12,8},{14,10},{16,20},{18,... | collective-permute-start | bytes 1327112 | tf_op jit(solution)/shard_map/ppermute | solution.py:257
  71.6 1.6 %collective-permute-done.18.outer_ref.refs_4_.refs_5_ = bf16[48,4608]{1,0:T(8,128)(2,1)S(1)} collective-permute-done((bf16[48,4608]{1,0:T(8,128)(2,1)S(1)}, bf16[48,4608]{1,0:T(8,128)(2,1)S(1)}, u32[]{:S(2)}, u32[]{:S(2)}) %collective-permute-start.18) | collective-permute-done | bytes 442400 | tf_op jit(solution)/shard_map/ppermute | solution.py:257
  73.3 2.0 %collective-permute-start.23 = (bf16[48,4608]{1,0:T(8,128)(2,1)S(1)}, bf16[48,4608]{1,0:T(8,128)(2,1)S(1)}, u32[]{:S(2)}, u32[]{:S(2)}) collective-permute-start(bf16[48,4608]{1,0:T(8,128)(2,1)S(1)} %pick.29), channel_id=1, source_target_pairs={{0,16},{2,18},{12,28},{14,30},{16,0},{18,2},{28,12},{30,14},{4,8},... | collective-permute-start | bytes 1327112 | tf_op jit(solution)/shard_map/ppermute | solution.py:257
  75.3 1.6 %collective-permute-start.27 = (bf16[48,4608]{1,0:T(8,128)(2,1)S(1)}, bf16[48,4608]{1,0:T(8,128)(2,1)S(1)}, u32[]{:S(2)}, u32[]{:S(2)}) collective-permute-start(bf16[48,4608]{1,0:T(8,128)(2,1)S(1)} %pick.30), channel_id=1, source_target_pairs={{0,2},{2,0},{12,14},{14,12},{16,18},{18,16},{28,30},{30,28},{4,8},... | collective-permute-start | bytes 1327112 | tf_op jit(solution)/shard_map/ppermute | solution.py:257
  76.9 1.5 %collective-permute-start.28 = (bf16[48,4608]{1,0:T(8,128)(2,1)S(1)}, bf16[48,4608]{1,0:T(8,128)(2,1)S(1)}, u32[]{:S(2)}, u32[]{:S(2)}) collective-permute-start(bf16[48,4608]{1,0:T(8,128)(2,1)S(1)} %pick.31), channel_id=1, source_target_pairs={{0,16},{2,18},{12,28},{14,30},{16,0},{18,2},{28,12},{30,14},{4,20}... | collective-permute-start | bytes 1327112 | tf_op jit(solution)/shard_map/ppermute | solution.py:257
  78.4 3.5 %collective-permute-done.21.refs_8_.refs_7_ = bf16[48,4608]{1,0:T(8,128)(2,1)S(1)} collective-permute-done((bf16[48,4608]{1,0:T(8,128)(2,1)S(1)}, bf16[48,4608]{1,0:T(8,128)(2,1)S(1)}, u32[]{:S(2)}, u32[]{:S(2)}) %collective-permute-start.21) | collective-permute-done | bytes 442400 | tf_op jit(solution)/shard_map/ppermute | solution.py:257
  81.9 2.3 %collective-permute-start.29 = (bf16[48,4608]{1,0:T(8,128)(2,1)S(1)}, bf16[48,4608]{1,0:T(8,128)(2,1)S(1)}, u32[]{:S(2)}, u32[]{:S(2)}) collective-permute-start(bf16[48,4608]{1,0:T(8,128)(2,1)S(1)} %pick.32), channel_id=1, source_target_pairs={{0,4},{2,6},{4,0},{6,2},{8,12},{10,14},{12,8},{14,10},{16,20},{18,... | collective-permute-start | bytes 1327112 | tf_op jit(solution)/shard_map/ppermute | solution.py:257
  84.2 1.1 rotate.6
  85.3 1.1 collective-permute-done.23.refs_6_.refs_10_
  86.4 1.1 rotate.7
  87.5 3.9 %collective-permute-start.33 = (bf16[48,4608]{1,0:T(8,128)(2,1)S(1)}, bf16[48,4608]{1,0:T(8,128)(2,1)S(1)}, u32[]{:S(2)}, u32[]{:S(2)}) collective-permute-start(bf16[48,4608]{1,0:T(8,128)(2,1)S(1)} %collective-permute-done.3.inner_ref.refs_1_.refs_0_), channel_id=1, source_target_pairs={{0,2},{2,0},{12,14},{14,12},{16,18},{18,16},{28,30},{30,28},{1,3},... | collective-permute-start | bytes 1327112 | tf_op jit(solution)/shard_map/ppermute | solution.py:257
  91.5 1.2 collective-permute-start.34
  92.7 3.4 %collective-permute-start.35 = (bf16[48,4608]{1,0:T(8,128)(2,1)S(1)}, bf16[48,4608]{1,0:T(8,128)(2,1)S(1)}, u32[]{:S(2)}, u32[]{:S(2)}) collective-permute-start(bf16[48,4608]{1,0:T(8,128)(2,1)S(1)} %collective-permute-done.3.inner_ref.refs_1_.refs_0_), channel_id=1, source_target_pairs={{0,16},{2,18},{12,28},{14,30},{16,0},{18,2},{28,12},{30,14},{1,17}... | collective-permute-start | bytes 1327112 | tf_op jit(solution)/shard_map/ppermute | solution.py:257
  96.7 2.1 %rotate.8 = (f32[96,256]{1,0:T(8,128)S(1)}, f32[96,256]{1,0:T(8,128)S(1)}) custom-call(bf16[256,4096]{1,0:T(8,128)(2,1)S(1)} %bitcast.14, bf16[256,14336]{1,0:T(8,128)(2,1)S(1)} %bitcast.9, bf16[48,4608]{1,0:T(8,128)(2,1)S(1)} %collective-permute-done.9.outer_ref.refs_2_.refs_0_, ...), custom_call_target="tpu_custom_call" | custom-call | flops 905969664 | bytes 5750784 | tf_op jit(solution)/shard_map/rotate/pallas_call | solution.py:228
  99.2 1.6 %collective-permute-start.39 = (bf16[24,384]{1,0:T(8,128)(2,1)S(1)}, bf16[24,384]{1,0:T(8,128)(2,1)S(1)}, u32[]{:S(2)}, u32[]{:S(2)}) collective-permute-start(bf16[24,384]{1,0:T(8,128)(2,1)S(1)} %get-tuple-element.584), channel_id=1, source_target_pairs={{0,2},{2,0},{4,6},{6,4},{8,10},{10,8},{12,14},{14,12},{1,3},{3,1},... | collective-permute-start | bytes 55304 | tf_op jit(solution)/shard_map/ppermute | solution.py:357
  101.0 2.9 %collective-permute-start.32 = (bf16[24,384]{1,0:T(8,128)(2,1)S(1)}, bf16[24,384]{1,0:T(8,128)(2,1)S(1)}, u32[]{:S(2)}, u32[]{:S(2)}) collective-permute-start(bf16[24,384]{1,0:T(8,128)(2,1)S(1)} %get-tuple-element.571), channel_id=1, source_target_pairs={{0,14},{2,12},{4,10},{6,8},{8,6},{10,4},{12,2},{14,0},{1,15},{3,13... | collective-permute-start | bytes 55304 | tf_op jit(solution)/shard_map/ppermute | solution.py:357
  103.9 2.4 %collective-permute-start.31 = (bf16[24,384]{1,0:T(8,128)(2,1)S(1)}, bf16[24,384]{1,0:T(8,128)(2,1)S(1)}, u32[]{:S(2)}, u32[]{:S(2)}) collective-permute-start(bf16[24,384]{1,0:T(8,128)(2,1)S(1)} %get-tuple-element.570), channel_id=1, source_target_pairs={{0,12},{2,14},{4,8},{6,10},{8,4},{10,6},{12,0},{14,2},{1,13},{3,15... | collective-permute-start | bytes 55304 | tf_op jit(solution)/shard_map/ppermute | solution.py:357
  106.5 1.9 %rotate.9 = (f32[48,256]{1,0:T(8,128)S(1)}, f32[48,256]{1,0:T(8,128)S(1)}) custom-call(bf16[256,4096]{1,0:T(8,128)(2,1)S(1)} %bitcast.15, bf16[256,14336]{1,0:T(8,128)(2,1)S(1)} %bitcast.10, bf16[48,4608]{1,0:T(8,128)(2,1)S(1)} %collective-permute-done.3.inner_ref.refs_1_.refs_0_, bf16[48,4608]{1,0:T(8,128)(2,1)S(1)} %collective-permute-done.6.outer_ref.refs_3_.refs_1_, ...), custom_call_target="tpu_custom_call" | custom-call | flops 452984832 | bytes 3096576 | tf_op jit(solution)/shard_map/rotate/pallas_call | solution.py:228
  108.6 3.6 %collective-permute-start.40 = (bf16[24,384]{1,0:T(8,128)(2,1)S(1)}, bf16[24,384]{1,0:T(8,128)(2,1)S(1)}, u32[]{:S(2)}, u32[]{:S(2)}) collective-permute-start(bf16[24,384]{1,0:T(8,128)(2,1)S(1)} %get-tuple-element.585), channel_id=1, source_target_pairs={{0,8},{2,10},{4,12},{6,14},{8,0},{10,2},{12,4},{14,6},{1,9},{3,11}... | collective-permute-start | bytes 55304 | tf_op jit(solution)/shard_map/ppermute | solution.py:357
  112.4 0.8 collective-permute-start.38
  113.2 1.5 %collective-permute-start.37 = (bf16[24,384]{1,0:T(8,128)(2,1)S(1)}, bf16[24,384]{1,0:T(8,128)(2,1)S(1)}, u32[]{:S(2)}, u32[]{:S(2)}) collective-permute-start(bf16[24,384]{1,0:T(8,128)(2,1)S(1)} %get-tuple-element.582), channel_id=1, source_target_pairs={{0,4},{2,6},{4,0},{6,2},{8,12},{10,14},{12,8},{14,10},{1,5},{3,7},... | collective-permute-start | bytes 55304 | tf_op jit(solution)/shard_map/ppermute | solution.py:357
  114.7 2.4 %collective-permute-done.38 = bf16[24,384]{1,0:T(8,128)(2,1)S(1)} collective-permute-done((bf16[24,384]{1,0:T(8,128)(2,1)S(1)}, bf16[24,384]{1,0:T(8,128)(2,1)S(1)}, u32[]{:S(2)}, u32[]{:S(2)}) %collective-permute-start.38) | collective-permute-done | bytes 18464 | tf_op jit(solution)/shard_map/ppermute | solution.py:357
  (78 shorter events, 4.5 us)
Async XLA Ops:
  0.0 2.0 %copy-start.3 = (bf16[4096,48]{0,1:T(8,128)(2,1)S(1)}, bf16[4096,48]{0,1:T(8,128)(2,1)}, u32[]{:S(2)}) copy-start(bf16[4096,48]{0,1:T(8,128)(2,1)} %param.6) | copy-start | bytes 1179652
  0.0 2.0 %copy-start.1 = (bf16[14336,48]{0,1:T(8,128)(2,1)S(1)}, bf16[14336,48]{0,1:T(8,128)(2,1)}, u32[]{:S(2)}) copy-start(bf16[14336,48]{0,1:T(8,128)(2,1)} %param.7) | copy-start | bytes 4128772
  2.0 54.3 %slice-start = ((s8[7340032]{0:T(1024)(128)(4,1)}), s8[4194304]{0:T(1024)(128)(4,1)S(1)}, s32[]{:S(2)}) async-start(s8[7340032]{0:T(1024)(128)(4,1)} %bitcast.4), calls=%async_computation | async-start | bytes 8388608
  2.1 14.3 %collective-permute-start = (bf16[48,4608]{1,0:T(8,128)(2,1)}, bf16[48,4608]{1,0:T(8,128)(2,1)S(1)}, u32[]{:S(2)}, u32[]{:S(2)}) collective-permute-start(bf16[48,4608]{1,0:T(8,128)(2,1)} %first_cut.1.refs_0_), channel_id=1, source_target_pairs={{0,4},{2,6},{4,0},{6,2},{8,12},{10,14},{12,8},{14,10},{16,20},{18,... | collective-permute-start | bytes 1327112 | tf_op jit(solution)/shard_map/ppermute | solution.py:257
  5.2 13.1 %collective-permute-start.1 = (bf16[48,4608]{1,0:T(8,128)(2,1)S(1)}, bf16[48,4608]{1,0:T(8,128)(2,1)S(1)}, u32[]{:S(2)}, u32[]{:S(2)}) collective-permute-start(bf16[48,4608]{1,0:T(8,128)(2,1)S(1)} %get-tuple-element.421.inner_ref.outer_ref.refs_2_), channel_id=1, source_target_pairs={{0,2},{2,0},{12,14},{14,12},{16,18},{18,16},{28,30},{30,28},{4,6},... | collective-permute-start | bytes 1327112 | tf_op jit(solution)/shard_map/ppermute | solution.py:257
  6.7 11.6 %collective-permute-start.2 = (bf16[48,4608]{1,0:T(8,128)(2,1)}, bf16[48,4608]{1,0:T(8,128)(2,1)S(1)}, u32[]{:S(2)}, u32[]{:S(2)}) collective-permute-start(bf16[48,4608]{1,0:T(8,128)(2,1)} %first_cut.1.refs_0_), channel_id=1, source_target_pairs={{4,8},{6,10},{8,4},{10,6},{20,24},{22,26},{24,20},{26,22},{5,9},{7... | collective-permute-start | bytes 1327112 | tf_op jit(solution)/shard_map/ppermute | solution.py:257
  7.5 18.4 %collective-permute-start.3 = (bf16[48,4608]{1,0:T(8,128)(2,1)S(1)}, bf16[48,4608]{1,0:T(8,128)(2,1)S(1)}, u32[]{:S(2)}, u32[]{:S(2)}) collective-permute-start(bf16[48,4608]{1,0:T(8,128)(2,1)S(1)} %pick.17), channel_id=1, source_target_pairs={{0,4},{2,6},{4,0},{6,2},{8,12},{10,14},{12,8},{14,10},{16,20},{18,... | collective-permute-start | bytes 1327112 | tf_op jit(solution)/shard_map/ppermute | solution.py:257
  11.9 16.0 %collective-permute-start.4 = (bf16[48,4608]{1,0:T(8,128)(2,1)}, bf16[48,4608]{1,0:T(8,128)(2,1)S(1)}, u32[]{:S(2)}, u32[]{:S(2)}) collective-permute-start(bf16[48,4608]{1,0:T(8,128)(2,1)} %first_cut.1.refs_0_), channel_id=1, source_target_pairs={{0,2},{2,0},{12,14},{14,12},{16,18},{18,16},{28,30},{30,28},{4,6},... | collective-permute-start | bytes 1327112 | tf_op jit(solution)/shard_map/ppermute | solution.py:257
  16.4 11.5 %collective-permute-start.5 = (bf16[48,4608]{1,0:T(8,128)(2,1)S(1)}, bf16[48,4608]{1,0:T(8,128)(2,1)S(1)}, u32[]{:S(2)}, u32[]{:S(2)}) collective-permute-start(bf16[48,4608]{1,0:T(8,128)(2,1)S(1)} %get-tuple-element.421.inner_ref.outer_ref.refs_2_), channel_id=1, source_target_pairs={{4,8},{6,10},{8,4},{10,6},{20,24},{22,26},{24,20},{26,22},{5,9},{7... | collective-permute-start | bytes 1327112 | tf_op jit(solution)/shard_map/ppermute | solution.py:257
  18.3 17.0 %collective-permute-start.6 = (bf16[48,4608]{1,0:T(8,128)(2,1)S(1)}, bf16[48,4608]{1,0:T(8,128)(2,1)S(1)}, u32[]{:S(2)}, u32[]{:S(2)}) collective-permute-start(bf16[48,4608]{1,0:T(8,128)(2,1)S(1)} %pick.18), channel_id=1, source_target_pairs={{0,4},{2,6},{4,0},{6,2},{8,12},{10,14},{12,8},{14,10},{16,20},{18,... | collective-permute-start | bytes 1327112 | tf_op jit(solution)/shard_map/ppermute | solution.py:257
  22.4 14.9 %collective-permute-start.7 = (bf16[48,4608]{1,0:T(8,128)(2,1)S(1)}, bf16[48,4608]{1,0:T(8,128)(2,1)S(1)}, u32[]{:S(2)}, u32[]{:S(2)}) collective-permute-start(bf16[48,4608]{1,0:T(8,128)(2,1)S(1)} %collective-permute-done.outer_ref.refs_0_), channel_id=1, source_target_pairs={{0,2},{2,0},{12,14},{14,12},{16,18},{18,16},{28,30},{30,28},{4,8},... | collective-permute-start | bytes 1327112 | tf_op jit(solution)/shard_map/ppermute | solution.py:257
  25.9 11.5 %collective-permute-start.8 = (bf16[48,4608]{1,0:T(8,128)(2,1)S(1)}, bf16[48,4608]{1,0:T(8,128)(2,1)S(1)}, u32[]{:S(2)}, u32[]{:S(2)}) collective-permute-start(bf16[48,4608]{1,0:T(8,128)(2,1)S(1)} %collective-permute-done.1.refs_3_.outer_ref), channel_id=1, source_target_pairs={{0,16},{2,18},{12,28},{14,30},{16,0},{18,2},{28,12},{30,14},{4,20}... | collective-permute-start | bytes 1327112 | tf_op jit(solution)/shard_map/ppermute | solution.py:257
  27.9 28.4 %slice-start.1 = ((s8[7340032]{0:T(1024)(128)(4,1)}), s8[3145728]{0:T(1024)(128)(4,1)S(1)}, s32[]{:S(2)}) async-start(s8[7340032]{0:T(1024)(128)(4,1)} %bitcast.4), calls=%async_computation.1 | async-start | bytes 6291456
  27.9 16.9 %collective-permute-start.9 = (bf16[48,4608]{1,0:T(8,128)(2,1)S(1)}, bf16[48,4608]{1,0:T(8,128)(2,1)S(1)}, u32[]{:S(2)}, u32[]{:S(2)}) collective-permute-start(bf16[48,4608]{1,0:T(8,128)(2,1)S(1)} %pick.19), channel_id=1, source_target_pairs={{0,4},{2,6},{4,0},{6,2},{8,12},{10,14},{12,8},{14,10},{16,20},{18,... | collective-permute-start | bytes 1327112 | tf_op jit(solution)/shard_map/ppermute | solution.py:257
  33.6 13.3 %collective-permute-start.10 = (bf16[48,4608]{1,0:T(8,128)(2,1)S(1)}, bf16[48,4608]{1,0:T(8,128)(2,1)S(1)}, u32[]{:S(2)}, u32[]{:S(2)}) collective-permute-start(bf16[48,4608]{1,0:T(8,128)(2,1)S(1)} %get-tuple-element.422.outer_ref.refs_4_), channel_id=1, source_target_pairs={{0,2},{2,0},{12,14},{14,12},{16,18},{18,16},{28,30},{30,28},{4,6},... | collective-permute-start | bytes 1327112 | tf_op jit(solution)/shard_map/ppermute | solution.py:257
  35.4 11.5 %collective-permute-start.11 = (bf16[48,4608]{1,0:T(8,128)(2,1)S(1)}, bf16[48,4608]{1,0:T(8,128)(2,1)S(1)}, u32[]{:S(2)}, u32[]{:S(2)}) collective-permute-start(bf16[48,4608]{1,0:T(8,128)(2,1)S(1)} %pick.20), channel_id=1, source_target_pairs={{0,16},{2,18},{12,28},{14,30},{16,0},{18,2},{28,12},{30,14},{4,8},... | collective-permute-start | bytes 1327112 | tf_op jit(solution)/shard_map/ppermute | solution.py:257
  37.4 16.9 %collective-permute-start.12 = (bf16[48,4608]{1,0:T(8,128)(2,1)S(1)}, bf16[48,4608]{1,0:T(8,128)(2,1)S(1)}, u32[]{:S(2)}, u32[]{:S(2)}) collective-permute-start(bf16[48,4608]{1,0:T(8,128)(2,1)S(1)} %pick.21), channel_id=1, source_target_pairs={{0,4},{2,6},{4,0},{6,2},{8,12},{10,14},{12,8},{14,10},{16,20},{18,... | collective-permute-start | bytes 1327112 | tf_op jit(solution)/shard_map/ppermute | solution.py:257
  43.1 13.2 %copy-start = (bf16[1,256,4096]{2,1,0:T(8,128)(2,1)S(1)}, bf16[1,256,4096]{2,1,0:T(8,128)(2,1)}, u32[]{:S(2)}) copy-start(bf16[1,256,4096]{2,1,0:T(8,128)(2,1)} %param.4) | copy-start | bytes 6291460
  43.1 13.2 %copy-start.2 = (bf16[48,4608]{1,0:T(8,128)(2,1)S(1)}, bf16[48,4608]{1,0:T(8,128)(2,1)}, u32[]{:S(2)}) copy-start(bf16[48,4608]{1,0:T(8,128)(2,1)} %first_cut.1.refs_0_) | copy-start | bytes 1327108
  43.1 16.3 %collective-permute-start.13 = (bf16[48,4608]{1,0:T(8,128)(2,1)S(1)}, bf16[48,4608]{1,0:T(8,128)(2,1)S(1)}, u32[]{:S(2)}, u32[]{:S(2)}) collective-permute-start(bf16[48,4608]{1,0:T(8,128)(2,1)S(1)} %pick.22), channel_id=1, source_target_pairs={{0,2},{2,0},{12,14},{14,12},{16,18},{18,16},{28,30},{30,28},{4,6},... | collective-permute-start | bytes 1327112 | tf_op jit(solution)/shard_map/ppermute | solution.py:257
  44.8 14.6 %collective-permute-start.14 = (bf16[48,4608]{1,0:T(8,128)(2,1)S(1)}, bf16[48,4608]{1,0:T(8,128)(2,1)S(1)}, u32[]{:S(2)}, u32[]{:S(2)}) collective-permute-start(bf16[48,4608]{1,0:T(8,128)(2,1)S(1)} %collective-permute-done.6.outer_ref.refs_3_.refs_1_), channel_id=1, source_target_pairs={{0,16},{2,18},{12,28},{14,30},{16,0},{18,2},{28,12},{30,14},{4,8},... | collective-permute-start | bytes 1327112 | tf_op jit(solution)/shard_map/ppermute | solution.py:257
  46.9 16.9 %collective-permute-start.15 = (bf16[48,4608]{1,0:T(8,128)(2,1)S(1)}, bf16[48,4608]{1,0:T(8,128)(2,1)S(1)}, u32[]{:S(2)}, u32[]{:S(2)}) collective-permute-start(bf16[48,4608]{1,0:T(8,128)(2,1)S(1)} %pick.23), channel_id=1, source_target_pairs={{0,4},{2,6},{4,0},{6,2},{8,12},{10,14},{12,8},{14,10},{16,20},{18,... | collective-permute-start | bytes 1327112 | tf_op jit(solution)/shard_map/ppermute | solution.py:257
  52.5 13.3 %collective-permute-start.16 = (bf16[48,4608]{1,0:T(8,128)(2,1)S(1)}, bf16[48,4608]{1,0:T(8,128)(2,1)S(1)}, u32[]{:S(2)}, u32[]{:S(2)}) collective-permute-start(bf16[48,4608]{1,0:T(8,128)(2,1)S(1)} %collective-permute-done.9.outer_ref.refs_2_.refs_0_), channel_id=1, source_target_pairs={{0,2},{2,0},{12,14},{14,12},{16,18},{18,16},{28,30},{30,28},{4,8},... | collective-permute-start | bytes 1327112 | tf_op jit(solution)/shard_map/ppermute | solution.py:257
  54.3 11.5 %collective-permute-start.17 = (bf16[48,4608]{1,0:T(8,128)(2,1)S(1)}, bf16[48,4608]{1,0:T(8,128)(2,1)S(1)}, u32[]{:S(2)}, u32[]{:S(2)}) collective-permute-start(bf16[48,4608]{1,0:T(8,128)(2,1)S(1)} %pick.24), channel_id=1, source_target_pairs={{0,16},{2,18},{12,28},{14,30},{16,0},{18,2},{28,12},{30,14},{4,20}... | collective-permute-start | bytes 1327112 | tf_op jit(solution)/shard_map/ppermute | solution.py:257
  59.5 13.8 %collective-permute-start.18 = (bf16[48,4608]{1,0:T(8,128)(2,1)S(1)}, bf16[48,4608]{1,0:T(8,128)(2,1)S(1)}, u32[]{:S(2)}, u32[]{:S(2)}) collective-permute-start(bf16[48,4608]{1,0:T(8,128)(2,1)S(1)} %pick.25), channel_id=1, source_target_pairs={{0,4},{2,6},{4,0},{6,2},{8,12},{10,14},{12,8},{14,10},{16,20},{18,... | collective-permute-start | bytes 1327112 | tf_op jit(solution)/shard_map/ppermute | solution.py:257
  62.0 13.2 %collective-permute-start.19 = (bf16[48,4608]{1,0:T(8,128)(2,1)S(1)}, bf16[48,4608]{1,0:T(8,128)(2,1)S(1)}, u32[]{:S(2)}, u32[]{:S(2)}) collective-permute-start(bf16[48,4608]{1,0:T(8,128)(2,1)S(1)} %pick.26), channel_id=1, source_target_pairs={{0,2},{2,0},{12,14},{14,12},{16,18},{18,16},{28,30},{30,28},{4,8},... | collective-permute-start | bytes 1327112 | tf_op jit(solution)/shard_map/ppermute | solution.py:257
  63.8 11.5 %collective-permute-start.20 = (bf16[48,4608]{1,0:T(8,128)(2,1)S(1)}, bf16[48,4608]{1,0:T(8,128)(2,1)S(1)}, u32[]{:S(2)}, u32[]{:S(2)}) collective-permute-start(bf16[48,4608]{1,0:T(8,128)(2,1)S(1)} %pick.27), channel_id=1, source_target_pairs={{0,16},{2,18},{12,28},{14,30},{16,0},{18,2},{28,12},{30,14},{4,20}... | collective-permute-start | bytes 1327112 | tf_op jit(solution)/shard_map/ppermute | solution.py:257
  65.8 16.2 %collective-permute-start.21 = (bf16[48,4608]{1,0:T(8,128)(2,1)S(1)}, bf16[48,4608]{1,0:T(8,128)(2,1)S(1)}, u32[]{:S(2)}, u32[]{:S(2)}) collective-permute-start(bf16[48,4608]{1,0:T(8,128)(2,1)S(1)} %collective-permute-done.16.outer_ref.refs_5_.refs_2_), channel_id=1, source_target_pairs={{0,4},{2,6},{4,0},{6,2},{8,12},{10,14},{12,8},{14,10},{16,20},{18,... | collective-permute-start | bytes 1327112 | tf_op jit(solution)/shard_map/ppermute | solution.py:257
  71.4 13.9 %collective-permute-start.22 = (bf16[48,4608]{1,0:T(8,128)(2,1)S(1)}, bf16[48,4608]{1,0:T(8,128)(2,1)S(1)}, u32[]{:S(2)}, u32[]{:S(2)}) collective-permute-start(bf16[48,4608]{1,0:T(8,128)(2,1)S(1)} %pick.28), channel_id=1, source_target_pairs={{0,2},{2,0},{12,14},{14,12},{16,18},{18,16},{28,30},{30,28},{4,6},... | collective-permute-start | bytes 1327112 | tf_op jit(solution)/shard_map/ppermute | solution.py:257
  73.3 13.1 %collective-permute-start.23 = (bf16[48,4608]{1,0:T(8,128)(2,1)S(1)}, bf16[48,4608]{1,0:T(8,128)(2,1)S(1)}, u32[]{:S(2)}, u32[]{:S(2)}) collective-permute-start(bf16[48,4608]{1,0:T(8,128)(2,1)S(1)} %pick.29), channel_id=1, source_target_pairs={{0,16},{2,18},{12,28},{14,30},{16,0},{18,2},{28,12},{30,14},{4,8},... | collective-permute-start | bytes 1327112 | tf_op jit(solution)/shard_map/ppermute | solution.py:257
  75.3 17.4 %collective-permute-start.27 = (bf16[48,4608]{1,0:T(8,128)(2,1)S(1)}, bf16[48,4608]{1,0:T(8,128)(2,1)S(1)}, u32[]{:S(2)}, u32[]{:S(2)}) collective-permute-start(bf16[48,4608]{1,0:T(8,128)(2,1)S(1)} %pick.30), channel_id=1, source_target_pairs={{0,2},{2,0},{12,14},{14,12},{16,18},{18,16},{28,30},{30,28},{4,8},... | collective-permute-start | bytes 1327112 | tf_op jit(solution)/shard_map/ppermute | solution.py:257
  76.9 19.2 %collective-permute-start.28 = (bf16[48,4608]{1,0:T(8,128)(2,1)S(1)}, bf16[48,4608]{1,0:T(8,128)(2,1)S(1)}, u32[]{:S(2)}, u32[]{:S(2)}) collective-permute-start(bf16[48,4608]{1,0:T(8,128)(2,1)S(1)} %pick.31), channel_id=1, source_target_pairs={{0,16},{2,18},{12,28},{14,30},{16,0},{18,2},{28,12},{30,14},{4,20}... | collective-permute-start | bytes 1327112 | tf_op jit(solution)/shard_map/ppermute | solution.py:257
  81.9 14.2 %collective-permute-start.29 = (bf16[48,4608]{1,0:T(8,128)(2,1)S(1)}, bf16[48,4608]{1,0:T(8,128)(2,1)S(1)}, u32[]{:S(2)}, u32[]{:S(2)}) collective-permute-start(bf16[48,4608]{1,0:T(8,128)(2,1)S(1)} %pick.32), channel_id=1, source_target_pairs={{0,4},{2,6},{4,0},{6,2},{8,12},{10,14},{12,8},{14,10},{16,20},{18,... | collective-permute-start | bytes 1327112 | tf_op jit(solution)/shard_map/ppermute | solution.py:257
  87.4 4.1 %collective-permute-start.26 = (f32[48,256]{1,0:T(8,128)S(1)}, f32[48,256]{1,0:T(8,128)S(1)}, u32[]{:S(2)}, u32[]{:S(2)}) collective-permute-start(f32[48,256]{1,0:T(8,128)S(1)} %get-tuple-element.550), channel_id=1, source_target_pairs={{0,1},{1,0},{2,3},{3,2},{4,5},{5,4},{6,7},{7,6},{8,9},{9,8},{10,11... | collective-permute-start | bytes 147464 | tf_op jit(solution)/shard_map/ppermute | solution.py:187
  87.5 16.3 %collective-permute-start.33 = (bf16[48,4608]{1,0:T(8,128)(2,1)S(1)}, bf16[48,4608]{1,0:T(8,128)(2,1)S(1)}, u32[]{:S(2)}, u32[]{:S(2)}) collective-permute-start(bf16[48,4608]{1,0:T(8,128)(2,1)S(1)} %collective-permute-done.3.inner_ref.refs_1_.refs_0_), channel_id=1, source_target_pairs={{0,2},{2,0},{12,14},{14,12},{16,18},{18,16},{28,30},{30,28},{1,3},... | collective-permute-start | bytes 1327112 | tf_op jit(solution)/shard_map/ppermute | solution.py:257
  91.5 14.8 %collective-permute-start.34 = (bf16[48,4608]{1,0:T(8,128)(2,1)S(1)}, bf16[48,4608]{1,0:T(8,128)(2,1)S(1)}, u32[]{:S(2)}, u32[]{:S(2)}) collective-permute-start(bf16[48,4608]{1,0:T(8,128)(2,1)S(1)} %pick.33), channel_id=1, source_target_pairs={{0,4},{2,6},{4,0},{6,2},{8,12},{10,14},{12,8},{14,10},{16,20},{18,... | collective-permute-start | bytes 1327112 | tf_op jit(solution)/shard_map/ppermute | solution.py:257
  92.7 13.8 %collective-permute-start.35 = (bf16[48,4608]{1,0:T(8,128)(2,1)S(1)}, bf16[48,4608]{1,0:T(8,128)(2,1)S(1)}, u32[]{:S(2)}, u32[]{:S(2)}) collective-permute-start(bf16[48,4608]{1,0:T(8,128)(2,1)S(1)} %collective-permute-done.3.inner_ref.refs_1_.refs_0_), channel_id=1, source_target_pairs={{0,16},{2,18},{12,28},{14,30},{16,0},{18,2},{28,12},{30,14},{1,17}... | collective-permute-start | bytes 1327112 | tf_op jit(solution)/shard_map/ppermute | solution.py:257
  96.1 2.9 %collective-permute-start.25 = (f32[288,256]{1,0:T(8,128)S(1)}, f32[288,256]{1,0:T(8,128)S(1)}, u32[]{:S(2)}, u32[]{:S(2)}) collective-permute-start(f32[288,256]{1,0:T(8,128)S(1)} %get-tuple-element.548.in_b), channel_id=1, source_target_pairs={{0,1},{1,0},{2,3},{3,2},{4,5},{5,4},{6,7},{7,6},{8,9},{9,8},{10,11... | collective-permute-start | bytes 884744 | tf_op jit(solution)/shard_map/ppermute | solution.py:187
  96.2 2.6 %collective-permute-start.24 = (f32[96,256]{1,0:T(8,128)S(1)}, f32[96,256]{1,0:T(8,128)S(1)}, u32[]{:S(2)}, u32[]{:S(2)}) collective-permute-start(f32[96,256]{1,0:T(8,128)S(1)} %get-tuple-element.547.in_a), channel_id=1, source_target_pairs={{0,1},{1,0},{2,3},{3,2},{4,5},{5,4},{6,7},{7,6},{8,9},{9,8},{10,11... | collective-permute-start | bytes 294920 | tf_op jit(solution)/shard_map/ppermute | solution.py:187
  98.8 2.0 %collective-permute-start.30 = (f32[96,256]{1,0:T(8,128)S(1)}, f32[96,256]{1,0:T(8,128)S(1)}, u32[]{:S(2)}, u32[]{:S(2)}) collective-permute-start(f32[96,256]{1,0:T(8,128)S(1)} %get-tuple-element.569), channel_id=1, source_target_pairs={{0,1},{1,0},{2,3},{3,2},{4,5},{5,4},{6,7},{7,6},{8,9},{9,8},{10,11... | collective-permute-start | bytes 294920 | tf_op jit(solution)/shard_map/ppermute | solution.py:187
  99.2 15.5 %collective-permute-start.39 = (bf16[24,384]{1,0:T(8,128)(2,1)S(1)}, bf16[24,384]{1,0:T(8,128)(2,1)S(1)}, u32[]{:S(2)}, u32[]{:S(2)}) collective-permute-start(bf16[24,384]{1,0:T(8,128)(2,1)S(1)} %get-tuple-element.584), channel_id=1, source_target_pairs={{0,2},{2,0},{4,6},{6,4},{8,10},{10,8},{12,14},{14,12},{1,3},{3,1},... | collective-permute-start | bytes 55304 | tf_op jit(solution)/shard_map/ppermute | solution.py:357
  101.0 7.6 %collective-permute-start.32 = (bf16[24,384]{1,0:T(8,128)(2,1)S(1)}, bf16[24,384]{1,0:T(8,128)(2,1)S(1)}, u32[]{:S(2)}, u32[]{:S(2)}) collective-permute-start(bf16[24,384]{1,0:T(8,128)(2,1)S(1)} %get-tuple-element.571), channel_id=1, source_target_pairs={{0,14},{2,12},{4,10},{6,8},{8,6},{10,4},{12,2},{14,0},{1,15},{3,13... | collective-permute-start | bytes 55304 | tf_op jit(solution)/shard_map/ppermute | solution.py:357
  103.9 8.3 %collective-permute-start.31 = (bf16[24,384]{1,0:T(8,128)(2,1)S(1)}, bf16[24,384]{1,0:T(8,128)(2,1)S(1)}, u32[]{:S(2)}, u32[]{:S(2)}) collective-permute-start(bf16[24,384]{1,0:T(8,128)(2,1)S(1)} %get-tuple-element.570), channel_id=1, source_target_pairs={{0,12},{2,14},{4,8},{6,10},{8,4},{10,6},{12,0},{14,2},{1,13},{3,15... | collective-permute-start | bytes 55304 | tf_op jit(solution)/shard_map/ppermute | solution.py:357
  108.4 3.8 %collective-permute-start.36 = (f32[48,256]{1,0:T(8,128)S(1)}, f32[48,256]{1,0:T(8,128)S(1)}, u32[]{:S(2)}, u32[]{:S(2)}) collective-permute-start(f32[48,256]{1,0:T(8,128)S(1)} %get-tuple-element.578), channel_id=1, source_target_pairs={{0,1},{1,0},{2,3},{3,2},{4,5},{5,4},{6,7},{7,6},{8,9},{9,8},{10,11... | collective-permute-start | bytes 147464 | tf_op jit(solution)/shard_map/ppermute | solution.py:187
  108.5 6.2 %collective-permute-start.41 = (bf16[24,384]{1,0:T(8,128)(2,1)S(1)}, bf16[24,384]{1,0:T(8,128)(2,1)S(1)}, u32[]{:S(2)}, u32[]{:S(2)}) collective-permute-start(bf16[24,384]{1,0:T(8,128)(2,1)S(1)} %get-tuple-element.586), channel_id=1, source_target_pairs={{0,10},{2,8},{4,14},{6,12},{8,2},{10,0},{12,6},{14,4},{1,11},{3,9}... | collective-permute-start | bytes 55304 | tf_op jit(solution)/shard_map/ppermute | solution.py:357
  108.6 6.1 %collective-permute-start.40 = (bf16[24,384]{1,0:T(8,128)(2,1)S(1)}, bf16[24,384]{1,0:T(8,128)(2,1)S(1)}, u32[]{:S(2)}, u32[]{:S(2)}) collective-permute-start(bf16[24,384]{1,0:T(8,128)(2,1)S(1)} %get-tuple-element.585), channel_id=1, source_target_pairs={{0,8},{2,10},{4,12},{6,14},{8,0},{10,2},{12,4},{14,6},{1,9},{3,11}... | collective-permute-start | bytes 55304 | tf_op jit(solution)/shard_map/ppermute | solution.py:357
  112.4 4.7 %collective-permute-start.38 = (bf16[24,384]{1,0:T(8,128)(2,1)S(1)}, bf16[24,384]{1,0:T(8,128)(2,1)S(1)}, u32[]{:S(2)}, u32[]{:S(2)}) collective-permute-start(bf16[24,384]{1,0:T(8,128)(2,1)S(1)} %get-tuple-element.583), channel_id=1, source_target_pairs={{0,6},{2,4},{4,2},{6,0},{8,14},{10,12},{12,10},{14,8},{1,7},{3,5},... | collective-permute-start | bytes 55304 | tf_op jit(solution)/shard_map/ppermute | solution.py:357
  113.2 4.0 %collective-permute-start.37 = (bf16[24,384]{1,0:T(8,128)(2,1)S(1)}, bf16[24,384]{1,0:T(8,128)(2,1)S(1)}, u32[]{:S(2)}, u32[]{:S(2)}) collective-permute-start(bf16[24,384]{1,0:T(8,128)(2,1)S(1)} %get-tuple-element.582), channel_id=1, source_target_pairs={{0,4},{2,6},{4,0},{6,2},{8,12},{10,14},{12,8},{14,10},{1,5},{3,7},... | collective-permute-start | bytes 55304 | tf_op jit(solution)/shard_map/ppermute | solution.py:357

commit v8 on v7

--- a/solution.py
+++ b/solution.py
@@ -367,7 +367,7 @@
         units[name] = value
     keep_b, send_b = rotate("23", ["m1", "t1"], [acc], 2 * rows, True)
     far = squares(squares_kernel, "squares", [block] * 4, rot_in, keep_b, swap_core(send_b))
-    waiting = {1: near[1], 4: far[0], 5: far[1], 6: far[2], 7: far[3]}
+    waiting = {6: far[2], 7: far[3]}
     early = near[0].astype(jnp.float32)
     for k in (6, 7):
         early = early + to_owner(k, waiting[k])
@@ -378,8 +378,9 @@
     early, come_c = lax.optimization_barrier((early, swap_core(send_c)))
     late = squares(squares_kernel, "squares", [block] * 2, rot_in, keep_c, come_c)
     total = early + to_owner(2, late[0]) + to_owner(3, late[1])
-    for k in (1, 4, 5):
-        total = total + to_owner(k, waiting[k])
+    got = to_owner(1, jnp.concatenate([near[1], far[1]], axis=0))
+    half = rows // 2
+    total = total + got[:half] + to_owner(4, far[0].astype(jnp.float32) + got[half:])
     return total * (1.0 / 8)
 
 

time: 118 us -> 123 us (1.042)
  waiting for transfers between devices: 20.9 us -> 30.4 us
  starting transfers between devices: 83.3 us -> 78.7 us
    ppermute x7 -> x6, starting transfers between devices: 12.8 us -> 8.26 us  [to_owner(): lax.ppermute(value, 'dp', [(i, i ^ k) for i in range(8)])]
    ppermute x30, waiting for transfers between devices: 18.5 us -> 22.8 us  [send(): return lax.ppermute(value, ('group', 'dp'), pairs)]
    ppermute x7 -> x6, waiting for transfers between devices: 2.44 us -> 6.66 us  [to_owner(): lax.ppermute(value, 'dp', [(i, i ^ k) for i in range(8)])]
  transfers between devices with their start and end apart: 42 -> 41, of which waited for: 12 -> 18; matrix products, arithmetic and copies ran while one was open for 0% -> 0% of each run, Pallas kernels for 9% -> 8%
where the time goes in v8:
time: 123 us
  starting transfers between devices  78.7 us (64%)
  waiting for transfers between devices  30.4 us (25%)
  Pallas kernels  12.5 us (10%)
    ppermute x30, starting transfers between devices, send(): return lax.ppermute(value, ('group', 'dp'), pairs)  69.6 us
    ppermute x30, waiting for transfers between devices, send(): return lax.ppermute(value, ('group', 'dp'), pairs)  22.8 us
    pallas_call x5, Pallas kernels, rotate(): pl.pallas_call(functools.partial(rotate_kernel, (terms, acc_from, last),...  9.2 us
    ppermute x6, starting transfers between devices, to_owner(): lax.ppermute(value, 'dp', [(i, i ^ k) for i in range(8)])  8.26 us
    ppermute x6, waiting for transfers between devices, to_owner(): lax.ppermute(value, 'dp', [(i, i ^ k) for i in range(8)])  6.66 us
  transfers between devices with their start and end apart: 41, of which 18 were waited for; matrix products, arithmetic and copies ran while one was open for 0% of the time, Pallas kernels for 8%

profile of v8, /device:TPU:0, one launch (start us, length us, event | category | flops | bytes accessed | tf_op | source)
XLA Modules:
  0.0 122.8 jit_solution(3268378773805412152)
XLA Ops:
  0.0 1.9 %first_cut.1.refs_0_ = bf16[48,4608]{1,0:T(8,128)(2,1)} custom-call(bf16[48,4096]{1,0:T(8,128)(2,1)} %bitcast.18, bf16[48,14336]{1,0:T(8,128)(2,1)} %bitcast.16), custom_call_target="tpu_custom_call" | custom-call | tf_op jit(solution)/shard_map/first_cut/pallas_call | solution.py:190
  2.1 3.1 %collective-permute-start = (bf16[48,4608]{1,0:T(8,128)(2,1)}, bf16[48,4608]{1,0:T(8,128)(2,1)S(1)}, u32[]{:S(2)}, u32[]{:S(2)}) collective-permute-start(bf16[48,4608]{1,0:T(8,128)(2,1)} %first_cut.1.refs_0_), channel_id=1, source_target_pairs={{0,4},{2,6},{4,0},{6,2},{8,12},{10,14},{12,8},{14,10},{16,20},{18,... | collective-permute-start | bytes 1327112 | tf_op jit(solution)/shard_map/ppermute | solution.py:257
  5.2 1.5 %collective-permute-start.1 = (bf16[48,4608]{1,0:T(8,128)(2,1)S(1)}, bf16[48,4608]{1,0:T(8,128)(2,1)S(1)}, u32[]{:S(2)}, u32[]{:S(2)}) collective-permute-start(bf16[48,4608]{1,0:T(8,128)(2,1)S(1)} %get-tuple-element.421.inner_ref.outer_ref.refs_2_), channel_id=1, source_target_pairs={{0,2},{2,0},{12,14},{14,12},{16,18},{18,16},{28,30},{30,28},{4,6},... | collective-permute-start | bytes 1327112 | tf_op jit(solution)/shard_map/ppermute | solution.py:257
  7.5 4.4 %collective-permute-start.3 = (bf16[48,4608]{1,0:T(8,128)(2,1)S(1)}, bf16[48,4608]{1,0:T(8,128)(2,1)S(1)}, u32[]{:S(2)}, u32[]{:S(2)}) collective-permute-start(bf16[48,4608]{1,0:T(8,128)(2,1)S(1)} %pick.17), channel_id=1, source_target_pairs={{0,4},{2,6},{4,0},{6,2},{8,12},{10,14},{12,8},{14,10},{16,20},{18,... | collective-permute-start | bytes 1327112 | tf_op jit(solution)/shard_map/ppermute | solution.py:257
  12.4 4.0 %collective-permute-done.outer_ref.refs_0_ = bf16[48,4608]{1,0:T(8,128)(2,1)S(1)} collective-permute-done((bf16[48,4608]{1,0:T(8,128)(2,1)}, bf16[48,4608]{1,0:T(8,128)(2,1)S(1)}, u32[]{:S(2)}, u32[]{:S(2)}) %collective-permute-start) | collective-permute-done | bytes 442400 | tf_op jit(solution)/shard_map/ppermute | solution.py:257
  17.1 1.2 collective-permute-done.1.refs_3_.outer_ref
  18.3 4.1 %collective-permute-start.6 = (bf16[48,4608]{1,0:T(8,128)(2,1)S(1)}, bf16[48,4608]{1,0:T(8,128)(2,1)S(1)}, u32[]{:S(2)}, u32[]{:S(2)}) collective-permute-start(bf16[48,4608]{1,0:T(8,128)(2,1)S(1)} %pick.18), channel_id=1, source_target_pairs={{0,4},{2,6},{4,0},{6,2},{8,12},{10,14},{12,8},{14,10},{16,20},{18,... | collective-permute-start | bytes 1327112 | tf_op jit(solution)/shard_map/ppermute | solution.py:257
  22.4 1.2 collective-permute-start.7
  23.6 2.3 %collective-permute-done.3.inner_ref.refs_1_.refs_0_ = bf16[48,4608]{1,0:T(8,128)(2,1)S(1)} collective-permute-done((bf16[48,4608]{1,0:T(8,128)(2,1)S(1)}, bf16[48,4608]{1,0:T(8,128)(2,1)S(1)}, u32[]{:S(2)}, u32[]{:S(2)}) %collective-permute-start.3) | collective-permute-done | bytes 442400 | tf_op jit(solution)/shard_map/ppermute | solution.py:257
  25.9 2.0 %collective-permute-start.8 = (bf16[48,4608]{1,0:T(8,128)(2,1)S(1)}, bf16[48,4608]{1,0:T(8,128)(2,1)S(1)}, u32[]{:S(2)}, u32[]{:S(2)}) collective-permute-start(bf16[48,4608]{1,0:T(8,128)(2,1)S(1)} %collective-permute-done.1.refs_3_.outer_ref), channel_id=1, source_target_pairs={{0,16},{2,18},{12,28},{14,30},{16,0},{18,2},{28,12},{30,14},{4,20}... | collective-permute-start | bytes 1327112 | tf_op jit(solution)/shard_map/ppermute | solution.py:257
  27.9 5.7 %collective-permute-start.9 = (bf16[48,4608]{1,0:T(8,128)(2,1)S(1)}, bf16[48,4608]{1,0:T(8,128)(2,1)S(1)}, u32[]{:S(2)}, u32[]{:S(2)}) collective-permute-start(bf16[48,4608]{1,0:T(8,128)(2,1)S(1)} %pick.19), channel_id=1, source_target_pairs={{0,4},{2,6},{4,0},{6,2},{8,12},{10,14},{12,8},{14,10},{16,20},{18,... | collective-permute-start | bytes 1327112 | tf_op jit(solution)/shard_map/ppermute | solution.py:257
  33.6 1.5 %collective-permute-start.10 = (bf16[48,4608]{1,0:T(8,128)(2,1)S(1)}, bf16[48,4608]{1,0:T(8,128)(2,1)S(1)}, u32[]{:S(2)}, u32[]{:S(2)}) collective-permute-start(bf16[48,4608]{1,0:T(8,128)(2,1)S(1)} %get-tuple-element.422.outer_ref.refs_4_), channel_id=1, source_target_pairs={{0,2},{2,0},{12,14},{14,12},{16,18},{18,16},{28,30},{30,28},{4,6},... | collective-permute-start | bytes 1327112 | tf_op jit(solution)/shard_map/ppermute | solution.py:257
  35.4 2.0 %collective-permute-start.11 = (bf16[48,4608]{1,0:T(8,128)(2,1)S(1)}, bf16[48,4608]{1,0:T(8,128)(2,1)S(1)}, u32[]{:S(2)}, u32[]{:S(2)}) collective-permute-start(bf16[48,4608]{1,0:T(8,128)(2,1)S(1)} %pick.20), channel_id=1, source_target_pairs={{0,16},{2,18},{12,28},{14,30},{16,0},{18,2},{28,12},{30,14},{4,8},... | collective-permute-start | bytes 1327112 | tf_op jit(solution)/shard_map/ppermute | solution.py:257
  37.4 5.7 %collective-permute-start.12 = (bf16[48,4608]{1,0:T(8,128)(2,1)S(1)}, bf16[48,4608]{1,0:T(8,128)(2,1)S(1)}, u32[]{:S(2)}, u32[]{:S(2)}) collective-permute-start(bf16[48,4608]{1,0:T(8,128)(2,1)S(1)} %pick.21), channel_id=1, source_target_pairs={{0,4},{2,6},{4,0},{6,2},{8,12},{10,14},{12,8},{14,10},{16,20},{18,... | collective-permute-start | bytes 1327112 | tf_op jit(solution)/shard_map/ppermute | solution.py:257
  43.3 1.6 %collective-permute-done.9.outer_ref.refs_2_.refs_0_ = bf16[48,4608]{1,0:T(8,128)(2,1)S(1)} collective-permute-done((bf16[48,4608]{1,0:T(8,128)(2,1)S(1)}, bf16[48,4608]{1,0:T(8,128)(2,1)S(1)}, u32[]{:S(2)}, u32[]{:S(2)}) %collective-permute-start.9) | collective-permute-done | bytes 442400 | tf_op jit(solution)/shard_map/ppermute | solution.py:257
  44.8 2.0 %collective-permute-start.14 = (bf16[48,4608]{1,0:T(8,128)(2,1)S(1)}, bf16[48,4608]{1,0:T(8,128)(2,1)S(1)}, u32[]{:S(2)}, u32[]{:S(2)}) collective-permute-start(bf16[48,4608]{1,0:T(8,128)(2,1)S(1)} %collective-permute-done.6.outer_ref.refs_3_.refs_1_), channel_id=1, source_target_pairs={{0,16},{2,18},{12,28},{14,30},{16,0},{18,2},{28,12},{30,14},{4,8},... | collective-permute-start | bytes 1327112 | tf_op jit(solution)/shard_map/ppermute | solution.py:257
  46.9 5.6 %collective-permute-start.15 = (bf16[48,4608]{1,0:T(8,128)(2,1)S(1)}, bf16[48,4608]{1,0:T(8,128)(2,1)S(1)}, u32[]{:S(2)}, u32[]{:S(2)}) collective-permute-start(bf16[48,4608]{1,0:T(8,128)(2,1)S(1)} %pick.23), channel_id=1, source_target_pairs={{0,4},{2,6},{4,0},{6,2},{8,12},{10,14},{12,8},{14,10},{16,20},{18,... | collective-permute-start | bytes 1327112 | tf_op jit(solution)/shard_map/ppermute | solution.py:257
  52.7 1.7 %collective-permute-done.12.inner_ref.refs_6_ = bf16[48,4608]{1,0:T(8,128)(2,1)S(1)} collective-permute-done((bf16[48,4608]{1,0:T(8,128)(2,1)S(1)}, bf16[48,4608]{1,0:T(8,128)(2,1)S(1)}, u32[]{:S(2)}, u32[]{:S(2)}) %collective-permute-start.12) | collective-permute-done | bytes 442400 | tf_op jit(solution)/shard_map/ppermute | solution.py:257
  54.3 2.0 %collective-permute-start.17 = (bf16[48,4608]{1,0:T(8,128)(2,1)S(1)}, bf16[48,4608]{1,0:T(8,128)(2,1)S(1)}, u32[]{:S(2)}, u32[]{:S(2)}) collective-permute-start(bf16[48,4608]{1,0:T(8,128)(2,1)S(1)} %pick.24), channel_id=1, source_target_pairs={{0,16},{2,18},{12,28},{14,30},{16,0},{18,2},{28,12},{30,14},{4,20}... | collective-permute-start | bytes 1327112 | tf_op jit(solution)/shard_map/ppermute | solution.py:257
  56.3 3.1 %rotate.5 = (f32[96,256]{1,0:T(8,128)S(1)}, f32[48,256]{1,0:T(8,128)S(1)}, f32[48,256]{1,0:T(8,128)S(1)}) custom-call(bf16[256,4096]{1,0:T(8,128)(2,1)S(1)} %bitcast.11, bf16[256,14336]{1,0:T(8,128)(2,1)S(1)} %bitcast.6, bf16[48,4608]{1,0:T(8,128)(2,1)S(1)} %copy-done.2, bf16[48,4608]{1,0:T(8,128)(2,1)S(1)} %collective-permute-done.4.outer_ref.refs_1_, ...), custom_call_target="tpu_custom_call" | custom-call | flops 905969664 | bytes 3538944 | tf_op jit(solution)/shard_map/rotate/pallas_call | solution.py:228
  59.5 2.5 %collective-permute-start.18 = (bf16[48,4608]{1,0:T(8,128)(2,1)S(1)}, bf16[48,4608]{1,0:T(8,128)(2,1)S(1)}, u32[]{:S(2)}, u32[]{:S(2)}) collective-permute-start(bf16[48,4608]{1,0:T(8,128)(2,1)S(1)} %pick.25), channel_id=1, source_target_pairs={{0,4},{2,6},{4,0},{6,2},{8,12},{10,14},{12,8},{14,10},{16,20},{18,... | collective-permute-start | bytes 1327112 | tf_op jit(solution)/shard_map/ppermute | solution.py:257
  62.0 0.7 collective-permute-start.19
  62.8 1.0 collective-permute-done.15.outer_ref.inner_ref.refs_3_
  63.8 2.0 %collective-permute-start.20 = (bf16[48,4608]{1,0:T(8,128)(2,1)S(1)}, bf16[48,4608]{1,0:T(8,128)(2,1)S(1)}, u32[]{:S(2)}, u32[]{:S(2)}) collective-permute-start(bf16[48,4608]{1,0:T(8,128)(2,1)S(1)} %pick.27), channel_id=1, source_target_pairs={{0,16},{2,18},{12,28},{14,30},{16,0},{18,2},{28,12},{30,14},{4,20}... | collective-permute-start | bytes 1327112 | tf_op jit(solution)/shard_map/ppermute | solution.py:257
  65.8 5.6 %collective-permute-start.21 = (bf16[48,4608]{1,0:T(8,128)(2,1)S(1)}, bf16[48,4608]{1,0:T(8,128)(2,1)S(1)}, u32[]{:S(2)}, u32[]{:S(2)}) collective-permute-start(bf16[48,4608]{1,0:T(8,128)(2,1)S(1)} %collective-permute-done.16.outer_ref.refs_5_.refs_2_), channel_id=1, source_target_pairs={{0,4},{2,6},{4,0},{6,2},{8,12},{10,14},{12,8},{14,10},{16,20},{18,... | collective-permute-start | bytes 1327112 | tf_op jit(solution)/shard_map/ppermute | solution.py:257
  71.6 1.6 %collective-permute-done.18.outer_ref.refs_4_.refs_5_ = bf16[48,4608]{1,0:T(8,128)(2,1)S(1)} collective-permute-done((bf16[48,4608]{1,0:T(8,128)(2,1)S(1)}, bf16[48,4608]{1,0:T(8,128)(2,1)S(1)}, u32[]{:S(2)}, u32[]{:S(2)}) %collective-permute-start.18) | collective-permute-done | bytes 442400 | tf_op jit(solution)/shard_map/ppermute | solution.py:257
  73.3 2.0 %collective-permute-start.23 = (bf16[48,4608]{1,0:T(8,128)(2,1)S(1)}, bf16[48,4608]{1,0:T(8,128)(2,1)S(1)}, u32[]{:S(2)}, u32[]{:S(2)}) collective-permute-start(bf16[48,4608]{1,0:T(8,128)(2,1)S(1)} %pick.29), channel_id=1, source_target_pairs={{0,16},{2,18},{12,28},{14,30},{16,0},{18,2},{28,12},{30,14},{4,8},... | collective-permute-start | bytes 1327112 | tf_op jit(solution)/shard_map/ppermute | solution.py:257
  75.3 1.6 %collective-permute-start.27 = (bf16[48,4608]{1,0:T(8,128)(2,1)S(1)}, bf16[48,4608]{1,0:T(8,128)(2,1)S(1)}, u32[]{:S(2)}, u32[]{:S(2)}) collective-permute-start(bf16[48,4608]{1,0:T(8,128)(2,1)S(1)} %pick.30), channel_id=1, source_target_pairs={{0,2},{2,0},{12,14},{14,12},{16,18},{18,16},{28,30},{30,28},{4,8},... | collective-permute-start | bytes 1327112 | tf_op jit(solution)/shard_map/ppermute | solution.py:257
  76.9 1.5 %collective-permute-start.28 = (bf16[48,4608]{1,0:T(8,128)(2,1)S(1)}, bf16[48,4608]{1,0:T(8,128)(2,1)S(1)}, u32[]{:S(2)}, u32[]{:S(2)}) collective-permute-start(bf16[48,4608]{1,0:T(8,128)(2,1)S(1)} %pick.31), channel_id=1, source_target_pairs={{0,16},{2,18},{12,28},{14,30},{16,0},{18,2},{28,12},{30,14},{4,20}... | collective-permute-start | bytes 1327112 | tf_op jit(solution)/shard_map/ppermute | solution.py:257
  78.4 3.5 %collective-permute-done.21.refs_8_.refs_7_ = bf16[48,4608]{1,0:T(8,128)(2,1)S(1)} collective-permute-done((bf16[48,4608]{1,0:T(8,128)(2,1)S(1)}, bf16[48,4608]{1,0:T(8,128)(2,1)S(1)}, u32[]{:S(2)}, u32[]{:S(2)}) %collective-permute-start.21) | collective-permute-done | bytes 442400 | tf_op jit(solution)/shard_map/ppermute | solution.py:257
  81.9 2.3 %collective-permute-start.29 = (bf16[48,4608]{1,0:T(8,128)(2,1)S(1)}, bf16[48,4608]{1,0:T(8,128)(2,1)S(1)}, u32[]{:S(2)}, u32[]{:S(2)}) collective-permute-start(bf16[48,4608]{1,0:T(8,128)(2,1)S(1)} %pick.32), channel_id=1, source_target_pairs={{0,4},{2,6},{4,0},{6,2},{8,12},{10,14},{12,8},{14,10},{16,20},{18,... | collective-permute-start | bytes 1327112 | tf_op jit(solution)/shard_map/ppermute | solution.py:257
  84.2 1.1 rotate.6
  85.3 1.1 collective-permute-done.23.refs_6_.refs_10_
  86.4 1.1 rotate.7
  87.5 3.9 %collective-permute-start.33 = (bf16[48,4608]{1,0:T(8,128)(2,1)S(1)}, bf16[48,4608]{1,0:T(8,128)(2,1)S(1)}, u32[]{:S(2)}, u32[]{:S(2)}) collective-permute-start(bf16[48,4608]{1,0:T(8,128)(2,1)S(1)} %collective-permute-done.3.inner_ref.refs_1_.refs_0_), channel_id=1, source_target_pairs={{0,2},{2,0},{12,14},{14,12},{16,18},{18,16},{28,30},{30,28},{1,3},... | collective-permute-start | bytes 1327112 | tf_op jit(solution)/shard_map/ppermute | solution.py:257
  91.5 1.2 collective-permute-start.34
  92.7 3.4 %collective-permute-start.35 = (bf16[48,4608]{1,0:T(8,128)(2,1)S(1)}, bf16[48,4608]{1,0:T(8,128)(2,1)S(1)}, u32[]{:S(2)}, u32[]{:S(2)}) collective-permute-start(bf16[48,4608]{1,0:T(8,128)(2,1)S(1)} %collective-permute-done.3.inner_ref.refs_1_.refs_0_), channel_id=1, source_target_pairs={{0,16},{2,18},{12,28},{14,30},{16,0},{18,2},{28,12},{30,14},{1,17}... | collective-permute-start | bytes 1327112 | tf_op jit(solution)/shard_map/ppermute | solution.py:257
  96.7 2.1 %rotate.8 = (f32[96,256]{1,0:T(8,128)S(1)}, f32[96,256]{1,0:T(8,128)S(1)}) custom-call(bf16[256,4096]{1,0:T(8,128)(2,1)S(1)} %bitcast.14, bf16[256,14336]{1,0:T(8,128)(2,1)S(1)} %bitcast.9, bf16[48,4608]{1,0:T(8,128)(2,1)S(1)} %collective-permute-done.9.outer_ref.refs_2_.refs_0_, ...), custom_call_target="tpu_custom_call" | custom-call | flops 905969664 | bytes 5750784 | tf_op jit(solution)/shard_map/rotate/pallas_call | solution.py:228
  99.2 1.0 collective-permute-done.30.come
  100.4 1.6 %collective-permute-start.39 = (bf16[48,384]{1,0:T(8,128)(2,1)S(1)}, bf16[48,384]{1,0:T(8,128)(2,1)S(1)}, u32[]{:S(2)}, u32[]{:S(2)}) collective-permute-start(bf16[48,384]{1,0:T(8,128)(2,1)S(1)} %pad_maximum_fusion), channel_id=1, source_target_pairs={{0,2},{2,0},{4,6},{6,4},{8,10},{10,8},{12,14},{14,12},{1,3},{3,1},... | collective-permute-start | bytes 110600 | tf_op jit(solution)/shard_map/ppermute | solution.py:357
  102.2 1.6 %collective-permute-done.34.refs_3_ = bf16[48,4608]{1,0:T(8,128)(2,1)S(1)} collective-permute-done((bf16[48,4608]{1,0:T(8,128)(2,1)S(1)}, bf16[48,4608]{1,0:T(8,128)(2,1)S(1)}, u32[]{:S(2)}, u32[]{:S(2)}) %collective-permute-start.34) | collective-permute-done | bytes 442400 | tf_op jit(solution)/shard_map/ppermute | solution.py:257
  103.9 2.7 %collective-permute-done.35.refs_4_ = bf16[48,4608]{1,0:T(8,128)(2,1)S(1)} collective-permute-done((bf16[48,4608]{1,0:T(8,128)(2,1)S(1)}, bf16[48,4608]{1,0:T(8,128)(2,1)S(1)}, u32[]{:S(2)}, u32[]{:S(2)}) %collective-permute-start.35) | collective-permute-done | bytes 442400 | tf_op jit(solution)/shard_map/ppermute | solution.py:257
  106.5 1.9 %rotate.9 = (f32[48,256]{1,0:T(8,128)S(1)}, f32[48,256]{1,0:T(8,128)S(1)}) custom-call(bf16[256,4096]{1,0:T(8,128)(2,1)S(1)} %bitcast.15, bf16[256,14336]{1,0:T(8,128)(2,1)S(1)} %bitcast.10, bf16[48,4608]{1,0:T(8,128)(2,1)S(1)} %collective-permute-done.3.inner_ref.refs_1_.refs_0_, bf16[48,4608]{1,0:T(8,128)(2,1)S(1)} %collective-permute-done.6.outer_ref.refs_3_.refs_1_, ...), custom_call_target="tpu_custom_call" | custom-call | flops 452984832 | bytes 3096576 | tf_op jit(solution)/shard_map/rotate/pallas_call | solution.py:228
  108.5 2.9 %collective-permute-start.32 = (bf16[24,384]{1,0:T(8,128)(2,1)S(1)}, bf16[24,384]{1,0:T(8,128)(2,1)S(1)}, u32[]{:S(2)}, u32[]{:S(2)}) collective-permute-start(bf16[24,384]{1,0:T(8,128)(2,1)S(1)} %get-tuple-element.571), channel_id=1, source_target_pairs={{0,14},{2,12},{4,10},{6,8},{8,6},{10,4},{12,2},{14,0},{1,15},{3,13... | collective-permute-start | bytes 55304 | tf_op jit(solution)/shard_map/ppermute | solution.py:357
  112.2 2.8 %collective-permute-done.32 = bf16[24,384]{1,0:T(8,128)(2,1)S(1)} collective-permute-done((bf16[24,384]{1,0:T(8,128)(2,1)S(1)}, bf16[24,384]{1,0:T(8,128)(2,1)S(1)}, u32[]{:S(2)}, u32[]{:S(2)}) %collective-permute-start.32) | collective-permute-done | bytes 18464 | tf_op jit(solution)/shard_map/ppermute | solution.py:357
  115.0 1.9 %collective-permute-done.31 = bf16[24,384]{1,0:T(8,128)(2,1)S(1)} collective-permute-done((bf16[24,384]{1,0:T(8,128)(2,1)S(1)}, bf16[24,384]{1,0:T(8,128)(2,1)S(1)}, u32[]{:S(2)}, u32[]{:S(2)}) %collective-permute-start.31) | collective-permute-done | bytes 18464 | tf_op jit(solution)/shard_map/ppermute | solution.py:357
  117.2 3.0 %collective-permute-start.37 = (bf16[24,384]{1,0:T(8,128)(2,1)S(1)}, bf16[24,384]{1,0:T(8,128)(2,1)S(1)}, u32[]{:S(2)}, u32[]{:S(2)}) collective-permute-start(bf16[24,384]{1,0:T(8,128)(2,1)S(1)} %get-tuple-element.582), channel_id=1, source_target_pairs={{0,4},{2,6},{4,0},{6,2},{8,12},{10,14},{12,8},{14,10},{1,5},{3,7},... | collective-permute-start | bytes 55304 | tf_op jit(solution)/shard_map/ppermute | solution.py:357
  120.2 1.7 %collective-permute-done.38 = bf16[24,384]{1,0:T(8,128)(2,1)S(1)} collective-permute-done((bf16[24,384]{1,0:T(8,128)(2,1)S(1)}, bf16[24,384]{1,0:T(8,128)(2,1)S(1)}, u32[]{:S(2)}, u32[]{:S(2)}) %collective-permute-start.38) | collective-permute-done | bytes 18464 | tf_op jit(solution)/shard_map/ppermute | solution.py:357
  (79 shorter events, 6.9 us)
Async XLA Ops:
  0.0 2.0 %copy-start.3 = (bf16[4096,48]{0,1:T(8,128)(2,1)S(1)}, bf16[4096,48]{0,1:T(8,128)(2,1)}, u32[]{:S(2)}) copy-start(bf16[4096,48]{0,1:T(8,128)(2,1)} %param.6) | copy-start | bytes 1179652
  0.0 2.0 %copy-start.1 = (bf16[14336,48]{0,1:T(8,128)(2,1)S(1)}, bf16[14336,48]{0,1:T(8,128)(2,1)}, u32[]{:S(2)}) copy-start(bf16[14336,48]{0,1:T(8,128)(2,1)} %param.7) | copy-start | bytes 4128772
  2.0 54.3 %slice-start = ((s8[7340032]{0:T(1024)(128)(4,1)}), s8[4194304]{0:T(1024)(128)(4,1)S(1)}, s32[]{:S(2)}) async-start(s8[7340032]{0:T(1024)(128)(4,1)} %bitcast.4), calls=%async_computation | async-start | bytes 8388608
  2.1 14.3 %collective-permute-start = (bf16[48,4608]{1,0:T(8,128)(2,1)}, bf16[48,4608]{1,0:T(8,128)(2,1)S(1)}, u32[]{:S(2)}, u32[]{:S(2)}) collective-permute-start(bf16[48,4608]{1,0:T(8,128)(2,1)} %first_cut.1.refs_0_), channel_id=1, source_target_pairs={{0,4},{2,6},{4,0},{6,2},{8,12},{10,14},{12,8},{14,10},{16,20},{18,... | collective-permute-start | bytes 1327112 | tf_op jit(solution)/shard_map/ppermute | solution.py:257
  5.2 13.1 %collective-permute-start.1 = (bf16[48,4608]{1,0:T(8,128)(2,1)S(1)}, bf16[48,4608]{1,0:T(8,128)(2,1)S(1)}, u32[]{:S(2)}, u32[]{:S(2)}) collective-permute-start(bf16[48,4608]{1,0:T(8,128)(2,1)S(1)} %get-tuple-element.421.inner_ref.outer_ref.refs_2_), channel_id=1, source_target_pairs={{0,2},{2,0},{12,14},{14,12},{16,18},{18,16},{28,30},{30,28},{4,6},... | collective-permute-start | bytes 1327112 | tf_op jit(solution)/shard_map/ppermute | solution.py:257
  6.7 11.6 %collective-permute-start.2 = (bf16[48,4608]{1,0:T(8,128)(2,1)}, bf16[48,4608]{1,0:T(8,128)(2,1)S(1)}, u32[]{:S(2)}, u32[]{:S(2)}) collective-permute-start(bf16[48,4608]{1,0:T(8,128)(2,1)} %first_cut.1.refs_0_), channel_id=1, source_target_pairs={{4,8},{6,10},{8,4},{10,6},{20,24},{22,26},{24,20},{26,22},{5,9},{7... | collective-permute-start | bytes 1327112 | tf_op jit(solution)/shard_map/ppermute | solution.py:257
  7.5 18.4 %collective-permute-start.3 = (bf16[48,4608]{1,0:T(8,128)(2,1)S(1)}, bf16[48,4608]{1,0:T(8,128)(2,1)S(1)}, u32[]{:S(2)}, u32[]{:S(2)}) collective-permute-start(bf16[48,4608]{1,0:T(8,128)(2,1)S(1)} %pick.17), channel_id=1, source_target_pairs={{0,4},{2,6},{4,0},{6,2},{8,12},{10,14},{12,8},{14,10},{16,20},{18,... | collective-permute-start | bytes 1327112 | tf_op jit(solution)/shard_map/ppermute | solution.py:257
  11.9 16.0 %collective-permute-start.4 = (bf16[48,4608]{1,0:T(8,128)(2,1)}, bf16[48,4608]{1,0:T(8,128)(2,1)S(1)}, u32[]{:S(2)}, u32[]{:S(2)}) collective-permute-start(bf16[48,4608]{1,0:T(8,128)(2,1)} %first_cut.1.refs_0_), channel_id=1, source_target_pairs={{0,2},{2,0},{12,14},{14,12},{16,18},{18,16},{28,30},{30,28},{4,6},... | collective-permute-start | bytes 1327112 | tf_op jit(solution)/shard_map/ppermute | solution.py:257
  16.4 11.5 %collective-permute-start.5 = (bf16[48,4608]{1,0:T(8,128)(2,1)S(1)}, bf16[48,4608]{1,0:T(8,128)(2,1)S(1)}, u32[]{:S(2)}, u32[]{:S(2)}) collective-permute-start(bf16[48,4608]{1,0:T(8,128)(2,1)S(1)} %get-tuple-element.421.inner_ref.outer_ref.refs_2_), channel_id=1, source_target_pairs={{4,8},{6,10},{8,4},{10,6},{20,24},{22,26},{24,20},{26,22},{5,9},{7... | collective-permute-start | bytes 1327112 | tf_op jit(solution)/shard_map/ppermute | solution.py:257
  18.3 17.0 %collective-permute-start.6 = (bf16[48,4608]{1,0:T(8,128)(2,1)S(1)}, bf16[48,4608]{1,0:T(8,128)(2,1)S(1)}, u32[]{:S(2)}, u32[]{:S(2)}) collective-permute-start(bf16[48,4608]{1,0:T(8,128)(2,1)S(1)} %pick.18), channel_id=1, source_target_pairs={{0,4},{2,6},{4,0},{6,2},{8,12},{10,14},{12,8},{14,10},{16,20},{18,... | collective-permute-start | bytes 1327112 | tf_op jit(solution)/shard_map/ppermute | solution.py:257
  22.4 14.9 %collective-permute-start.7 = (bf16[48,4608]{1,0:T(8,128)(2,1)S(1)}, bf16[48,4608]{1,0:T(8,128)(2,1)S(1)}, u32[]{:S(2)}, u32[]{:S(2)}) collective-permute-start(bf16[48,4608]{1,0:T(8,128)(2,1)S(1)} %collective-permute-done.outer_ref.refs_0_), channel_id=1, source_target_pairs={{0,2},{2,0},{12,14},{14,12},{16,18},{18,16},{28,30},{30,28},{4,8},... | collective-permute-start | bytes 1327112 | tf_op jit(solution)/shard_map/ppermute | solution.py:257
  25.9 11.5 %collective-permute-start.8 = (bf16[48,4608]{1,0:T(8,128)(2,1)S(1)}, bf16[48,4608]{1,0:T(8,128)(2,1)S(1)}, u32[]{:S(2)}, u32[]{:S(2)}) collective-permute-start(bf16[48,4608]{1,0:T(8,128)(2,1)S(1)} %collective-permute-done.1.refs_3_.outer_ref), channel_id=1, source_target_pairs={{0,16},{2,18},{12,28},{14,30},{16,0},{18,2},{28,12},{30,14},{4,20}... | collective-permute-start | bytes 1327112 | tf_op jit(solution)/shard_map/ppermute | solution.py:257
  27.9 28.4 %slice-start.1 = ((s8[7340032]{0:T(1024)(128)(4,1)}), s8[3145728]{0:T(1024)(128)(4,1)S(1)}, s32[]{:S(2)}) async-start(s8[7340032]{0:T(1024)(128)(4,1)} %bitcast.4), calls=%async_computation.1 | async-start | bytes 6291456
  27.9 16.9 %collective-permute-start.9 = (bf16[48,4608]{1,0:T(8,128)(2,1)S(1)}, bf16[48,4608]{1,0:T(8,128)(2,1)S(1)}, u32[]{:S(2)}, u32[]{:S(2)}) collective-permute-start(bf16[48,4608]{1,0:T(8,128)(2,1)S(1)} %pick.19), channel_id=1, source_target_pairs={{0,4},{2,6},{4,0},{6,2},{8,12},{10,14},{12,8},{14,10},{16,20},{18,... | collective-permute-start | bytes 1327112 | tf_op jit(solution)/shard_map/ppermute | solution.py:257
  33.6 13.3 %collective-permute-start.10 = (bf16[48,4608]{1,0:T(8,128)(2,1)S(1)}, bf16[48,4608]{1,0:T(8,128)(2,1)S(1)}, u32[]{:S(2)}, u32[]{:S(2)}) collective-permute-start(bf16[48,4608]{1,0:T(8,128)(2,1)S(1)} %get-tuple-element.422.outer_ref.refs_4_), channel_id=1, source_target_pairs={{0,2},{2,0},{12,14},{14,12},{16,18},{18,16},{28,30},{30,28},{4,6},... | collective-permute-start | bytes 1327112 | tf_op jit(solution)/shard_map/ppermute | solution.py:257
  35.4 11.5 %collective-permute-start.11 = (bf16[48,4608]{1,0:T(8,128)(2,1)S(1)}, bf16[48,4608]{1,0:T(8,128)(2,1)S(1)}, u32[]{:S(2)}, u32[]{:S(2)}) collective-permute-start(bf16[48,4608]{1,0:T(8,128)(2,1)S(1)} %pick.20), channel_id=1, source_target_pairs={{0,16},{2,18},{12,28},{14,30},{16,0},{18,2},{28,12},{30,14},{4,8},... | collective-permute-start | bytes 1327112 | tf_op jit(solution)/shard_map/ppermute | solution.py:257
  37.4 16.9 %collective-permute-start.12 = (bf16[48,4608]{1,0:T(8,128)(2,1)S(1)}, bf16[48,4608]{1,0:T(8,128)(2,1)S(1)}, u32[]{:S(2)}, u32[]{:S(2)}) collective-permute-start(bf16[48,4608]{1,0:T(8,128)(2,1)S(1)} %pick.21), channel_id=1, source_target_pairs={{0,4},{2,6},{4,0},{6,2},{8,12},{10,14},{12,8},{14,10},{16,20},{18,... | collective-permute-start | bytes 1327112 | tf_op jit(solution)/shard_map/ppermute | solution.py:257
  43.1 13.2 %copy-start = (bf16[1,256,4096]{2,1,0:T(8,128)(2,1)S(1)}, bf16[1,256,4096]{2,1,0:T(8,128)(2,1)}, u32[]{:S(2)}) copy-start(bf16[1,256,4096]{2,1,0:T(8,128)(2,1)} %param.4) | copy-start | bytes 6291460
  43.1 13.2 %copy-start.2 = (bf16[48,4608]{1,0:T(8,128)(2,1)S(1)}, bf16[48,4608]{1,0:T(8,128)(2,1)}, u32[]{:S(2)}) copy-start(bf16[48,4608]{1,0:T(8,128)(2,1)} %first_cut.1.refs_0_) | copy-start | bytes 1327108
  43.1 16.3 %collective-permute-start.13 = (bf16[48,4608]{1,0:T(8,128)(2,1)S(1)}, bf16[48,4608]{1,0:T(8,128)(2,1)S(1)}, u32[]{:S(2)}, u32[]{:S(2)}) collective-permute-start(bf16[48,4608]{1,0:T(8,128)(2,1)S(1)} %pick.22), channel_id=1, source_target_pairs={{0,2},{2,0},{12,14},{14,12},{16,18},{18,16},{28,30},{30,28},{4,6},... | collective-permute-start | bytes 1327112 | tf_op jit(solution)/shard_map/ppermute | solution.py:257
  44.8 14.6 %collective-permute-start.14 = (bf16[48,4608]{1,0:T(8,128)(2,1)S(1)}, bf16[48,4608]{1,0:T(8,128)(2,1)S(1)}, u32[]{:S(2)}, u32[]{:S(2)}) collective-permute-start(bf16[48,4608]{1,0:T(8,128)(2,1)S(1)} %collective-permute-done.6.outer_ref.refs_3_.refs_1_), channel_id=1, source_target_pairs={{0,16},{2,18},{12,28},{14,30},{16,0},{18,2},{28,12},{30,14},{4,8},... | collective-permute-start | bytes 1327112 | tf_op jit(solution)/shard_map/ppermute | solution.py:257
  46.9 16.9 %collective-permute-start.15 = (bf16[48,4608]{1,0:T(8,128)(2,1)S(1)}, bf16[48,4608]{1,0:T(8,128)(2,1)S(1)}, u32[]{:S(2)}, u32[]{:S(2)}) collective-permute-start(bf16[48,4608]{1,0:T(8,128)(2,1)S(1)} %pick.23), channel_id=1, source_target_pairs={{0,4},{2,6},{4,0},{6,2},{8,12},{10,14},{12,8},{14,10},{16,20},{18,... | collective-permute-start | bytes 1327112 | tf_op jit(solution)/shard_map/ppermute | solution.py:257
  52.5 13.3 %collective-permute-start.16 = (bf16[48,4608]{1,0:T(8,128)(2,1)S(1)}, bf16[48,4608]{1,0:T(8,128)(2,1)S(1)}, u32[]{:S(2)}, u32[]{:S(2)}) collective-permute-start(bf16[48,4608]{1,0:T(8,128)(2,1)S(1)} %collective-permute-done.9.outer_ref.refs_2_.refs_0_), channel_id=1, source_target_pairs={{0,2},{2,0},{12,14},{14,12},{16,18},{18,16},{28,30},{30,28},{4,8},... | collective-permute-start | bytes 1327112 | tf_op jit(solution)/shard_map/ppermute | solution.py:257
  54.3 11.5 %collective-permute-start.17 = (bf16[48,4608]{1,0:T(8,128)(2,1)S(1)}, bf16[48,4608]{1,0:T(8,128)(2,1)S(1)}, u32[]{:S(2)}, u32[]{:S(2)}) collective-permute-start(bf16[48,4608]{1,0:T(8,128)(2,1)S(1)} %pick.24), channel_id=1, source_target_pairs={{0,16},{2,18},{12,28},{14,30},{16,0},{18,2},{28,12},{30,14},{4,20}... | collective-permute-start | bytes 1327112 | tf_op jit(solution)/shard_map/ppermute | solution.py:257
  59.5 13.8 %collective-permute-start.18 = (bf16[48,4608]{1,0:T(8,128)(2,1)S(1)}, bf16[48,4608]{1,0:T(8,128)(2,1)S(1)}, u32[]{:S(2)}, u32[]{:S(2)}) collective-permute-start(bf16[48,4608]{1,0:T(8,128)(2,1)S(1)} %pick.25), channel_id=1, source_target_pairs={{0,4},{2,6},{4,0},{6,2},{8,12},{10,14},{12,8},{14,10},{16,20},{18,... | collective-permute-start | bytes 1327112 | tf_op jit(solution)/shard_map/ppermute | solution.py:257
  62.0 13.2 %collective-permute-start.19 = (bf16[48,4608]{1,0:T(8,128)(2,1)S(1)}, bf16[48,4608]{1,0:T(8,128)(2,1)S(1)}, u32[]{:S(2)}, u32[]{:S(2)}) collective-permute-start(bf16[48,4608]{1,0:T(8,128)(2,1)S(1)} %pick.26), channel_id=1, source_target_pairs={{0,2},{2,0},{12,14},{14,12},{16,18},{18,16},{28,30},{30,28},{4,8},... | collective-permute-start | bytes 1327112 | tf_op jit(solution)/shard_map/ppermute | solution.py:257
  63.8 11.5 %collective-permute-start.20 = (bf16[48,4608]{1,0:T(8,128)(2,1)S(1)}, bf16[48,4608]{1,0:T(8,128)(2,1)S(1)}, u32[]{:S(2)}, u32[]{:S(2)}) collective-permute-start(bf16[48,4608]{1,0:T(8,128)(2,1)S(1)} %pick.27), channel_id=1, source_target_pairs={{0,16},{2,18},{12,28},{14,30},{16,0},{18,2},{28,12},{30,14},{4,20}... | collective-permute-start | bytes 1327112 | tf_op jit(solution)/shard_map/ppermute | solution.py:257
  65.8 16.2 %collective-permute-start.21 = (bf16[48,4608]{1,0:T(8,128)(2,1)S(1)}, bf16[48,4608]{1,0:T(8,128)(2,1)S(1)}, u32[]{:S(2)}, u32[]{:S(2)}) collective-permute-start(bf16[48,4608]{1,0:T(8,128)(2,1)S(1)} %collective-permute-done.16.outer_ref.refs_5_.refs_2_), channel_id=1, source_target_pairs={{0,4},{2,6},{4,0},{6,2},{8,12},{10,14},{12,8},{14,10},{16,20},{18,... | collective-permute-start | bytes 1327112 | tf_op jit(solution)/shard_map/ppermute | solution.py:257
  71.4 13.9 %collective-permute-start.22 = (bf16[48,4608]{1,0:T(8,128)(2,1)S(1)}, bf16[48,4608]{1,0:T(8,128)(2,1)S(1)}, u32[]{:S(2)}, u32[]{:S(2)}) collective-permute-start(bf16[48,4608]{1,0:T(8,128)(2,1)S(1)} %pick.28), channel_id=1, source_target_pairs={{0,2},{2,0},{12,14},{14,12},{16,18},{18,16},{28,30},{30,28},{4,6},... | collective-permute-start | bytes 1327112 | tf_op jit(solution)/shard_map/ppermute | solution.py:257
  73.3 13.1 %collective-permute-start.23 = (bf16[48,4608]{1,0:T(8,128)(2,1)S(1)}, bf16[48,4608]{1,0:T(8,128)(2,1)S(1)}, u32[]{:S(2)}, u32[]{:S(2)}) collective-permute-start(bf16[48,4608]{1,0:T(8,128)(2,1)S(1)} %pick.29), channel_id=1, source_target_pairs={{0,16},{2,18},{12,28},{14,30},{16,0},{18,2},{28,12},{30,14},{4,8},... | collective-permute-start | bytes 1327112 | tf_op jit(solution)/shard_map/ppermute | solution.py:257
  75.3 17.4 %collective-permute-start.27 = (bf16[48,4608]{1,0:T(8,128)(2,1)S(1)}, bf16[48,4608]{1,0:T(8,128)(2,1)S(1)}, u32[]{:S(2)}, u32[]{:S(2)}) collective-permute-start(bf16[48,4608]{1,0:T(8,128)(2,1)S(1)} %pick.30), channel_id=1, source_target_pairs={{0,2},{2,0},{12,14},{14,12},{16,18},{18,16},{28,30},{30,28},{4,8},... | collective-permute-start | bytes 1327112 | tf_op jit(solution)/shard_map/ppermute | solution.py:257
  76.9 19.2 %collective-permute-start.28 = (bf16[48,4608]{1,0:T(8,128)(2,1)S(1)}, bf16[48,4608]{1,0:T(8,128)(2,1)S(1)}, u32[]{:S(2)}, u32[]{:S(2)}) collective-permute-start(bf16[48,4608]{1,0:T(8,128)(2,1)S(1)} %pick.31), channel_id=1, source_target_pairs={{0,16},{2,18},{12,28},{14,30},{16,0},{18,2},{28,12},{30,14},{4,20}... | collective-permute-start | bytes 1327112 | tf_op jit(solution)/shard_map/ppermute | solution.py:257
  81.9 14.2 %collective-permute-start.29 = (bf16[48,4608]{1,0:T(8,128)(2,1)S(1)}, bf16[48,4608]{1,0:T(8,128)(2,1)S(1)}, u32[]{:S(2)}, u32[]{:S(2)}) collective-permute-start(bf16[48,4608]{1,0:T(8,128)(2,1)S(1)} %pick.32), channel_id=1, source_target_pairs={{0,4},{2,6},{4,0},{6,2},{8,12},{10,14},{12,8},{14,10},{16,20},{18,... | collective-permute-start | bytes 1327112 | tf_op jit(solution)/shard_map/ppermute | solution.py:257
  87.4 4.1 %collective-permute-start.26 = (f32[48,256]{1,0:T(8,128)S(1)}, f32[48,256]{1,0:T(8,128)S(1)}, u32[]{:S(2)}, u32[]{:S(2)}) collective-permute-start(f32[48,256]{1,0:T(8,128)S(1)} %get-tuple-element.550), channel_id=1, source_target_pairs={{0,1},{1,0},{2,3},{3,2},{4,5},{5,4},{6,7},{7,6},{8,9},{9,8},{10,11... | collective-permute-start | bytes 147464 | tf_op jit(solution)/shard_map/ppermute | solution.py:187
  87.5 14.7 %collective-permute-start.33 = (bf16[48,4608]{1,0:T(8,128)(2,1)S(1)}, bf16[48,4608]{1,0:T(8,128)(2,1)S(1)}, u32[]{:S(2)}, u32[]{:S(2)}) collective-permute-start(bf16[48,4608]{1,0:T(8,128)(2,1)S(1)} %collective-permute-done.3.inner_ref.refs_1_.refs_0_), channel_id=1, source_target_pairs={{0,2},{2,0},{12,14},{14,12},{16,18},{18,16},{28,30},{30,28},{1,3},... | collective-permute-start | bytes 1327112 | tf_op jit(solution)/shard_map/ppermute | solution.py:257
  91.5 12.3 %collective-permute-start.34 = (bf16[48,4608]{1,0:T(8,128)(2,1)S(1)}, bf16[48,4608]{1,0:T(8,128)(2,1)S(1)}, u32[]{:S(2)}, u32[]{:S(2)}) collective-permute-start(bf16[48,4608]{1,0:T(8,128)(2,1)S(1)} %pick.33), channel_id=1, source_target_pairs={{0,4},{2,6},{4,0},{6,2},{8,12},{10,14},{12,8},{14,10},{16,20},{18,... | collective-permute-start | bytes 1327112 | tf_op jit(solution)/shard_map/ppermute | solution.py:257
  92.7 13.8 %collective-permute-start.35 = (bf16[48,4608]{1,0:T(8,128)(2,1)S(1)}, bf16[48,4608]{1,0:T(8,128)(2,1)S(1)}, u32[]{:S(2)}, u32[]{:S(2)}) collective-permute-start(bf16[48,4608]{1,0:T(8,128)(2,1)S(1)} %collective-permute-done.3.inner_ref.refs_1_.refs_0_), channel_id=1, source_target_pairs={{0,16},{2,18},{12,28},{14,30},{16,0},{18,2},{28,12},{30,14},{1,17}... | collective-permute-start | bytes 1327112 | tf_op jit(solution)/shard_map/ppermute | solution.py:257
  96.1 2.9 %collective-permute-start.25 = (f32[288,256]{1,0:T(8,128)S(1)}, f32[288,256]{1,0:T(8,128)S(1)}, u32[]{:S(2)}, u32[]{:S(2)}) collective-permute-start(f32[288,256]{1,0:T(8,128)S(1)} %get-tuple-element.548.in_b), channel_id=1, source_target_pairs={{0,1},{1,0},{2,3},{3,2},{4,5},{5,4},{6,7},{7,6},{8,9},{9,8},{10,11... | collective-permute-start | bytes 884744 | tf_op jit(solution)/shard_map/ppermute | solution.py:187
  96.2 2.6 %collective-permute-start.24 = (f32[96,256]{1,0:T(8,128)S(1)}, f32[96,256]{1,0:T(8,128)S(1)}, u32[]{:S(2)}, u32[]{:S(2)}) collective-permute-start(f32[96,256]{1,0:T(8,128)S(1)} %get-tuple-element.547.in_a), channel_id=1, source_target_pairs={{0,1},{1,0},{2,3},{3,2},{4,5},{5,4},{6,7},{7,6},{8,9},{9,8},{10,11... | collective-permute-start | bytes 294920 | tf_op jit(solution)/shard_map/ppermute | solution.py:187
  98.8 1.4 %collective-permute-start.30 = (f32[96,256]{1,0:T(8,128)S(1)}, f32[96,256]{1,0:T(8,128)S(1)}, u32[]{:S(2)}, u32[]{:S(2)}) collective-permute-start(f32[96,256]{1,0:T(8,128)S(1)} %get-tuple-element.569), channel_id=1, source_target_pairs={{0,1},{1,0},{2,3},{3,2},{4,5},{5,4},{6,7},{7,6},{8,9},{9,8},{10,11... | collective-permute-start | bytes 294920 | tf_op jit(solution)/shard_map/ppermute | solution.py:187
  100.4 11.7 %collective-permute-start.39 = (bf16[48,384]{1,0:T(8,128)(2,1)S(1)}, bf16[48,384]{1,0:T(8,128)(2,1)S(1)}, u32[]{:S(2)}, u32[]{:S(2)}) collective-permute-start(bf16[48,384]{1,0:T(8,128)(2,1)S(1)} %pad_maximum_fusion), channel_id=1, source_target_pairs={{0,2},{2,0},{4,6},{6,4},{8,10},{10,8},{12,14},{14,12},{1,3},{3,1},... | collective-permute-start | bytes 110600 | tf_op jit(solution)/shard_map/ppermute | solution.py:357
  108.4 8.5 %collective-permute-start.36 = (f32[48,256]{1,0:T(8,128)S(1)}, f32[48,256]{1,0:T(8,128)S(1)}, u32[]{:S(2)}, u32[]{:S(2)}) collective-permute-start(f32[48,256]{1,0:T(8,128)S(1)} %get-tuple-element.578), channel_id=1, source_target_pairs={{0,1},{1,0},{2,3},{3,2},{4,5},{5,4},{6,7},{7,6},{8,9},{9,8},{10,11... | collective-permute-start | bytes 147464 | tf_op jit(solution)/shard_map/ppermute | solution.py:187
  108.5 6.5 %collective-permute-start.32 = (bf16[24,384]{1,0:T(8,128)(2,1)S(1)}, bf16[24,384]{1,0:T(8,128)(2,1)S(1)}, u32[]{:S(2)}, u32[]{:S(2)}) collective-permute-start(bf16[24,384]{1,0:T(8,128)(2,1)S(1)} %get-tuple-element.571), channel_id=1, source_target_pairs={{0,14},{2,12},{4,10},{6,8},{8,6},{10,4},{12,2},{14,0},{1,15},{3,13... | collective-permute-start | bytes 55304 | tf_op jit(solution)/shard_map/ppermute | solution.py:357
  111.3 5.6 %collective-permute-start.31 = (bf16[24,384]{1,0:T(8,128)(2,1)S(1)}, bf16[24,384]{1,0:T(8,128)(2,1)S(1)}, u32[]{:S(2)}, u32[]{:S(2)}) collective-permute-start(bf16[24,384]{1,0:T(8,128)(2,1)S(1)} %get-tuple-element.570), channel_id=1, source_target_pairs={{0,12},{2,14},{4,8},{6,10},{8,4},{10,6},{12,0},{14,2},{1,13},{3,15... | collective-permute-start | bytes 55304 | tf_op jit(solution)/shard_map/ppermute | solution.py:357
  112.1 10.0 %collective-permute-start.40 = (f32[24,384]{1,0:T(8,128)S(1)}, f32[24,384]{1,0:T(8,128)S(1)}, u32[]{:S(2)}, u32[]{:S(2)}) collective-permute-start(f32[24,384]{1,0:T(8,128)S(1)} %slice_add_fusion), channel_id=1, source_target_pairs={{0,8},{2,10},{4,12},{6,14},{8,0},{10,2},{12,4},{14,6},{1,9},{3,11}... | collective-permute-start | bytes 110600 | tf_op jit(solution)/shard_map/ppermute | solution.py:357
  117.1 4.7 %collective-permute-start.38 = (bf16[24,384]{1,0:T(8,128)(2,1)S(1)}, bf16[24,384]{1,0:T(8,128)(2,1)S(1)}, u32[]{:S(2)}, u32[]{:S(2)}) collective-permute-start(bf16[24,384]{1,0:T(8,128)(2,1)S(1)} %get-tuple-element.583), channel_id=1, source_target_pairs={{0,6},{2,4},{4,2},{6,0},{8,14},{10,12},{12,10},{14,8},{1,7},{3,5},... | collective-permute-start | bytes 55304 | tf_op jit(solution)/shard_map/ppermute | solution.py:357
  117.2 4.9 %collective-permute-start.37 = (bf16[24,384]{1,0:T(8,128)(2,1)S(1)}, bf16[24,384]{1,0:T(8,128)(2,1)S(1)}, u32[]{:S(2)}, u32[]{:S(2)}) collective-permute-start(bf16[24,384]{1,0:T(8,128)(2,1)S(1)} %get-tuple-element.582), channel_id=1, source_target_pairs={{0,4},{2,6},{4,0},{6,2},{8,12},{10,14},{12,8},{14,10},{1,5},{3,7},... | collective-permute-start | bytes 55304 | tf_op jit(solution)/shard_map/ppermute | solution.py:357
